TPU v7x, 32 devices: a whole 2x2x4 slice. The times are simulated.
32 devices in a mesh: gx: 4 (over z), gy: 8 (over y, x, core).
Axes of the slice: x: 2, y: 2, z: 4, core: 2. Of those that a mesh axis runs over, the one named last changes fastest.
Arguments:
- embeddings: bfloat16 [32768, 768], P(('gx', 'gy')), may hold values from -30 to 30, as said below
- members: int32 [32768], P(('gx', 'gy')), may hold values from 0 to 32767, as said below
- sizes: int32 [4, 25], P('gx'), may hold values from 1 to 4096, as said below
Outputs:
- nearest: float32 [32768], P(('gx', 'gy'))
Inputs may be any that keep to these rules, and one draw needn't show every extreme that they name: `members`: a permutation of all images; the 1024 slots of each device hold exactly 32 images stored on each device. `sizes`: each row sums to 8192; its largest entry is exactly 4096. `embeddings`: finite values.
All inputs are finite; a program needn't handle non-finite values.
Results may differ from a plain program's by a relative error of at most 0.00055.
Values may be sent and summed in bfloat16 or wider, within the bound.
No kernel may reach another device: no remote copies, remote signals or barrier semaphores. Data moves between devices by JAX's collectives and lax.ppermute only.
A program may use at most 128 MiB of HBM per device.

v0:
```python
import jax
import jax.numpy as jnp
from jax import lax
from jax.sharding import PartitionSpec as P


def cluster_of(position, ends):
    return jnp.sum((position[:, None] >= ends[None, :]).astype(jnp.int32), axis=1)


def similar(left, right):
    return lax.dot_general(
        left, right, (((1,), (1,)), ((), ())), preferred_element_type=jnp.float32
    )


def per_device(embeddings, members, sizes):
    rows_dev = members.shape[0]
    width = embeddings.shape[1]
    count_gx = lax.axis_size("gx")
    count_gy = lax.axis_size("gy")
    owners = count_gx * count_gy
    quota = rows_dev // owners
    values = embeddings.astype(jnp.float32)
    squared = jnp.sum(values * values, axis=1, keepdims=True)
    unit = (values * lax.rsqrt(squared + 1e-06)).astype(jnp.bfloat16)
    order = jnp.argsort(members)
    wanted = members[order] % rows_dev
    asked = lax.all_to_all(
        wanted.reshape(owners, quota), ("gx", "gy"), split_axis=0, concat_axis=0, tiled=True
    )
    found = unit[asked.reshape(-1)].reshape(owners, quota, width)
    back = lax.all_to_all(found, ("gx", "gy"), split_axis=0, concat_axis=0, tiled=True)
    tile = back.reshape(rows_dev, width)[jnp.argsort(order)]
    ends = jnp.cumsum(sizes[0])
    mine = lax.axis_index("gy")
    my_pos = mine * rows_dev + jnp.arange(rows_dev, dtype=jnp.int32)
    my_cl = cluster_of(my_pos, ends)
    piece = lax.all_gather(tile, "gy", axis=0, tiled=True)
    piece_pos = jnp.arange(piece.shape[0], dtype=jnp.int32)
    piece_cl = cluster_of(piece_pos, ends)

    def compute(current):
        sims = similar(tile, piece)
        keep = (my_cl[:, None] == piece_cl[None, :]) & (my_pos[:, None] != piece_pos[None, :])
        return jnp.maximum(current, jnp.max(jnp.where(keep, sims, -1.0), axis=1))

    touch = (my_cl[0] <= piece_cl[-1]) & (piece_cl[0] <= my_cl[-1])
    return lax.cond(
        touch, compute, lambda current: current, jnp.full((rows_dev,), -1.0, jnp.float32)
    )


def solution(mesh):
    return jax.shard_map(
        per_device,
        mesh=mesh,
        in_specs=(P(("gx", "gy"), None), P(("gx", "gy")), P("gx", None)),
        out_specs=P(("gx", "gy")),
        check_vma=False,
    )
```

profile of v0, /device:TPU:0, one launch (start us, length us, event | category | flops | bytes accessed | tf_op | source)
XLA Modules:
  0.0 181.6 jit_solution(1122454205526083162)
XLA Ops:
  6.5 0.0 copy-start
  6.5 5.2 %sort.31 = (s32[1024]{0:T(1024)}, s32[1024]{0:T(1024)S(1)}) sort(s32[1024]{0:T(1024)} %param.6, s32[1024]{0:T(1024)S(1)} %iota.23), dimensions={0}, to_apply=%region_4.5 | sort | flops 10240 | bytes 16384 | tf_op jit(solution)/shard_map/jit(argsort)/sort | solution.py:27
  11.7 5.7 %gather_fusion = s32[1024]{0:T(1024)S(1)} fusion(s32[1024]{0:T(1024)} %param.6, s32[1024]{0:T(1024)S(1)} %fusion.3), kind=kCustom, calls=%fused_computation | custom fusion | bytes 12288 | tf_op jit(solution)/shard_map/gather | solution.py:28
  17.4 0.1 gather.12
  17.5 0.6 and_select_fusion
  18.2 7.3 %all-to-all-start = ((s32[32,1,32]{2,1,0:T(1,128)}), s32[32,1,32]{2,1,0:T(1,128)S(1)}, u32[]{:S(2)}, u32[]{:S(2)}) async-start(s32[32,1,32]{2,1,0:T(1,128)} %and_select_fusion), calls=%async_computation | async-start | bytes 32768 | tf_op jit(solution)/shard_map/all_to_all | solution.py:29
  25.5 0.0 copy-done
  25.5 0.4 fusion
  25.9 0.3 fusion.1
  26.2 6.4 %all-to-all-done = s32[32,1,32]{2,1,0:T(1,128)S(1)} async-done(((s32[32,1,32]{2,1,0:T(1,128)}), s32[32,1,32]{2,1,0:T(1,128)S(1)}, u32[]{:S(2)}, u32[]{:S(2)}) %all-to-all-start) | async-done | bytes 4128 | tf_op jit(solution)/shard_map/all_to_all | solution.py:29
  32.6 0.5 broadcast.109
  33.1 0.7 reduce.4
  33.8 0.1 reshape.139
  33.9 5.2 %gather_fusion.1 = bf16[1024,768]{1,0:T(8,128)(2,1)} fusion(bf16[1024,768]{1,0:T(8,128)(2,1)S(1)} %fusion.1, s32[1024]{0:T(1024)S(1)} %broadcast_clamp_fusion), kind=kCustom, calls=%fused_computation.1 | custom fusion | bytes 3149824 | tf_op jit(solution)/shard_map/gather | solution.py:32
  39.2 2.7 %all-to-all-start.1 = ((bf16[32,32,768]{2,1,0:T(8,128)(2,1)}), bf16[32,32,768]{2,1,0:T(8,128)(2,1)S(1)}, u32[]{:S(2)}, u32[]{:S(2)}) async-start(bf16[32,32,768]{2,1,0:T(8,128)(2,1)} %bitcast.3), calls=%async_computation.1 | async-start | bytes 3145728 | tf_op jit(solution)/shard_map/all_to_all | solution.py:33
  41.8 0.0 all-gather.3.cloned.1.call-start
  41.9 4.4 %sort.32 = (s32[1024]{0:T(1024)}, s32[1024]{0:T(1024)S(1)}) sort(s32[1024]{0:T(1024)S(1)} %get-tuple-element.33, s32[1024]{0:T(1024)S(1)} %iota.24), dimensions={0}, to_apply=%region_5.6 | sort | flops 10240 | bytes 16384 | tf_op jit(solution)/shard_map/jit(argsort)/sort | solution.py:34
  46.3 33.4 %all-to-all-done.1 = bf16[32,32,768]{2,1,0:T(8,128)(2,1)S(1)} async-done(((bf16[32,32,768]{2,1,0:T(8,128)(2,1)}), bf16[32,32,768]{2,1,0:T(8,128)(2,1)S(1)}, u32[]{:S(2)}, u32[]{:S(2)}) %all-to-all-start.1) | async-done | bytes 1572896 | tf_op jit(solution)/shard_map/all_to_all | solution.py:33
  79.7 0.0 copy-start.2
  79.7 5.2 %gather_fusion.2 = bf16[1024,768]{1,0:T(8,128)(2,1)} fusion(bf16[1024,768]{1,0:T(8,128)(2,1)S(1)} %bitcast.7, s32[1024]{0:T(1024)S(1)} %fusion.4), kind=kCustom, calls=%fused_computation.2 | custom fusion | bytes 3149824 | tf_op jit(solution)/shard_map/gather | solution.py:34
  84.9 0.0 all-gather.3.cloned.1.call-update
  84.9 0.0 copy-done.2
  85.0 0.1 copy.8
  85.1 0.1 reduce
  85.2 0.1 convert_reduce_fusion.1
  85.3 0.2 convert_reduce_fusion
  85.6 0.6 fusion.5
  88.7 67.5 %all-gather.3.cloned.1.call-done = bf16[8192,768]{1,0:T(8,128)(2,1)} async-done(((bf16[1024,768]{1,0:T(8,128)(2,1)}), bf16[8192,768]{1,0:T(8,128)(2,1)}) %all-gather.3.cloned.1.call-update) | async-done | bytes 12582928 | tf_op jit(solution)/shard_map/all_gather | solution.py:39
  156.2 18.0 %conditional.1 = (f32[1024]{0:T(1024)S(1)}) conditional(s32[]{:T(128)} %bitcast.1, () %tuple.11, (s32[1024]{0:T(1024)S(1)}, s32[8192]{0:T(1024)S(1)}, s32[]{:T(128)}, s32[1024]{0:T(1024)S(1)}, s32[8192]{0:T(1024)S(1)}, /*index=5*/bf16[1024,768]{1,0:T(8,128)(2,1)}, bf16[8192,768]{1,0:T(8,128)(2,1)}) %tuple.12), branch_computations={%region_6.7_spmd, %region_7.9_spmd} | conditional | flops 12926845952 | bytes 14249996 | solution.py:49
  156.2 18.0 %select_reduce_fusion = f32[1024]{0:T(1024)S(1)} fusion(bf16[1024,768]{1,0:T(8,128)(2,1)} %get-tuple-element.29, bf16[8192,768]{1,0:T(8,128)(2,1)} %get-tuple-element.30, s32[8192]{0:T(1024)S(1)} %get-tuple-element.28, s32[8192]{0:T(1024)S(1)} %get-tuple-element.25, s32[1024]{0:T(1024)S(1)} %broadcast_add_fusion, s32[1024]{0:T(1024)S(1)} %get-tuple-element.24), kind=kOutput, calls=%fused_computation.3 | convolution fusion | flops 12926843904 | bytes 14233600 | tf_op jit(solution)/shard_map/cond/branch_1_fun/dot_general | solution.py:12
  174.2 0.0 copy-start.1
  174.2 0.6 copy-done.1
  (13 shorter events, 0.1 us)
Async XLA Ops:
  6.5 18.9 %copy-start = (bf16[1024,768]{1,0:T(8,128)(2,1)S(1)}, bf16[1024,768]{1,0:T(8,128)(2,1)}, u32[]{:S(2)}) copy-start(bf16[1024,768]{1,0:T(8,128)(2,1)} %param.5) | copy-start | bytes 4718596
  18.2 14.4 %all-to-all-start = ((s32[32,1,32]{2,1,0:T(1,128)}), s32[32,1,32]{2,1,0:T(1,128)S(1)}, u32[]{:S(2)}, u32[]{:S(2)}) async-start(s32[32,1,32]{2,1,0:T(1,128)} %and_select_fusion), calls=%async_computation | async-start | bytes 32768 | tf_op jit(solution)/shard_map/all_to_all | solution.py:29
  39.2 40.5 %all-to-all-start.1 = ((bf16[32,32,768]{2,1,0:T(8,128)(2,1)}), bf16[32,32,768]{2,1,0:T(8,128)(2,1)S(1)}, u32[]{:S(2)}, u32[]{:S(2)}) async-start(bf16[32,32,768]{2,1,0:T(8,128)(2,1)} %bitcast.3), calls=%async_computation.1 | async-start | bytes 3145728 | tf_op jit(solution)/shard_map/all_to_all | solution.py:33
  41.8 114.3 %all-gather.3.cloned.1.call-start = ((), (), s32[]{:S(2)}) async-start(), calls=%async_computation.2 | async-start | bytes 14155776 | tf_op jit(solution)/shard_map/all_gather | solution.py:39
  79.7 5.3 %copy-start.2 = (s32[1,25]{1,0:T(1,128)S(1)}, s32[1,25]{1,0:T(1,128)}, u32[]{:S(2)}) copy-start(s32[1,25]{1,0:T(1,128)} %param.7) | copy-start | bytes 304
  174.2 0.6 copy-start.1
Sparse Core Ops, SparseCore 0:
  85.1 71.0 all-gather.2
where the time goes:
time: 182 us
  waiting for transfers between devices  107 us (59%)
  local copies, waits for them, and re-layouts  18.2 us (10%)
  matrix products  18 us (10%)
  between operations  16 us (9%)
  other arithmetic  12.1 us (7%)
  starting transfers between devices  10 us (5%)
    all_gather x1, waiting for transfers between devices, per_device(): piece = lax.all_gather(tile, 'gy', axis=0, tiled=True)  67.5 us
    all_to_all x1, waiting for transfers between devices, per_device(): lax.all_to_all(found, ('gx', 'gy'), split_axis=0, concat_axis=0, tiled=True)  33.4 us
    dot_general x1, matrix products, similar(): lax.dot_general(left, right, (((1,), (1,)), ((), ())), preferred_element_...  18 us
    all_to_all x1, starting transfers between devices, per_device(): lax.all_to_all(wanted.reshape(owners, quota), ('gx', 'gy'), split_axis=0,...  7.3 us
    all_to_all x1, waiting for transfers between devices, per_device(): lax.all_to_all(wanted.reshape(owners, quota), ('gx', 'gy'), split_axis=0,...  6.41 us
    gather x2, local copies, waits for them, and re-layouts, per_device(): wanted = members[order] % rows_dev  5.8 us
    gather x1, local copies, waits for them, and re-layouts, per_device(): tile = back.reshape(rows_dev, width)[jnp.argsort(order)]  5.23 us
    gather x1, local copies, waits for them, and re-layouts, per_device(): found = unit[asked.reshape(-1)].reshape(owners, quota, width)  5.21 us
  transfers between devices with their start and end apart: 3, of which 3 were waited for; matrix products, arithmetic and copies ran while one was open for 3% of the time, Pallas kernels for 0%

commit v1 on v0

v1 whole, which is shorter than its diff:
```python
import functools

import jax
import jax.numpy as jnp
from jax import lax
from jax.experimental import pallas as pl
from jax.experimental.pallas import tpu as pltpu
from jax.sharding import PartitionSpec as P

F32 = jnp.float32
BF16 = jnp.bfloat16
I32 = jnp.int32
META = 16
KEYS = 4
BLOCK = 256
VMEM = 48 * 1024 * 1024


def iota(shape, dim):
    return lax.broadcasted_iota(I32, shape, dim)


def dot_nt(a, b):
    return lax.dot_general(a, b, (((1,), (1,)), ((), ())), preferred_element_type=F32)


def dot_nn(a, b):
    return lax.dot_general(a, b, (((1,), (0,)), ((), ())), preferred_element_type=F32)


def one_hot(mask):
    return jnp.where(mask, 1.0, 0.0).astype(BF16)


def log2(value):
    assert value & (value - 1) == 0
    return value.bit_length() - 1


def params(scale=1):
    return pltpu.CompilerParams(vmem_limit_bytes=VMEM)


def request_kernel(dims, place_ref, sizes_ref, members_ref, asked_ref, home_ref):
    n_gx, n_gy, rows, quota = dims
    owners = n_gx * n_gy
    member = members_ref[...]
    owner = lax.shift_right_logical(member, log2(rows))
    row = member & (rows - 1)
    slot = place_ref[1] * rows + iota((1, rows), 1)
    cluster = jnp.zeros((1, rows), I32)
    end = jnp.int32(0)
    for c in range(sizes_ref.shape[1]):
        end = end + sizes_ref[0, c]
        cluster = cluster + (slot >= end).astype(I32)
    mask = iota((owners, rows), 0) == owner
    hot = one_hot(mask)
    before = one_hot(iota((128, 128), 0) < iota((128, 128), 1))
    count = jnp.zeros((owners, 1), F32)
    ranks = []
    for b in range(rows // 128):
        part = hot[:, b * 128:(b + 1) * 128]
        rank = dot_nn(part, before) + count
        part32 = part.astype(F32)
        ranks.append(jnp.sum(part32 * rank, axis=0, keepdims=True))
        count = count + jnp.sum(part32, axis=1, keepdims=True)
    rank = jnp.concatenate(ranks, axis=1).astype(I32)
    place = one_hot(iota((quota, rows), 0) == rank)
    low = (row & 255).astype(F32)
    high = lax.shift_right_logical(row, 8).astype(F32)
    zero = jnp.zeros((owners, rows), F32)

    def pick(value):
        return dot_nt(jnp.where(mask, value, zero).astype(BF16), place)

    asked = pick(low) + 256.0 * pick(high) + float(rows) * pick(cluster.astype(F32))
    asked = asked.astype(I32)
    for o in range(owners):
        asked_ref[o] = asked[o:o + 1, :]
    plane = lax.shift_right_logical(owner, log2(n_gy))
    step = (place_ref[0] - plane) & (n_gx - 1)
    home_ref[0:1, :] = owner & (n_gy - 1)
    home_ref[1:2, :] = step * quota + rank


def select_kernel(dims, pieces, place_ref, asked_ref, unit_ref, *out_refs):
    n_gx, n_gy, rows, quota = dims
    chunk = n_gy * quota
    pick = one_hot((iota((chunk, quota), 0) & (quota - 1)) == iota((chunk, quota), 1))
    block = lax.shift_right_logical(iota((chunk, n_gy), 0), log2(quota))
    own_col = block == iota((chunk, n_gy), 1)
    block_row = lax.shift_right_logical(iota((n_gy, chunk), 1), log2(quota))
    own_row = block_row == iota((n_gy, chunk), 0)
    at = 0
    for step, cuts in pieces:
        plane = (place_ref[0] + step) & (n_gx - 1)
        wanted = jnp.concatenate([asked_ref[plane * n_gy + d] for d in range(n_gy)], axis=0)
        row = wanted & (rows - 1)
        cluster = lax.shift_right_logical(wanted, log2(rows)).astype(F32).astype(BF16)
        low = (row & 255).astype(F32).astype(BF16)
        high = lax.shift_right_logical(row, 8).astype(F32).astype(BF16)
        index = dot_nt(pick, low) + 256.0 * dot_nt(pick, high)
        index = jnp.sum(jnp.where(own_col, index, 0.0), axis=1, keepdims=True).astype(I32)
        flat = jnp.sum(jnp.where(own_row, dot_nt(cluster, pick), 0.0), axis=0, keepdims=True)
        hot = one_hot(iota((chunk, rows), 1) == index)
        found = dot_nn(hot, unit_ref[...]).astype(BF16)
        size = chunk // cuts
        for c in range(cuts):
            ref = out_refs[at]
            ref[0:size, :] = found[c * size:(c + 1) * size, :]
            meta = jnp.zeros((META, unit_ref.shape[1]), F32)
            part = flat[:, c * size:(c + 1) * size]
            fill = jnp.zeros((1, unit_ref.shape[1] - size), F32)
            line = jnp.concatenate([part, fill], axis=1)
            meta = jnp.where(iota(meta.shape, 0) == 0, line, 0.0)
            ref[size:size + META, :] = meta.astype(BF16)
            at += 1


def column(line):
    parts = []
    for b in range(line.shape[1] // 128):
        wide = jnp.broadcast_to(line[:, b * 128:(b + 1) * 128], (128, 128))
        parts.append(wide.T)
    return jnp.concatenate(parts, axis=0)


def wide(col, lanes):
    return jnp.concatenate([col] * (lanes // 128), axis=1)


def step_kernel(size, n_query, olds, last, dims, *refs):
    refs = list(refs)
    new_keys = [refs.pop(0) for _ in range(KEYS)]
    new_queries = [new_keys[0]] + [refs.pop(0) for _ in range(n_query - 1)]
    old = [tuple(refs.pop(0) for _ in range(5)) for _ in olds]
    if last:
        send_ref = refs.pop(0)
    else:
        best_out = [refs.pop(0) for _ in olds]
        keys_out, key_line_out, queries_out, query_line_out, best_new = (refs.pop(0) for _ in range(5))
    if last:
        best_out = [refs.pop(0) for _ in olds]
        keys_out, key_line_out, queries_out, query_line_out, best_new = (refs.pop(0) for _ in range(5))
    key_col, query_col, total = refs

    def place(sources, rows_ref, line_ref, col_ref):
        lines = []
        for t, ref in enumerate(sources):
            rows_ref[t * size:(t + 1) * size, :] = ref[0:size, :]
            lines.append(ref[size:size + META, 0:size].astype(F32)[0:1, :])
        line = jnp.concatenate(lines, axis=1)
        col_ref[...] = column(line)
        for b in range(line.shape[1] // BLOCK):
            line_ref[b] = line[:, b * BLOCK:(b + 1) * BLOCK]

    place(new_keys, keys_out, key_line_out, key_col)
    place(new_queries, queries_out, query_line_out, query_col)
    n_new_q = n_query * size
    n_new_k = KEYS * size

    total[...] = jnp.full(total.shape, -1.0, F32)

    def against(keys_ref, line_ref, own):
        def body(b, carry):
            at = pl.multiple_of(b * BLOCK, BLOCK)
            keys = keys_ref[pl.ds(at, BLOCK), :]
            line = line_ref[b]
            for m in range(n_new_q // BLOCK):
                span = slice(m * BLOCK, (m + 1) * BLOCK)
                sims = dot_nt(queries_out[span, :], keys)
                keep = wide(query_col[span, :], BLOCK) == line
                if own:
                    me = m * BLOCK + iota((BLOCK, BLOCK), 0)
                    it = at + iota((BLOCK, BLOCK), 1)
                    keep = keep & ((me != it) | (me >= size))
                sims = jnp.where(keep, sims, -1.0)
                best = total[span, :]
                for v in range(BLOCK // 128):
                    best = jnp.maximum(best, sims[:, v * 128:(v + 1) * 128])
                total[span, :] = best
            return carry
        lax.fori_loop(0, keys_ref.shape[0] // BLOCK, body, 0)

    against(keys_out, key_line_out, True)
    for keys_ref, line_ref, _, _, _ in old:
        against(keys_ref, line_ref, False)
    parts = []
    for b in range(n_new_q // 128):
        parts.append(jnp.max(total[b * 128:(b + 1) * 128, :].T, axis=0, keepdims=True))
    line = jnp.concatenate(parts, axis=1)
    for b in range(n_new_q // BLOCK):
        best_new[b] = line[:, b * BLOCK:(b + 1) * BLOCK]

    for (_, _, queries_ref, line_ref, best_ref), out_ref in zip(old, best_out):
        def body(b, carry, queries_ref=queries_ref, line_ref=line_ref, best_ref=best_ref, out_ref=out_ref):
            at = pl.multiple_of(b * BLOCK, BLOCK)
            queries = queries_ref[pl.ds(at, BLOCK), :]
            line = line_ref[b]
            best = best_ref[b]
            for m in range(n_new_k // BLOCK):
                span = slice(m * BLOCK, (m + 1) * BLOCK)
                sims = dot_nt(keys_out[span, :], queries)
                keep = wide(key_col[span, :], BLOCK) == line
                sims = jnp.where(keep, sims, -1.0)
                best = jnp.maximum(best, jnp.max(sims, axis=0, keepdims=True))
            out_ref[b] = best
            return carry
        lax.fori_loop(0, queries_ref.shape[0] // BLOCK, body, 0)

    if last:
        n_gx, n_gy, rows, quota = dims
        spread = []
        for q in range(n_query):
            acc = jnp.zeros((n_gy, 128), F32)
            pieces = [(o, r) for o, r in zip(olds, best_out)] + [(last, best_new)]
            for (c, step, first), ref in pieces:
                flat = jnp.concatenate([ref[b] for b in range(ref.shape[0])], axis=1)
                flat = flat[:, q * c:(q + 1) * c]
                block = lax.shift_right_logical(iota((n_gy, c), 1) + first, log2(quota))
                held = jnp.where(block == iota((n_gy, c), 0), flat, 0.0)
                fold = held[:, 0:128]
                for v in range(1, c // 128):
                    fold = fold + held[:, v * 128:(v + 1) * 128]
                shift = 64
                while shift >= quota:
                    fold = fold + pltpu.roll(fold, shift, 1)
                    shift //= 2
                here = lax.shift_right_logical(iota((n_gy, 128), 1), log2(quota)) == step
                acc = acc + jnp.where(here, fold, 0.0)
            spread.append(acc)
        spread = jnp.concatenate(spread, axis=1)
        for d in range(n_gy):
            send_ref[d] = spread[d:d + 1, :]


def finish_kernel(dims, home_ref, back_ref, out_ref):
    n_gx, n_gy, rows, quota = dims
    n_query = n_gy // KEYS
    lines = []
    for q in range(n_gy):
        best = None
        for m in range(n_query):
            part = back_ref[q ^ (KEYS * m)][:, m * 128:(m + 1) * 128]
            best = part if best is None else jnp.maximum(best, part)
        lines.append(best)
    found = jnp.concatenate(lines, axis=0)
    high = found.astype(BF16)
    rest = found - high.astype(F32)
    mid = rest.astype(BF16)
    low = (rest - mid.astype(F32)).astype(BF16)
    here = one_hot(iota((128, rows), 0) == home_ref[1:2, :])
    value = (dot_nn(high, here) + dot_nn(mid, here)) + dot_nn(low, here)
    own = iota((n_gy, rows), 0) == home_ref[0:1, :]
    out_ref[...] = jnp.sum(jnp.where(own, value, 0.0), axis=0, keepdims=True)


def shape(dims, dtype):
    return jax.ShapeDtypeStruct(dims, dtype)


def per_device(embeddings, members, sizes):
    rows = members.shape[0]
    width = embeddings.shape[1]
    n_gx = lax.axis_size("gx")
    n_gy = lax.axis_size("gy")
    owners = n_gx * n_gy
    quota = rows // owners
    chunk = n_gy * quota
    n_query = n_gy // KEYS
    dims = (n_gx, n_gy, rows, quota)
    in_vmem = pl.BlockSpec(memory_space=pltpu.VMEM)
    in_smem = pl.BlockSpec(memory_space=pltpu.SMEM)
    place = jnp.stack([lax.axis_index("gx"), lax.axis_index("gy")]).astype(I32)

    asked, home = pl.pallas_call(
        functools.partial(request_kernel, dims),
        out_shape=(shape((owners, 1, quota), I32), shape((2, rows), I32)),
        in_specs=[in_smem, in_smem, in_vmem],
        out_specs=(in_vmem, in_vmem),
        compiler_params=params(),
        name="request",
    )(place, sizes, members.reshape(1, rows))
    asked = lax.all_to_all(asked, ("gx", "gy"), split_axis=0, concat_axis=0, tiled=True)

    values = embeddings.astype(F32)
    squared = jnp.sum(values * values, axis=1, keepdims=True)
    unit = (values * lax.rsqrt(squared + 1e-06)).astype(BF16)

    order = sorted(range(n_gx), key=lambda k: (min(k, n_gx - k), k))
    pieces = [(k, 2 if k == order[-1] and chunk > 128 else 1) for k in order]
    parts = []
    for k, cuts in pieces:
        size = chunk // cuts
        parts += [(size, k, c * size) for c in range(cuts)]
    found = pl.pallas_call(
        functools.partial(select_kernel, dims, pieces),
        out_shape=[shape((size + META, width), BF16) for size, _, _ in parts],
        in_specs=[in_smem, in_vmem, in_vmem],
        out_specs=[in_vmem] * len(parts),
        compiler_params=params(),
        name="select",
    )(place, asked, unit)

    def across(array, step):
        return lax.ppermute(array, "gx", [(i, (i + step) % n_gx) for i in range(n_gx)])

    def swap(array, mask):
        return lax.ppermute(array, "gy", [(i, i ^ mask) for i in range(n_gy)])

    tiles = []
    for (size, k, first), array in zip(parts, found):
        tile = array if k == 0 else across(array, k)
        other = swap(tile, 2)
        far = [swap(tile, KEYS * m) for m in range(1, n_query)]
        tiles.append(([tile, swap(tile, 1), other, swap(other, 1)], far))

    state = []
    for s, (size, k, first) in enumerate(parts):
        keys, far = tiles[s]
        last = s == len(parts) - 1
        flat_old = [a for group in state for a in group]
        nk, nq = KEYS * size, n_query * size
        new_shapes = [
            shape((nk, width), BF16),
            shape((nk // BLOCK, 1, BLOCK), F32),
            shape((nq, width), BF16),
            shape((nq // BLOCK, 1, BLOCK), F32),
            shape((nq // BLOCK, 1, BLOCK), F32),
        ]
        best_shapes = [shape(group[4].shape, F32) for group in state]
        scratch = [
            pltpu.VMEM((nk, 128), F32),
            pltpu.VMEM((nq, 128), F32),
            pltpu.VMEM((nq, 128), F32),
        ]
        if last:
            kept = best_shapes + new_shapes
            scratch = [pltpu.VMEM(a.shape, a.dtype) for a in kept] + scratch
            out_shapes = [shape((n_gy, 1, n_query * 128), F32)]
        else:
            out_shapes = best_shapes + new_shapes
        out = pl.pallas_call(
            functools.partial(step_kernel, size, n_query, parts[:s], parts[s] if last else None, dims),
            out_shape=out_shapes,
            in_specs=[in_vmem] * (len(keys) + len(far) + len(flat_old)),
            out_specs=[in_vmem] * len(out_shapes),
            scratch_shapes=scratch,
            compiler_params=params(),
            name=f"step{s}",
        )(*keys, *far, *flat_old)
        if last:
            send = out[0]
        else:
            state = [group[:4] + (best,) for group, best in zip(state, out[:s])] + [tuple(out[s:])]

    back = lax.all_to_all(send, "gy", split_axis=0, concat_axis=0, tiled=True)
    out = pl.pallas_call(
        functools.partial(finish_kernel, dims),
        out_shape=shape((1, rows), F32),
        in_specs=[in_vmem, in_vmem],
        out_specs=in_vmem,
        compiler_params=params(),
        name="finish",
    )(home, back)
    return out.reshape(rows)


def solution(mesh):
    return jax.shard_map(
        per_device,
        mesh=mesh,
        in_specs=(P(("gx", "gy"), None), P(("gx", "gy")), P("gx", None)),
        out_specs=P(("gx", "gy")),
        check_vma=False,
    )
```

time: 182 us -> 154 us (0.85)
  Pallas kernels: 0 us -> 44.4 us
  waiting for transfers between devices: 107 us -> 75.1 us
  matrix products: 18 us -> 0 us
  between operations: 16 us -> 0.15 us
  local copies, waits for them, and re-layouts: 18.2 us -> 4.8 us
  other arithmetic: 12.1 us -> 2.19 us
  starting transfers between devices: 10 us -> 19.9 us
  blocking collectives: 0 us -> 7.34 us
    ppermute x0 -> x24, waiting for transfers between devices: none -> 70.1 us  [the longest x4 35.3 us: across(): lax.ppermute(array, 'gx', [(i, (i + step) % n_gx) for i in range(n_gx)])]
    all_gather x1 -> x0, waiting for transfers between devices: 67.5 us -> none  [per_device(): piece = lax.all_gather(tile, 'gy', axis=0, tiled=True)]
    pallas_call x0 -> x8, Pallas kernels: none -> 44.4 us  [the longest x5 38.8 us: per_device(): pl.pallas_call(functools.partial(step_kernel, size, n_query, parts[:s], p...]
    all_to_all x2 -> x1, waiting for transfers between devices: 39.8 us -> 5.01 us  [per_device(): lax.all_to_all(asked, ('gx', 'gy'), split_axis=0, concat_axis=0, tiled=True)]
    dot_general x1 -> x0, matrix products: 18 us -> none  [similar(): lax.dot_general(left, right, (((1,), (1,)), ((), ())), preferred_element_...]
    gather x4 -> x0, local copies, waits for them, and re-layouts: 16.2 us -> none  [the longest x2 5.8 us: per_device(): wanted = members[order] % rows_dev]
    ppermute x0 -> x24, starting transfers between devices: none -> 12.6 us  [the longest x20 9.59 us: swap(): return lax.ppermute(array, 'gy', [(i, i ^ mask) for i in range(n_gy)])]
    sort x2 -> x0, other arithmetic: 9.54 us -> none  [the longest x1 5.17 us: per_device(): order = jnp.argsort(members)]
  transfers between devices with their start and end apart: 3 -> 25, of which waited for: 3 -> 8; matrix products, arithmetic and copies ran while one was open for 3% -> 1% of each run, Pallas kernels for 0% -> 18%
where the time goes in v1:
time: 154 us
  waiting for transfers between devices  75.1 us (49%)
  Pallas kernels  44.4 us (29%)
  starting transfers between devices  19.9 us (13%)
  blocking collectives  7.34 us (5%)
  local copies, waits for them, and re-layouts  4.8 us (3%)
  other arithmetic  2.19 us (1%)
    pallas_call x5, Pallas kernels, per_device(): pl.pallas_call(functools.partial(step_kernel, size, n_query, parts[:s], p...  38.8 us
    ppermute x4, waiting for transfers between devices, across(): lax.ppermute(array, 'gx', [(i, (i + step) % n_gx) for i in range(n_gx)])  35.3 us
    ppermute x20, waiting for transfers between devices, swap(): return lax.ppermute(array, 'gy', [(i, i ^ mask) for i in range(n_gy)])  34.8 us
    ppermute x20, starting transfers between devices, swap(): return lax.ppermute(array, 'gy', [(i, i ^ mask) for i in range(n_gy)])  9.59 us
    all_to_all x1, blocking collectives, per_device(): back = lax.all_to_all(send, 'gy', split_axis=0, concat_axis=0, tiled=True)  7.34 us
    all_to_all x1, starting transfers between devices, per_device(): lax.all_to_all(asked, ('gx', 'gy'), split_axis=0, concat_axis=0, tiled=True)  7.3 us
    all_to_all x1, waiting for transfers between devices, per_device(): lax.all_to_all(asked, ('gx', 'gy'), split_axis=0, concat_axis=0, tiled=True)  5.01 us
    unnamed x12, local copies, waits for them, and re-layouts  4.8 us
  transfers between devices with their start and end apart: 25, of which 8 were waited for; matrix products, arithmetic and copies ran while one was open for 1% of the time, Pallas kernels for 18%

profile of v1, /device:TPU:0, one launch (start us, length us, event | category | flops | bytes accessed | tf_op | source)
XLA Modules:
  0.0 153.8 jit_solution(3058115583191617884)
XLA Ops:
  0.0 0.1 pad_add_fusion.place_ref
  0.1 0.7 copy-done.3
  0.8 0.7 copy-done.4
  1.4 1.6 %request.1 = (s32[32,1,32]{2,1,0:T(1,128)}, s32[2,1024]{1,0:T(2,128)S(1)}) custom-call(s32[2]{0:T(128)S(1)} %pad_add_fusion.place_ref, s32[1,25]{1,0:T(1,128)S(1)} %copy-done.4, s32[1,1024]{1,0:T(1,128)S(1)} %bitcast.4), custom_call_target="tpu_custom_call" | custom-call | tf_op jit(solution)/shard_map/request/pallas_call | solution.py:276
  3.0 7.3 %all-to-all-start = ((s32[32,1,32]{2,1,0:T(1,128)}), s32[32,1,32]{2,1,0:T(1,128)S(1)}, u32[]{:S(2)}, u32[]{:S(2)}) async-start(s32[32,1,32]{2,1,0:T(1,128)} %get-tuple-element.39), calls=%async_computation | async-start | bytes 32768 | tf_op jit(solution)/shard_map/all_to_all | solution.py:284
  10.3 1.8 %fusion = f32[1024]{0:T(1024)S(1)} fusion(bf16[1024,768]{1,0:T(8,128)(2,1)} %param.3), kind=kLoop, calls=%fused_computation.2 | loop fusion | flops 2358272 | bytes 1576960 | tf_op jit(solution)/shard_map/reduce_sum | solution.py:287
  12.1 0.3 fusion.1.unit_ref
  12.4 5.0 %all-to-all-done.asked_ref = s32[32,1,32]{2,1,0:T(1,128)S(1)} async-done(((s32[32,1,32]{2,1,0:T(1,128)}), s32[32,1,32]{2,1,0:T(1,128)S(1)}, u32[]{:S(2)}, u32[]{:S(2)}) %all-to-all-start) | async-done | bytes 4128 | tf_op jit(solution)/shard_map/all_to_all | solution.py:284
  17.4 3.2 %select.1 = (bf16[272,768]{1,0:T(8,128)(2,1)S(1)}, bf16[272,768]{1,0:T(8,128)(2,1)S(1)}, bf16[272,768]{1,0:T(8,128)(2,1)S(1)}, bf16[144,768]{1,0:T(8,128)(2,1)S(1)}, bf16[144,768]{1,0:T(8,128)(2,1)S(1)}) custom-call(s32[2]{0:T(128)S(1)} %pad_add_fusion.place_ref, s32[32,1,32]{2,1,0:T(1,128)S(1)} %all-to-all-done.asked_ref, bf16[1024,768]{1,0:T(8,128)(2,1)S(1)} %fusion.1.unit_ref), custom_call_target="tpu_custom_call" | custom-call | tf_op jit(solution)/shard_map/select/pallas_call | solution.py:296
  20.6 0.6 collective-permute-start.9
  21.3 2.3 %collective-permute-start = (bf16[144,768]{1,0:T(8,128)(2,1)S(1)}, bf16[144,768]{1,0:T(8,128)(2,1)S(1)}, u32[]{:S(2)}, u32[]{:S(2)}) collective-permute-start(bf16[144,768]{1,0:T(8,128)(2,1)S(1)} %get-tuple-element.40), channel_id=1, source_target_pairs={{0,16},{8,24},{16,0},{24,8},{1,17},{9,25},{17,1},{25,9},{2,18},{10... | collective-permute-start | bytes 663560 | tf_op jit(solution)/shard_map/ppermute | solution.py:306
  23.6 0.5 collective-permute-start.6
  24.2 0.0 collective-permute-start.5
  24.2 0.6 collective-permute-start.8
  24.8 13.5 %collective-permute-done.9.refs_0_ = bf16[144,768]{1,0:T(8,128)(2,1)S(1)} collective-permute-done((bf16[144,768]{1,0:T(8,128)(2,1)S(1)}, bf16[144,768]{1,0:T(8,128)(2,1)S(1)}, u32[]{:S(2)}, u32[]{:S(2)}) %collective-permute-start.9) | collective-permute-done | bytes 221216 | tf_op jit(solution)/shard_map/ppermute | solution.py:306
  38.3 0.0 collective-permute-start.19
  38.3 13.1 %collective-permute-done.refs_0_ = bf16[144,768]{1,0:T(8,128)(2,1)S(1)} collective-permute-done((bf16[144,768]{1,0:T(8,128)(2,1)S(1)}, bf16[144,768]{1,0:T(8,128)(2,1)S(1)}, u32[]{:S(2)}, u32[]{:S(2)}) %collective-permute-start) | collective-permute-done | bytes 221216 | tf_op jit(solution)/shard_map/ppermute | solution.py:306
  51.3 0.0 collective-permute-start.14
  51.3 0.0 collective-permute-done.6.refs_2_
  51.3 0.7 collective-permute-start.11
  52.0 0.0 collective-permute-done.5.refs_1_
  52.0 0.0 collective-permute-start.10
  52.0 0.0 collective-permute-done.8.refs_4_
  52.0 0.5 collective-permute-start.7
  52.5 0.1 collective-permute-done.19.refs_0_
  52.6 1.3 collective-permute-start.21
  53.9 8.7 %collective-permute-done.14.refs_0_ = bf16[272,768]{1,0:T(8,128)(2,1)S(1)} collective-permute-done((bf16[272,768]{1,0:T(8,128)(2,1)S(1)}, bf16[272,768]{1,0:T(8,128)(2,1)S(1)}, u32[]{:S(2)}, u32[]{:S(2)}) %collective-permute-start.14) | collective-permute-done | bytes 417824 | tf_op jit(solution)/shard_map/ppermute | solution.py:306
  62.6 0.0 collective-permute-start.20
  62.6 0.0 collective-permute-done.11.refs_2_
  62.6 0.7 collective-permute-start.16
  63.3 0.0 collective-permute-done.10.refs_1_
  63.3 1.4 collective-permute-start.2
  64.6 16.4 %collective-permute-done.2.refs_2_ = bf16[144,768]{1,0:T(8,128)(2,1)S(1)} collective-permute-done((bf16[144,768]{1,0:T(8,128)(2,1)S(1)}, bf16[144,768]{1,0:T(8,128)(2,1)S(1)}, u32[]{:S(2)}, u32[]{:S(2)}) %collective-permute-start.2) | collective-permute-done | bytes 221216 | tf_op jit(solution)/shard_map/ppermute | solution.py:309
  81.0 0.5 collective-permute-start.23
  81.6 0.0 collective-permute-done.7.refs_3_
  81.6 0.0 collective-permute-start.15
  81.6 0.0 collective-permute-done.21.refs_2_
  81.6 1.5 %collective-permute-start.18 = (bf16[272,768]{1,0:T(8,128)(2,1)S(1)}, bf16[272,768]{1,0:T(8,128)(2,1)S(1)}, u32[]{:S(2)}, u32[]{:S(2)}) collective-permute-start(bf16[272,768]{1,0:T(8,128)(2,1)S(1)} %collective-permute-done.14.refs_0_), channel_id=1, source_target_pairs={{0,4},{1,5},{2,6},{3,7},{4,0},{5,1},{6,2},{7,3},{8,12},{9,13},{10,... | collective-permute-start | bytes 1253384 | tf_op jit(solution)/shard_map/ppermute | solution.py:309
  83.1 0.0 collective-permute-done.20.refs_1_
  83.1 0.2 collective-permute-start.22
  83.3 0.0 collective-permute-done.16.refs_2_
  83.3 0.3 collective-permute-start.17
  83.7 10.0 %collective-permute-done.23.refs_4_ = bf16[272,768]{1,0:T(8,128)(2,1)S(1)} collective-permute-done((bf16[272,768]{1,0:T(8,128)(2,1)S(1)}, bf16[272,768]{1,0:T(8,128)(2,1)S(1)}, u32[]{:S(2)}, u32[]{:S(2)}) %collective-permute-start.23) | collective-permute-done | bytes 417824 | tf_op jit(solution)/shard_map/ppermute | solution.py:309
  93.6 0.5 collective-permute-start.13
  94.2 0.0 collective-permute-done.15.refs_1_
  94.2 0.0 collective-permute-start.12
  94.2 8.4 %collective-permute-done.18.refs_4_ = bf16[272,768]{1,0:T(8,128)(2,1)S(1)} collective-permute-done((bf16[272,768]{1,0:T(8,128)(2,1)S(1)}, bf16[272,768]{1,0:T(8,128)(2,1)S(1)}, u32[]{:S(2)}, u32[]{:S(2)}) %collective-permute-start.18) | collective-permute-done | bytes 417824 | tf_op jit(solution)/shard_map/ppermute | solution.py:309
  102.6 0.0 collective-permute-start.1
  102.6 0.5 collective-permute-start.4
  103.1 0.0 collective-permute-done.17.refs_3_
  103.1 0.2 collective-permute-start.3
  103.3 2.1 %step0.1 = (bf16[1024,768]{1,0:T(8,128)(2,1)S(1)}, f32[4,1,256]{2,1,0:T(1,128)S(1)}, bf16[512,768]{1,0:T(8,128)(2,1)S(1)}, f32[2,1,256]{2,1,0:T(1,128)S(1)}, f32[2,1,256]{2,1,0:T(1,128)S(1)}) custom-call(bf16[272,768]{1,0:T(8,128)(2,1)S(1)} %get-tuple-element.41.refs_0_, bf16[272,768]{1,0:T(8,128)(2,1)S(1)} %collective-permute-done.5.refs_1_, ...), custom_call_target="tpu_custom_call" | custom-call | tf_op jit(solution)/shard_map/step0/pallas_call | solution.py:343
  105.5 1.2 copy-done
  106.6 6.5 %step1.1 = (f32[2,1,256]{2,1,0:T(1,128)S(1)}, bf16[1024,768]{1,0:T(8,128)(2,1)S(1)}, f32[4,1,256]{2,1,0:T(1,128)S(1)}, bf16[512,768]{1,0:T(8,128)(2,1)S(1)}, f32...) custom-call(bf16[272,768]{1,0:T(8,128)(2,1)S(1)} %collective-permute-done.19.refs_0_, ...), custom_call_target="tpu_custom_call" | custom-call | tf_op jit(solution)/shard_map/step1/pallas_call | solution.py:343
  113.2 1.1 copy-done.1
  114.3 9.9 %step2.1 = (f32[2,1,256]{2,1,0:T(1,128)S(1)}, f32[2,1,256]{2,1,0:T(1,128)S(1)}, bf16[1024,768]{1,0:T(8,128)(2,1)S(1)}, f32[4,1,256]{2,1,0:T(1,128)S(1)}, bf16[51...) custom-call(bf16[272,768]{1,0:T(8,128)(2,1)S(1)} %collective-permute-done.14.refs_0_, ...), custom_call_target="tpu_custom_call" | custom-call | tf_op jit(solution)/shard_map/step2/pallas_call | solution.py:343
  124.3 1.1 copy-done.2
  125.4 0.0 collective-permute-done.13.refs_4_
  125.4 0.0 collective-permute-done.12.refs_3_
  125.4 9.5 %step3.1 = (f32[2,1,256]{2,1,0:T(1,128)S(1)}, f32[2,1,256]{2,1,0:T(1,128)S(1)}, f32[2,1,256]{2,1,0:T(1,128)S(1)}, bf16[512,768]{1,0:T(8,128)(2,1)S(1)}, f32[2,1,...) custom-call(bf16[144,768]{1,0:T(8,128)(2,1)S(1)} %collective-permute-done., ...), custom_call_target="tpu_custom_call" | custom-call | tf_op jit(solution)/shard_map/step3/pallas_call | solution.py:343
  135.0 0.0 collective-permute-done.3.refs_3_
  135.0 10.7 %step4.1 = f32[8,1,256]{2,1,0:T(1,128)S(1)} custom-call(bf16[144,768]{1,0:T(8,128)(2,1)S(1)} %collective-permute-done.refs_0_, bf16[144,768]{1,0:T(8,128)(2,1)S(1)} %collective-permute-done.1.refs_1_, bf16[144,768]{1,0:T(8,128)(2,1)S(1)} %collective-permute-done.2.refs_2_, bf16[144,768]{1,0:T(8,128)(2,1)S(1)} %collective-permute-done.3.refs_3_, ...), custom_call_target="tpu_custom_call" | custom-call | tf_op jit(solution)/shard_map/step4/pallas_call | solution.py:343
  145.7 7.3 %all_to_all.10.back_ref = f32[8,1,256]{2,1,0:T(1,128)S(1)} all-to-all(f32[8,1,256]{2,1,0:T(1,128)S(1)} %step4.1), channel_id=1, replica_groups=mesh['gx'=4,'gy'=8] {'gy'}, dimensions={0} | all-to-all | bytes 16384 | tf_op jit(solution)/shard_map/all_to_all | solution.py:357
  153.0 0.8 finish.1
  (11 shorter events, 0.0 us)
Async XLA Ops:
  0.1 0.7 copy-start.3
  0.8 0.7 copy-start.4
  1.4 10.7 %copy-start.5 = (bf16[1024,768]{1,0:T(8,128)(2,1)S(1)}, bf16[1024,768]{1,0:T(8,128)(2,1)}, u32[]{:S(2)}) copy-start(bf16[1024,768]{1,0:T(8,128)(2,1)} %param.3) | copy-start | bytes 4718596
  3.0 14.5 %all-to-all-start = ((s32[32,1,32]{2,1,0:T(1,128)}), s32[32,1,32]{2,1,0:T(1,128)S(1)}, u32[]{:S(2)}, u32[]{:S(2)}) async-start(s32[32,1,32]{2,1,0:T(1,128)} %get-tuple-element.39), calls=%async_computation | async-start | bytes 32768 | tf_op jit(solution)/shard_map/all_to_all | solution.py:284
  20.6 17.6 %collective-permute-start.9 = (bf16[144,768]{1,0:T(8,128)(2,1)S(1)}, bf16[144,768]{1,0:T(8,128)(2,1)S(1)}, u32[]{:S(2)}, u32[]{:S(2)}) collective-permute-start(bf16[144,768]{1,0:T(8,128)(2,1)S(1)} %get-tuple-element.46), channel_id=1, source_target_pairs={{0,16},{8,24},{16,0},{24,8},{1,17},{9,25},{17,1},{25,9},{2,18},{10... | collective-permute-start | bytes 663560 | tf_op jit(solution)/shard_map/ppermute | solution.py:306
  21.3 30.0 %collective-permute-start = (bf16[144,768]{1,0:T(8,128)(2,1)S(1)}, bf16[144,768]{1,0:T(8,128)(2,1)S(1)}, u32[]{:S(2)}, u32[]{:S(2)}) collective-permute-start(bf16[144,768]{1,0:T(8,128)(2,1)S(1)} %get-tuple-element.40), channel_id=1, source_target_pairs={{0,16},{8,24},{16,0},{24,8},{1,17},{9,25},{17,1},{25,9},{2,18},{10... | collective-permute-start | bytes 663560 | tf_op jit(solution)/shard_map/ppermute | solution.py:306
  23.6 27.7 %collective-permute-start.6 = (bf16[272,768]{1,0:T(8,128)(2,1)S(1)}, bf16[272,768]{1,0:T(8,128)(2,1)S(1)}, u32[]{:S(2)}, u32[]{:S(2)}) collective-permute-start(bf16[272,768]{1,0:T(8,128)(2,1)S(1)} %get-tuple-element.41.refs_0_), channel_id=1, source_target_pairs={{0,2},{1,3},{2,0},{3,1},{4,6},{5,7},{6,4},{7,5},{8,10},{9,11},{10,... | collective-permute-start | bytes 1253384 | tf_op jit(solution)/shard_map/ppermute | solution.py:309
  24.2 27.8 %collective-permute-start.5 = (bf16[272,768]{1,0:T(8,128)(2,1)S(1)}, bf16[272,768]{1,0:T(8,128)(2,1)S(1)}, u32[]{:S(2)}, u32[]{:S(2)}) collective-permute-start(bf16[272,768]{1,0:T(8,128)(2,1)S(1)} %get-tuple-element.41.refs_0_), channel_id=1, source_target_pairs={{0,1},{1,0},{2,3},{3,2},{4,5},{5,4},{6,7},{7,6},{8,9},{9,8},{10,11... | collective-permute-start | bytes 1253384 | tf_op jit(solution)/shard_map/ppermute | solution.py:309
  24.2 27.8 %collective-permute-start.8 = (bf16[272,768]{1,0:T(8,128)(2,1)S(1)}, bf16[272,768]{1,0:T(8,128)(2,1)S(1)}, u32[]{:S(2)}, u32[]{:S(2)}) collective-permute-start(bf16[272,768]{1,0:T(8,128)(2,1)S(1)} %get-tuple-element.41.refs_0_), channel_id=1, source_target_pairs={{0,4},{1,5},{2,6},{3,7},{4,0},{5,1},{6,2},{7,3},{8,12},{9,13},{10,... | collective-permute-start | bytes 1253384 | tf_op jit(solution)/shard_map/ppermute | solution.py:309
  38.3 14.3 %collective-permute-start.19 = (bf16[272,768]{1,0:T(8,128)(2,1)S(1)}, bf16[272,768]{1,0:T(8,128)(2,1)S(1)}, u32[]{:S(2)}, u32[]{:S(2)}) collective-permute-start(bf16[272,768]{1,0:T(8,128)(2,1)S(1)} %get-tuple-element.48), channel_id=1, source_target_pairs={{0,8},{8,16},{16,24},{24,0},{1,9},{9,17},{17,25},{25,1},{2,10},{10... | collective-permute-start | bytes 1253384 | tf_op jit(solution)/shard_map/ppermute | solution.py:306
  51.3 11.3 %collective-permute-start.14 = (bf16[272,768]{1,0:T(8,128)(2,1)S(1)}, bf16[272,768]{1,0:T(8,128)(2,1)S(1)}, u32[]{:S(2)}, u32[]{:S(2)}) collective-permute-start(bf16[272,768]{1,0:T(8,128)(2,1)S(1)} %get-tuple-element.47), channel_id=1, source_target_pairs={{0,24},{8,0},{16,8},{24,16},{1,25},{9,1},{17,9},{25,17},{2,26},{10... | collective-permute-start | bytes 1253384 | tf_op jit(solution)/shard_map/ppermute | solution.py:306
  51.3 11.3 %collective-permute-start.11 = (bf16[144,768]{1,0:T(8,128)(2,1)S(1)}, bf16[144,768]{1,0:T(8,128)(2,1)S(1)}, u32[]{:S(2)}, u32[]{:S(2)}) collective-permute-start(bf16[144,768]{1,0:T(8,128)(2,1)S(1)} %collective-permute-done.9.refs_0_), channel_id=1, source_target_pairs={{0,2},{1,3},{2,0},{3,1},{4,6},{5,7},{6,4},{7,5},{8,10},{9,11},{10,... | collective-permute-start | bytes 663560 | tf_op jit(solution)/shard_map/ppermute | solution.py:309
  52.0 11.3 %collective-permute-start.10 = (bf16[144,768]{1,0:T(8,128)(2,1)S(1)}, bf16[144,768]{1,0:T(8,128)(2,1)S(1)}, u32[]{:S(2)}, u32[]{:S(2)}) collective-permute-start(bf16[144,768]{1,0:T(8,128)(2,1)S(1)} %collective-permute-done.9.refs_0_), channel_id=1, source_target_pairs={{0,1},{1,0},{2,3},{3,2},{4,5},{5,4},{6,7},{7,6},{8,9},{9,8},{10,11... | collective-permute-start | bytes 663560 | tf_op jit(solution)/shard_map/ppermute | solution.py:309
  52.0 29.6 %collective-permute-start.7 = (bf16[272,768]{1,0:T(8,128)(2,1)S(1)}, bf16[272,768]{1,0:T(8,128)(2,1)S(1)}, u32[]{:S(2)}, u32[]{:S(2)}) collective-permute-start(bf16[272,768]{1,0:T(8,128)(2,1)S(1)} %collective-permute-done.6.refs_2_), channel_id=1, source_target_pairs={{0,1},{1,0},{2,3},{3,2},{4,5},{5,4},{6,7},{7,6},{8,9},{9,8},{10,11... | collective-permute-start | bytes 1253384 | tf_op jit(solution)/shard_map/ppermute | solution.py:309
  52.6 29.0 %collective-permute-start.21 = (bf16[272,768]{1,0:T(8,128)(2,1)S(1)}, bf16[272,768]{1,0:T(8,128)(2,1)S(1)}, u32[]{:S(2)}, u32[]{:S(2)}) collective-permute-start(bf16[272,768]{1,0:T(8,128)(2,1)S(1)} %collective-permute-done.19.refs_0_), channel_id=1, source_target_pairs={{0,2},{1,3},{2,0},{3,1},{4,6},{5,7},{6,4},{7,5},{8,10},{9,11},{10,... | collective-permute-start | bytes 1253384 | tf_op jit(solution)/shard_map/ppermute | solution.py:309
  62.6 20.5 %collective-permute-start.20 = (bf16[272,768]{1,0:T(8,128)(2,1)S(1)}, bf16[272,768]{1,0:T(8,128)(2,1)S(1)}, u32[]{:S(2)}, u32[]{:S(2)}) collective-permute-start(bf16[272,768]{1,0:T(8,128)(2,1)S(1)} %collective-permute-done.19.refs_0_), channel_id=1, source_target_pairs={{0,1},{1,0},{2,3},{3,2},{4,5},{5,4},{6,7},{7,6},{8,9},{9,8},{10,11... | collective-permute-start | bytes 1253384 | tf_op jit(solution)/shard_map/ppermute | solution.py:309
  62.6 20.7 %collective-permute-start.16 = (bf16[272,768]{1,0:T(8,128)(2,1)S(1)}, bf16[272,768]{1,0:T(8,128)(2,1)S(1)}, u32[]{:S(2)}, u32[]{:S(2)}) collective-permute-start(bf16[272,768]{1,0:T(8,128)(2,1)S(1)} %collective-permute-done.14.refs_0_), channel_id=1, source_target_pairs={{0,2},{1,3},{2,0},{3,1},{4,6},{5,7},{6,4},{7,5},{8,10},{9,11},{10,... | collective-permute-start | bytes 1253384 | tf_op jit(solution)/shard_map/ppermute | solution.py:309
  63.3 17.8 %collective-permute-start.2 = (bf16[144,768]{1,0:T(8,128)(2,1)S(1)}, bf16[144,768]{1,0:T(8,128)(2,1)S(1)}, u32[]{:S(2)}, u32[]{:S(2)}) collective-permute-start(bf16[144,768]{1,0:T(8,128)(2,1)S(1)} %collective-permute-done.refs_0_), channel_id=1, source_target_pairs={{0,2},{1,3},{2,0},{3,1},{4,6},{5,7},{6,4},{7,5},{8,10},{9,11},{10,... | collective-permute-start | bytes 663560 | tf_op jit(solution)/shard_map/ppermute | solution.py:309
  81.0 12.6 %collective-permute-start.23 = (bf16[272,768]{1,0:T(8,128)(2,1)S(1)}, bf16[272,768]{1,0:T(8,128)(2,1)S(1)}, u32[]{:S(2)}, u32[]{:S(2)}) collective-permute-start(bf16[272,768]{1,0:T(8,128)(2,1)S(1)} %collective-permute-done.19.refs_0_), channel_id=1, source_target_pairs={{0,4},{1,5},{2,6},{3,7},{4,0},{5,1},{6,2},{7,3},{8,12},{9,13},{10,... | collective-permute-start | bytes 1253384 | tf_op jit(solution)/shard_map/ppermute | solution.py:309
  81.6 12.6 %collective-permute-start.15 = (bf16[272,768]{1,0:T(8,128)(2,1)S(1)}, bf16[272,768]{1,0:T(8,128)(2,1)S(1)}, u32[]{:S(2)}, u32[]{:S(2)}) collective-permute-start(bf16[272,768]{1,0:T(8,128)(2,1)S(1)} %collective-permute-done.14.refs_0_), channel_id=1, source_target_pairs={{0,1},{1,0},{2,3},{3,2},{4,5},{5,4},{6,7},{7,6},{8,9},{9,8},{10,11... | collective-permute-start | bytes 1253384 | tf_op jit(solution)/shard_map/ppermute | solution.py:309
  81.6 21.0 %collective-permute-start.18 = (bf16[272,768]{1,0:T(8,128)(2,1)S(1)}, bf16[272,768]{1,0:T(8,128)(2,1)S(1)}, u32[]{:S(2)}, u32[]{:S(2)}) collective-permute-start(bf16[272,768]{1,0:T(8,128)(2,1)S(1)} %collective-permute-done.14.refs_0_), channel_id=1, source_target_pairs={{0,4},{1,5},{2,6},{3,7},{4,0},{5,1},{6,2},{7,3},{8,12},{9,13},{10,... | collective-permute-start | bytes 1253384 | tf_op jit(solution)/shard_map/ppermute | solution.py:309
  83.1 19.4 %collective-permute-start.22 = (bf16[272,768]{1,0:T(8,128)(2,1)S(1)}, bf16[272,768]{1,0:T(8,128)(2,1)S(1)}, u32[]{:S(2)}, u32[]{:S(2)}) collective-permute-start(bf16[272,768]{1,0:T(8,128)(2,1)S(1)} %collective-permute-done.21.refs_2_), channel_id=1, source_target_pairs={{0,1},{1,0},{2,3},{3,2},{4,5},{5,4},{6,7},{7,6},{8,9},{9,8},{10,11... | collective-permute-start | bytes 1253384 | tf_op jit(solution)/shard_map/ppermute | solution.py:309
  83.3 19.8 %collective-permute-start.17 = (bf16[272,768]{1,0:T(8,128)(2,1)S(1)}, bf16[272,768]{1,0:T(8,128)(2,1)S(1)}, u32[]{:S(2)}, u32[]{:S(2)}) collective-permute-start(bf16[272,768]{1,0:T(8,128)(2,1)S(1)} %collective-permute-done.16.refs_2_), channel_id=1, source_target_pairs={{0,1},{1,0},{2,3},{3,2},{4,5},{5,4},{6,7},{7,6},{8,9},{9,8},{10,11... | collective-permute-start | bytes 1253384 | tf_op jit(solution)/shard_map/ppermute | solution.py:309
  93.6 31.8 %collective-permute-start.13 = (bf16[144,768]{1,0:T(8,128)(2,1)S(1)}, bf16[144,768]{1,0:T(8,128)(2,1)S(1)}, u32[]{:S(2)}, u32[]{:S(2)}) collective-permute-start(bf16[144,768]{1,0:T(8,128)(2,1)S(1)} %collective-permute-done.9.refs_0_), channel_id=1, source_target_pairs={{0,4},{1,5},{2,6},{3,7},{4,0},{5,1},{6,2},{7,3},{8,12},{9,13},{10,... | collective-permute-start | bytes 663560 | tf_op jit(solution)/shard_map/ppermute | solution.py:309
  94.2 31.3 %collective-permute-start.12 = (bf16[144,768]{1,0:T(8,128)(2,1)S(1)}, bf16[144,768]{1,0:T(8,128)(2,1)S(1)}, u32[]{:S(2)}, u32[]{:S(2)}) collective-permute-start(bf16[144,768]{1,0:T(8,128)(2,1)S(1)} %collective-permute-done.11.refs_2_), channel_id=1, source_target_pairs={{0,1},{1,0},{2,3},{3,2},{4,5},{5,4},{6,7},{7,6},{8,9},{9,8},{10,11... | collective-permute-start | bytes 663560 | tf_op jit(solution)/shard_map/ppermute | solution.py:309
  102.6 32.4 %collective-permute-start.1 = (bf16[144,768]{1,0:T(8,128)(2,1)S(1)}, bf16[144,768]{1,0:T(8,128)(2,1)S(1)}, u32[]{:S(2)}, u32[]{:S(2)}) collective-permute-start(bf16[144,768]{1,0:T(8,128)(2,1)S(1)} %collective-permute-done.refs_0_), channel_id=1, source_target_pairs={{0,1},{1,0},{2,3},{3,2},{4,5},{5,4},{6,7},{7,6},{8,9},{9,8},{10,11... | collective-permute-start | bytes 663560 | tf_op jit(solution)/shard_map/ppermute | solution.py:309
  102.6 32.4 %collective-permute-start.4 = (bf16[144,768]{1,0:T(8,128)(2,1)S(1)}, bf16[144,768]{1,0:T(8,128)(2,1)S(1)}, u32[]{:S(2)}, u32[]{:S(2)}) collective-permute-start(bf16[144,768]{1,0:T(8,128)(2,1)S(1)} %collective-permute-done.refs_0_), channel_id=1, source_target_pairs={{0,4},{1,5},{2,6},{3,7},{4,0},{5,1},{6,2},{7,3},{8,12},{9,13},{10,... | collective-permute-start | bytes 663560 | tf_op jit(solution)/shard_map/ppermute | solution.py:309
  103.1 31.8 %collective-permute-start.3 = (bf16[144,768]{1,0:T(8,128)(2,1)S(1)}, bf16[144,768]{1,0:T(8,128)(2,1)S(1)}, u32[]{:S(2)}, u32[]{:S(2)}) collective-permute-start(bf16[144,768]{1,0:T(8,128)(2,1)S(1)} %collective-permute-done.2.refs_2_), channel_id=1, source_target_pairs={{0,1},{1,0},{2,3},{3,2},{4,5},{5,4},{6,7},{7,6},{8,9},{9,8},{10,11... | collective-permute-start | bytes 663560 | tf_op jit(solution)/shard_map/ppermute | solution.py:309
  105.5 1.2 copy-start
  113.2 1.1 copy-start.1
  124.3 1.2 copy-start.2

commit v2 on v1

--- a/solution.py
+++ b/solution.py
@@ -13,7 +13,7 @@
 META = 16
 KEYS = 4
 BLOCK = 256
-VMEM = 48 * 1024 * 1024
+VMEM = 24 * 1024 * 1024
 
 
 def iota(shape, dim):
@@ -37,8 +37,12 @@
     return value.bit_length() - 1
 
 
-def params(scale=1):
+def params():
     return pltpu.CompilerParams(vmem_limit_bytes=VMEM)
+
+
+def cost(flops, size):
+    return pl.CostEstimate(flops=flops, bytes_accessed=size, transcendentals=0)
 
 
 def request_kernel(dims, place_ref, sizes_ref, members_ref, asked_ref, home_ref):
@@ -162,25 +166,19 @@
     total[...] = jnp.full(total.shape, -1.0, F32)
 
     def against(keys_ref, line_ref, own):
-        def body(b, carry):
-            at = pl.multiple_of(b * BLOCK, BLOCK)
-            keys = keys_ref[pl.ds(at, BLOCK), :]
-            line = line_ref[b]
-            for m in range(n_new_q // BLOCK):
-                span = slice(m * BLOCK, (m + 1) * BLOCK)
-                sims = dot_nt(queries_out[span, :], keys)
-                keep = wide(query_col[span, :], BLOCK) == line
-                if own:
-                    me = m * BLOCK + iota((BLOCK, BLOCK), 0)
-                    it = at + iota((BLOCK, BLOCK), 1)
-                    keep = keep & ((me != it) | (me >= size))
-                sims = jnp.where(keep, sims, -1.0)
-                best = total[span, :]
-                for v in range(BLOCK // 128):
-                    best = jnp.maximum(best, sims[:, v * 128:(v + 1) * 128])
-                total[span, :] = best
-            return carry
-        lax.fori_loop(0, keys_ref.shape[0] // BLOCK, body, 0)
+        n_keys = keys_ref.shape[0]
+        sims = dot_nt(queries_out[...], keys_ref[...])
+        line = jnp.concatenate([line_ref[b] for b in range(n_keys // BLOCK)], axis=1)
+        keep = wide(query_col[...], n_keys) == line
+        if own:
+            me = iota((n_new_q, n_keys), 0)
+            it = iota((n_new_q, n_keys), 1)
+            keep = keep & ((me != it) | (me >= size))
+        sims = jnp.where(keep, sims, -1.0)
+        best = total[...]
+        for v in range(n_keys // 128):
+            best = jnp.maximum(best, sims[:, v * 128:(v + 1) * 128])
+        total[...] = best
 
     against(keys_out, key_line_out, True)
     for keys_ref, line_ref, _, _, _ in old:
@@ -193,20 +191,13 @@
         best_new[b] = line[:, b * BLOCK:(b + 1) * BLOCK]
 
     for (_, _, queries_ref, line_ref, best_ref), out_ref in zip(old, best_out):
-        def body(b, carry, queries_ref=queries_ref, line_ref=line_ref, best_ref=best_ref, out_ref=out_ref):
-            at = pl.multiple_of(b * BLOCK, BLOCK)
-            queries = queries_ref[pl.ds(at, BLOCK), :]
-            line = line_ref[b]
-            best = best_ref[b]
-            for m in range(n_new_k // BLOCK):
-                span = slice(m * BLOCK, (m + 1) * BLOCK)
-                sims = dot_nt(keys_out[span, :], queries)
-                keep = wide(key_col[span, :], BLOCK) == line
-                sims = jnp.where(keep, sims, -1.0)
-                best = jnp.maximum(best, jnp.max(sims, axis=0, keepdims=True))
-            out_ref[b] = best
-            return carry
-        lax.fori_loop(0, queries_ref.shape[0] // BLOCK, body, 0)
+        n_queries = queries_ref.shape[0]
+        sims = dot_nt(keys_out[...], queries_ref[...])
+        line = jnp.concatenate([line_ref[b] for b in range(n_queries // BLOCK)], axis=1)
+        keep = wide(key_col[...], n_queries) == line
+        best = jnp.max(jnp.where(keep, sims, -1.0), axis=0, keepdims=True)
+        for b in range(n_queries // BLOCK):
+            out_ref[b] = jnp.maximum(best_ref[b], best[:, b * BLOCK:(b + 1) * BLOCK])
 
     if last:
         n_gx, n_gy, rows, quota = dims
@@ -346,6 +337,7 @@
             in_specs=[in_vmem] * (len(keys) + len(far) + len(flat_old)),
             out_specs=[in_vmem] * len(out_shapes),
             scratch_shapes=scratch,
+            cost_estimate=cost(2 * width * (nq * nk + sum(nq * a[0].shape[0] + nk * a[2].shape[0] for a in state)), nk * width),
             compiler_params=params(),
             name=f"step{s}",
         )(*keys, *far, *flat_old)

time: 154 us -> 105 us (0.68)
  the two profiles are of different devices: /device:TPU:0 before, /device:TPU:8 now
where the time goes in v2:
time: 105 us; the launch traced here: 104 us
  waiting for transfers between devices  50 us (48%)
  starting transfers between devices  23 us (22%)
  Pallas kernels  20.2 us (19%)
  blocking collectives  7.53 us (7%)
  other arithmetic  2.19 us (2%)
  local copies, waits for them, and re-layouts  1.34 us (1%)
    ppermute x4, waiting for transfers between devices, across(): lax.ppermute(array, 'gx', [(i, (i + step) % n_gx) for i in range(n_gx)])  25.5 us
    ppermute x20, waiting for transfers between devices, swap(): return lax.ppermute(array, 'gy', [(i, i ^ mask) for i in range(n_gy)])  20.6 us
    pallas_call x5, Pallas kernels, per_device(): pl.pallas_call(functools.partial(step_kernel, size, n_query, parts[:s], p...  14.6 us
    ppermute x20, starting transfers between devices, swap(): return lax.ppermute(array, 'gy', [(i, i ^ mask) for i in range(n_gy)])  9.74 us
    all_to_all x1, blocking collectives, per_device(): back = lax.all_to_all(send, 'gy', split_axis=0, concat_axis=0, tiled=True)  7.53 us
    ppermute x4, starting transfers between devices, across(): lax.ppermute(array, 'gx', [(i, (i + step) % n_gx) for i in range(n_gx)])  7.23 us
    all_to_all x1, starting transfers between devices, per_device(): lax.all_to_all(asked, ('gx', 'gy'), split_axis=0, concat_axis=0, tiled=True)  6.04 us
    all_to_all x1, waiting for transfers between devices, per_device(): lax.all_to_all(asked, ('gx', 'gy'), split_axis=0, concat_axis=0, tiled=True)  3.81 us
  transfers between devices with their start and end apart: 25, of which 10 were waited for; matrix products, arithmetic and copies ran while one was open for 2% of the time, Pallas kernels for 11%

profile of v2, /device:TPU:8, one launch (start us, length us, event | category | flops | bytes accessed | tf_op | source)
XLA Modules:
  0.0 104.4 jit_solution(18324139326027208012)
XLA Ops:
  0.0 0.1 pad_add_fusion.place_ref
  0.1 0.7 copy-done
  0.8 0.7 copy-done.1
  1.4 1.6 %request.1 = (s32[32,1,32]{2,1,0:T(1,128)}, s32[2,1024]{1,0:T(2,128)S(1)}) custom-call(s32[2]{0:T(128)S(1)} %pad_add_fusion.place_ref, s32[1,25]{1,0:T(1,128)S(1)} %copy-done.1, s32[1,1024]{1,0:T(1,128)S(1)} %bitcast.4), custom_call_target="tpu_custom_call" | custom-call | tf_op jit(solution)/shard_map/request/pallas_call | solution.py:267
  3.0 6.0 %all-to-all-start = ((s32[32,1,32]{2,1,0:T(1,128)}), s32[32,1,32]{2,1,0:T(1,128)S(1)}, u32[]{:S(2)}, u32[]{:S(2)}) async-start(s32[32,1,32]{2,1,0:T(1,128)} %get-tuple-element.39), calls=%async_computation | async-start | bytes 32768 | tf_op jit(solution)/shard_map/all_to_all | solution.py:275
  9.1 1.8 %fusion = f32[1024]{0:T(1024)S(1)} fusion(bf16[1024,768]{1,0:T(8,128)(2,1)} %param.3), kind=kLoop, calls=%fused_computation.2 | loop fusion | flops 2358272 | bytes 1576960 | tf_op jit(solution)/shard_map/reduce_sum | solution.py:278
  10.9 0.3 fusion.1.unit_ref
  11.2 3.8 %all-to-all-done.asked_ref = s32[32,1,32]{2,1,0:T(1,128)S(1)} async-done(((s32[32,1,32]{2,1,0:T(1,128)}), s32[32,1,32]{2,1,0:T(1,128)S(1)}, u32[]{:S(2)}, u32[]{:S(2)}) %all-to-all-start) | async-done | bytes 4128 | tf_op jit(solution)/shard_map/all_to_all | solution.py:275
  15.0 3.2 %select.1 = (bf16[272,768]{1,0:T(8,128)(2,1)S(1)}, bf16[272,768]{1,0:T(8,128)(2,1)S(1)}, bf16[272,768]{1,0:T(8,128)(2,1)S(1)}, bf16[144,768]{1,0:T(8,128)(2,1)S(1)}, bf16[144,768]{1,0:T(8,128)(2,1)S(1)}) custom-call(s32[2]{0:T(128)S(1)} %pad_add_fusion.place_ref, s32[32,1,32]{2,1,0:T(1,128)S(1)} %all-to-all-done.asked_ref, bf16[1024,768]{1,0:T(8,128)(2,1)S(1)} %fusion.1.unit_ref), custom_call_target="tpu_custom_call" | custom-call | tf_op jit(solution)/shard_map/select/pallas_call | solution.py:287
  18.2 0.6 collective-permute-start.19
  18.8 3.2 %collective-permute-start.9 = (bf16[144,768]{1,0:T(8,128)(2,1)S(1)}, bf16[144,768]{1,0:T(8,128)(2,1)S(1)}, u32[]{:S(2)}, u32[]{:S(2)}) collective-permute-start(bf16[144,768]{1,0:T(8,128)(2,1)S(1)} %get-tuple-element.46), channel_id=1, source_target_pairs={{0,16},{8,24},{16,0},{24,8},{1,17},{9,25},{17,1},{25,9},{2,18},{10... | collective-permute-start | bytes 663560 | tf_op jit(solution)/shard_map/ppermute | solution.py:297
  22.1 0.5 collective-permute-start.6
  22.6 0.0 collective-permute-start.5
  22.6 0.0 collective-permute-start.14
  22.6 23.4 %collective-permute-done.9.refs_0_ = bf16[144,768]{1,0:T(8,128)(2,1)S(1)} collective-permute-done((bf16[144,768]{1,0:T(8,128)(2,1)S(1)}, bf16[144,768]{1,0:T(8,128)(2,1)S(1)}, u32[]{:S(2)}, u32[]{:S(2)}) %collective-permute-start.9) | collective-permute-done | bytes 221216 | tf_op jit(solution)/shard_map/ppermute | solution.py:297
  46.1 0.6 collective-permute-start.8
  46.7 0.0 collective-permute-done.19.refs_0_
  46.7 0.5 collective-permute-start.21
  47.2 0.0 collective-permute-done.6.refs_2_
  47.2 0.0 collective-permute-start.7
  47.3 0.0 collective-permute-done.5.refs_1_
  47.3 0.5 collective-permute-start.20
  47.8 1.5 %collective-permute-done.14.refs_0_ = bf16[272,768]{1,0:T(8,128)(2,1)S(1)} collective-permute-done((bf16[272,768]{1,0:T(8,128)(2,1)S(1)}, bf16[272,768]{1,0:T(8,128)(2,1)S(1)}, u32[]{:S(2)}, u32[]{:S(2)}) %collective-permute-start.14) | collective-permute-done | bytes 417824 | tf_op jit(solution)/shard_map/ppermute | solution.py:297
  49.2 0.7 collective-permute-start.16
  49.9 6.6 %collective-permute-done.8.refs_4_ = bf16[272,768]{1,0:T(8,128)(2,1)S(1)} collective-permute-done((bf16[272,768]{1,0:T(8,128)(2,1)S(1)}, bf16[272,768]{1,0:T(8,128)(2,1)S(1)}, u32[]{:S(2)}, u32[]{:S(2)}) %collective-permute-start.8) | collective-permute-done | bytes 417824 | tf_op jit(solution)/shard_map/ppermute | solution.py:300
  56.5 0.7 collective-permute-start.23
  57.2 2.1 %collective-permute-done.21.refs_2_ = bf16[272,768]{1,0:T(8,128)(2,1)S(1)} collective-permute-done((bf16[272,768]{1,0:T(8,128)(2,1)S(1)}, bf16[272,768]{1,0:T(8,128)(2,1)S(1)}, u32[]{:S(2)}, u32[]{:S(2)}) %collective-permute-start.21) | collective-permute-done | bytes 417824 | tf_op jit(solution)/shard_map/ppermute | solution.py:300
  59.3 0.0 collective-permute-start.22
  59.3 0.0 collective-permute-done.7.refs_3_
  59.3 0.5 collective-permute-start.15
  59.8 0.0 collective-permute-done.20.refs_1_
  59.8 1.4 %collective-permute-start.18 = (bf16[272,768]{1,0:T(8,128)(2,1)S(1)}, bf16[272,768]{1,0:T(8,128)(2,1)S(1)}, u32[]{:S(2)}, u32[]{:S(2)}) collective-permute-start(bf16[272,768]{1,0:T(8,128)(2,1)S(1)} %collective-permute-done.14.refs_0_), channel_id=1, source_target_pairs={{0,4},{1,5},{2,6},{3,7},{4,0},{5,1},{6,2},{7,3},{8,12},{9,13},{10,... | collective-permute-start | bytes 1253384 | tf_op jit(solution)/shard_map/ppermute | solution.py:300
  61.2 4.7 %collective-permute-done.16.refs_2_ = bf16[272,768]{1,0:T(8,128)(2,1)S(1)} collective-permute-done((bf16[272,768]{1,0:T(8,128)(2,1)S(1)}, bf16[272,768]{1,0:T(8,128)(2,1)S(1)}, u32[]{:S(2)}, u32[]{:S(2)}) %collective-permute-start.16) | collective-permute-done | bytes 417824 | tf_op jit(solution)/shard_map/ppermute | solution.py:300
  65.9 0.0 collective-permute-start.17
  65.9 1.1 %step0.1 = (bf16[1024,768]{1,0:T(8,128)(2,1)S(1)}, f32[4,1,256]{2,1,0:T(1,128)S(1)}, bf16[512,768]{1,0:T(8,128)(2,1)S(1)}, f32[2,1,256]{2,1,0:T(1,128)S(1)}, f32[2,1,256]{2,1,0:T(1,128)S(1)}) custom-call(bf16[272,768]{1,0:T(8,128)(2,1)S(1)} %get-tuple-element.41.refs_0_, bf16[272,768]{1,0:T(8,128)(2,1)S(1)} %collective-permute-done.5.refs_1_, ...), custom_call_target="tpu_custom_call" | custom-call | flops 805306368 | bytes 786432 | tf_op jit(solution)/shard_map/step0/pallas_call | solution.py:334
  67.0 2.0 %collective-permute-done.23.refs_4_ = bf16[272,768]{1,0:T(8,128)(2,1)S(1)} collective-permute-done((bf16[272,768]{1,0:T(8,128)(2,1)S(1)}, bf16[272,768]{1,0:T(8,128)(2,1)S(1)}, u32[]{:S(2)}, u32[]{:S(2)}) %collective-permute-start.23) | collective-permute-done | bytes 417824 | tf_op jit(solution)/shard_map/ppermute | solution.py:300
  69.0 3.4 %collective-permute-start = (bf16[144,768]{1,0:T(8,128)(2,1)S(1)}, bf16[144,768]{1,0:T(8,128)(2,1)S(1)}, u32[]{:S(2)}, u32[]{:S(2)}) collective-permute-start(bf16[144,768]{1,0:T(8,128)(2,1)S(1)} %get-tuple-element.40), channel_id=1, source_target_pairs={{0,16},{8,24},{16,0},{24,8},{1,17},{9,25},{17,1},{25,9},{2,18},{10... | collective-permute-start | bytes 663560 | tf_op jit(solution)/shard_map/ppermute | solution.py:297
  72.4 0.0 collective-permute-done.22.refs_3_
  72.4 0.8 collective-permute-start.11
  73.2 2.7 %step1.1 = (f32[2,1,256]{2,1,0:T(1,128)S(1)}, bf16[1024,768]{1,0:T(8,128)(2,1)S(1)}, f32[4,1,256]{2,1,0:T(1,128)S(1)}, bf16[512,768]{1,0:T(8,128)(2,1)S(1)}, f32...) custom-call(bf16[272,768]{1,0:T(8,128)(2,1)S(1)} %collective-permute-done.19.refs_0_, ...), custom_call_target="tpu_custom_call" | custom-call | flops 2415919104 | bytes 786432 | tf_op jit(solution)/shard_map/step1/pallas_call | solution.py:334
  76.0 0.6 collective-permute-done.refs_0_
  76.6 0.0 collective-permute-start.10
  76.6 1.8 %collective-permute-done.11.refs_2_ = bf16[144,768]{1,0:T(8,128)(2,1)S(1)} collective-permute-done((bf16[144,768]{1,0:T(8,128)(2,1)S(1)}, bf16[144,768]{1,0:T(8,128)(2,1)S(1)}, u32[]{:S(2)}, u32[]{:S(2)}) %collective-permute-start.11) | collective-permute-done | bytes 221216 | tf_op jit(solution)/shard_map/ppermute | solution.py:300
  78.4 1.0 collective-permute-start.13
  79.3 0.0 collective-permute-done.15.refs_1_
  79.3 0.8 collective-permute-start.2
  80.1 0.0 collective-permute-done.18.refs_4_
  80.1 0.0 collective-permute-start.1
  80.1 0.0 collective-permute-done.17.refs_3_
  80.2 0.5 collective-permute-start.12
  80.7 4.4 %step2.1 = (f32[2,1,256]{2,1,0:T(1,128)S(1)}, f32[2,1,256]{2,1,0:T(1,128)S(1)}, bf16[1024,768]{1,0:T(8,128)(2,1)S(1)}, f32[4,1,256]{2,1,0:T(1,128)S(1)}, bf16[51...) custom-call(bf16[272,768]{1,0:T(8,128)(2,1)S(1)} %collective-permute-done.14.refs_0_, ...), custom_call_target="tpu_custom_call" | custom-call | flops 4026531840 | bytes 786432 | tf_op jit(solution)/shard_map/step2/pallas_call | solution.py:334
  85.0 0.0 collective-permute-done.10.refs_1_
  85.0 1.1 %collective-permute-start.4 = (bf16[144,768]{1,0:T(8,128)(2,1)S(1)}, bf16[144,768]{1,0:T(8,128)(2,1)S(1)}, u32[]{:S(2)}, u32[]{:S(2)}) collective-permute-start(bf16[144,768]{1,0:T(8,128)(2,1)S(1)} %collective-permute-done.refs_0_), channel_id=1, source_target_pairs={{0,4},{1,5},{2,6},{3,7},{4,0},{5,1},{6,2},{7,3},{8,12},{9,13},{10,... | collective-permute-start | bytes 663560 | tf_op jit(solution)/shard_map/ppermute | solution.py:300
  86.2 0.0 collective-permute-done.2.refs_2_
  86.2 0.0 collective-permute-start.3
  86.2 0.0 collective-permute-done.13.refs_4_
  86.2 0.0 collective-permute-done.12.refs_3_
  86.2 2.9 %step3.1 = (f32[2,1,256]{2,1,0:T(1,128)S(1)}, f32[2,1,256]{2,1,0:T(1,128)S(1)}, f32[2,1,256]{2,1,0:T(1,128)S(1)}, bf16[512,768]{1,0:T(8,128)(2,1)S(1)}, f32[2,1,...) custom-call(bf16[144,768]{1,0:T(8,128)(2,1)S(1)} %collective-permute-done., ...), custom_call_target="tpu_custom_call" | custom-call | flops 2617245696 | bytes 393216 | tf_op jit(solution)/shard_map/step3/pallas_call | solution.py:334
  89.1 0.0 collective-permute-done.1.refs_1_
  89.1 3.4 %collective-permute-done.4.refs_4_ = bf16[144,768]{1,0:T(8,128)(2,1)S(1)} collective-permute-done((bf16[144,768]{1,0:T(8,128)(2,1)S(1)}, bf16[144,768]{1,0:T(8,128)(2,1)S(1)}, u32[]{:S(2)}, u32[]{:S(2)}) %collective-permute-start.4) | collective-permute-done | bytes 221216 | tf_op jit(solution)/shard_map/ppermute | solution.py:300
  92.5 0.0 collective-permute-done.3.refs_3_
  92.5 3.5 %step4.1 = f32[8,1,256]{2,1,0:T(1,128)S(1)} custom-call(bf16[144,768]{1,0:T(8,128)(2,1)S(1)} %collective-permute-done.refs_0_, bf16[144,768]{1,0:T(8,128)(2,1)S(1)} %collective-permute-done.1.refs_1_, bf16[144,768]{1,0:T(8,128)(2,1)S(1)} %collective-permute-done.2.refs_2_, bf16[144,768]{1,0:T(8,128)(2,1)S(1)} %collective-permute-done.3.refs_3_, ...), custom_call_target="tpu_custom_call" | custom-call | flops 3019898880 | bytes 393216 | tf_op jit(solution)/shard_map/step4/pallas_call | solution.py:334
  96.0 7.5 %all_to_all.10.back_ref = f32[8,1,256]{2,1,0:T(1,128)S(1)} all-to-all(f32[8,1,256]{2,1,0:T(1,128)S(1)} %step4.1), channel_id=1, replica_groups=mesh['gx'=4,'gy'=8] {'gy'}, dimensions={0} | all-to-all | bytes 16384 | tf_op jit(solution)/shard_map/all_to_all | solution.py:349
  103.5 0.8 finish.1
  (5 shorter events, 0.0 us)
Async XLA Ops:
  0.1 0.7 copy-start
  0.8 0.7 copy-start.1
  1.4 9.4 %copy-start.2 = (bf16[1024,768]{1,0:T(8,128)(2,1)S(1)}, bf16[1024,768]{1,0:T(8,128)(2,1)}, u32[]{:S(2)}) copy-start(bf16[1024,768]{1,0:T(8,128)(2,1)} %param.3) | copy-start | bytes 4718596
  3.0 12.0 %all-to-all-start = ((s32[32,1,32]{2,1,0:T(1,128)}), s32[32,1,32]{2,1,0:T(1,128)S(1)}, u32[]{:S(2)}, u32[]{:S(2)}) async-start(s32[32,1,32]{2,1,0:T(1,128)} %get-tuple-element.39), calls=%async_computation | async-start | bytes 32768 | tf_op jit(solution)/shard_map/all_to_all | solution.py:275
  18.2 28.5 %collective-permute-start.19 = (bf16[272,768]{1,0:T(8,128)(2,1)S(1)}, bf16[272,768]{1,0:T(8,128)(2,1)S(1)}, u32[]{:S(2)}, u32[]{:S(2)}) collective-permute-start(bf16[272,768]{1,0:T(8,128)(2,1)S(1)} %get-tuple-element.48), channel_id=1, source_target_pairs={{0,8},{8,16},{16,24},{24,0},{1,9},{9,17},{17,25},{25,1},{2,10},{10... | collective-permute-start | bytes 1253384 | tf_op jit(solution)/shard_map/ppermute | solution.py:297
  18.8 27.2 %collective-permute-start.9 = (bf16[144,768]{1,0:T(8,128)(2,1)S(1)}, bf16[144,768]{1,0:T(8,128)(2,1)S(1)}, u32[]{:S(2)}, u32[]{:S(2)}) collective-permute-start(bf16[144,768]{1,0:T(8,128)(2,1)S(1)} %get-tuple-element.46), channel_id=1, source_target_pairs={{0,16},{8,24},{16,0},{24,8},{1,17},{9,25},{17,1},{25,9},{2,18},{10... | collective-permute-start | bytes 663560 | tf_op jit(solution)/shard_map/ppermute | solution.py:297
  22.1 25.2 %collective-permute-start.6 = (bf16[272,768]{1,0:T(8,128)(2,1)S(1)}, bf16[272,768]{1,0:T(8,128)(2,1)S(1)}, u32[]{:S(2)}, u32[]{:S(2)}) collective-permute-start(bf16[272,768]{1,0:T(8,128)(2,1)S(1)} %get-tuple-element.41.refs_0_), channel_id=1, source_target_pairs={{0,2},{1,3},{2,0},{3,1},{4,6},{5,7},{6,4},{7,5},{8,10},{9,11},{10,... | collective-permute-start | bytes 1253384 | tf_op jit(solution)/shard_map/ppermute | solution.py:300
  22.6 24.6 %collective-permute-start.5 = (bf16[272,768]{1,0:T(8,128)(2,1)S(1)}, bf16[272,768]{1,0:T(8,128)(2,1)S(1)}, u32[]{:S(2)}, u32[]{:S(2)}) collective-permute-start(bf16[272,768]{1,0:T(8,128)(2,1)S(1)} %get-tuple-element.41.refs_0_), channel_id=1, source_target_pairs={{0,1},{1,0},{2,3},{3,2},{4,5},{5,4},{6,7},{7,6},{8,9},{9,8},{10,11... | collective-permute-start | bytes 1253384 | tf_op jit(solution)/shard_map/ppermute | solution.py:300
  22.6 26.6 %collective-permute-start.14 = (bf16[272,768]{1,0:T(8,128)(2,1)S(1)}, bf16[272,768]{1,0:T(8,128)(2,1)S(1)}, u32[]{:S(2)}, u32[]{:S(2)}) collective-permute-start(bf16[272,768]{1,0:T(8,128)(2,1)S(1)} %get-tuple-element.47), channel_id=1, source_target_pairs={{0,24},{8,0},{16,8},{24,16},{1,25},{9,1},{17,9},{25,17},{2,26},{10... | collective-permute-start | bytes 1253384 | tf_op jit(solution)/shard_map/ppermute | solution.py:297
  46.1 10.4 %collective-permute-start.8 = (bf16[272,768]{1,0:T(8,128)(2,1)S(1)}, bf16[272,768]{1,0:T(8,128)(2,1)S(1)}, u32[]{:S(2)}, u32[]{:S(2)}) collective-permute-start(bf16[272,768]{1,0:T(8,128)(2,1)S(1)} %get-tuple-element.41.refs_0_), channel_id=1, source_target_pairs={{0,4},{1,5},{2,6},{3,7},{4,0},{5,1},{6,2},{7,3},{8,12},{9,13},{10,... | collective-permute-start | bytes 1253384 | tf_op jit(solution)/shard_map/ppermute | solution.py:300
  46.7 12.6 %collective-permute-start.21 = (bf16[272,768]{1,0:T(8,128)(2,1)S(1)}, bf16[272,768]{1,0:T(8,128)(2,1)S(1)}, u32[]{:S(2)}, u32[]{:S(2)}) collective-permute-start(bf16[272,768]{1,0:T(8,128)(2,1)S(1)} %collective-permute-done.19.refs_0_), channel_id=1, source_target_pairs={{0,2},{1,3},{2,0},{3,1},{4,6},{5,7},{6,4},{7,5},{8,10},{9,11},{10,... | collective-permute-start | bytes 1253384 | tf_op jit(solution)/shard_map/ppermute | solution.py:300
  47.2 12.0 %collective-permute-start.7 = (bf16[272,768]{1,0:T(8,128)(2,1)S(1)}, bf16[272,768]{1,0:T(8,128)(2,1)S(1)}, u32[]{:S(2)}, u32[]{:S(2)}) collective-permute-start(bf16[272,768]{1,0:T(8,128)(2,1)S(1)} %collective-permute-done.6.refs_2_), channel_id=1, source_target_pairs={{0,1},{1,0},{2,3},{3,2},{4,5},{5,4},{6,7},{7,6},{8,9},{9,8},{10,11... | collective-permute-start | bytes 1253384 | tf_op jit(solution)/shard_map/ppermute | solution.py:300
  47.3 12.5 %collective-permute-start.20 = (bf16[272,768]{1,0:T(8,128)(2,1)S(1)}, bf16[272,768]{1,0:T(8,128)(2,1)S(1)}, u32[]{:S(2)}, u32[]{:S(2)}) collective-permute-start(bf16[272,768]{1,0:T(8,128)(2,1)S(1)} %collective-permute-done.19.refs_0_), channel_id=1, source_target_pairs={{0,1},{1,0},{2,3},{3,2},{4,5},{5,4},{6,7},{7,6},{8,9},{9,8},{10,11... | collective-permute-start | bytes 1253384 | tf_op jit(solution)/shard_map/ppermute | solution.py:300
  49.2 16.6 %collective-permute-start.16 = (bf16[272,768]{1,0:T(8,128)(2,1)S(1)}, bf16[272,768]{1,0:T(8,128)(2,1)S(1)}, u32[]{:S(2)}, u32[]{:S(2)}) collective-permute-start(bf16[272,768]{1,0:T(8,128)(2,1)S(1)} %collective-permute-done.14.refs_0_), channel_id=1, source_target_pairs={{0,2},{1,3},{2,0},{3,1},{4,6},{5,7},{6,4},{7,5},{8,10},{9,11},{10,... | collective-permute-start | bytes 1253384 | tf_op jit(solution)/shard_map/ppermute | solution.py:300
  56.5 12.6 %collective-permute-start.23 = (bf16[272,768]{1,0:T(8,128)(2,1)S(1)}, bf16[272,768]{1,0:T(8,128)(2,1)S(1)}, u32[]{:S(2)}, u32[]{:S(2)}) collective-permute-start(bf16[272,768]{1,0:T(8,128)(2,1)S(1)} %collective-permute-done.19.refs_0_), channel_id=1, source_target_pairs={{0,4},{1,5},{2,6},{3,7},{4,0},{5,1},{6,2},{7,3},{8,12},{9,13},{10,... | collective-permute-start | bytes 1253384 | tf_op jit(solution)/shard_map/ppermute | solution.py:300
  59.3 13.1 %collective-permute-start.22 = (bf16[272,768]{1,0:T(8,128)(2,1)S(1)}, bf16[272,768]{1,0:T(8,128)(2,1)S(1)}, u32[]{:S(2)}, u32[]{:S(2)}) collective-permute-start(bf16[272,768]{1,0:T(8,128)(2,1)S(1)} %collective-permute-done.21.refs_2_), channel_id=1, source_target_pairs={{0,1},{1,0},{2,3},{3,2},{4,5},{5,4},{6,7},{7,6},{8,9},{9,8},{10,11... | collective-permute-start | bytes 1253384 | tf_op jit(solution)/shard_map/ppermute | solution.py:300
  59.3 20.0 %collective-permute-start.15 = (bf16[272,768]{1,0:T(8,128)(2,1)S(1)}, bf16[272,768]{1,0:T(8,128)(2,1)S(1)}, u32[]{:S(2)}, u32[]{:S(2)}) collective-permute-start(bf16[272,768]{1,0:T(8,128)(2,1)S(1)} %collective-permute-done.14.refs_0_), channel_id=1, source_target_pairs={{0,1},{1,0},{2,3},{3,2},{4,5},{5,4},{6,7},{7,6},{8,9},{9,8},{10,11... | collective-permute-start | bytes 1253384 | tf_op jit(solution)/shard_map/ppermute | solution.py:300
  59.8 20.3 %collective-permute-start.18 = (bf16[272,768]{1,0:T(8,128)(2,1)S(1)}, bf16[272,768]{1,0:T(8,128)(2,1)S(1)}, u32[]{:S(2)}, u32[]{:S(2)}) collective-permute-start(bf16[272,768]{1,0:T(8,128)(2,1)S(1)} %collective-permute-done.14.refs_0_), channel_id=1, source_target_pairs={{0,4},{1,5},{2,6},{3,7},{4,0},{5,1},{6,2},{7,3},{8,12},{9,13},{10,... | collective-permute-start | bytes 1253384 | tf_op jit(solution)/shard_map/ppermute | solution.py:300
  65.9 14.3 %collective-permute-start.17 = (bf16[272,768]{1,0:T(8,128)(2,1)S(1)}, bf16[272,768]{1,0:T(8,128)(2,1)S(1)}, u32[]{:S(2)}, u32[]{:S(2)}) collective-permute-start(bf16[272,768]{1,0:T(8,128)(2,1)S(1)} %collective-permute-done.16.refs_2_), channel_id=1, source_target_pairs={{0,1},{1,0},{2,3},{3,2},{4,5},{5,4},{6,7},{7,6},{8,9},{9,8},{10,11... | collective-permute-start | bytes 1253384 | tf_op jit(solution)/shard_map/ppermute | solution.py:300
  69.0 7.5 %collective-permute-start = (bf16[144,768]{1,0:T(8,128)(2,1)S(1)}, bf16[144,768]{1,0:T(8,128)(2,1)S(1)}, u32[]{:S(2)}, u32[]{:S(2)}) collective-permute-start(bf16[144,768]{1,0:T(8,128)(2,1)S(1)} %get-tuple-element.40), channel_id=1, source_target_pairs={{0,16},{8,24},{16,0},{24,8},{1,17},{9,25},{17,1},{25,9},{2,18},{10... | collective-permute-start | bytes 663560 | tf_op jit(solution)/shard_map/ppermute | solution.py:297
  72.4 5.9 %collective-permute-start.11 = (bf16[144,768]{1,0:T(8,128)(2,1)S(1)}, bf16[144,768]{1,0:T(8,128)(2,1)S(1)}, u32[]{:S(2)}, u32[]{:S(2)}) collective-permute-start(bf16[144,768]{1,0:T(8,128)(2,1)S(1)} %collective-permute-done.9.refs_0_), channel_id=1, source_target_pairs={{0,2},{1,3},{2,0},{3,1},{4,6},{5,7},{6,4},{7,5},{8,10},{9,11},{10,... | collective-permute-start | bytes 663560 | tf_op jit(solution)/shard_map/ppermute | solution.py:300
  76.6 8.5 %collective-permute-start.10 = (bf16[144,768]{1,0:T(8,128)(2,1)S(1)}, bf16[144,768]{1,0:T(8,128)(2,1)S(1)}, u32[]{:S(2)}, u32[]{:S(2)}) collective-permute-start(bf16[144,768]{1,0:T(8,128)(2,1)S(1)} %collective-permute-done.9.refs_0_), channel_id=1, source_target_pairs={{0,1},{1,0},{2,3},{3,2},{4,5},{5,4},{6,7},{7,6},{8,9},{9,8},{10,11... | collective-permute-start | bytes 663560 | tf_op jit(solution)/shard_map/ppermute | solution.py:300
  78.4 7.8 %collective-permute-start.13 = (bf16[144,768]{1,0:T(8,128)(2,1)S(1)}, bf16[144,768]{1,0:T(8,128)(2,1)S(1)}, u32[]{:S(2)}, u32[]{:S(2)}) collective-permute-start(bf16[144,768]{1,0:T(8,128)(2,1)S(1)} %collective-permute-done.9.refs_0_), channel_id=1, source_target_pairs={{0,4},{1,5},{2,6},{3,7},{4,0},{5,1},{6,2},{7,3},{8,12},{9,13},{10,... | collective-permute-start | bytes 663560 | tf_op jit(solution)/shard_map/ppermute | solution.py:300
  79.3 6.8 %collective-permute-start.2 = (bf16[144,768]{1,0:T(8,128)(2,1)S(1)}, bf16[144,768]{1,0:T(8,128)(2,1)S(1)}, u32[]{:S(2)}, u32[]{:S(2)}) collective-permute-start(bf16[144,768]{1,0:T(8,128)(2,1)S(1)} %collective-permute-done.refs_0_), channel_id=1, source_target_pairs={{0,2},{1,3},{2,0},{3,1},{4,6},{5,7},{6,4},{7,5},{8,10},{9,11},{10,... | collective-permute-start | bytes 663560 | tf_op jit(solution)/shard_map/ppermute | solution.py:300
  80.1 9.0 %collective-permute-start.1 = (bf16[144,768]{1,0:T(8,128)(2,1)S(1)}, bf16[144,768]{1,0:T(8,128)(2,1)S(1)}, u32[]{:S(2)}, u32[]{:S(2)}) collective-permute-start(bf16[144,768]{1,0:T(8,128)(2,1)S(1)} %collective-permute-done.refs_0_), channel_id=1, source_target_pairs={{0,1},{1,0},{2,3},{3,2},{4,5},{5,4},{6,7},{7,6},{8,9},{9,8},{10,11... | collective-permute-start | bytes 663560 | tf_op jit(solution)/shard_map/ppermute | solution.py:300
  80.2 6.0 %collective-permute-start.12 = (bf16[144,768]{1,0:T(8,128)(2,1)S(1)}, bf16[144,768]{1,0:T(8,128)(2,1)S(1)}, u32[]{:S(2)}, u32[]{:S(2)}) collective-permute-start(bf16[144,768]{1,0:T(8,128)(2,1)S(1)} %collective-permute-done.11.refs_2_), channel_id=1, source_target_pairs={{0,1},{1,0},{2,3},{3,2},{4,5},{5,4},{6,7},{7,6},{8,9},{9,8},{10,11... | collective-permute-start | bytes 663560 | tf_op jit(solution)/shard_map/ppermute | solution.py:300
  85.0 7.5 %collective-permute-start.4 = (bf16[144,768]{1,0:T(8,128)(2,1)S(1)}, bf16[144,768]{1,0:T(8,128)(2,1)S(1)}, u32[]{:S(2)}, u32[]{:S(2)}) collective-permute-start(bf16[144,768]{1,0:T(8,128)(2,1)S(1)} %collective-permute-done.refs_0_), channel_id=1, source_target_pairs={{0,4},{1,5},{2,6},{3,7},{4,0},{5,1},{6,2},{7,3},{8,12},{9,13},{10,... | collective-permute-start | bytes 663560 | tf_op jit(solution)/shard_map/ppermute | solution.py:300
  86.2 6.3 %collective-permute-start.3 = (bf16[144,768]{1,0:T(8,128)(2,1)S(1)}, bf16[144,768]{1,0:T(8,128)(2,1)S(1)}, u32[]{:S(2)}, u32[]{:S(2)}) collective-permute-start(bf16[144,768]{1,0:T(8,128)(2,1)S(1)} %collective-permute-done.2.refs_2_), channel_id=1, source_target_pairs={{0,1},{1,0},{2,3},{3,2},{4,5},{5,4},{6,7},{7,6},{8,9},{9,8},{10,11... | collective-permute-start | bytes 663560 | tf_op jit(solution)/shard_map/ppermute | solution.py:300

commit v3 on v2

v3 whole, which is shorter than its diff:
```python
import functools

import jax
import jax.numpy as jnp
from jax import lax
from jax.experimental import pallas as pl
from jax.experimental.pallas import tpu as pltpu
from jax.sharding import PartitionSpec as P

F32 = jnp.float32
BF16 = jnp.bfloat16
I32 = jnp.int32
META = 16
KEYS = 4
VMEM = 24 * 1024 * 1024


def iota(shape, dim):
    return lax.broadcasted_iota(I32, shape, dim)


def dot_nt(a, b):
    return lax.dot_general(a, b, (((1,), (1,)), ((), ())), preferred_element_type=F32)


def dot_nn(a, b):
    return lax.dot_general(a, b, (((1,), (0,)), ((), ())), preferred_element_type=F32)


def one_hot(mask):
    return jnp.where(mask, 1.0, 0.0).astype(BF16)


def log2(value):
    assert value & (value - 1) == 0
    return value.bit_length() - 1


def params():
    return pltpu.CompilerParams(vmem_limit_bytes=VMEM)


def cost(flops, size):
    return pl.CostEstimate(flops=flops, bytes_accessed=size, transcendentals=0)


def request_kernel(dims, place_ref, sizes_ref, members_ref, asked_ref, home_ref):
    n_gx, n_gy, rows, quota = dims
    owners = n_gx * n_gy
    member = members_ref[...]
    owner = lax.shift_right_logical(member, log2(rows))
    row = member & (rows - 1)
    slot = place_ref[1] * rows + iota((1, rows), 1)
    cluster = jnp.zeros((1, rows), I32)
    end = jnp.int32(0)
    for c in range(sizes_ref.shape[1]):
        end = end + sizes_ref[0, c]
        cluster = cluster + (slot >= end).astype(I32)
    mask = iota((owners, rows), 0) == owner
    hot = one_hot(mask)
    before = one_hot(iota((128, 128), 0) < iota((128, 128), 1))
    count = jnp.zeros((owners, 1), F32)
    ranks = []
    for b in range(rows // 128):
        part = hot[:, b * 128:(b + 1) * 128]
        rank = dot_nn(part, before) + count
        part32 = part.astype(F32)
        ranks.append(jnp.sum(part32 * rank, axis=0, keepdims=True))
        count = count + jnp.sum(part32, axis=1, keepdims=True)
    rank = jnp.concatenate(ranks, axis=1).astype(I32)
    place = one_hot(iota((quota, rows), 0) == rank)
    low = (row & 255).astype(F32)
    high = lax.shift_right_logical(row, 8).astype(F32)
    zero = jnp.zeros((owners, rows), F32)

    def pick(value):
        return dot_nt(jnp.where(mask, value, zero).astype(BF16), place)

    asked = pick(low) + 256.0 * pick(high) + float(rows) * pick(cluster.astype(F32))
    asked = asked.astype(I32)
    for o in range(owners):
        asked_ref[o] = asked[o:o + 1, :]
    plane = lax.shift_right_logical(owner, log2(n_gy))
    step = (place_ref[0] - plane) & (n_gx - 1)
    home_ref[0:1, :] = owner & (n_gy - 1)
    home_ref[1:2, :] = step * quota + rank


def select_kernel(dims, steps, place_ref, asked_ref, unit_ref, *out_refs):
    n_gx, n_gy, rows, quota = dims
    chunk = n_gy * quota
    pick = one_hot((iota((chunk, quota), 0) & (quota - 1)) == iota((chunk, quota), 1))
    block = lax.shift_right_logical(iota((chunk, n_gy), 0), log2(quota))
    own_col = block == iota((chunk, n_gy), 1)
    block_row = lax.shift_right_logical(iota((n_gy, chunk), 1), log2(quota))
    own_row = block_row == iota((n_gy, chunk), 0)
    for step, ref in zip(steps, out_refs):
        plane = (place_ref[0] + step) & (n_gx - 1)
        wanted = jnp.concatenate([asked_ref[plane * n_gy + d] for d in range(n_gy)], axis=0)
        row = wanted & (rows - 1)
        cluster = lax.shift_right_logical(wanted, log2(rows)).astype(F32).astype(BF16)
        low = (row & 255).astype(F32).astype(BF16)
        high = lax.shift_right_logical(row, 8).astype(F32).astype(BF16)
        index = dot_nt(pick, low) + 256.0 * dot_nt(pick, high)
        index = jnp.sum(jnp.where(own_col, index, 0.0), axis=1, keepdims=True).astype(I32)
        flat = jnp.sum(jnp.where(own_row, dot_nt(cluster, pick), 0.0), axis=0, keepdims=True)
        hot = one_hot(iota((chunk, rows), 1) == index)
        ref[0:chunk, :] = dot_nn(hot, unit_ref[...]).astype(BF16)
        width = unit_ref.shape[1]
        line = jnp.concatenate([flat, jnp.zeros((1, width - chunk), F32)], axis=1)
        ref[chunk:chunk + META, :] = jnp.where(iota((META, width), 0) == 0, line, 0.0).astype(BF16)


def column(line):
    parts = []
    for b in range(line.shape[1] // 128):
        wide = jnp.broadcast_to(line[:, b * 128:(b + 1) * 128], (128, 128))
        parts.append(wide.T)
    return jnp.concatenate(parts, axis=0)


def wide(col, lanes):
    return jnp.concatenate([col] * (lanes // 128), axis=1)


def cluster_line(ref, size, chunk):
    block = ref[size:size + META, 0:chunk].astype(F32)
    return jnp.concatenate([block[r:r + 1, :] for r in range(size // chunk)], axis=1)


def pack_kernel(groups, sizes, chunk, *refs):
    refs = list(refs)
    outs = refs[sum(len(g) for g in groups):]
    for group, out_ref in zip(groups, outs):
        at = 0
        total = sum(sizes[n] for n in group)
        width = out_ref.shape[1]
        meta = jnp.zeros((META, width), F32)
        for name in group:
            ref, size = refs.pop(0), sizes[name]
            out_ref[at:at + size, :] = ref[0:size, :]
            lines = ref[size:size + META, :].astype(F32)
            for r in range(size // chunk):
                meta = jnp.where(iota((META, width), 0) == at // chunk + r, lines[r:r + 1, :], meta)
            at += size
        out_ref[total:total + META, :] = meta.astype(BF16)


def product_kernel(pairs, sizes, chunk, started, close, *refs):
    names = sorted({n for q, ks in pairs for n in [q] + ks})
    queries = [q for q, _ in pairs]
    refs = list(refs)
    rows = {n: refs.pop(0) for n in names}
    state = {q: (refs.pop(0), refs.pop(0)) for q in queries if q in started}
    for q, keys in pairs:
        n_q = sizes[q]
        if close:
            out_ref = refs.pop(0)
        else:
            col_ref, out_ref = refs.pop(0), refs.pop(0)
        if q in started:
            col = state[q][0][...]
            best = state[q][1][...]
        else:
            col = column(cluster_line(rows[q], n_q, chunk))
            best = jnp.full((n_q, 128), -1.0, F32)
        if not close:
            col_ref[...] = col
        for k in keys:
            n_k = sizes[k]
            sims = dot_nt(rows[q][0:n_q, :], rows[k][0:n_k, :])
            keep = wide(col, n_k) == cluster_line(rows[k], n_k, chunk)
            if k == q:
                keep = keep & (iota((n_q, n_k), 0) != iota((n_q, n_k), 1))
            sims = jnp.where(keep, sims, -1.0)
            for v in range(n_k // 128):
                best = jnp.maximum(best, sims[:, v * 128:(v + 1) * 128])
        if close:
            parts = [jnp.max(best[b * 128:(b + 1) * 128, :].T, axis=0, keepdims=True) for b in range(n_q // 128)]
            out_ref[...] = jnp.concatenate(parts, axis=1)
        else:
            out_ref[...] = best


def last_kernel(dims, queries, size, *refs):
    n_gx, n_gy, rows, quota = dims
    chunk = n_gy * quota
    refs = list(refs)
    key_ref = refs.pop(0)
    send_ref = refs.pop()
    keys = key_ref[0:size, :]
    col = column(cluster_line(key_ref, size, chunk))
    spread = {}
    for (m, steps, n_q), row_ref, best_ref in zip(queries, refs[0::2], refs[1::2]):
        sims = dot_nt(keys, row_ref[0:n_q, :])
        keep = wide(col, n_q) == cluster_line(row_ref, n_q, chunk)
        line = jnp.max(jnp.where(keep, sims, -1.0), axis=0, keepdims=True)
        line = jnp.maximum(line, best_ref[...])
        for c, step in enumerate(steps):
            flat = line[:, c * chunk:(c + 1) * chunk]
            block = lax.shift_right_logical(iota((n_gy, chunk), 1), log2(quota))
            held = jnp.where(block == iota((n_gy, chunk), 0), flat, 0.0)
            fold = held[:, 0:128]
            for v in range(1, chunk // 128):
                fold = fold + held[:, v * 128:(v + 1) * 128]
            shift = 64
            while shift >= quota:
                fold = fold + pltpu.roll(fold, shift, 1)
                shift //= 2
            here = lax.shift_right_logical(iota((n_gy, 128), 1), log2(quota)) == step
            fold = jnp.where(here, fold, 0.0)
            spread[m] = spread[m] + fold if m in spread else fold
    spread = jnp.concatenate([spread[m] for m in sorted(spread)], axis=1)
    for d in range(n_gy):
        send_ref[d] = spread[d:d + 1, :]


def finish_kernel(dims, home_ref, back_ref, out_ref):
    n_gx, n_gy, rows, quota = dims
    n_query = n_gy // KEYS
    lines = []
    for q in range(n_gy):
        best = None
        for m in range(n_query):
            part = back_ref[q ^ (KEYS * m)][:, m * 128:(m + 1) * 128]
            best = part if best is None else jnp.maximum(best, part)
        lines.append(best)
    found = jnp.concatenate(lines, axis=0)
    high = found.astype(BF16)
    rest = found - high.astype(F32)
    mid = rest.astype(BF16)
    low = (rest - mid.astype(F32)).astype(BF16)
    here = one_hot(iota((128, rows), 0) == home_ref[1:2, :])
    value = (dot_nn(high, here) + dot_nn(mid, here)) + dot_nn(low, here)
    own = iota((n_gy, rows), 0) == home_ref[0:1, :]
    out_ref[...] = jnp.sum(jnp.where(own, value, 0.0), axis=0, keepdims=True)


def shape(dims, dtype):
    return jax.ShapeDtypeStruct(dims, dtype)


def per_device(embeddings, members, sizes):
    rows = members.shape[0]
    width = embeddings.shape[1]
    n_gx = lax.axis_size("gx")
    n_gy = lax.axis_size("gy")
    owners = n_gx * n_gy
    quota = rows // owners
    chunk = n_gy * quota
    n_query = n_gy // KEYS
    dims = (n_gx, n_gy, rows, quota)
    in_vmem = pl.BlockSpec(memory_space=pltpu.VMEM)
    in_smem = pl.BlockSpec(memory_space=pltpu.SMEM)
    place = jnp.stack([lax.axis_index("gx"), lax.axis_index("gy")]).astype(I32)

    asked, home = pl.pallas_call(
        functools.partial(request_kernel, dims),
        out_shape=(shape((owners, 1, quota), I32), shape((2, rows), I32)),
        in_specs=[in_smem, in_smem, in_vmem],
        out_specs=(in_vmem, in_vmem),
        compiler_params=params(),
        name="request",
    )(place, sizes, members.reshape(1, rows))
    asked = lax.all_to_all(asked, ("gx", "gy"), split_axis=0, concat_axis=0, tiled=True)

    values = embeddings.astype(F32)
    squared = jnp.sum(values * values, axis=1, keepdims=True)
    unit = (values * lax.rsqrt(squared + 1e-06)).astype(BF16)

    stages = [[0], [1, n_gx - 1], list(range(2, n_gx - 1))]

    def select(steps, unit):
        found = pl.pallas_call(
            functools.partial(select_kernel, dims, steps),
            out_shape=[shape((chunk + (2 if k else 1) * META, width), BF16) for k in steps],
            in_specs=[in_smem, in_vmem, in_vmem],
            out_specs=[in_vmem] * len(steps),
            cost_estimate=cost(2 * len(steps) * chunk * rows * width, rows * width),
            compiler_params=params(),
            name="select",
        )(place, asked, unit)
        return dict(zip(steps, found))

    def meet(*arrays):
        return lax.optimization_barrier(arrays)

    found = select(stages[1], unit)
    unit, *first = meet(unit, *found.values())
    found = {**dict(zip(found, first)), **select(stages[0] + stages[2], unit)}

    def across(array, step):
        return lax.ppermute(array, "gx", [(i, (i + step) % n_gx) for i in range(n_gx)])

    def swap(array, mask):
        return lax.ppermute(array, "gy", [(i, i ^ mask) for i in range(n_gy)])

    far = ["Y%d" % m for m in range(1, n_query)]
    edge = stages[1]
    rest = [k for k in stages[2]]
    names = ["%d" % k for k in stages[0] + stages[1]] + ["b"]
    piece = {}
    size = {}
    state = {}
    for n in names:
        for kind in ["T", "N", "X", "Z"] + far:
            size[kind + n] = chunk * (len(rest) if n == "b" else 1)
    for k in range(n_gx):
        size["z%d" % k] = chunk

    def pack(groups):
        flat = [n for g in groups.values() for n in g]
        for name, group in groups.items():
            size[name] = sum(size[n] for n in group)
        out = pl.pallas_call(
            functools.partial(pack_kernel, list(groups.values()), size, chunk),
            out_shape=[shape((size[n] + META, width), BF16) for n in groups],
            in_specs=[in_vmem] * len(flat),
            out_specs=[in_vmem] * len(groups),
            cost_estimate=cost(0, 4 * sum(size[n] for n in flat) * width),
            compiler_params=params(),
            name="pack",
        )(*[piece[n] for n in flat])
        piece.update(zip(groups, out))

    def near(n):
        piece["X" + n] = swap(piece["T" + n], 2)
        for m, kind in enumerate(far):
            piece[kind + n] = swap(piece["T" + n], KEYS * (m + 1))

    def join(names):
        arrays = [piece[n] for n in names] + [a for q in state for a in state[q]]
        arrays = list(meet(*arrays))
        for name in names:
            piece[name] = arrays.pop(0)
        for q in state:
            state[q] = (arrays.pop(0), arrays.pop(0))

    def kinds(kinds, names):
        return [k + n for n in names for k in kinds]

    for k in edge:
        piece["z%d" % k] = across(found[k], k)
    piece["T0"] = found[0]
    near("0")
    piece["N0"] = swap(piece["T0"], 1)
    for k in rest:
        piece["f%d" % k] = found[k]
    join(["z%d" % k for k in edge] + ["f%d" % k for k in rest] + kinds(["T", "X", "N"] + far, ["0"]))
    for k in rest:
        piece["z%d" % k] = across(piece["f%d" % k], k)
    pack({"T%d" % k: ["z%d" % k] for k in edge})
    for k in edge:
        near("%d" % k)

    def products(pairs, close=False):
        names = sorted({n for q, ks in pairs for n in [q] + ks})
        queries = [q for q, _ in pairs]
        started = [q for q in queries if q in state]
        inputs = [piece[n] for n in names] + [a for q in started for a in state[q]]
        outs = []
        for q in queries:
            if close:
                outs.append(shape((1, size[q]), F32))
            else:
                outs += [shape((size[q], 128), F32)] * 2
        flops = sum(2 * width * size[q] * size[k] for q, ks in pairs for k in ks)
        out = pl.pallas_call(
            functools.partial(product_kernel, pairs, size, chunk, started, close),
            out_shape=outs,
            in_specs=[in_vmem] * len(inputs),
            out_specs=[in_vmem] * len(outs),
            cost_estimate=cost(flops, 0),
            compiler_params=params(),
            name="products",
        )(*inputs)
        for i, q in enumerate(queries):
            state[q] = out[i] if close else (out[2 * i], out[2 * i + 1])

    one = ["0"] + ["%d" % k for k in edge]
    side = one[1:]
    tops = kinds(["T"], one) + kinds(far, ["0"])
    keys = ["N0", "X0"] + kinds(["T"], one)
    products([(q, keys) for q in tops])
    join(["z%d" % k for k in rest] + kinds(["T", "X"] + far, side))
    pack({"Tb": ["z%d" % k for k in rest], "P": kinds(["T"], side) + kinds(["X"], one)})
    near("b")
    piece["Nb"] = swap(piece["Tb"], 1)
    piece["Q"] = swap(piece["P"], 1)
    size["Q"] = size["P"]
    late = kinds(far, side)
    sides = kinds(["X"], side)
    products(
        [(q, sides + ["Tb"]) for q in tops]
        + [(q, keys + sides + ["Tb"]) for q in late + ["Tb"]]
    )
    before = tops + late + ["Tb"]
    products([(q, ["Q", "Nb"]) for q in before])
    join(["Tb", "Xb", "Nb", "Q"] + kinds(far, ["b"]))
    piece["Zb"] = swap(piece["Xb"], 1)
    products([(q, ["Xb"]) for q in before] + [(q, keys + sides + ["Tb", "Q", "Nb", "Xb"]) for q in kinds(far, ["b"])], close=True)

    order = []
    inputs = []
    for n in names:
        for m, kind in enumerate(["T"] + far):
            q = kind + n
            order.append((m, rest if n == "b" else [int(n)], size[q]))
            inputs += [piece[q], state[q]]
    send = pl.pallas_call(
        functools.partial(last_kernel, dims, order, size["Zb"]),
        out_shape=shape((n_gy, 1, n_query * 128), F32),
        in_specs=[in_vmem] * (1 + len(inputs)),
        out_specs=in_vmem,
        cost_estimate=cost(2 * width * size["Zb"] * n_query * rows, 0),
        compiler_params=params(),
        name="last",
    )(piece["Zb"], *inputs)

    back = lax.all_to_all(send, "gy", split_axis=0, concat_axis=0, tiled=True)
    out = pl.pallas_call(
        functools.partial(finish_kernel, dims),
        out_shape=shape((1, rows), F32),
        in_specs=[in_vmem, in_vmem],
        out_specs=in_vmem,
        compiler_params=params(),
        name="finish",
    )(home, back)
    return out.reshape(rows)


def solution(mesh):
    return jax.shard_map(
        per_device,
        mesh=mesh,
        in_specs=(P(("gx", "gy"), None), P(("gx", "gy")), P("gx", None)),
        out_specs=P(("gx", "gy")),
        check_vma=False,
    )
```

time: 105 us -> 88.5 us (0.84)
  the two profiles are of different devices: /device:TPU:8 before, /device:TPU:0 now
where the time goes in v3:
time: 88.5 us; the launch traced here: 88.2 us
  waiting for transfers between devices  35.2 us (40%)
  starting transfers between devices  21.2 us (24%)
  Pallas kernels  21.1 us (24%)
  blocking collectives  7.06 us (8%)
  other arithmetic  2.19 us (2%)
  local copies, waits for them, and re-layouts  1.34 us (2%)
    ppermute x12, waiting for transfers between devices, swap(): return lax.ppermute(array, 'gy', [(i, i ^ mask) for i in range(n_gy)])  26.9 us
    pallas_call x4, Pallas kernels, products(): pl.pallas_call(functools.partial(product_kernel, pairs, size, chunk, star...  13.4 us
    ppermute x12, starting transfers between devices, swap(): return lax.ppermute(array, 'gy', [(i, i ^ mask) for i in range(n_gy)])  7.87 us
    all_to_all x1, starting transfers between devices, per_device(): lax.all_to_all(asked, ('gx', 'gy'), split_axis=0, concat_axis=0, tiled=True)  7.3 us
    all_to_all x1, blocking collectives, per_device(): back = lax.all_to_all(send, 'gy', split_axis=0, concat_axis=0, tiled=True)  7.06 us
    ppermute x3, starting transfers between devices, across(): lax.ppermute(array, 'gx', [(i, (i + step) % n_gx) for i in range(n_gx)])  6.04 us
    all_to_all x1, waiting for transfers between devices, per_device(): lax.all_to_all(asked, ('gx', 'gy'), split_axis=0, concat_axis=0, tiled=True)  5.01 us
    pallas_call x2, Pallas kernels, select(): pl.pallas_call(functools.partial(select_kernel, dims, steps), out_shape=[...  3.86 us
  transfers between devices with their start and end apart: 16, of which 10 were waited for; matrix products, arithmetic and copies ran while one was open for 2% of the time, Pallas kernels for 18%

profile of v3, /device:TPU:0, one launch (start us, length us, event | category | flops | bytes accessed | tf_op | source)
XLA Modules:
  0.0 88.2 jit_solution(6194218193594995330)
XLA Ops:
  0.0 0.1 pad_add_fusion.place_ref
  0.1 0.0 copy-start
  0.1 0.7 copy-done
  0.8 0.0 copy-start.1
  0.8 0.7 copy-done.1
  1.4 0.0 copy-start.2
  1.4 1.6 %request.1 = (s32[32,1,32]{2,1,0:T(1,128)}, s32[2,1024]{1,0:T(2,128)S(1)}) custom-call(s32[2]{0:T(128)S(1)} %pad_add_fusion.place_ref, s32[1,25]{1,0:T(1,128)S(1)} %copy-done.1, s32[1,1024]{1,0:T(1,128)S(1)} %bitcast.4), custom_call_target="tpu_custom_call" | custom-call | tf_op jit(solution)/shard_map/request/pallas_call | solution.py:257
  3.0 7.3 %all-to-all-start = ((s32[32,1,32]{2,1,0:T(1,128)}), s32[32,1,32]{2,1,0:T(1,128)S(1)}, u32[]{:S(2)}, u32[]{:S(2)}) async-start(s32[32,1,32]{2,1,0:T(1,128)} %get-tuple-element.104), calls=%async_computation | async-start | bytes 32768 | tf_op jit(solution)/shard_map/all_to_all | solution.py:265
  10.3 1.8 %fusion = f32[1024]{0:T(1024)S(1)} fusion(bf16[1024,768]{1,0:T(8,128)(2,1)} %param.3), kind=kLoop, calls=%fused_computation.2 | loop fusion | flops 2358272 | bytes 1576960 | tf_op jit(solution)/shard_map/reduce_sum | solution.py:268
  12.1 0.0 copy-done.2
  12.1 0.3 fusion.1.unit_ref
  12.4 5.0 %all-to-all-done.asked_ref = s32[32,1,32]{2,1,0:T(1,128)S(1)} async-done(((s32[32,1,32]{2,1,0:T(1,128)}), s32[32,1,32]{2,1,0:T(1,128)S(1)}, u32[]{:S(2)}, u32[]{:S(2)}) %all-to-all-start) | async-done | bytes 4128 | tf_op jit(solution)/shard_map/all_to_all | solution.py:265
  17.4 1.9 %select.2 = (bf16[288,768]{1,0:T(8,128)(2,1)S(1)}, bf16[288,768]{1,0:T(8,128)(2,1)S(1)}) custom-call(s32[2]{0:T(128)S(1)} %pad_add_fusion.place_ref, s32[32,1,32]{2,1,0:T(1,128)S(1)} %all-to-all-done.asked_ref, bf16[1024,768]{1,0:T(8,128)(2,1)S(1)} %fusion.1.unit_ref), custom_call_target="tpu_custom_call" | custom-call | flops 805306368 | bytes 786432 | tf_op jit(solution)/shard_map/select/pallas_call | solution.py:274
  19.4 0.6 collective-permute-start
  20.0 3.2 %collective-permute-start.1 = (bf16[288,768]{1,0:T(8,128)(2,1)S(1)}, bf16[288,768]{1,0:T(8,128)(2,1)S(1)}, u32[]{:S(2)}, u32[]{:S(2)}) collective-permute-start(bf16[288,768]{1,0:T(8,128)(2,1)S(1)} %get-tuple-element.108), channel_id=1, source_target_pairs={{0,24},{8,0},{16,8},{24,16},{1,25},{9,1},{17,9},{25,17},{2,26},{10... | collective-permute-start | bytes 1327112 | tf_op jit(solution)/shard_map/ppermute | solution.py:293
  23.3 1.9 %select.3 = (bf16[272,768]{1,0:T(8,128)(2,1)S(1)}, bf16[288,768]{1,0:T(8,128)(2,1)S(1)}) custom-call(s32[2]{0:T(128)S(1)} %pad_add_fusion.place_ref, s32[32,1,32]{2,1,0:T(1,128)S(1)} %all-to-all-done.asked_ref, bf16[1024,768]{1,0:T(8,128)(2,1)S(1)} %fusion.1.unit_ref), custom_call_target="tpu_custom_call" | custom-call | flops 805306368 | bytes 786432 | tf_op jit(solution)/shard_map/select/pallas_call | solution.py:274
  25.2 0.6 collective-permute-start.2
  25.8 0.0 collective-permute-start.3
  25.8 0.6 collective-permute-start.4
  26.4 9.7 %collective-permute-done.2.refs_4_.refs_3_.refs_5_.refs_7_ = bf16[272,768]{1,0:T(8,128)(2,1)S(1)} collective-permute-done((bf16[272,768]{1,0:T(8,128)(2,1)S(1)}, bf16[272,768]{1,0:T(8,128)(2,1)S(1)}, u32[]{:S(2)}, u32[]{:S(2)}) %collective-permute-start.2) | collective-permute-done | bytes 417824 | tf_op jit(solution)/shard_map/ppermute | solution.py:296
  36.1 0.0 collective-permute-done.3.refs_0_
  36.1 1.7 %collective-permute-done.4.refs_5_.refs_8_.refs_6_.refs_11_.refs_3_ = bf16[272,768]{1,0:T(8,128)(2,1)S(1)} collective-permute-done((bf16[272,768]{1,0:T(8,128)(2,1)S(1)}, bf16[272,768]{1,0:T(8,128)(2,1)S(1)}, u32[]{:S(2)}, u32[]{:S(2)}) %collective-permute-start.4) | collective-permute-done | bytes 417824 | tf_op jit(solution)/shard_map/ppermute | solution.py:296
  37.9 0.0 collective-permute-done.refs_0_
  37.9 3.2 %collective-permute-done.1.refs_1_ = bf16[288,768]{1,0:T(8,128)(2,1)S(1)} collective-permute-done((bf16[288,768]{1,0:T(8,128)(2,1)S(1)}, bf16[288,768]{1,0:T(8,128)(2,1)S(1)}, u32[]{:S(2)}, u32[]{:S(2)}) %collective-permute-start.1) | collective-permute-done | bytes 442400 | tf_op jit(solution)/shard_map/ppermute | solution.py:293
  41.1 2.2 %collective-permute-start.5 = (bf16[288,768]{1,0:T(8,128)(2,1)S(1)}, bf16[288,768]{1,0:T(8,128)(2,1)S(1)}, u32[]{:S(2)}, u32[]{:S(2)}) collective-permute-start(bf16[288,768]{1,0:T(8,128)(2,1)S(1)} %get-tuple-element.112), channel_id=1, source_target_pairs={{0,16},{8,24},{16,0},{24,8},{1,17},{9,25},{17,1},{25,9},{2,18},{10... | collective-permute-start | bytes 1327112 | tf_op jit(solution)/shard_map/ppermute | solution.py:293
  43.3 0.1 pack.2
  43.3 0.6 collective-permute-start.6
  43.9 0.5 collective-permute-start.7
  44.5 1.5 %collective-permute-start.8 = (bf16[272,768]{1,0:T(8,128)(2,1)S(1)}, bf16[272,768]{1,0:T(8,128)(2,1)S(1)}, u32[]{:S(2)}, u32[]{:S(2)}) collective-permute-start(bf16[272,768]{1,0:T(8,128)(2,1)S(1)} %get-tuple-element.131.refs_3_.refs_2_.refs_4_.refs_5_.refs_9_), channel_id=1, source_target_pairs={{0,2},{1,3},{2,0},{3,1},{4,6},{5,7},{6,4},{7,5},{8,10},{9,11},{10,... | collective-permute-start | bytes 1253384 | tf_op jit(solution)/shard_map/ppermute | solution.py:296
  45.9 1.5 %collective-permute-start.9 = (bf16[272,768]{1,0:T(8,128)(2,1)S(1)}, bf16[272,768]{1,0:T(8,128)(2,1)S(1)}, u32[]{:S(2)}, u32[]{:S(2)}) collective-permute-start(bf16[272,768]{1,0:T(8,128)(2,1)S(1)} %get-tuple-element.131.refs_3_.refs_2_.refs_4_.refs_5_.refs_9_), channel_id=1, source_target_pairs={{0,4},{1,5},{2,6},{3,7},{4,0},{5,1},{6,2},{7,3},{8,12},{9,13},{10,... | collective-permute-start | bytes 1253384 | tf_op jit(solution)/shard_map/ppermute | solution.py:296
  47.4 2.3 %products.4 = (f32[256,128]{1,0:T(8,128)S(1)}, f32[256,128]{1,0:T(8,128)S(1)}, f32[256,128]{1,0:T(8,128)S(1)}, f32[256,128]{1,0:T(8,128)S(1)}, f32[256,128]{1,0:...) custom-call(bf16[272,768]{1,0:T(8,128)(2,1)S(1)} %collective-permute-done.3.refs_0_, ...), custom_call_target="tpu_custom_call" | custom-call | flops 2013265920 | tf_op jit(solution)/shard_map/products/pallas_call | solution.py:368
  49.8 6.2 %collective-permute-done.6.refs_4_.refs_6_.refs_8_ = bf16[272,768]{1,0:T(8,128)(2,1)S(1)} collective-permute-done((bf16[272,768]{1,0:T(8,128)(2,1)S(1)}, bf16[272,768]{1,0:T(8,128)(2,1)S(1)}, u32[]{:S(2)}, u32[]{:S(2)}) %collective-permute-start.6) | collective-permute-done | bytes 417824 | tf_op jit(solution)/shard_map/ppermute | solution.py:296
  56.0 0.5 collective-permute-done.7.refs_9_.refs_7_.refs_12_
  56.5 6.2 %collective-permute-done.8.refs_5_.refs_7_.refs_9_ = bf16[272,768]{1,0:T(8,128)(2,1)S(1)} collective-permute-done((bf16[272,768]{1,0:T(8,128)(2,1)S(1)}, bf16[272,768]{1,0:T(8,128)(2,1)S(1)}, u32[]{:S(2)}, u32[]{:S(2)}) %collective-permute-start.8) | collective-permute-done | bytes 417824 | tf_op jit(solution)/shard_map/ppermute | solution.py:296
  62.7 0.3 collective-permute-done.9.refs_10_.refs_8_.refs_13_.refs_11_
  62.9 0.0 collective-permute-done.5.refs_0_
  62.9 0.2 pack.3
  63.1 0.1 collective-permute-start.12
  63.2 0.5 collective-permute-start.11
  63.7 1.5 %collective-permute-start.10 = (bf16[272,768]{1,0:T(8,128)(2,1)S(1)}, bf16[272,768]{1,0:T(8,128)(2,1)S(1)}, u32[]{:S(2)}, u32[]{:S(2)}) collective-permute-start(bf16[272,768]{1,0:T(8,128)(2,1)S(1)} %get-tuple-element.177.refs_4_.refs_5_.refs_6_.refs_13_), channel_id=1, source_target_pairs={{0,2},{1,3},{2,0},{3,1},{4,6},{5,7},{6,4},{7,5},{8,10},{9,11},{10,... | collective-permute-start | bytes 1253384 | tf_op jit(solution)/shard_map/ppermute | solution.py:296
  65.2 0.5 collective-permute-start.13
  65.6 4.0 %products.5 = (f32[256,128]{1,0:T(8,128)S(1)}, f32[256,128]{1,0:T(8,128)S(1)}, f32[256,128]{1,0:T(8,128)S(1)}, f32[256,128]{1,0:T(8,128)S(1)}, f32[256,128]{1,0:...) custom-call(bf16[272,768]{1,0:T(8,128)(2,1)S(1)} %collective-permute, ...), custom_call_target="tpu_custom_call" | custom-call | flops 3623878656 | tf_op jit(solution)/shard_map/products/pallas_call | solution.py:368
  69.6 0.0 collective-permute-done.11.refs_0_.refs_1_
  69.6 0.0 collective-permute-done.12.refs_1_.refs_2_
  69.6 4.6 %products.6 = (f32[256,128]{1,0:T(8,128)S(1)}, f32[256,128]{1,0:T(8,128)S(1)}, f32[256,128]{1,0:T(8,128)S(1)}, f32[256,128]{1,0:T(8,128)S(1)}, f32[256,128]{1,0:...) custom-call(bf16[272,768]{1,0:T(8,128)(2,1)S(1)} %collective-permute, ...), custom_call_target="tpu_custom_call" | custom-call | flops 4227858432 | tf_op jit(solution)/shard_map/products/pallas_call | solution.py:368
  74.2 1.1 %collective-permute-done.10.refs_10_ = bf16[272,768]{1,0:T(8,128)(2,1)S(1)} collective-permute-done((bf16[272,768]{1,0:T(8,128)(2,1)S(1)}, bf16[272,768]{1,0:T(8,128)(2,1)S(1)}, u32[]{:S(2)}, u32[]{:S(2)}) %collective-permute-start.10) | collective-permute-done | bytes 417824 | tf_op jit(solution)/shard_map/ppermute | solution.py:296
  75.3 1.2 %collective-permute-done.13.refs_14_.refs_15_ = bf16[272,768]{1,0:T(8,128)(2,1)S(1)} collective-permute-done((bf16[272,768]{1,0:T(8,128)(2,1)S(1)}, bf16[272,768]{1,0:T(8,128)(2,1)S(1)}, u32[]{:S(2)}, u32[]{:S(2)}) %collective-permute-start.13) | collective-permute-done | bytes 417824 | tf_op jit(solution)/shard_map/ppermute | solution.py:296
  76.5 0.0 collective-permute-start.14
  76.5 2.6 %products.7 = (f32[1,256]{1,0:T(1,128)S(1)}, f32[1,256]{1,0:T(1,128)S(1)}, f32[1,256]{1,0:T(1,128)S(1)}, f32[1,256]{1,0:T(1,128)S(1)}, f32[1,256]{1,0:T(1,128)S(...) custom-call(bf16[272,768]{1,0:T(8,128)(2,1)S(1)} %collective-permute-done.3.refs_0_, ...), custom_call_target="tpu_custom_call" | custom-call | flops 2214592512 | tf_op jit(solution)/shard_map/products/pallas_call | solution.py:368
  79.1 0.0 collective-permute-done.14.refs_0_
  79.1 1.2 %last.1 = f32[8,1,256]{2,1,0:T(1,128)S(1)} custom-call(bf16[272,768]{1,0:T(8,128)(2,1)S(1)} %collective-permute-done.14.refs_0_, bf16[272,768]{1,0:T(8,128)(2,1)S(1)} %get-tuple-element.118.refs_1_.refs_2_.refs_3_, f32[1,256]{1,0:T(1,128)S(1)} %get-tuple-element.193.refs_2_, ...), custom_call_target="tpu_custom_call" | custom-call | flops 805306368 | tf_op jit(solution)/shard_map/last/pallas_call | solution.py:410
  80.3 7.1 %all_to_all.10.back_ref = f32[8,1,256]{2,1,0:T(1,128)S(1)} all-to-all(f32[8,1,256]{2,1,0:T(1,128)S(1)} %last.1), channel_id=1, replica_groups=mesh['gx'=4,'gy'=8] {'gy'}, dimensions={0} | all-to-all | bytes 16384 | tf_op jit(solution)/shard_map/all_to_all | solution.py:420
  87.4 0.8 finish.1
  (1 shorter events, 0.0 us)
Async XLA Ops:
  0.1 0.7 copy-start
  0.8 0.7 copy-start.1
  1.4 10.7 %copy-start.2 = (bf16[1024,768]{1,0:T(8,128)(2,1)S(1)}, bf16[1024,768]{1,0:T(8,128)(2,1)}, u32[]{:S(2)}) copy-start(bf16[1024,768]{1,0:T(8,128)(2,1)} %param.3) | copy-start | bytes 4718596
  3.0 14.5 %all-to-all-start = ((s32[32,1,32]{2,1,0:T(1,128)}), s32[32,1,32]{2,1,0:T(1,128)S(1)}, u32[]{:S(2)}, u32[]{:S(2)}) async-start(s32[32,1,32]{2,1,0:T(1,128)} %get-tuple-element.104), calls=%async_computation | async-start | bytes 32768 | tf_op jit(solution)/shard_map/all_to_all | solution.py:265
  19.4 18.5 %collective-permute-start = (bf16[288,768]{1,0:T(8,128)(2,1)S(1)}, bf16[288,768]{1,0:T(8,128)(2,1)S(1)}, u32[]{:S(2)}, u32[]{:S(2)}) collective-permute-start(bf16[288,768]{1,0:T(8,128)(2,1)S(1)} %get-tuple-element.107), channel_id=1, source_target_pairs={{0,8},{8,16},{16,24},{24,0},{1,9},{9,17},{17,25},{25,1},{2,10},{10... | collective-permute-start | bytes 1327112 | tf_op jit(solution)/shard_map/ppermute | solution.py:293
  20.0 21.1 %collective-permute-start.1 = (bf16[288,768]{1,0:T(8,128)(2,1)S(1)}, bf16[288,768]{1,0:T(8,128)(2,1)S(1)}, u32[]{:S(2)}, u32[]{:S(2)}) collective-permute-start(bf16[288,768]{1,0:T(8,128)(2,1)S(1)} %get-tuple-element.108), channel_id=1, source_target_pairs={{0,24},{8,0},{16,8},{24,16},{1,25},{9,1},{17,9},{25,17},{2,26},{10... | collective-permute-start | bytes 1327112 | tf_op jit(solution)/shard_map/ppermute | solution.py:293
  25.2 10.9 %collective-permute-start.2 = (bf16[272,768]{1,0:T(8,128)(2,1)S(1)}, bf16[272,768]{1,0:T(8,128)(2,1)S(1)}, u32[]{:S(2)}, u32[]{:S(2)}) collective-permute-start(bf16[272,768]{1,0:T(8,128)(2,1)S(1)} %get-tuple-element.118.refs_1_.refs_2_.refs_3_), channel_id=1, source_target_pairs={{0,2},{1,3},{2,0},{3,1},{4,6},{5,7},{6,4},{7,5},{8,10},{9,11},{10,... | collective-permute-start | bytes 1253384 | tf_op jit(solution)/shard_map/ppermute | solution.py:296
  25.8 10.3 %collective-permute-start.3 = (bf16[272,768]{1,0:T(8,128)(2,1)S(1)}, bf16[272,768]{1,0:T(8,128)(2,1)S(1)}, u32[]{:S(2)}, u32[]{:S(2)}) collective-permute-start(bf16[272,768]{1,0:T(8,128)(2,1)S(1)} %get-tuple-element.118.refs_1_.refs_2_.refs_3_), channel_id=1, source_target_pairs={{0,1},{1,0},{2,3},{3,2},{4,5},{5,4},{6,7},{7,6},{8,9},{9,8},{10,11... | collective-permute-start | bytes 1253384 | tf_op jit(solution)/shard_map/ppermute | solution.py:296
  25.8 12.1 %collective-permute-start.4 = (bf16[272,768]{1,0:T(8,128)(2,1)S(1)}, bf16[272,768]{1,0:T(8,128)(2,1)S(1)}, u32[]{:S(2)}, u32[]{:S(2)}) collective-permute-start(bf16[272,768]{1,0:T(8,128)(2,1)S(1)} %get-tuple-element.118.refs_1_.refs_2_.refs_3_), channel_id=1, source_target_pairs={{0,4},{1,5},{2,6},{3,7},{4,0},{5,1},{6,2},{7,3},{8,12},{9,13},{10,... | collective-permute-start | bytes 1253384 | tf_op jit(solution)/shard_map/ppermute | solution.py:296
  41.1 21.8 %collective-permute-start.5 = (bf16[288,768]{1,0:T(8,128)(2,1)S(1)}, bf16[288,768]{1,0:T(8,128)(2,1)S(1)}, u32[]{:S(2)}, u32[]{:S(2)}) collective-permute-start(bf16[288,768]{1,0:T(8,128)(2,1)S(1)} %get-tuple-element.112), channel_id=1, source_target_pairs={{0,16},{8,24},{16,0},{24,8},{1,17},{9,25},{17,1},{25,9},{2,18},{10... | collective-permute-start | bytes 1327112 | tf_op jit(solution)/shard_map/ppermute | solution.py:293
  43.3 12.6 %collective-permute-start.6 = (bf16[272,768]{1,0:T(8,128)(2,1)S(1)}, bf16[272,768]{1,0:T(8,128)(2,1)S(1)}, u32[]{:S(2)}, u32[]{:S(2)}) collective-permute-start(bf16[272,768]{1,0:T(8,128)(2,1)S(1)} %get-tuple-element.130.refs_2_.refs_1_.refs_3_.refs_4_.refs_5_), channel_id=1, source_target_pairs={{0,2},{1,3},{2,0},{3,1},{4,6},{5,7},{6,4},{7,5},{8,10},{9,11},{10,... | collective-permute-start | bytes 1253384 | tf_op jit(solution)/shard_map/ppermute | solution.py:296
  43.9 12.6 %collective-permute-start.7 = (bf16[272,768]{1,0:T(8,128)(2,1)S(1)}, bf16[272,768]{1,0:T(8,128)(2,1)S(1)}, u32[]{:S(2)}, u32[]{:S(2)}) collective-permute-start(bf16[272,768]{1,0:T(8,128)(2,1)S(1)} %get-tuple-element.130.refs_2_.refs_1_.refs_3_.refs_4_.refs_5_), channel_id=1, source_target_pairs={{0,4},{1,5},{2,6},{3,7},{4,0},{5,1},{6,2},{7,3},{8,12},{9,13},{10,... | collective-permute-start | bytes 1253384 | tf_op jit(solution)/shard_map/ppermute | solution.py:296
  44.5 18.2 %collective-permute-start.8 = (bf16[272,768]{1,0:T(8,128)(2,1)S(1)}, bf16[272,768]{1,0:T(8,128)(2,1)S(1)}, u32[]{:S(2)}, u32[]{:S(2)}) collective-permute-start(bf16[272,768]{1,0:T(8,128)(2,1)S(1)} %get-tuple-element.131.refs_3_.refs_2_.refs_4_.refs_5_.refs_9_), channel_id=1, source_target_pairs={{0,2},{1,3},{2,0},{3,1},{4,6},{5,7},{6,4},{7,5},{8,10},{9,11},{10,... | collective-permute-start | bytes 1253384 | tf_op jit(solution)/shard_map/ppermute | solution.py:296
  45.9 17.0 %collective-permute-start.9 = (bf16[272,768]{1,0:T(8,128)(2,1)S(1)}, bf16[272,768]{1,0:T(8,128)(2,1)S(1)}, u32[]{:S(2)}, u32[]{:S(2)}) collective-permute-start(bf16[272,768]{1,0:T(8,128)(2,1)S(1)} %get-tuple-element.131.refs_3_.refs_2_.refs_4_.refs_5_.refs_9_), channel_id=1, source_target_pairs={{0,4},{1,5},{2,6},{3,7},{4,0},{5,1},{6,2},{7,3},{8,12},{9,13},{10,... | collective-permute-start | bytes 1253384 | tf_op jit(solution)/shard_map/ppermute | solution.py:296
  63.1 6.5 %collective-permute-start.12 = (bf16[1296,768]{1,0:T(8,128)(2,1)S(1)}, bf16[1296,768]{1,0:T(8,128)(2,1)S(1)}, u32[]{:S(2)}, u32[]{:S(2)}) collective-permute-start(bf16[1296,768]{1,0:T(8,128)(2,1)S(1)} %get-tuple-element.135), channel_id=1, source_target_pairs={{0,1},{1,0},{2,3},{3,2},{4,5},{5,4},{6,7},{7,6},{8,9},{9,8},{10,11... | collective-permute-start | bytes 5971976 | tf_op jit(solution)/shard_map/ppermute | solution.py:296
  63.2 6.4 %collective-permute-start.11 = (bf16[272,768]{1,0:T(8,128)(2,1)S(1)}, bf16[272,768]{1,0:T(8,128)(2,1)S(1)}, u32[]{:S(2)}, u32[]{:S(2)}) collective-permute-start(bf16[272,768]{1,0:T(8,128)(2,1)S(1)} %get-tuple-element.177.refs_4_.refs_5_.refs_6_.refs_13_), channel_id=1, source_target_pairs={{0,1},{1,0},{2,3},{3,2},{4,5},{5,4},{6,7},{7,6},{8,9},{9,8},{10,11... | collective-permute-start | bytes 1253384 | tf_op jit(solution)/shard_map/ppermute | solution.py:296
  63.7 11.6 %collective-permute-start.10 = (bf16[272,768]{1,0:T(8,128)(2,1)S(1)}, bf16[272,768]{1,0:T(8,128)(2,1)S(1)}, u32[]{:S(2)}, u32[]{:S(2)}) collective-permute-start(bf16[272,768]{1,0:T(8,128)(2,1)S(1)} %get-tuple-element.177.refs_4_.refs_5_.refs_6_.refs_13_), channel_id=1, source_target_pairs={{0,2},{1,3},{2,0},{3,1},{4,6},{5,7},{6,4},{7,5},{8,10},{9,11},{10,... | collective-permute-start | bytes 1253384 | tf_op jit(solution)/shard_map/ppermute | solution.py:296
  65.2 11.3 %collective-permute-start.13 = (bf16[272,768]{1,0:T(8,128)(2,1)S(1)}, bf16[272,768]{1,0:T(8,128)(2,1)S(1)}, u32[]{:S(2)}, u32[]{:S(2)}) collective-permute-start(bf16[272,768]{1,0:T(8,128)(2,1)S(1)} %get-tuple-element.177.refs_4_.refs_5_.refs_6_.refs_13_), channel_id=1, source_target_pairs={{0,4},{1,5},{2,6},{3,7},{4,0},{5,1},{6,2},{7,3},{8,12},{9,13},{10,... | collective-permute-start | bytes 1253384 | tf_op jit(solution)/shard_map/ppermute | solution.py:296
  76.5 2.6 %collective-permute-start.14 = (bf16[272,768]{1,0:T(8,128)(2,1)S(1)}, bf16[272,768]{1,0:T(8,128)(2,1)S(1)}, u32[]{:S(2)}, u32[]{:S(2)}) collective-permute-start(bf16[272,768]{1,0:T(8,128)(2,1)S(1)} %collective-permute-done.10.refs_10_), channel_id=1, source_target_pairs={{0,1},{1,0},{2,3},{3,2},{4,5},{5,4},{6,7},{7,6},{8,9},{9,8},{10,11... | collective-permute-start | bytes 1253384 | tf_op jit(solution)/shard_map/ppermute | solution.py:296

commit v4 on v3

--- a/solution.py
+++ b/solution.py
@@ -10,7 +10,7 @@
 F32 = jnp.float32
 BF16 = jnp.bfloat16
 I32 = jnp.int32
-META = 16
+SPARE = 8
 KEYS = 4
 VMEM = 24 * 1024 * 1024
 
@@ -36,21 +36,29 @@
     return value.bit_length() - 1
 
 
-def params():
-    return pltpu.CompilerParams(vmem_limit_bytes=VMEM)
+def params(limit=VMEM):
+    return pltpu.CompilerParams(vmem_limit_bytes=limit)
 
 
 def cost(flops, size):
     return pl.CostEstimate(flops=flops, bytes_accessed=size, transcendentals=0)
 
 
-def request_kernel(dims, place_ref, sizes_ref, members_ref, asked_ref, home_ref):
+def request_kernel(dims, sizes_hbm, members_hbm, asked_ref, home_ref, sizes_ref, members_ref, sems):
     n_gx, n_gy, rows, quota = dims
+    copies = [
+        pltpu.make_async_copy(members_hbm, members_ref, sems.at[0]),
+        pltpu.make_async_copy(sizes_hbm, sizes_ref, sems.at[1]),
+    ]
+    for copy in copies:
+        copy.start()
+    for copy in copies:
+        copy.wait()
     owners = n_gx * n_gy
     member = members_ref[...]
     owner = lax.shift_right_logical(member, log2(rows))
     row = member & (rows - 1)
-    slot = place_ref[1] * rows + iota((1, rows), 1)
+    slot = lax.axis_index("gy") * rows + iota((1, rows), 1)
     cluster = jnp.zeros((1, rows), I32)
     end = jnp.int32(0)
     for c in range(sizes_ref.shape[1]):
@@ -81,12 +89,12 @@
     for o in range(owners):
         asked_ref[o] = asked[o:o + 1, :]
     plane = lax.shift_right_logical(owner, log2(n_gy))
-    step = (place_ref[0] - plane) & (n_gx - 1)
+    step = (lax.axis_index("gx") - plane) & (n_gx - 1)
     home_ref[0:1, :] = owner & (n_gy - 1)
     home_ref[1:2, :] = step * quota + rank
 
 
-def select_kernel(dims, steps, place_ref, asked_ref, unit_ref, *out_refs):
+def select_kernel(dims, steps, asked_ref, unit_ref, *out_refs):
     n_gx, n_gy, rows, quota = dims
     chunk = n_gy * quota
     pick = one_hot((iota((chunk, quota), 0) & (quota - 1)) == iota((chunk, quota), 1))
@@ -95,7 +103,7 @@
     block_row = lax.shift_right_logical(iota((n_gy, chunk), 1), log2(quota))
     own_row = block_row == iota((n_gy, chunk), 0)
     for step, ref in zip(steps, out_refs):
-        plane = (place_ref[0] + step) & (n_gx - 1)
+        plane = (lax.axis_index("gx") + step) & (n_gx - 1)
         wanted = jnp.concatenate([asked_ref[plane * n_gy + d] for d in range(n_gy)], axis=0)
         row = wanted & (rows - 1)
         cluster = lax.shift_right_logical(wanted, log2(rows)).astype(F32).astype(BF16)
@@ -108,7 +116,7 @@
         ref[0:chunk, :] = dot_nn(hot, unit_ref[...]).astype(BF16)
         width = unit_ref.shape[1]
         line = jnp.concatenate([flat, jnp.zeros((1, width - chunk), F32)], axis=1)
-        ref[chunk:chunk + META, :] = jnp.where(iota((META, width), 0) == 0, line, 0.0).astype(BF16)
+        ref[chunk:chunk + SPARE, :] = jnp.where(iota((SPARE, width), 0) == 0, line, 0.0).astype(BF16)
 
 
 def column(line):
@@ -123,8 +131,12 @@
     return jnp.concatenate([col] * (lanes // 128), axis=1)
 
 
+def more(chunks):
+    return -(-chunks // SPARE) * SPARE
+
+
 def cluster_line(ref, size, chunk):
-    block = ref[size:size + META, 0:chunk].astype(F32)
+    block = ref[size:size + more(size // chunk), 0:chunk].astype(F32)
     return jnp.concatenate([block[r:r + 1, :] for r in range(size // chunk)], axis=1)
 
 
@@ -135,15 +147,16 @@
         at = 0
         total = sum(sizes[n] for n in group)
         width = out_ref.shape[1]
-        meta = jnp.zeros((META, width), F32)
+        extra = more(total // chunk)
+        meta = jnp.zeros((extra, width), F32)
         for name in group:
             ref, size = refs.pop(0), sizes[name]
             out_ref[at:at + size, :] = ref[0:size, :]
-            lines = ref[size:size + META, :].astype(F32)
+            lines = ref[size:size + more(size // chunk), :].astype(F32)
             for r in range(size // chunk):
-                meta = jnp.where(iota((META, width), 0) == at // chunk + r, lines[r:r + 1, :], meta)
+                meta = jnp.where(iota((extra, width), 0) == at // chunk + r, lines[r:r + 1, :], meta)
             at += size
-        out_ref[total:total + META, :] = meta.astype(BF16)
+        out_ref[total:total + extra, :] = meta.astype(BF16)
 
 
 def product_kernel(pairs, sizes, chunk, started, close, *refs):
@@ -251,17 +264,21 @@
     n_query = n_gy // KEYS
     dims = (n_gx, n_gy, rows, quota)
     in_vmem = pl.BlockSpec(memory_space=pltpu.VMEM)
-    in_smem = pl.BlockSpec(memory_space=pltpu.SMEM)
-    place = jnp.stack([lax.axis_index("gx"), lax.axis_index("gy")]).astype(I32)
-
+
+    in_hbm = pl.BlockSpec(memory_space=pltpu.HBM)
     asked, home = pl.pallas_call(
         functools.partial(request_kernel, dims),
         out_shape=(shape((owners, 1, quota), I32), shape((2, rows), I32)),
-        in_specs=[in_smem, in_smem, in_vmem],
+        in_specs=[in_hbm, in_hbm],
         out_specs=(in_vmem, in_vmem),
-        compiler_params=params(),
+        scratch_shapes=[
+            pltpu.SMEM(sizes.shape, I32),
+            pltpu.VMEM((1, rows), I32),
+            pltpu.SemaphoreType.DMA((2,)),
+        ],
+        compiler_params=params(56 * 1024 * 1024),
         name="request",
-    )(place, sizes, members.reshape(1, rows))
+    )(sizes, members.reshape(1, rows))
     asked = lax.all_to_all(asked, ("gx", "gy"), split_axis=0, concat_axis=0, tiled=True)
 
     values = embeddings.astype(F32)
@@ -270,24 +287,22 @@
 
     stages = [[0], [1, n_gx - 1], list(range(2, n_gx - 1))]
 
-    def select(steps, unit):
-        found = pl.pallas_call(
+    def meet(*arrays):
+        return lax.optimization_barrier(arrays)
+
+    found = {}
+    for steps in [stages[1][:1], stages[0], stages[1][1:] + stages[2]]:
+        out = pl.pallas_call(
             functools.partial(select_kernel, dims, steps),
-            out_shape=[shape((chunk + (2 if k else 1) * META, width), BF16) for k in steps],
-            in_specs=[in_smem, in_vmem, in_vmem],
+            out_shape=[shape((chunk + (2 if k else 1) * SPARE, width), BF16) for k in steps],
+            in_specs=[in_vmem, in_vmem],
             out_specs=[in_vmem] * len(steps),
             cost_estimate=cost(2 * len(steps) * chunk * rows * width, rows * width),
             compiler_params=params(),
             name="select",
-        )(place, asked, unit)
-        return dict(zip(steps, found))
-
-    def meet(*arrays):
-        return lax.optimization_barrier(arrays)
-
-    found = select(stages[1], unit)
-    unit, *first = meet(unit, *found.values())
-    found = {**dict(zip(found, first)), **select(stages[0] + stages[2], unit)}
+        )(asked, unit)
+        unit, *out = meet(unit, *out)
+        found.update(zip(steps, out))
 
     def across(array, step):
         return lax.ppermute(array, "gx", [(i, (i + step) % n_gx) for i in range(n_gx)])
@@ -314,7 +329,7 @@
             size[name] = sum(size[n] for n in group)
         out = pl.pallas_call(
             functools.partial(pack_kernel, list(groups.values()), size, chunk),
-            out_shape=[shape((size[n] + META, width), BF16) for n in groups],
+            out_shape=[shape((size[n] + more(size[n] // chunk), width), BF16) for n in groups],
             in_specs=[in_vmem] * len(flat),
             out_specs=[in_vmem] * len(groups),
             cost_estimate=cost(0, 4 * sum(size[n] for n in flat) * width),
@@ -338,20 +353,6 @@
 
     def kinds(kinds, names):
         return [k + n for n in names for k in kinds]
-
-    for k in edge:
-        piece["z%d" % k] = across(found[k], k)
-    piece["T0"] = found[0]
-    near("0")
-    piece["N0"] = swap(piece["T0"], 1)
-    for k in rest:
-        piece["f%d" % k] = found[k]
-    join(["z%d" % k for k in edge] + ["f%d" % k for k in rest] + kinds(["T", "X", "N"] + far, ["0"]))
-    for k in rest:
-        piece["z%d" % k] = across(piece["f%d" % k], k)
-    pack({"T%d" % k: ["z%d" % k] for k in edge})
-    for k in edge:
-        near("%d" % k)
 
     def products(pairs, close=False):
         names = sorted({n for q, ks in pairs for n in [q] + ks})
@@ -377,28 +378,55 @@
         for i, q in enumerate(queries):
             state[q] = out[i] if close else (out[2 * i], out[2 * i + 1])
 
-    one = ["0"] + ["%d" % k for k in edge]
-    side = one[1:]
-    tops = kinds(["T"], one) + kinds(far, ["0"])
-    keys = ["N0", "X0"] + kinds(["T"], one)
-    products([(q, keys) for q in tops])
-    join(["z%d" % k for k in rest] + kinds(["T", "X"] + far, side))
-    pack({"Tb": ["z%d" % k for k in rest], "P": kinds(["T"], side) + kinds(["X"], one)})
+    def swap_core(name, group):
+        pack({"P": group})
+        piece[name] = swap(piece["P"], 1)
+        size[name] = size["P"]
+
+    first, second = edge
+    a, b = "%d" % first, "%d" % second
+    for k in edge:
+        piece["z%d" % k] = across(found[k], k)
+    piece["T0"] = found[0]
+    near("0")
+    piece["N0"] = swap(piece["T0"], 1)
+    for k in rest:
+        piece["f%d" % k] = found[k]
+    join(["z" + a] + ["f%d" % k for k in rest] + kinds(["T", "X", "N"] + far, ["0"]))
+
+    for k in rest:
+        piece["z%d" % k] = across(piece["f%d" % k], k)
+    pack({"T" + a: ["z" + a]})
+    near(a)
+    piece["Z0"] = swap(piece["X0"], 1)
+    keys = ["T0", "N0", "X0", "T" + a]
+    before = ["T0"] + kinds(far, ["0"]) + ["T" + a]
+    products([(q, keys) for q in before])
+    join(["z" + b, "Z0"] + kinds(["T", "X"] + far, [a]))
+
+    pack({"T" + b: ["z" + b]})
+    near(b)
+    new = ["X" + a, "T" + b, "Z0"]
+    keys = keys + new
+    late = kinds(far, [a]) + ["T" + b]
+    products([(q, new) for q in before] + [(q, keys) for q in late])
+    before = before + late
+    join(["z%d" % k for k in rest] + kinds(["T", "X"] + far, [b]))
+
+    pack({"Tb": ["z%d" % k for k in rest]})
     near("b")
-    piece["Nb"] = swap(piece["Tb"], 1)
-    piece["Q"] = swap(piece["P"], 1)
-    size["Q"] = size["P"]
-    late = kinds(far, side)
-    sides = kinds(["X"], side)
-    products(
-        [(q, sides + ["Tb"]) for q in tops]
-        + [(q, keys + sides + ["Tb"]) for q in late + ["Tb"]]
-    )
-    before = tops + late + ["Tb"]
-    products([(q, ["Q", "Nb"]) for q in before])
-    join(["Tb", "Xb", "Nb", "Q"] + kinds(far, ["b"]))
+    swap_core("Q", kinds(["T", "X"], [a, b]) + ["Tb"])
+    new = ["X" + b, "Tb"]
+    keys = keys + new
+    late = kinds(far, [b]) + ["Tb"]
+    products([(q, new) for q in before] + [(q, keys) for q in late])
+    before = before + late
+    products([(q, ["Q"]) for q in before])
+    keys = keys + ["Q", "Xb"]
+    join(["Tb", "Xb", "Q"] + kinds(far, ["b"]))
+
     piece["Zb"] = swap(piece["Xb"], 1)
-    products([(q, ["Xb"]) for q in before] + [(q, keys + sides + ["Tb", "Q", "Nb", "Xb"]) for q in kinds(far, ["b"])], close=True)
+    products([(q, ["Xb"]) for q in before] + [(q, keys) for q in kinds(far, ["b"])], close=True)
 
     order = []
     inputs = []

time: 88.5 us -> 81.9 us (0.925)
  starting transfers between devices: 21.2 us -> 17.7 us
  waiting for transfers between devices: 35.2 us -> 33.1 us
  local copies, waits for them, and re-layouts: 1.34 us -> 0.01 us
    ppermute x12, waiting for transfers between devices: 26.9 us -> 14.7 us  [swap(): return lax.ppermute(array, 'gy', [(i, i ^ mask) for i in range(n_gy)])]
    ppermute x3, waiting for transfers between devices: 3.25 us -> 13.4 us  [across(): lax.ppermute(array, 'gx', [(i, (i + step) % n_gx) for i in range(n_gx)])]
    ppermute x12, starting transfers between devices: 7.87 us -> 5.79 us  [swap(): return lax.ppermute(array, 'gy', [(i, i ^ mask) for i in range(n_gy)])]
    ppermute x3, starting transfers between devices: 6.04 us -> 4.65 us  [across(): lax.ppermute(array, 'gx', [(i, (i + step) % n_gx) for i in range(n_gx)])]
    unnamed x6 -> x4, local copies, waits for them, and re-layouts: 1.34 us -> 0.01 us
    pallas_call x2 -> x3, Pallas kernels: 3.86 us -> 3.06 us  [per_device(): pl.pallas_call(functools.partial(select_kernel, dims, steps), out_shape=[...]
    pallas_call x4 -> x5, Pallas kernels: 13.4 us -> 14 us  [products(): pl.pallas_call(functools.partial(product_kernel, pairs, size, chunk, star...]
  transfers between devices with their start and end apart: 16 -> 16, of which waited for: 10 -> 10; matrix products, arithmetic and copies ran while one was open for 2% -> 3% of each run, Pallas kernels for 18% -> 20%
where the time goes in v4:
time: 81.9 us; the launch traced here: 81.7 us
  waiting for transfers between devices  33.1 us (40%)
  Pallas kernels  21.1 us (26%)
  starting transfers between devices  17.7 us (22%)
  blocking collectives  7.38 us (9%)
  other arithmetic  2.11 us (3%)
    ppermute x12, waiting for transfers between devices, swap(): return lax.ppermute(array, 'gy', [(i, i ^ mask) for i in range(n_gy)])  14.7 us
    pallas_call x5, Pallas kernels, products(): pl.pallas_call(functools.partial(product_kernel, pairs, size, chunk, star...  14 us
    ppermute x3, waiting for transfers between devices, across(): lax.ppermute(array, 'gx', [(i, (i + step) % n_gx) for i in range(n_gx)])  13.4 us
    all_to_all x1, blocking collectives, per_device(): back = lax.all_to_all(send, 'gy', split_axis=0, concat_axis=0, tiled=True)  7.38 us
    all_to_all x1, starting transfers between devices, per_device(): lax.all_to_all(asked, ('gx', 'gy'), split_axis=0, concat_axis=0, tiled=True)  7.3 us
    ppermute x12, starting transfers between devices, swap(): return lax.ppermute(array, 'gy', [(i, i ^ mask) for i in range(n_gy)])  5.79 us
    all_to_all x1, waiting for transfers between devices, per_device(): lax.all_to_all(asked, ('gx', 'gy'), split_axis=0, concat_axis=0, tiled=True)  5 us
    ppermute x3, starting transfers between devices, across(): lax.ppermute(array, 'gx', [(i, (i + step) % n_gx) for i in range(n_gx)])  4.65 us
  transfers between devices with their start and end apart: 16, of which 10 were waited for; matrix products, arithmetic and copies ran while one was open for 3% of the time, Pallas kernels for 20%

profile of v4, /device:TPU:0, one launch (start us, length us, event | category | flops | bytes accessed | tf_op | source)
XLA Modules:
  0.0 81.7 jit_solution(17084150023203347947)
XLA Ops:
  0.0 0.0 copy-start.1
  0.0 1.9 %request.1 = (s32[32,1,32]{2,1,0:T(1,128)}, s32[2,1024]{1,0:T(2,128)}) custom-call(s32[1,25]{1,0:T(1,128)} %sizes_hbm.1, s32[1,1024]{1,0:T(1,128)} %bitcast.2), custom_call_target="tpu_custom_call" | custom-call | tf_op jit(solution)/shard_map/request/pallas_call | solution.py:269
  1.9 7.3 %all-to-all-start = ((s32[32,1,32]{2,1,0:T(1,128)}), s32[32,1,32]{2,1,0:T(1,128)S(1)}, u32[]{:S(2)}, u32[]{:S(2)}) async-start(s32[32,1,32]{2,1,0:T(1,128)} %get-tuple-element.117), calls=%async_computation | async-start | bytes 32768 | tf_op jit(solution)/shard_map/all_to_all | solution.py:282
  9.2 1.8 %fusion = f32[1024]{0:T(1024)S(1)} fusion(bf16[1024,768]{1,0:T(8,128)(2,1)} %param.3), kind=kLoop, calls=%fused_computation.2 | loop fusion | flops 2358272 | bytes 1576960 | tf_op jit(solution)/shard_map/reduce_sum | solution.py:285
  11.0 0.0 copy-done.1
  11.0 0.3 fusion.1.unit_ref
  11.3 5.0 %all-to-all-done.asked_ref = s32[32,1,32]{2,1,0:T(1,128)S(1)} async-done(((s32[32,1,32]{2,1,0:T(1,128)}), s32[32,1,32]{2,1,0:T(1,128)S(1)}, u32[]{:S(2)}, u32[]{:S(2)}) %all-to-all-start) | async-done | bytes 4128 | tf_op jit(solution)/shard_map/all_to_all | solution.py:282
  16.3 0.8 %select.3 = bf16[272,768]{1,0:T(8,128)(2,1)S(1)} custom-call(s32[32,1,32]{2,1,0:T(1,128)S(1)} %all-to-all-done.asked_ref, bf16[1024,768]{1,0:T(8,128)(2,1)S(1)} %fusion.1.unit_ref), custom_call_target="tpu_custom_call" | custom-call | flops 402653184 | bytes 786432 | tf_op jit(solution)/shard_map/select/pallas_call | solution.py:295
  17.2 0.6 collective-permute-start
  17.8 0.8 %select.4.refs_1_.refs_2_ = bf16[264,768]{1,0:T(8,128)(2,1)S(1)} custom-call(s32[32,1,32]{2,1,0:T(1,128)S(1)} %all-to-all-done.asked_ref, bf16[1024,768]{1,0:T(8,128)(2,1)S(1)} %fusion.1.unit_ref), custom_call_target="tpu_custom_call" | custom-call | flops 402653184 | bytes 786432 | tf_op jit(solution)/shard_map/select/pallas_call | solution.py:295
  18.6 0.6 collective-permute-start.1
  19.2 0.0 collective-permute-start.2
  19.3 0.6 collective-permute-start.3
  19.9 1.4 %select.5 = (bf16[272,768]{1,0:T(8,128)(2,1)S(1)}, bf16[272,768]{1,0:T(8,128)(2,1)S(1)}) custom-call(s32[32,1,32]{2,1,0:T(1,128)S(1)} %all-to-all-done.asked_ref, bf16[1024,768]{1,0:T(8,128)(2,1)S(1)} %fusion.1.unit_ref), custom_call_target="tpu_custom_call" | custom-call | flops 805306368 | bytes 786432 | tf_op jit(solution)/shard_map/select/pallas_call | solution.py:295
  21.3 3.5 %collective-permute-start.5 = (bf16[272,768]{1,0:T(8,128)(2,1)S(1)}, bf16[272,768]{1,0:T(8,128)(2,1)S(1)}, u32[]{:S(2)}, u32[]{:S(2)}) collective-permute-start(bf16[272,768]{1,0:T(8,128)(2,1)S(1)} %get-tuple-element.126), channel_id=1, source_target_pairs={{0,24},{8,0},{16,8},{24,16},{1,25},{9,1},{17,9},{25,17},{2,26},{10... | collective-permute-start | bytes 1253384 | tf_op jit(solution)/shard_map/ppermute | solution.py:308
  24.8 4.5 %collective-permute-done.1.refs_3_.refs_4_.refs_5_.refs_6_ = bf16[264,768]{1,0:T(8,128)(2,1)S(1)} collective-permute-done((bf16[264,768]{1,0:T(8,128)(2,1)S(1)}, bf16[264,768]{1,0:T(8,128)(2,1)S(1)}, u32[]{:S(2)}, u32[]{:S(2)}) %collective-permute-start.1) | collective-permute-done | bytes 405536 | tf_op jit(solution)/shard_map/ppermute | solution.py:311
  29.3 0.0 collective-permute-done.2.refs_0_
  29.3 1.7 %collective-permute-done.3.refs_4_.refs_6_.refs_8_.refs_5_.refs_10_.refs_3_ = bf16[264,768]{1,0:T(8,128)(2,1)S(1)} collective-permute-done((bf16[264,768]{1,0:T(8,128)(2,1)S(1)}, bf16[264,768]{1,0:T(8,128)(2,1)S(1)}, u32[]{:S(2)}, u32[]{:S(2)}) %collective-permute-start.3) | collective-permute-done | bytes 405536 | tf_op jit(solution)/shard_map/ppermute | solution.py:311
  31.0 0.6 collective-permute-done.refs_0_
  31.6 0.1 collective-permute-start.6
  31.7 1.0 %collective-permute-start.7 = (bf16[264,768]{1,0:T(8,128)(2,1)S(1)}, bf16[264,768]{1,0:T(8,128)(2,1)S(1)}, u32[]{:S(2)}, u32[]{:S(2)}) collective-permute-start(bf16[264,768]{1,0:T(8,128)(2,1)S(1)} %pack.4.refs_2_.refs_0_.refs_3_.refs_5_), channel_id=1, source_target_pairs={{0,2},{1,3},{2,0},{3,1},{4,6},{5,7},{6,4},{7,5},{8,10},{9,11},{10,... | collective-permute-start | bytes 1216520 | tf_op jit(solution)/shard_map/ppermute | solution.py:311
  32.7 0.6 collective-permute-start.8
  33.3 0.5 collective-permute-start.4
  33.8 1.4 %products.5 = (f32[256,128]{1,0:T(8,128)S(1)}, f32[256,128]{1,0:T(8,128)S(1)}, f32[256,128]{1,0:T(8,128)S(1)}, f32[256,128]{1,0:T(8,128)S(1)}, f32[256,128]{1,0:T(8,128)S(1)}, /*index=5*/f32[256,128]{1,0:T(8,128)S(1)}) custom-call(bf16[264,768]{1,0:T(8,128)(2,1)S(1)} %collective-permute-done.2.refs_0_, bf16[264,768]{1,0:T(8,128)(2,1)S(1)} %select.4.refs_1_.refs_2_, ...), custom_call_target="tpu_custom_call" | custom-call | flops 1207959552 | tf_op jit(solution)/shard_map/products/pallas_call | solution.py:369
  35.2 4.1 %collective-permute-done.5.refs_0_ = bf16[272,768]{1,0:T(8,128)(2,1)S(1)} collective-permute-done((bf16[272,768]{1,0:T(8,128)(2,1)S(1)}, bf16[272,768]{1,0:T(8,128)(2,1)S(1)}, u32[]{:S(2)}, u32[]{:S(2)}) %collective-permute-start.5) | collective-permute-done | bytes 417824 | tf_op jit(solution)/shard_map/ppermute | solution.py:308
  39.4 0.0 collective-permute-done.6.refs_8_.refs_11_.refs_14_
  39.4 4.1 %collective-permute-done.7.refs_5_.refs_1_.refs_6_.refs_7_ = bf16[264,768]{1,0:T(8,128)(2,1)S(1)} collective-permute-done((bf16[264,768]{1,0:T(8,128)(2,1)S(1)}, bf16[264,768]{1,0:T(8,128)(2,1)S(1)}, u32[]{:S(2)}, u32[]{:S(2)}) %collective-permute-start.7) | collective-permute-done | bytes 405536 | tf_op jit(solution)/shard_map/ppermute | solution.py:311
  43.5 0.7 collective-permute-done.8.refs_7_.refs_9_.refs_6_.refs_11_
  44.2 0.6 collective-permute-start.10
  44.8 1.1 %collective-permute-start.9 = (bf16[264,768]{1,0:T(8,128)(2,1)S(1)}, bf16[264,768]{1,0:T(8,128)(2,1)S(1)}, u32[]{:S(2)}, u32[]{:S(2)}) collective-permute-start(bf16[264,768]{1,0:T(8,128)(2,1)S(1)} %pack.5.refs_3_.refs_2_.refs_4_.refs_9_), channel_id=1, source_target_pairs={{0,2},{1,3},{2,0},{3,1},{4,6},{5,7},{6,4},{7,5},{8,10},{9,11},{10,... | collective-permute-start | bytes 1216520 | tf_op jit(solution)/shard_map/ppermute | solution.py:311
  45.9 2.7 %products.6 = (f32[256,128]{1,0:T(8,128)S(1)}, f32[256,128]{1,0:T(8,128)S(1)}, f32[256,128]{1,0:T(8,128)S(1)}, f32[256,128]{1,0:T(8,128)S(1)}, f32[256,128]{1,0:...) custom-call(bf16[264,768]{1,0:T(8,128)(2,1)S(1)} %collective-permute, ...), custom_call_target="tpu_custom_call" | custom-call | flops 2315255808 | tf_op jit(solution)/shard_map/products/pallas_call | solution.py:369
  48.6 8.7 %collective-permute-done.4.refs_0_ = bf16[272,768]{1,0:T(8,128)(2,1)S(1)} collective-permute-done((bf16[272,768]{1,0:T(8,128)(2,1)S(1)}, bf16[272,768]{1,0:T(8,128)(2,1)S(1)}, u32[]{:S(2)}, u32[]{:S(2)}) %collective-permute-start.4) | collective-permute-done | bytes 417824 | tf_op jit(solution)/shard_map/ppermute | solution.py:308
  57.3 0.0 collective-permute-done.10.refs_10_.refs_7_.refs_12_.refs_11_
  57.3 0.0 collective-permute-done.9.refs_3_.refs_7_.refs_8_
  57.3 0.1 pack.7
  57.5 0.1 collective-permute-start.12
  57.6 0.6 collective-permute-start.11
  58.2 0.5 collective-permute-start.13
  58.7 3.2 %products.7 = (f32[256,128]{1,0:T(8,128)S(1)}, f32[256,128]{1,0:T(8,128)S(1)}, f32[256,128]{1,0:T(8,128)S(1)}, f32[256,128]{1,0:T(8,128)S(1)}, f32[256,128]{1,0:...) custom-call(bf16[264,768]{1,0:T(8,128)(2,1)S(1)} %collective-permute, ...), custom_call_target="tpu_custom_call" | custom-call | flops 2818572288 | tf_op jit(solution)/shard_map/products/pallas_call | solution.py:369
  61.9 0.0 collective-permute-done.12.refs_0_.refs_1_
  61.9 4.1 %products.8 = (f32[256,128]{1,0:T(8,128)S(1)}, f32[256,128]{1,0:T(8,128)S(1)}, f32[256,128]{1,0:T(8,128)S(1)}, f32[256,128]{1,0:T(8,128)S(1)}, f32[256,128]{1,0:...) custom-call(bf16[1288,768]{1,0:T(8,128)(2,1)S(1)} %collective-permut, ...), custom_call_target="tpu_custom_call" | custom-call | flops 3523215360 | tf_op jit(solution)/shard_map/products/pallas_call | solution.py:369
  66.0 3.4 %collective-permute-done.11.refs_9_ = bf16[264,768]{1,0:T(8,128)(2,1)S(1)} collective-permute-done((bf16[264,768]{1,0:T(8,128)(2,1)S(1)}, bf16[264,768]{1,0:T(8,128)(2,1)S(1)}, u32[]{:S(2)}, u32[]{:S(2)}) %collective-permute-start.11) | collective-permute-done | bytes 405536 | tf_op jit(solution)/shard_map/ppermute | solution.py:311
  69.4 0.2 collective-permute-done.13.refs_13_.refs_15_
  69.6 0.0 collective-permute-start.14
  69.6 2.6 %products.9 = (f32[1,256]{1,0:T(1,128)S(1)}, f32[1,256]{1,0:T(1,128)S(1)}, f32[1,256]{1,0:T(1,128)S(1)}, f32[1,256]{1,0:T(1,128)S(1)}, f32[1,256]{1,0:T(1,128)S(...) custom-call(bf16[264,768]{1,0:T(8,128)(2,1)S(1)} %collective-permute-done.2.refs_0_, ...), custom_call_target="tpu_custom_call" | custom-call | flops 2214592512 | tf_op jit(solution)/shard_map/products/pallas_call | solution.py:369
  72.2 0.0 copy-start
  72.3 0.0 collective-permute-done.14.refs_0_
  72.3 1.2 %last.1 = f32[8,1,256]{2,1,0:T(1,128)S(1)} custom-call(bf16[264,768]{1,0:T(8,128)(2,1)S(1)} %collective-permute-done.14.refs_0_, bf16[264,768]{1,0:T(8,128)(2,1)S(1)} %select.4.refs_1_.refs_2_, f32[1,256]{1,0:T(1,128)S(1)} %get-tuple-element.219.refs_2_, bf16[264,768]{1,0:T(8,128)(2,1)S(1)} %collective-permute-done.3.refs_4_.refs_6_.refs_8_.refs_5_.refs_10_.refs_3_, ...), custom_call_target="tpu_custom_call" | custom-call | flops 805306368 | tf_op jit(solution)/shard_map/last/pallas_call | solution.py:438
  73.4 7.4 %all_to_all.10.back_ref = f32[8,1,256]{2,1,0:T(1,128)S(1)} all-to-all(f32[8,1,256]{2,1,0:T(1,128)S(1)} %last.1), channel_id=1, replica_groups=mesh['gx'=4,'gy'=8] {'gy'}, dimensions={0} | all-to-all | bytes 16384 | tf_op jit(solution)/shard_map/all_to_all | solution.py:448
  80.8 0.0 copy-done
  80.8 0.8 %finish.1 = f32[1,1024]{1,0:T(1,128)} custom-call(s32[2,1024]{1,0:T(2,128)S(1)} %copy-done, f32[8,1,256]{2,1,0:T(1,128)S(1)} %all_to_all.10.back_ref), custom_call_target="tpu_custom_call" | custom-call | tf_op jit(solution)/shard_map/finish/pallas_call | solution.py:449
  (4 shorter events, 0.1 us)
Async XLA Ops:
  0.0 11.0 %copy-start.1 = (bf16[1024,768]{1,0:T(8,128)(2,1)S(1)}, bf16[1024,768]{1,0:T(8,128)(2,1)}, u32[]{:S(2)}) copy-start(bf16[1024,768]{1,0:T(8,128)(2,1)} %param.3) | copy-start | bytes 4718596
  1.9 14.5 %all-to-all-start = ((s32[32,1,32]{2,1,0:T(1,128)}), s32[32,1,32]{2,1,0:T(1,128)S(1)}, u32[]{:S(2)}, u32[]{:S(2)}) async-start(s32[32,1,32]{2,1,0:T(1,128)} %get-tuple-element.117), calls=%async_computation | async-start | bytes 32768 | tf_op jit(solution)/shard_map/all_to_all | solution.py:282
  17.2 14.4 %collective-permute-start = (bf16[272,768]{1,0:T(8,128)(2,1)S(1)}, bf16[272,768]{1,0:T(8,128)(2,1)S(1)}, u32[]{:S(2)}, u32[]{:S(2)}) collective-permute-start(bf16[272,768]{1,0:T(8,128)(2,1)S(1)} %select.3), channel_id=1, source_target_pairs={{0,8},{8,16},{16,24},{24,0},{1,9},{9,17},{17,25},{25,1},{2,10},{10... | collective-permute-start | bytes 1253384 | tf_op jit(solution)/shard_map/ppermute | solution.py:308
  18.6 10.7 %collective-permute-start.1 = (bf16[264,768]{1,0:T(8,128)(2,1)S(1)}, bf16[264,768]{1,0:T(8,128)(2,1)S(1)}, u32[]{:S(2)}, u32[]{:S(2)}) collective-permute-start(bf16[264,768]{1,0:T(8,128)(2,1)S(1)} %select.4.refs_1_.refs_2_), channel_id=1, source_target_pairs={{0,2},{1,3},{2,0},{3,1},{4,6},{5,7},{6,4},{7,5},{8,10},{9,11},{10,... | collective-permute-start | bytes 1216520 | tf_op jit(solution)/shard_map/ppermute | solution.py:311
  19.2 10.1 %collective-permute-start.2 = (bf16[264,768]{1,0:T(8,128)(2,1)S(1)}, bf16[264,768]{1,0:T(8,128)(2,1)S(1)}, u32[]{:S(2)}, u32[]{:S(2)}) collective-permute-start(bf16[264,768]{1,0:T(8,128)(2,1)S(1)} %select.4.refs_1_.refs_2_), channel_id=1, source_target_pairs={{0,1},{1,0},{2,3},{3,2},{4,5},{5,4},{6,7},{7,6},{8,9},{9,8},{10,11... | collective-permute-start | bytes 1216520 | tf_op jit(solution)/shard_map/ppermute | solution.py:311
  19.3 11.8 %collective-permute-start.3 = (bf16[264,768]{1,0:T(8,128)(2,1)S(1)}, bf16[264,768]{1,0:T(8,128)(2,1)S(1)}, u32[]{:S(2)}, u32[]{:S(2)}) collective-permute-start(bf16[264,768]{1,0:T(8,128)(2,1)S(1)} %select.4.refs_1_.refs_2_), channel_id=1, source_target_pairs={{0,4},{1,5},{2,6},{3,7},{4,0},{5,1},{6,2},{7,3},{8,12},{9,13},{10,... | collective-permute-start | bytes 1216520 | tf_op jit(solution)/shard_map/ppermute | solution.py:311
  21.3 18.1 %collective-permute-start.5 = (bf16[272,768]{1,0:T(8,128)(2,1)S(1)}, bf16[272,768]{1,0:T(8,128)(2,1)S(1)}, u32[]{:S(2)}, u32[]{:S(2)}) collective-permute-start(bf16[272,768]{1,0:T(8,128)(2,1)S(1)} %get-tuple-element.126), channel_id=1, source_target_pairs={{0,24},{8,0},{16,8},{24,16},{1,25},{9,1},{17,9},{25,17},{2,26},{10... | collective-permute-start | bytes 1253384 | tf_op jit(solution)/shard_map/ppermute | solution.py:308
  31.6 7.8 %collective-permute-start.6 = (bf16[264,768]{1,0:T(8,128)(2,1)S(1)}, bf16[264,768]{1,0:T(8,128)(2,1)S(1)}, u32[]{:S(2)}, u32[]{:S(2)}) collective-permute-start(bf16[264,768]{1,0:T(8,128)(2,1)S(1)} %collective-permute-done.1.refs_3_.refs_4_.refs_5_.refs_6_), channel_id=1, source_target_pairs={{0,1},{1,0},{2,3},{3,2},{4,5},{5,4},{6,7},{7,6},{8,9},{9,8},{10,11... | collective-permute-start | bytes 1216520 | tf_op jit(solution)/shard_map/ppermute | solution.py:311
  31.7 11.8 %collective-permute-start.7 = (bf16[264,768]{1,0:T(8,128)(2,1)S(1)}, bf16[264,768]{1,0:T(8,128)(2,1)S(1)}, u32[]{:S(2)}, u32[]{:S(2)}) collective-permute-start(bf16[264,768]{1,0:T(8,128)(2,1)S(1)} %pack.4.refs_2_.refs_0_.refs_3_.refs_5_), channel_id=1, source_target_pairs={{0,2},{1,3},{2,0},{3,1},{4,6},{5,7},{6,4},{7,5},{8,10},{9,11},{10,... | collective-permute-start | bytes 1216520 | tf_op jit(solution)/shard_map/ppermute | solution.py:311
  32.7 11.4 %collective-permute-start.8 = (bf16[264,768]{1,0:T(8,128)(2,1)S(1)}, bf16[264,768]{1,0:T(8,128)(2,1)S(1)}, u32[]{:S(2)}, u32[]{:S(2)}) collective-permute-start(bf16[264,768]{1,0:T(8,128)(2,1)S(1)} %pack.4.refs_2_.refs_0_.refs_3_.refs_5_), channel_id=1, source_target_pairs={{0,4},{1,5},{2,6},{3,7},{4,0},{5,1},{6,2},{7,3},{8,12},{9,13},{10,... | collective-permute-start | bytes 1216520 | tf_op jit(solution)/shard_map/ppermute | solution.py:311
  33.3 24.0 %collective-permute-start.4 = (bf16[272,768]{1,0:T(8,128)(2,1)S(1)}, bf16[272,768]{1,0:T(8,128)(2,1)S(1)}, u32[]{:S(2)}, u32[]{:S(2)}) collective-permute-start(bf16[272,768]{1,0:T(8,128)(2,1)S(1)} %get-tuple-element.125), channel_id=1, source_target_pairs={{0,16},{8,24},{16,0},{24,8},{1,17},{9,25},{17,1},{25,9},{2,18},{10... | collective-permute-start | bytes 1253384 | tf_op jit(solution)/shard_map/ppermute | solution.py:308
  44.2 13.1 %collective-permute-start.10 = (bf16[264,768]{1,0:T(8,128)(2,1)S(1)}, bf16[264,768]{1,0:T(8,128)(2,1)S(1)}, u32[]{:S(2)}, u32[]{:S(2)}) collective-permute-start(bf16[264,768]{1,0:T(8,128)(2,1)S(1)} %pack.5.refs_3_.refs_2_.refs_4_.refs_9_), channel_id=1, source_target_pairs={{0,4},{1,5},{2,6},{3,7},{4,0},{5,1},{6,2},{7,3},{8,12},{9,13},{10,... | collective-permute-start | bytes 1216520 | tf_op jit(solution)/shard_map/ppermute | solution.py:311
  44.8 12.5 %collective-permute-start.9 = (bf16[264,768]{1,0:T(8,128)(2,1)S(1)}, bf16[264,768]{1,0:T(8,128)(2,1)S(1)}, u32[]{:S(2)}, u32[]{:S(2)}) collective-permute-start(bf16[264,768]{1,0:T(8,128)(2,1)S(1)} %pack.5.refs_3_.refs_2_.refs_4_.refs_9_), channel_id=1, source_target_pairs={{0,2},{1,3},{2,0},{3,1},{4,6},{5,7},{6,4},{7,5},{8,10},{9,11},{10,... | collective-permute-start | bytes 1216520 | tf_op jit(solution)/shard_map/ppermute | solution.py:311
  57.5 4.4 %collective-permute-start.12 = (bf16[1288,768]{1,0:T(8,128)(2,1)S(1)}, bf16[1288,768]{1,0:T(8,128)(2,1)S(1)}, u32[]{:S(2)}, u32[]{:S(2)}) collective-permute-start(bf16[1288,768]{1,0:T(8,128)(2,1)S(1)} %pack.7), channel_id=1, source_target_pairs={{0,1},{1,0},{2,3},{3,2},{4,5},{5,4},{6,7},{7,6},{8,9},{9,8},{10,11... | collective-permute-start | bytes 5935112 | tf_op jit(solution)/shard_map/ppermute | solution.py:311
  57.6 11.8 %collective-permute-start.11 = (bf16[264,768]{1,0:T(8,128)(2,1)S(1)}, bf16[264,768]{1,0:T(8,128)(2,1)S(1)}, u32[]{:S(2)}, u32[]{:S(2)}) collective-permute-start(bf16[264,768]{1,0:T(8,128)(2,1)S(1)} %pack.6.refs_4_.refs_5_.refs_13_), channel_id=1, source_target_pairs={{0,2},{1,3},{2,0},{3,1},{4,6},{5,7},{6,4},{7,5},{8,10},{9,11},{10,... | collective-permute-start | bytes 1216520 | tf_op jit(solution)/shard_map/ppermute | solution.py:311
  58.2 11.4 %collective-permute-start.13 = (bf16[264,768]{1,0:T(8,128)(2,1)S(1)}, bf16[264,768]{1,0:T(8,128)(2,1)S(1)}, u32[]{:S(2)}, u32[]{:S(2)}) collective-permute-start(bf16[264,768]{1,0:T(8,128)(2,1)S(1)} %pack.6.refs_4_.refs_5_.refs_13_), channel_id=1, source_target_pairs={{0,4},{1,5},{2,6},{3,7},{4,0},{5,1},{6,2},{7,3},{8,12},{9,13},{10,... | collective-permute-start | bytes 1216520 | tf_op jit(solution)/shard_map/ppermute | solution.py:311
  69.6 2.6 %collective-permute-start.14 = (bf16[264,768]{1,0:T(8,128)(2,1)S(1)}, bf16[264,768]{1,0:T(8,128)(2,1)S(1)}, u32[]{:S(2)}, u32[]{:S(2)}) collective-permute-start(bf16[264,768]{1,0:T(8,128)(2,1)S(1)} %collective-permute-done.11.refs_9_), channel_id=1, source_target_pairs={{0,1},{1,0},{2,3},{3,2},{4,5},{5,4},{6,7},{7,6},{8,9},{9,8},{10,11... | collective-permute-start | bytes 1216520 | tf_op jit(solution)/shard_map/ppermute | solution.py:311
  72.2 8.6 %copy-start = (s32[2,1024]{1,0:T(2,128)S(1)}, s32[2,1024]{1,0:T(2,128)}, u32[]{:S(2)}) copy-start(s32[2,1024]{1,0:T(2,128)} %get-tuple-element.116.home_ref) | copy-start | bytes 24580

commit v5 on v4

--- a/solution.py
+++ b/solution.py
@@ -159,26 +159,24 @@
         out_ref[total:total + extra, :] = meta.astype(BF16)
 
 
-def product_kernel(pairs, sizes, chunk, started, close, *refs):
+def product_kernel(pairs, sizes, chunk, started, turned, close, *refs):
     names = sorted({n for q, ks in pairs for n in [q] + ks})
     queries = [q for q, _ in pairs]
     refs = list(refs)
     rows = {n: refs.pop(0) for n in names}
     state = {q: (refs.pop(0), refs.pop(0)) for q in queries if q in started}
+    turns = {}
     for q, keys in pairs:
         n_q = sizes[q]
-        if close:
-            out_ref = refs.pop(0)
-        else:
-            col_ref, out_ref = refs.pop(0), refs.pop(0)
         if q in started:
             col = state[q][0][...]
             best = state[q][1][...]
         else:
             col = column(cluster_line(rows[q], n_q, chunk))
             best = jnp.full((n_q, 128), -1.0, F32)
-        if not close:
-            col_ref[...] = col
+            if not close:
+                refs.pop(0)[...] = col
+        out_ref = refs.pop(0)
         for k in keys:
             n_k = sizes[k]
             sims = dot_nt(rows[q][0:n_q, :], rows[k][0:n_k, :])
@@ -188,31 +186,37 @@
             sims = jnp.where(keep, sims, -1.0)
             for v in range(n_k // 128):
                 best = jnp.maximum(best, sims[:, v * 128:(v + 1) * 128])
+            if (q, k) in turned:
+                line = jnp.max(sims, axis=0, keepdims=True)
+                turns[k] = jnp.maximum(turns[k], line) if k in turns else line
         if close:
-            parts = [jnp.max(best[b * 128:(b + 1) * 128, :].T, axis=0, keepdims=True) for b in range(n_q // 128)]
-            out_ref[...] = jnp.concatenate(parts, axis=1)
+            out_ref[...] = lined(best)
         else:
             out_ref[...] = best
-
-
-def last_kernel(dims, queries, size, *refs):
+    for k in sorted(turns):
+        refs.pop(0)[...] = turns[k]
+
+
+def lined(best):
+    rows = best.shape[0]
+    parts = [jnp.max(best[b * 128:(b + 1) * 128, :].T, axis=0, keepdims=True) for b in range(rows // 128)]
+    return jnp.concatenate(parts, axis=1)
+
+
+def last_kernel(dims, queries, stage, size, key_ref, turn_t_ref, turn_n_ref, turn_x_ref, *refs):
     n_gx, n_gy, rows, quota = dims
     chunk = n_gy * quota
     refs = list(refs)
-    key_ref = refs.pop(0)
     send_ref = refs.pop()
     keys = key_ref[0:size, :]
     col = column(cluster_line(key_ref, size, chunk))
-    spread = {}
-    for (m, steps, n_q), row_ref, best_ref in zip(queries, refs[0::2], refs[1::2]):
-        sims = dot_nt(keys, row_ref[0:n_q, :])
-        keep = wide(col, n_q) == cluster_line(row_ref, n_q, chunk)
-        line = jnp.max(jnp.where(keep, sims, -1.0), axis=0, keepdims=True)
-        line = jnp.maximum(line, best_ref[...])
-        for c, step in enumerate(steps):
+    blocks = {}
+
+    def spread(block, line, groups):
+        for c, group in enumerate(groups):
             flat = line[:, c * chunk:(c + 1) * chunk]
-            block = lax.shift_right_logical(iota((n_gy, chunk), 1), log2(quota))
-            held = jnp.where(block == iota((n_gy, chunk), 0), flat, 0.0)
+            target = lax.shift_right_logical(iota((n_gy, chunk), 1), log2(quota))
+            held = jnp.where(target == iota((n_gy, chunk), 0), flat, 0.0)
             fold = held[:, 0:128]
             for v in range(1, chunk // 128):
                 fold = fold + held[:, v * 128:(v + 1) * 128]
@@ -220,25 +224,43 @@
             while shift >= quota:
                 fold = fold + pltpu.roll(fold, shift, 1)
                 shift //= 2
-            here = lax.shift_right_logical(iota((n_gy, 128), 1), log2(quota)) == step
+            here = lax.shift_right_logical(iota((n_gy, 128), 1), log2(quota)) == group
             fold = jnp.where(here, fold, 0.0)
-            spread[m] = spread[m] + fold if m in spread else fold
-    spread = jnp.concatenate([spread[m] for m in sorted(spread)], axis=1)
+            blocks[block] = blocks[block] + fold if block in blocks else fold
+
+    turn = jnp.full((size, 128), -1.0, F32)
+    for (m, steps, n_q), row_ref, best_ref in zip(queries, refs[0::2], refs[1::2]):
+        sims = dot_nt(keys, row_ref[0:n_q, :])
+        keep = wide(col, n_q) == cluster_line(row_ref, n_q, chunk)
+        sims = jnp.where(keep, sims, -1.0)
+        line = jnp.maximum(jnp.max(sims, axis=0, keepdims=True), best_ref[...])
+        if m and steps != stage:
+            for v in range(n_q // 128):
+                turn = jnp.maximum(turn, sims[:, v * 128:(v + 1) * 128])
+        if not m and steps == stage:
+            line = jnp.maximum(line, turn_t_ref[...])
+        spread(m, line, steps)
+    last = len(blocks)
+    for t, line in enumerate([turn_n_ref[...], turn_x_ref[...], lined(turn)]):
+        spread(last, line, range(t * len(stage), (t + 1) * len(stage)))
+    whole = jnp.concatenate([blocks[b] for b in range(last + 1)], axis=1)
     for d in range(n_gy):
-        send_ref[d] = spread[d:d + 1, :]
-
-
-def finish_kernel(dims, home_ref, back_ref, out_ref):
+        send_ref[d] = whole[d:d + 1, :]
+
+
+def finish_kernel(dims, stage, home_ref, back_ref, out_ref):
     n_gx, n_gy, rows, quota = dims
     n_query = n_gy // KEYS
-    lines = []
-    for q in range(n_gy):
-        best = None
-        for m in range(n_query):
-            part = back_ref[q ^ (KEYS * m)][:, m * 128:(m + 1) * 128]
-            best = part if best is None else jnp.maximum(best, part)
-        lines.append(best)
-    found = jnp.concatenate(lines, axis=0)
+    low, high = stage[0] * quota, (stage[-1] + 1) * quota
+    lane = iota((n_gy, 128), 1)
+    found = None
+    for m in range(n_query):
+        part = jnp.concatenate([back_ref[q ^ (KEYS * m)][:, m * 128:(m + 1) * 128] for q in range(n_gy)], axis=0)
+        found = part if found is None else jnp.maximum(found, part)
+    for t in range(1, KEYS):
+        part = jnp.concatenate([back_ref[q ^ t][:, n_query * 128:] for q in range(n_gy)], axis=0)
+        part = pltpu.roll(part, (low - (t - 1) * (high - low)) % 128, 1)
+        found = jnp.where((lane >= low) & (lane < high), jnp.maximum(found, part), found)
     high = found.astype(BF16)
     rest = found - high.astype(F32)
     mid = rest.astype(BF16)
@@ -354,7 +376,7 @@
     def kinds(kinds, names):
         return [k + n for n in names for k in kinds]
 
-    def products(pairs, close=False):
+    def products(pairs, turned=(), close=False):
         names = sorted({n for q, ks in pairs for n in [q] + ks})
         queries = [q for q, _ in pairs]
         started = [q for q in queries if q in state]
@@ -364,10 +386,12 @@
             if close:
                 outs.append(shape((1, size[q]), F32))
             else:
-                outs += [shape((size[q], 128), F32)] * 2
+                outs += [shape((size[q], 128), F32)] * (1 if q in started else 2)
+        turned = {(q, k) for q, ks in pairs for k in ks if k in turned and q[0] == "Y" and q[1:] != "b"}
+        outs += [shape((1, size[k]), F32) for k in sorted({k for _, k in turned})]
         flops = sum(2 * width * size[q] * size[k] for q, ks in pairs for k in ks)
         out = pl.pallas_call(
-            functools.partial(product_kernel, pairs, size, chunk, started, close),
+            functools.partial(product_kernel, pairs, size, chunk, started, turned, close),
             out_shape=outs,
             in_specs=[in_vmem] * len(inputs),
             out_specs=[in_vmem] * len(outs),
@@ -375,8 +399,14 @@
             compiler_params=params(),
             name="products",
         )(*inputs)
-        for i, q in enumerate(queries):
-            state[q] = out[i] if close else (out[2 * i], out[2 * i + 1])
+        out = list(out)
+        for q in queries:
+            if close:
+                state[q] = out.pop(0)
+            else:
+                col = state[q][0] if q in started else out.pop(0)
+                state[q] = (col, out.pop(0))
+        return out
 
     def swap_core(name, group):
         pack({"P": group})
@@ -415,18 +445,18 @@
 
     pack({"Tb": ["z%d" % k for k in rest]})
     near("b")
-    swap_core("Q", kinds(["T", "X"], [a, b]) + ["Tb"])
+    piece["Nb"] = swap(piece["Tb"], 1)
+    swap_core("Q", kinds(["T", "X"], [a, b]))
     new = ["X" + b, "Tb"]
     keys = keys + new
     late = kinds(far, [b]) + ["Tb"]
-    products([(q, new) for q in before] + [(q, keys) for q in late])
+    turn_t = products([(q, new) for q in before] + [(q, keys) for q in late], ["Tb"])
     before = before + late
-    products([(q, ["Q"]) for q in before])
-    keys = keys + ["Q", "Xb"]
-    join(["Tb", "Xb", "Q"] + kinds(far, ["b"]))
+    turn_n = products([(q, ["Q", "Nb"]) for q in before], ["Nb"])
+    join(["Tb", "Nb", "Xb"] + kinds(far, ["b"]))
 
     piece["Zb"] = swap(piece["Xb"], 1)
-    products([(q, ["Xb"]) for q in before] + [(q, keys) for q in kinds(far, ["b"])], close=True)
+    turn_x = products([(q, ["Xb"]) for q in before] + [(q, ["Tb", "Nb", "Xb"]) for q in kinds(far, ["b"])], ["Xb"], close=True)
 
     order = []
     inputs = []
@@ -435,19 +465,20 @@
             q = kind + n
             order.append((m, rest if n == "b" else [int(n)], size[q]))
             inputs += [piece[q], state[q]]
+    inputs = [piece["Zb"]] + turn_t + turn_n + turn_x + inputs
     send = pl.pallas_call(
-        functools.partial(last_kernel, dims, order, size["Zb"]),
-        out_shape=shape((n_gy, 1, n_query * 128), F32),
-        in_specs=[in_vmem] * (1 + len(inputs)),
+        functools.partial(last_kernel, dims, order, rest, size["Zb"]),
+        out_shape=shape((n_gy, 1, (n_query + 1) * 128), F32),
+        in_specs=[in_vmem] * len(inputs),
         out_specs=in_vmem,
         cost_estimate=cost(2 * width * size["Zb"] * n_query * rows, 0),
         compiler_params=params(),
         name="last",
-    )(piece["Zb"], *inputs)
+    )(*inputs)
 
     back = lax.all_to_all(send, "gy", split_axis=0, concat_axis=0, tiled=True)
     out = pl.pallas_call(
-        functools.partial(finish_kernel, dims),
+        functools.partial(finish_kernel, dims, rest),
         out_shape=shape((1, rows), F32),
         in_specs=[in_vmem, in_vmem],
         out_specs=in_vmem,

time: 81.9 us -> 81 us (0.989)
  Pallas kernels: 21.1 us -> 19.9 us
    ppermute x3, waiting for transfers between devices: 13.4 us -> 14.7 us  [across(): lax.ppermute(array, 'gx', [(i, (i + step) % n_gx) for i in range(n_gx)])]
    pallas_call x5, Pallas kernels: 14 us -> 12.7 us  [products(): pl.pallas_call(functools.partial(product_kernel, pairs, size, chunk, star...]
    ppermute x12 -> x13, waiting for transfers between devices: 14.7 us -> 14 us  [swap(): return lax.ppermute(array, 'gy', [(i, i ^ mask) for i in range(n_gy)])]
    ppermute x12 -> x13, starting transfers between devices: 5.79 us -> 5.78 us  [swap(): return lax.ppermute(array, 'gy', [(i, i ^ mask) for i in range(n_gy)])]
  transfers between devices with their start and end apart: 16 -> 17, of which waited for: 10 -> 11; matrix products, arithmetic and copies ran while one was open for 3% -> 3% of each run, Pallas kernels for 20% -> 19%
where the time goes in v5:
time: 81 us; the launch traced here: 80.8 us
  waiting for transfers between devices  33.7 us (42%)
  Pallas kernels  19.9 us (25%)
  starting transfers between devices  17.7 us (22%)
  blocking collectives  7.29 us (9%)
  other arithmetic  2.11 us (3%)
    ppermute x3, waiting for transfers between devices, across(): lax.ppermute(array, 'gx', [(i, (i + step) % n_gx) for i in range(n_gx)])  14.7 us
    ppermute x13, waiting for transfers between devices, swap(): return lax.ppermute(array, 'gy', [(i, i ^ mask) for i in range(n_gy)])  14 us
    pallas_call x5, Pallas kernels, products(): pl.pallas_call(functools.partial(product_kernel, pairs, size, chunk, star...  12.7 us
    all_to_all x1, starting transfers between devices, per_device(): lax.all_to_all(asked, ('gx', 'gy'), split_axis=0, concat_axis=0, tiled=True)  7.3 us
    all_to_all x1, blocking collectives, per_device(): back = lax.all_to_all(send, 'gy', split_axis=0, concat_axis=0, tiled=True)  7.29 us
    ppermute x13, starting transfers between devices, swap(): return lax.ppermute(array, 'gy', [(i, i ^ mask) for i in range(n_gy)])  5.78 us
    all_to_all x1, waiting for transfers between devices, per_device(): lax.all_to_all(asked, ('gx', 'gy'), split_axis=0, concat_axis=0, tiled=True)  4.99 us
    ppermute x3, starting transfers between devices, across(): lax.ppermute(array, 'gx', [(i, (i + step) % n_gx) for i in range(n_gx)])  4.61 us
  transfers between devices with their start and end apart: 17, of which 11 were waited for; matrix products, arithmetic and copies ran while one was open for 3% of the time, Pallas kernels for 19%

profile of v5, /device:TPU:0, one launch (start us, length us, event | category | flops | bytes accessed | tf_op | source)
XLA Modules:
  0.0 80.8 jit_solution(637307917631543389)
XLA Ops:
  0.0 0.0 copy-start.1
  0.0 1.9 %request.1 = (s32[32,1,32]{2,1,0:T(1,128)}, s32[2,1024]{1,0:T(2,128)}) custom-call(s32[1,25]{1,0:T(1,128)} %sizes_hbm.1, s32[1,1024]{1,0:T(1,128)} %bitcast.2), custom_call_target="tpu_custom_call" | custom-call | tf_op jit(solution)/shard_map/request/pallas_call | solution.py:291
  1.9 7.3 %all-to-all-start = ((s32[32,1,32]{2,1,0:T(1,128)}), s32[32,1,32]{2,1,0:T(1,128)S(1)}, u32[]{:S(2)}, u32[]{:S(2)}) async-start(s32[32,1,32]{2,1,0:T(1,128)} %get-tuple-element.105), calls=%async_computation | async-start | bytes 32768 | tf_op jit(solution)/shard_map/all_to_all | solution.py:304
  9.2 1.8 %fusion = f32[1024]{0:T(1024)S(1)} fusion(bf16[1024,768]{1,0:T(8,128)(2,1)} %param.3), kind=kLoop, calls=%fused_computation.2 | loop fusion | flops 2358272 | bytes 1576960 | tf_op jit(solution)/shard_map/reduce_sum | solution.py:307
  11.0 0.0 copy-done.1
  11.0 0.3 fusion.1.unit_ref
  11.3 5.0 %all-to-all-done.asked_ref = s32[32,1,32]{2,1,0:T(1,128)S(1)} async-done(((s32[32,1,32]{2,1,0:T(1,128)}), s32[32,1,32]{2,1,0:T(1,128)S(1)}, u32[]{:S(2)}, u32[]{:S(2)}) %all-to-all-start) | async-done | bytes 4128 | tf_op jit(solution)/shard_map/all_to_all | solution.py:304
  16.3 0.8 %select.3 = bf16[272,768]{1,0:T(8,128)(2,1)S(1)} custom-call(s32[32,1,32]{2,1,0:T(1,128)S(1)} %all-to-all-done.asked_ref, bf16[1024,768]{1,0:T(8,128)(2,1)S(1)} %fusion.1.unit_ref), custom_call_target="tpu_custom_call" | custom-call | flops 402653184 | bytes 786432 | tf_op jit(solution)/shard_map/select/pallas_call | solution.py:317
  17.2 0.6 collective-permute-start
  17.8 0.8 %select.4.refs_1_.refs_2_.refs_0_ = bf16[264,768]{1,0:T(8,128)(2,1)S(1)} custom-call(s32[32,1,32]{2,1,0:T(1,128)S(1)} %all-to-all-done.asked_ref, bf16[1024,768]{1,0:T(8,128)(2,1)S(1)} %fusion.1.unit_ref), custom_call_target="tpu_custom_call" | custom-call | flops 402653184 | bytes 786432 | tf_op jit(solution)/shard_map/select/pallas_call | solution.py:317
  18.6 0.6 collective-permute-start.1
  19.2 0.0 collective-permute-start.2
  19.2 0.6 collective-permute-start.3
  19.9 1.4 %select.5 = (bf16[272,768]{1,0:T(8,128)(2,1)S(1)}, bf16[272,768]{1,0:T(8,128)(2,1)S(1)}) custom-call(s32[32,1,32]{2,1,0:T(1,128)S(1)} %all-to-all-done.asked_ref, bf16[1024,768]{1,0:T(8,128)(2,1)S(1)} %fusion.1.unit_ref), custom_call_target="tpu_custom_call" | custom-call | flops 805306368 | bytes 786432 | tf_op jit(solution)/shard_map/select/pallas_call | solution.py:317
  21.3 3.5 %collective-permute-start.5 = (bf16[272,768]{1,0:T(8,128)(2,1)S(1)}, bf16[272,768]{1,0:T(8,128)(2,1)S(1)}, u32[]{:S(2)}, u32[]{:S(2)}) collective-permute-start(bf16[272,768]{1,0:T(8,128)(2,1)S(1)} %get-tuple-element.114), channel_id=1, source_target_pairs={{0,24},{8,0},{16,8},{24,16},{1,25},{9,1},{17,9},{25,17},{2,26},{10... | collective-permute-start | bytes 1253384 | tf_op jit(solution)/shard_map/ppermute | solution.py:330
  24.8 4.6 %collective-permute-done.1.refs_3_.refs_4_.refs_5_ = bf16[264,768]{1,0:T(8,128)(2,1)S(1)} collective-permute-done((bf16[264,768]{1,0:T(8,128)(2,1)S(1)}, bf16[264,768]{1,0:T(8,128)(2,1)S(1)}, u32[]{:S(2)}, u32[]{:S(2)}) %collective-permute-start.1) | collective-permute-done | bytes 405536 | tf_op jit(solution)/shard_map/ppermute | solution.py:333
  29.3 0.0 collective-permute-done.2.refs_0_
  29.3 1.7 %collective-permute-done.3.refs_4_.refs_6_.refs_8_.refs_2_ = bf16[264,768]{1,0:T(8,128)(2,1)S(1)} collective-permute-done((bf16[264,768]{1,0:T(8,128)(2,1)S(1)}, bf16[264,768]{1,0:T(8,128)(2,1)S(1)}, u32[]{:S(2)}, u32[]{:S(2)}) %collective-permute-start.3) | collective-permute-done | bytes 405536 | tf_op jit(solution)/shard_map/ppermute | solution.py:333
  31.0 0.6 collective-permute-done.refs_0_
  31.6 1.0 %collective-permute-start.7 = (bf16[264,768]{1,0:T(8,128)(2,1)S(1)}, bf16[264,768]{1,0:T(8,128)(2,1)S(1)}, u32[]{:S(2)}, u32[]{:S(2)}) collective-permute-start(bf16[264,768]{1,0:T(8,128)(2,1)S(1)} %pack.4.refs_2_.refs_0_.refs_3_.refs_4_), channel_id=1, source_target_pairs={{0,2},{1,3},{2,0},{3,1},{4,6},{5,7},{6,4},{7,5},{8,10},{9,11},{10,... | collective-permute-start | bytes 1216520 | tf_op jit(solution)/shard_map/ppermute | solution.py:333
  32.6 0.6 collective-permute-start.8
  33.2 0.0 collective-permute-start.6
  33.2 0.5 collective-permute-start.4
  33.7 1.4 %products.5 = (f32[256,128]{1,0:T(8,128)S(1)}, f32[256,128]{1,0:T(8,128)S(1)}, f32[256,128]{1,0:T(8,128)S(1)}, f32[256,128]{1,0:T(8,128)S(1)}, f32[256,128]{1,0:T(8,128)S(1)}, /*index=5*/f32[256,128]{1,0:T(8,128)S(1)}) custom-call(bf16[264,768]{1,0:T(8,128)(2,1)S(1)} %collective-permute-done.2.refs_0_, bf16[264,768]{1,0:T(8,128)(2,1)S(1)} %select.4.refs_1_.refs_2_.refs_0_, ...), custom_call_target="tpu_custom_call" | custom-call | flops 1207959552 | tf_op jit(solution)/shard_map/products/pallas_call | solution.py:393
  35.1 4.2 %collective-permute-done.5.refs_0_ = bf16[272,768]{1,0:T(8,128)(2,1)S(1)} collective-permute-done((bf16[272,768]{1,0:T(8,128)(2,1)S(1)}, bf16[272,768]{1,0:T(8,128)(2,1)S(1)}, u32[]{:S(2)}, u32[]{:S(2)}) %collective-permute-start.5) | collective-permute-done | bytes 417824 | tf_op jit(solution)/shard_map/ppermute | solution.py:330
  39.4 2.8 %collective-permute-done.7.refs_5_.refs_1_.refs_6_ = bf16[264,768]{1,0:T(8,128)(2,1)S(1)} collective-permute-done((bf16[264,768]{1,0:T(8,128)(2,1)S(1)}, bf16[264,768]{1,0:T(8,128)(2,1)S(1)}, u32[]{:S(2)}, u32[]{:S(2)}) %collective-permute-start.7) | collective-permute-done | bytes 405536 | tf_op jit(solution)/shard_map/ppermute | solution.py:333
  42.1 1.2 %collective-permute-done.8.refs_7_.refs_9_.refs_6_ = bf16[264,768]{1,0:T(8,128)(2,1)S(1)} collective-permute-done((bf16[264,768]{1,0:T(8,128)(2,1)S(1)}, bf16[264,768]{1,0:T(8,128)(2,1)S(1)}, u32[]{:S(2)}, u32[]{:S(2)}) %collective-permute-start.8) | collective-permute-done | bytes 405536 | tf_op jit(solution)/shard_map/ppermute | solution.py:333
  43.4 0.0 collective-permute-done.6.refs_8_.refs_11_
  43.4 0.6 collective-permute-start.10
  44.0 0.6 collective-permute-start.9
  44.6 2.7 %products.6 = (f32[256,128]{1,0:T(8,128)S(1)}, f32[256,128]{1,0:T(8,128)S(1)}, f32[256,128]{1,0:T(8,128)S(1)}, f32[256,128]{1,0:T(8,128)S(1)}, f32[256,128]{1,0:...) custom-call(bf16[264,768]{1,0:T(8,128)(2,1)S(1)} %collective-permute-done.2.refs_0_, ...), custom_call_target="tpu_custom_call" | custom-call | flops 2315255808 | tf_op jit(solution)/shard_map/products/pallas_call | solution.py:393
  47.3 10.0 %collective-permute-done.4.refs_0_ = bf16[272,768]{1,0:T(8,128)(2,1)S(1)} collective-permute-done((bf16[272,768]{1,0:T(8,128)(2,1)S(1)}, bf16[272,768]{1,0:T(8,128)(2,1)S(1)}, u32[]{:S(2)}, u32[]{:S(2)}) %collective-permute-start.4) | collective-permute-done | bytes 417824 | tf_op jit(solution)/shard_map/ppermute | solution.py:330
  57.3 0.0 collective-permute-done.10.refs_10_.refs_8_
  57.3 0.0 collective-permute-done.9.refs_3_.refs_7_
  57.3 0.1 pack.7
  57.4 0.1 collective-permute-start.14
  57.6 0.5 collective-permute-start.11
  58.1 0.5 collective-permute-start.12
  58.6 0.5 collective-permute-start.13
  59.2 3.2 %products.7 = (f32[256,128]{1,0:T(8,128)S(1)}, f32[256,128]{1,0:T(8,128)S(1)}, f32[256,128]{1,0:T(8,128)S(1)}, f32[256,128]{1,0:T(8,128)S(1)}, f32[256,128]{1,0:...) custom-call(bf16[264,768]{1,0:T(8,128)(2,1)S(1)} %collective-permute, ...), custom_call_target="tpu_custom_call" | custom-call | flops 2818572288 | tf_op jit(solution)/shard_map/products/pallas_call | solution.py:393
  62.4 0.0 collective-permute-done.11.refs_0_
  62.4 0.0 collective-permute-done.14.refs_1_
  62.4 4.0 %products.8 = (f32[256,128]{1,0:T(8,128)S(1)}, f32[256,128]{1,0:T(8,128)S(1)}, f32[256,128]{1,0:T(8,128)S(1)}, f32[256,128]{1,0:T(8,128)S(1)}, f32[256,128]{1,0:...) custom-call(bf16[264,768]{1,0:T(8,128)(2,1)S(1)} %collective-permute-done.11.refs_0_, ...), custom_call_target="tpu_custom_call" | custom-call | flops 3523215360 | tf_op jit(solution)/shard_map/products/pallas_call | solution.py:393
  66.4 3.1 %collective-permute-done.12.refs_5_ = bf16[264,768]{1,0:T(8,128)(2,1)S(1)} collective-permute-done((bf16[264,768]{1,0:T(8,128)(2,1)S(1)}, bf16[264,768]{1,0:T(8,128)(2,1)S(1)}, u32[]{:S(2)}, u32[]{:S(2)}) %collective-permute-start.12) | collective-permute-done | bytes 405536 | tf_op jit(solution)/shard_map/ppermute | solution.py:333
  69.5 0.3 collective-permute-done.13.refs_9_.refs_14_
  69.7 0.0 collective-permute-start.15
  69.7 1.4 %products.9 = (f32[1,256]{1,0:T(1,128)S(1)}, f32[1,256]{1,0:T(1,128)S(1)}, f32[1,256]{1,0:T(1,128)S(1)}, f32[1,256]{1,0:T(1,128)S(1)}, f32[1,256]{1,0:T(1,128)S(...) custom-call(bf16[264,768]{1,0:T(8,128)(2,1)S(1)} %collective-permute-done.11.refs, ...), custom_call_target="tpu_custom_call" | custom-call | flops 1006632960 | tf_op jit(solution)/shard_map/products/pallas_call | solution.py:393
  71.1 0.4 collective-permute-done.15.key_ref
  71.5 0.0 copy-start
  71.5 1.2 %last.1 = f32[8,1,384]{2,1,0:T(1,128)S(1)} custom-call(bf16[264,768]{1,0:T(8,128)(2,1)S(1)} %collective-permute-done.15.key_ref, f32[1,256]{1,0:T(1,128)S(1)} %get-tuple-element.175.turn_t_ref, f32[1,256]{1,0:T(1,128)S(1)} %get-tuple-element.176.turn_n_ref, f32[1,256]{1,0:T(1,128)S(1)} %get-tuple-element.194.turn_x_ref, ...), custom_call_target="tpu_custom_call" | custom-call | flops 805306368 | tf_op jit(solution)/shard_map/last/pallas_call | solution.py:469
  72.6 7.3 %all_to_all.10.back_ref = f32[8,1,384]{2,1,0:T(1,128)S(1)} all-to-all(f32[8,1,384]{2,1,0:T(1,128)S(1)} %last.1), channel_id=1, replica_groups=mesh['gx'=4,'gy'=8] {'gy'}, dimensions={0} | all-to-all | bytes 24576 | tf_op jit(solution)/shard_map/all_to_all | solution.py:479
  79.9 0.0 copy-done
  79.9 0.9 %finish.1 = f32[1,1024]{1,0:T(1,128)} custom-call(s32[2,1024]{1,0:T(2,128)S(1)} %copy-done, f32[8,1,384]{2,1,0:T(1,128)S(1)} %all_to_all.10.back_ref), custom_call_target="tpu_custom_call" | custom-call | tf_op jit(solution)/shard_map/finish/pallas_call | solution.py:480
  (4 shorter events, 0.1 us)
Async XLA Ops:
  0.0 11.0 %copy-start.1 = (bf16[1024,768]{1,0:T(8,128)(2,1)S(1)}, bf16[1024,768]{1,0:T(8,128)(2,1)}, u32[]{:S(2)}) copy-start(bf16[1024,768]{1,0:T(8,128)(2,1)} %param.3) | copy-start | bytes 4718596
  1.9 14.4 %all-to-all-start = ((s32[32,1,32]{2,1,0:T(1,128)}), s32[32,1,32]{2,1,0:T(1,128)S(1)}, u32[]{:S(2)}, u32[]{:S(2)}) async-start(s32[32,1,32]{2,1,0:T(1,128)} %get-tuple-element.105), calls=%async_computation | async-start | bytes 32768 | tf_op jit(solution)/shard_map/all_to_all | solution.py:304
  17.2 14.4 %collective-permute-start = (bf16[272,768]{1,0:T(8,128)(2,1)S(1)}, bf16[272,768]{1,0:T(8,128)(2,1)S(1)}, u32[]{:S(2)}, u32[]{:S(2)}) collective-permute-start(bf16[272,768]{1,0:T(8,128)(2,1)S(1)} %select.3), channel_id=1, source_target_pairs={{0,8},{8,16},{16,24},{24,0},{1,9},{9,17},{17,25},{25,1},{2,10},{10... | collective-permute-start | bytes 1253384 | tf_op jit(solution)/shard_map/ppermute | solution.py:330
  18.6 10.7 %collective-permute-start.1 = (bf16[264,768]{1,0:T(8,128)(2,1)S(1)}, bf16[264,768]{1,0:T(8,128)(2,1)S(1)}, u32[]{:S(2)}, u32[]{:S(2)}) collective-permute-start(bf16[264,768]{1,0:T(8,128)(2,1)S(1)} %select.4.refs_1_.refs_2_.refs_0_), channel_id=1, source_target_pairs={{0,2},{1,3},{2,0},{3,1},{4,6},{5,7},{6,4},{7,5},{8,10},{9,11},{10,... | collective-permute-start | bytes 1216520 | tf_op jit(solution)/shard_map/ppermute | solution.py:333
  19.2 10.1 %collective-permute-start.2 = (bf16[264,768]{1,0:T(8,128)(2,1)S(1)}, bf16[264,768]{1,0:T(8,128)(2,1)S(1)}, u32[]{:S(2)}, u32[]{:S(2)}) collective-permute-start(bf16[264,768]{1,0:T(8,128)(2,1)S(1)} %select.4.refs_1_.refs_2_.refs_0_), channel_id=1, source_target_pairs={{0,1},{1,0},{2,3},{3,2},{4,5},{5,4},{6,7},{7,6},{8,9},{9,8},{10,11... | collective-permute-start | bytes 1216520 | tf_op jit(solution)/shard_map/ppermute | solution.py:333
  19.2 11.8 %collective-permute-start.3 = (bf16[264,768]{1,0:T(8,128)(2,1)S(1)}, bf16[264,768]{1,0:T(8,128)(2,1)S(1)}, u32[]{:S(2)}, u32[]{:S(2)}) collective-permute-start(bf16[264,768]{1,0:T(8,128)(2,1)S(1)} %select.4.refs_1_.refs_2_.refs_0_), channel_id=1, source_target_pairs={{0,4},{1,5},{2,6},{3,7},{4,0},{5,1},{6,2},{7,3},{8,12},{9,13},{10,... | collective-permute-start | bytes 1216520 | tf_op jit(solution)/shard_map/ppermute | solution.py:333
  21.3 18.1 %collective-permute-start.5 = (bf16[272,768]{1,0:T(8,128)(2,1)S(1)}, bf16[272,768]{1,0:T(8,128)(2,1)S(1)}, u32[]{:S(2)}, u32[]{:S(2)}) collective-permute-start(bf16[272,768]{1,0:T(8,128)(2,1)S(1)} %get-tuple-element.114), channel_id=1, source_target_pairs={{0,24},{8,0},{16,8},{24,16},{1,25},{9,1},{17,9},{25,17},{2,26},{10... | collective-permute-start | bytes 1253384 | tf_op jit(solution)/shard_map/ppermute | solution.py:330
  31.6 10.5 %collective-permute-start.7 = (bf16[264,768]{1,0:T(8,128)(2,1)S(1)}, bf16[264,768]{1,0:T(8,128)(2,1)S(1)}, u32[]{:S(2)}, u32[]{:S(2)}) collective-permute-start(bf16[264,768]{1,0:T(8,128)(2,1)S(1)} %pack.4.refs_2_.refs_0_.refs_3_.refs_4_), channel_id=1, source_target_pairs={{0,2},{1,3},{2,0},{3,1},{4,6},{5,7},{6,4},{7,5},{8,10},{9,11},{10,... | collective-permute-start | bytes 1216520 | tf_op jit(solution)/shard_map/ppermute | solution.py:333
  32.6 10.7 %collective-permute-start.8 = (bf16[264,768]{1,0:T(8,128)(2,1)S(1)}, bf16[264,768]{1,0:T(8,128)(2,1)S(1)}, u32[]{:S(2)}, u32[]{:S(2)}) collective-permute-start(bf16[264,768]{1,0:T(8,128)(2,1)S(1)} %pack.4.refs_2_.refs_0_.refs_3_.refs_4_), channel_id=1, source_target_pairs={{0,4},{1,5},{2,6},{3,7},{4,0},{5,1},{6,2},{7,3},{8,12},{9,13},{10,... | collective-permute-start | bytes 1216520 | tf_op jit(solution)/shard_map/ppermute | solution.py:333
  33.2 10.2 %collective-permute-start.6 = (bf16[264,768]{1,0:T(8,128)(2,1)S(1)}, bf16[264,768]{1,0:T(8,128)(2,1)S(1)}, u32[]{:S(2)}, u32[]{:S(2)}) collective-permute-start(bf16[264,768]{1,0:T(8,128)(2,1)S(1)} %collective-permute-done.1.refs_3_.refs_4_.refs_5_), channel_id=1, source_target_pairs={{0,1},{1,0},{2,3},{3,2},{4,5},{5,4},{6,7},{7,6},{8,9},{9,8},{10,11... | collective-permute-start | bytes 1216520 | tf_op jit(solution)/shard_map/ppermute | solution.py:333
  33.2 24.1 %collective-permute-start.4 = (bf16[272,768]{1,0:T(8,128)(2,1)S(1)}, bf16[272,768]{1,0:T(8,128)(2,1)S(1)}, u32[]{:S(2)}, u32[]{:S(2)}) collective-permute-start(bf16[272,768]{1,0:T(8,128)(2,1)S(1)} %get-tuple-element.113), channel_id=1, source_target_pairs={{0,16},{8,24},{16,0},{24,8},{1,17},{9,25},{17,1},{25,9},{2,18},{10... | collective-permute-start | bytes 1253384 | tf_op jit(solution)/shard_map/ppermute | solution.py:330
  43.4 13.9 %collective-permute-start.10 = (bf16[264,768]{1,0:T(8,128)(2,1)S(1)}, bf16[264,768]{1,0:T(8,128)(2,1)S(1)}, u32[]{:S(2)}, u32[]{:S(2)}) collective-permute-start(bf16[264,768]{1,0:T(8,128)(2,1)S(1)} %pack.5.refs_3_.refs_2_.refs_4_.refs_8_), channel_id=1, source_target_pairs={{0,4},{1,5},{2,6},{3,7},{4,0},{5,1},{6,2},{7,3},{8,12},{9,13},{10,... | collective-permute-start | bytes 1216520 | tf_op jit(solution)/shard_map/ppermute | solution.py:333
  44.0 13.3 %collective-permute-start.9 = (bf16[264,768]{1,0:T(8,128)(2,1)S(1)}, bf16[264,768]{1,0:T(8,128)(2,1)S(1)}, u32[]{:S(2)}, u32[]{:S(2)}) collective-permute-start(bf16[264,768]{1,0:T(8,128)(2,1)S(1)} %pack.5.refs_3_.refs_2_.refs_4_.refs_8_), channel_id=1, source_target_pairs={{0,2},{1,3},{2,0},{3,1},{4,6},{5,7},{6,4},{7,5},{8,10},{9,11},{10,... | collective-permute-start | bytes 1216520 | tf_op jit(solution)/shard_map/ppermute | solution.py:333
  57.4 4.9 %collective-permute-start.14 = (bf16[1032,768]{1,0:T(8,128)(2,1)S(1)}, bf16[1032,768]{1,0:T(8,128)(2,1)S(1)}, u32[]{:S(2)}, u32[]{:S(2)}) collective-permute-start(bf16[1032,768]{1,0:T(8,128)(2,1)S(1)} %pack.7), channel_id=1, source_target_pairs={{0,1},{1,0},{2,3},{3,2},{4,5},{5,4},{6,7},{7,6},{8,9},{9,8},{10,11... | collective-permute-start | bytes 4755464 | tf_op jit(solution)/shard_map/ppermute | solution.py:333
  57.6 4.8 %collective-permute-start.11 = (bf16[264,768]{1,0:T(8,128)(2,1)S(1)}, bf16[264,768]{1,0:T(8,128)(2,1)S(1)}, u32[]{:S(2)}, u32[]{:S(2)}) collective-permute-start(bf16[264,768]{1,0:T(8,128)(2,1)S(1)} %pack.6.refs_4_.refs_5_.refs_12_), channel_id=1, source_target_pairs={{0,1},{1,0},{2,3},{3,2},{4,5},{5,4},{6,7},{7,6},{8,9},{9,8},{10,11... | collective-permute-start | bytes 1216520 | tf_op jit(solution)/shard_map/ppermute | solution.py:333
  58.1 11.4 %collective-permute-start.12 = (bf16[264,768]{1,0:T(8,128)(2,1)S(1)}, bf16[264,768]{1,0:T(8,128)(2,1)S(1)}, u32[]{:S(2)}, u32[]{:S(2)}) collective-permute-start(bf16[264,768]{1,0:T(8,128)(2,1)S(1)} %pack.6.refs_4_.refs_5_.refs_12_), channel_id=1, source_target_pairs={{0,2},{1,3},{2,0},{3,1},{4,6},{5,7},{6,4},{7,5},{8,10},{9,11},{10,... | collective-permute-start | bytes 1216520 | tf_op jit(solution)/shard_map/ppermute | solution.py:333
  58.6 11.1 %collective-permute-start.13 = (bf16[264,768]{1,0:T(8,128)(2,1)S(1)}, bf16[264,768]{1,0:T(8,128)(2,1)S(1)}, u32[]{:S(2)}, u32[]{:S(2)}) collective-permute-start(bf16[264,768]{1,0:T(8,128)(2,1)S(1)} %pack.6.refs_4_.refs_5_.refs_12_), channel_id=1, source_target_pairs={{0,4},{1,5},{2,6},{3,7},{4,0},{5,1},{6,2},{7,3},{8,12},{9,13},{10,... | collective-permute-start | bytes 1216520 | tf_op jit(solution)/shard_map/ppermute | solution.py:333
  69.7 1.7 %collective-permute-start.15 = (bf16[264,768]{1,0:T(8,128)(2,1)S(1)}, bf16[264,768]{1,0:T(8,128)(2,1)S(1)}, u32[]{:S(2)}, u32[]{:S(2)}) collective-permute-start(bf16[264,768]{1,0:T(8,128)(2,1)S(1)} %collective-permute-done.12.refs_5_), channel_id=1, source_target_pairs={{0,1},{1,0},{2,3},{3,2},{4,5},{5,4},{6,7},{7,6},{8,9},{9,8},{10,11... | collective-permute-start | bytes 1216520 | tf_op jit(solution)/shard_map/ppermute | solution.py:333
  71.5 8.5 %copy-start = (s32[2,1024]{1,0:T(2,128)S(1)}, s32[2,1024]{1,0:T(2,128)}, u32[]{:S(2)}) copy-start(s32[2,1024]{1,0:T(2,128)} %get-tuple-element.104.home_ref) | copy-start | bytes 24580

commit v6 on v5

--- a/solution.py
+++ b/solution.py
@@ -141,21 +141,20 @@
 
 
 def pack_kernel(groups, sizes, chunk, *refs):
-    refs = list(refs)
-    outs = refs[sum(len(g) for g in groups):]
+    outs = refs[len(sizes):]
     for group, out_ref in zip(groups, outs):
         at = 0
-        total = sum(sizes[n] for n in group)
+        total = sum(count for _, _, count in group)
         width = out_ref.shape[1]
         extra = more(total // chunk)
         meta = jnp.zeros((extra, width), F32)
-        for name in group:
-            ref, size = refs.pop(0), sizes[name]
-            out_ref[at:at + size, :] = ref[0:size, :]
+        for i, low, count in group:
+            ref, size = refs[i], sizes[i]
+            out_ref[at:at + count, :] = ref[low:low + count, :]
             lines = ref[size:size + more(size // chunk), :].astype(F32)
-            for r in range(size // chunk):
-                meta = jnp.where(iota((extra, width), 0) == at // chunk + r, lines[r:r + 1, :], meta)
-            at += size
+            for r in range(count // chunk):
+                meta = jnp.where(iota((extra, width), 0) == at // chunk + r, lines[low // chunk + r:low // chunk + r + 1, :], meta)
+            at += count
         out_ref[total:total + extra, :] = meta.astype(BF16)
 
 
@@ -174,27 +173,30 @@
         else:
             col = column(cluster_line(rows[q], n_q, chunk))
             best = jnp.full((n_q, 128), -1.0, F32)
-            if not close:
+            if q not in close:
                 refs.pop(0)[...] = col
         out_ref = refs.pop(0)
-        for k in keys:
-            n_k = sizes[k]
-            sims = dot_nt(rows[q][0:n_q, :], rows[k][0:n_k, :])
-            keep = wide(col, n_k) == cluster_line(rows[k], n_k, chunk)
-            if k == q:
-                keep = keep & (iota((n_q, n_k), 0) != iota((n_q, n_k), 1))
-            sims = jnp.where(keep, sims, -1.0)
-            for v in range(n_k // 128):
-                best = jnp.maximum(best, sims[:, v * 128:(v + 1) * 128])
-            if (q, k) in turned:
-                line = jnp.max(sims, axis=0, keepdims=True)
-                turns[k] = jnp.maximum(turns[k], line) if k in turns else line
-        if close:
-            out_ref[...] = lined(best)
-        else:
-            out_ref[...] = best
+        best = meet_keys(q, keys, rows, sizes, chunk, col, best, turned, turns)
+        out_ref[...] = lined(best) if q in close else best
     for k in sorted(turns):
         refs.pop(0)[...] = turns[k]
+
+
+def meet_keys(q, keys, rows, sizes, chunk, col, best, turned, turns):
+    n_q = sizes[q]
+    for k in keys:
+        n_k = sizes[k]
+        sims = dot_nt(rows[q][0:n_q, :], rows[k][0:n_k, :])
+        keep = wide(col, n_k) == cluster_line(rows[k], n_k, chunk)
+        if k == q:
+            keep = keep & (iota((n_q, n_k), 0) != iota((n_q, n_k), 1))
+        sims = jnp.where(keep, sims, -1.0)
+        for v in range(n_k // 128):
+            best = jnp.maximum(best, sims[:, v * 128:(v + 1) * 128])
+        if (q, k) in turned:
+            line = jnp.max(sims, axis=0, keepdims=True)
+            turns[k] = jnp.maximum(turns[k], line) if k in turns else line
+    return best
 
 
 def lined(best):
@@ -203,20 +205,29 @@
     return jnp.concatenate(parts, axis=1)
 
 
-def last_kernel(dims, queries, stage, size, key_ref, turn_t_ref, turn_n_ref, turn_x_ref, *refs):
+def final_kernel(dims, kinds, pairs, groups, sizes, turned, row_names, line_names, *refs):
     n_gx, n_gy, rows, quota = dims
     chunk = n_gy * quota
     refs = list(refs)
-    send_ref = refs.pop()
-    keys = key_ref[0:size, :]
-    col = column(cluster_line(key_ref, size, chunk))
-    blocks = {}
-
-    def spread(block, line, groups):
-        for c, group in enumerate(groups):
-            flat = line[:, c * chunk:(c + 1) * chunk]
-            target = lax.shift_right_logical(iota((n_gy, chunk), 1), log2(quota))
-            held = jnp.where(target == iota((n_gy, chunk), 0), flat, 0.0)
+    row_refs = {n: refs.pop(0) for n in row_names}
+    line_refs = {n: refs.pop(0) for n in line_names}
+    col_ref, best_ref, send_ref = refs
+    lines = {n: ref[...] for n, ref in line_refs.items()}
+    for q, keys in pairs:
+        n_q = sizes[q]
+        if q == "Tb":
+            col, best = col_ref[...], best_ref[...]
+        else:
+            col = column(cluster_line(row_refs[q], n_q, chunk))
+            best = jnp.full((n_q, 128), -1.0, F32)
+        line = lined(meet_keys(q, keys, row_refs, sizes, chunk, col, best, turned, lines))
+        lines[q] = jnp.maximum(lines[q], line) if q in lines else line
+    blocks = [jnp.full((n_gy, 128), -1.0, F32)] * len(kinds)
+    own = lax.shift_right_logical(iota((n_gy, chunk), 1), log2(quota)) == iota((n_gy, chunk), 0)
+    lane = lax.shift_right_logical(iota((n_gy, 128), 1), log2(quota))
+    for name in sorted(lines):
+        for c, (kind, group) in enumerate(groups[name]):
+            held = jnp.where(own, lines[name][:, c * chunk:(c + 1) * chunk], 0.0)
             fold = held[:, 0:128]
             for v in range(1, chunk // 128):
                 fold = fold + held[:, v * 128:(v + 1) * 128]
@@ -224,28 +235,16 @@
             while shift >= quota:
                 fold = fold + pltpu.roll(fold, shift, 1)
                 shift //= 2
-            here = lax.shift_right_logical(iota((n_gy, 128), 1), log2(quota)) == group
-            fold = jnp.where(here, fold, 0.0)
-            blocks[block] = blocks[block] + fold if block in blocks else fold
-
-    turn = jnp.full((size, 128), -1.0, F32)
-    for (m, steps, n_q), row_ref, best_ref in zip(queries, refs[0::2], refs[1::2]):
-        sims = dot_nt(keys, row_ref[0:n_q, :])
-        keep = wide(col, n_q) == cluster_line(row_ref, n_q, chunk)
-        sims = jnp.where(keep, sims, -1.0)
-        line = jnp.maximum(jnp.max(sims, axis=0, keepdims=True), best_ref[...])
-        if m and steps != stage:
-            for v in range(n_q // 128):
-                turn = jnp.maximum(turn, sims[:, v * 128:(v + 1) * 128])
-        if not m and steps == stage:
-            line = jnp.maximum(line, turn_t_ref[...])
-        spread(m, line, steps)
-    last = len(blocks)
-    for t, line in enumerate([turn_n_ref[...], turn_x_ref[...], lined(turn)]):
-        spread(last, line, range(t * len(stage), (t + 1) * len(stage)))
-    whole = jnp.concatenate([blocks[b] for b in range(last + 1)], axis=1)
+            at = kinds.index(kind)
+            blocks[at] = jnp.where(lane == group, fold, blocks[at])
+    whole = jnp.concatenate(blocks, axis=1)
     for d in range(n_gy):
         send_ref[d] = whole[d:d + 1, :]
+
+
+def far_place(q, m):
+    row = q // KEYS
+    return q ^ (KEYS * m) ^ (1 if row < row ^ m else 0)
 
 
 def finish_kernel(dims, stage, home_ref, back_ref, out_ref):
@@ -253,14 +252,18 @@
     n_query = n_gy // KEYS
     low, high = stage[0] * quota, (stage[-1] + 1) * quota
     lane = iota((n_gy, 128), 1)
-    found = None
-    for m in range(n_query):
-        part = jnp.concatenate([back_ref[q ^ (KEYS * m)][:, m * 128:(m + 1) * 128] for q in range(n_gy)], axis=0)
-        found = part if found is None else jnp.maximum(found, part)
+    late = (lane >= low) & (lane < high)
+
+    def taken(place, block):
+        return jnp.concatenate([back_ref[place(q)][:, block * 128:(block + 1) * 128] for q in range(n_gy)], axis=0)
+
+    found = taken(lambda q: q, 0)
+    for m in range(1, n_query):
+        part = taken(lambda q, m=m: q ^ (KEYS * m), m)
+        last = taken(lambda q, m=m: far_place(q, m), m)
+        found = jnp.maximum(found, jnp.where(late, last, part))
     for t in range(1, KEYS):
-        part = jnp.concatenate([back_ref[q ^ t][:, n_query * 128:] for q in range(n_gy)], axis=0)
-        part = pltpu.roll(part, (low - (t - 1) * (high - low)) % 128, 1)
-        found = jnp.where((lane >= low) & (lane < high), jnp.maximum(found, part), found)
+        found = jnp.maximum(found, taken(lambda q, t=t: q ^ t, n_query - 1 + t))
     high = found.astype(BF16)
     rest = found - high.astype(F32)
     mid = rest.astype(BF16)
@@ -339,6 +342,7 @@
     piece = {}
     size = {}
     state = {}
+    lines = {}
     for n in names:
         for kind in ["T", "N", "X", "Z"] + far:
             size[kind + n] = chunk * (len(rest) if n == "b" else 1)
@@ -346,15 +350,17 @@
         size["z%d" % k] = chunk
 
     def pack(groups):
-        flat = [n for g in groups.values() for n in g]
+        groups = {name: [(g, 0, size[g]) if isinstance(g, str) else g for g in group] for name, group in groups.items()}
+        flat = sorted({g[0] for group in groups.values() for g in group})
         for name, group in groups.items():
-            size[name] = sum(size[n] for n in group)
+            size[name] = sum(count for _, _, count in group)
+        stretches = [[(flat.index(n), low, count) for n, low, count in group] for group in groups.values()]
         out = pl.pallas_call(
-            functools.partial(pack_kernel, list(groups.values()), size, chunk),
+            functools.partial(pack_kernel, stretches, [size[n] for n in flat], chunk),
             out_shape=[shape((size[n] + more(size[n] // chunk), width), BF16) for n in groups],
             in_specs=[in_vmem] * len(flat),
             out_specs=[in_vmem] * len(groups),
-            cost_estimate=cost(0, 4 * sum(size[n] for n in flat) * width),
+            cost_estimate=cost(0, 4 * sum(size[n] for n in groups) * width),
             compiler_params=params(),
             name="pack",
         )(*[piece[n] for n in flat])
@@ -376,22 +382,22 @@
     def kinds(kinds, names):
         return [k + n for n in names for k in kinds]
 
-    def products(pairs, turned=(), close=False):
+    def products(pairs, turned=(), close=()):
         names = sorted({n for q, ks in pairs for n in [q] + ks})
         queries = [q for q, _ in pairs]
         started = [q for q in queries if q in state]
         inputs = [piece[n] for n in names] + [a for q in started for a in state[q]]
         outs = []
         for q in queries:
-            if close:
+            if q in close:
                 outs.append(shape((1, size[q]), F32))
             else:
                 outs += [shape((size[q], 128), F32)] * (1 if q in started else 2)
-        turned = {(q, k) for q, ks in pairs for k in ks if k in turned and q[0] == "Y" and q[1:] != "b"}
-        outs += [shape((1, size[k]), F32) for k in sorted({k for _, k in turned})]
+        turns = sorted({k for _, k in turned})
+        outs += [shape((1, size[k]), F32) for k in turns]
         flops = sum(2 * width * size[q] * size[k] for q, ks in pairs for k in ks)
         out = pl.pallas_call(
-            functools.partial(product_kernel, pairs, size, chunk, started, turned, close),
+            functools.partial(product_kernel, pairs, size, chunk, started, set(turned), close),
             out_shape=outs,
             in_specs=[in_vmem] * len(inputs),
             out_specs=[in_vmem] * len(outs),
@@ -401,12 +407,15 @@
         )(*inputs)
         out = list(out)
         for q in queries:
-            if close:
-                state[q] = out.pop(0)
+            if q in close:
+                del state[q]
+                lines[q] = out.pop(0)
             else:
                 col = state[q][0] if q in started else out.pop(0)
                 state[q] = (col, out.pop(0))
-        return out
+        for k, line in zip(turns, out):
+            assert k not in lines
+            lines[k] = line
 
     def swap_core(name, group):
         pack({"P": group})
@@ -415,6 +424,7 @@
 
     first, second = edge
     a, b = "%d" % first, "%d" % second
+    one = ["0", a, b]
     for k in edge:
         piece["z%d" % k] = across(found[k], k)
     piece["T0"] = found[0]
@@ -444,36 +454,55 @@
     join(["z%d" % k for k in rest] + kinds(["T", "X"] + far, [b]))
 
     pack({"Tb": ["z%d" % k for k in rest]})
-    near("b")
-    piece["Nb"] = swap(piece["Tb"], 1)
-    swap_core("Q", kinds(["T", "X"], [a, b]))
-    new = ["X" + b, "Tb"]
-    keys = keys + new
-    late = kinds(far, [b]) + ["Tb"]
-    turn_t = products([(q, new) for q in before] + [(q, keys) for q in late], ["Tb"])
-    before = before + late
-    turn_n = products([(q, ["Q", "Nb"]) for q in before], ["Nb"])
+    piece["Xb"] = swap(piece["Tb"], 2)
+    for m, kind in enumerate(far):
+        size[kind + "b"] = size["Tb"]
+        piece[kind + "b"] = lax.ppermute(piece["Tb"], "gy", [(q, far_place(q, m + 1)) for q in range(n_gy)])
+    swap_core("Q", kinds(["T", "X"], [a, b]) + ["Tb"])
+    count = [size["T" + a], size["X" + a], size["T" + b], size["X" + b], size["Tb"]]
+    start = [sum(count[:i]) for i in range(len(count))]
+    take = [("Q", start[i], count[i]) for i in range(len(count))]
+    pack({"Ns": [take[0], take[2]], "Zs": [take[1], take[3]], "Nb": [take[4]]})
+    third = kinds(far, [b])
+    keys = keys + ["X" + b]
+    sides = kinds(["X"], one)
+    products(
+        [(q, ["X" + b, "Tb"]) for q in before]
+        + [(q, keys + ["Tb"]) for q in third]
+        + [("Tb", ["N0", "Z0"] + sides + ["Tb"])],
+        [(q, "Tb") for q in before + third] + [("Tb", k) for k in sides + ["Z0"]],
+    )
+    before = before + third
+    olds = kinds(far, one)
+    products(
+        [(q, ["Ns", "Zs", "Nb"]) for q in before + ["Tb"]],
+        [(q, "Nb") for q in olds] + [("Tb", "Zs")],
+        before,
+    )
     join(["Tb", "Nb", "Xb"] + kinds(far, ["b"]))
 
-    piece["Zb"] = swap(piece["Xb"], 1)
-    turn_x = products([(q, ["Xb"]) for q in before] + [(q, ["Tb", "Nb", "Xb"]) for q in kinds(far, ["b"])], ["Xb"], close=True)
-
-    order = []
-    inputs = []
-    for n in names:
-        for m, kind in enumerate(["T"] + far):
-            q = kind + n
-            order.append((m, rest if n == "b" else [int(n)], size[q]))
-            inputs += [piece[q], state[q]]
-    inputs = [piece["Zb"]] + turn_t + turn_n + turn_x + inputs
+    news = kinds(far, ["b"])
+    pairs = [("Tb", ["Xb"]), ("Nb", ["Xb"])] + [(q, sides + ["Z0", "Zs", "Tb", "Nb", "Xb"]) for q in news]
+    turned = {(q, k) for q in news for k in sides + ["Z0", "Zs", "Xb"]}
+    groups = {}
+    for n in one:
+        for kind in ["T", "X", "Z"] + far:
+            groups[kind + n] = [(kind, int(n))]
+    for kind in ["T", "N", "X"] + far:
+        groups[kind + "b"] = [(kind, k) for k in rest]
+    groups["Zs"] = [("Z", first), ("Z", second)]
+    row_names = sorted({n for q, ks in pairs for n in [q] + ks})
+    line_names = sorted(lines)
+    inputs = [piece[n] for n in row_names] + [lines[n] for n in line_names] + list(state["Tb"])
+    shown = ["T"] + far + ["N", "X", "Z"]
     send = pl.pallas_call(
-        functools.partial(last_kernel, dims, order, rest, size["Zb"]),
-        out_shape=shape((n_gy, 1, (n_query + 1) * 128), F32),
+        functools.partial(final_kernel, dims, shown, pairs, groups, size, turned, row_names, line_names),
+        out_shape=shape((n_gy, 1, len(shown) * 128), F32),
         in_specs=[in_vmem] * len(inputs),
         out_specs=in_vmem,
-        cost_estimate=cost(2 * width * size["Zb"] * n_query * rows, 0),
+        cost_estimate=cost(sum(2 * width * size[q] * size[k] for q, ks in pairs for k in ks), 0),
         compiler_params=params(),
-        name="last",
+        name="final",
     )(*inputs)
 
     back = lax.all_to_all(send, "gy", split_axis=0, concat_axis=0, tiled=True)

time: 81 us -> 79.6 us (0.983)
  Pallas kernels: 19.9 us -> 18.9 us
    pallas_call x5 -> x4, Pallas kernels: 12.7 us -> 11.2 us  [products(): pl.pallas_call(functools.partial(product_kernel, pairs, size, chunk, star...]
    ppermute x3, waiting for transfers between devices: 14.7 us -> 13.5 us  [across(): lax.ppermute(array, 'gx', [(i, (i + step) % n_gx) for i in range(n_gx)])]
    ppermute x13 -> x10, waiting for transfers between devices: 14 us -> 14.9 us  [swap(): return lax.ppermute(array, 'gy', [(i, i ^ mask) for i in range(n_gy)])]
    ppermute x13 -> x10, starting transfers between devices: 5.78 us -> 5.15 us  [swap(): return lax.ppermute(array, 'gy', [(i, i ^ mask) for i in range(n_gy)])]
    pallas_call x5 -> x6, Pallas kernels: 1.39 us -> 1.98 us  [the longest x1 1.61 us: per_device(): pl.pallas_call(functools.partial(final_kernel, dims, shown, pairs, groups...]
  transfers between devices with their start and end apart: 17 -> 15, of which waited for: 11 -> 11; matrix products, arithmetic and copies ran while one was open for 3% -> 3% of each run, Pallas kernels for 19% -> 17%
where the time goes in v6:
time: 79.6 us; the launch traced here: 79.4 us
  waiting for transfers between devices  33.7 us (42%)
  Pallas kernels  18.9 us (24%)
  starting transfers between devices  17.2 us (22%)
  blocking collectives  7.33 us (9%)
  other arithmetic  2.11 us (3%)
    ppermute x10, waiting for transfers between devices, swap(): return lax.ppermute(array, 'gy', [(i, i ^ mask) for i in range(n_gy)])  14.9 us
    ppermute x3, waiting for transfers between devices, across(): lax.ppermute(array, 'gx', [(i, (i + step) % n_gx) for i in range(n_gx)])  13.5 us
    pallas_call x4, Pallas kernels, products(): pl.pallas_call(functools.partial(product_kernel, pairs, size, chunk, star...  11.2 us
    all_to_all x1, blocking collectives, per_device(): back = lax.all_to_all(send, 'gy', split_axis=0, concat_axis=0, tiled=True)  7.33 us
    all_to_all x1, starting transfers between devices, per_device(): lax.all_to_all(asked, ('gx', 'gy'), split_axis=0, concat_axis=0, tiled=True)  7.3 us
    ppermute x10, starting transfers between devices, swap(): return lax.ppermute(array, 'gy', [(i, i ^ mask) for i in range(n_gy)])  5.15 us
    all_to_all x1, waiting for transfers between devices, per_device(): lax.all_to_all(asked, ('gx', 'gy'), split_axis=0, concat_axis=0, tiled=True)  5 us
    ppermute x3, starting transfers between devices, across(): lax.ppermute(array, 'gx', [(i, (i + step) % n_gx) for i in range(n_gx)])  4.47 us
  transfers between devices with their start and end apart: 15, of which 11 were waited for; matrix products, arithmetic and copies ran while one was open for 3% of the time, Pallas kernels for 17%

profile of v6, /device:TPU:0, one launch (start us, length us, event | category | flops | bytes accessed | tf_op | source)
XLA Modules:
  0.0 79.4 jit_solution(11344160100361638142)
XLA Ops:
  0.0 0.0 copy-start.1
  0.0 1.9 %request.1 = (s32[32,1,32]{2,1,0:T(1,128)}, s32[2,1024]{1,0:T(2,128)}) custom-call(s32[1,25]{1,0:T(1,128)} %sizes_hbm.1, s32[1,1024]{1,0:T(1,128)} %bitcast.2), custom_call_target="tpu_custom_call" | custom-call | tf_op jit(solution)/shard_map/request/pallas_call | solution.py:294
  1.9 7.3 %all-to-all-start = ((s32[32,1,32]{2,1,0:T(1,128)}), s32[32,1,32]{2,1,0:T(1,128)S(1)}, u32[]{:S(2)}, u32[]{:S(2)}) async-start(s32[32,1,32]{2,1,0:T(1,128)} %get-tuple-element.92), calls=%async_computation | async-start | bytes 32768 | tf_op jit(solution)/shard_map/all_to_all | solution.py:307
  9.2 1.8 %fusion = f32[1024]{0:T(1024)S(1)} fusion(bf16[1024,768]{1,0:T(8,128)(2,1)} %param.3), kind=kLoop, calls=%fused_computation.2 | loop fusion | flops 2358272 | bytes 1576960 | tf_op jit(solution)/shard_map/reduce_sum | solution.py:310
  11.0 0.0 copy-done.1
  11.0 0.3 fusion.1.unit_ref
  11.3 5.0 %all-to-all-done.asked_ref = s32[32,1,32]{2,1,0:T(1,128)S(1)} async-done(((s32[32,1,32]{2,1,0:T(1,128)}), s32[32,1,32]{2,1,0:T(1,128)S(1)}, u32[]{:S(2)}, u32[]{:S(2)}) %all-to-all-start) | async-done | bytes 4128 | tf_op jit(solution)/shard_map/all_to_all | solution.py:307
  16.3 0.8 %select.3 = bf16[272,768]{1,0:T(8,128)(2,1)S(1)} custom-call(s32[32,1,32]{2,1,0:T(1,128)S(1)} %all-to-all-done.asked_ref, bf16[1024,768]{1,0:T(8,128)(2,1)S(1)} %fusion.1.unit_ref), custom_call_target="tpu_custom_call" | custom-call | flops 402653184 | bytes 786432 | tf_op jit(solution)/shard_map/select/pallas_call | solution.py:320
  17.2 0.6 collective-permute-start
  17.8 0.8 %select.4.refs_1_.refs_2_ = bf16[264,768]{1,0:T(8,128)(2,1)S(1)} custom-call(s32[32,1,32]{2,1,0:T(1,128)S(1)} %all-to-all-done.asked_ref, bf16[1024,768]{1,0:T(8,128)(2,1)S(1)} %fusion.1.unit_ref), custom_call_target="tpu_custom_call" | custom-call | flops 402653184 | bytes 786432 | tf_op jit(solution)/shard_map/select/pallas_call | solution.py:320
  18.6 0.6 collective-permute-start.1
  19.2 0.0 collective-permute-start.2
  19.2 0.7 collective-permute-start.3
  19.9 1.4 %select.5 = (bf16[272,768]{1,0:T(8,128)(2,1)S(1)}, bf16[272,768]{1,0:T(8,128)(2,1)S(1)}) custom-call(s32[32,1,32]{2,1,0:T(1,128)S(1)} %all-to-all-done.asked_ref, bf16[1024,768]{1,0:T(8,128)(2,1)S(1)} %fusion.1.unit_ref), custom_call_target="tpu_custom_call" | custom-call | flops 805306368 | bytes 786432 | tf_op jit(solution)/shard_map/select/pallas_call | solution.py:320
  21.3 3.3 %collective-permute-start.5 = (bf16[272,768]{1,0:T(8,128)(2,1)S(1)}, bf16[272,768]{1,0:T(8,128)(2,1)S(1)}, u32[]{:S(2)}, u32[]{:S(2)}) collective-permute-start(bf16[272,768]{1,0:T(8,128)(2,1)S(1)} %get-tuple-element.101), channel_id=1, source_target_pairs={{0,24},{8,0},{16,8},{24,16},{1,25},{9,1},{17,9},{25,17},{2,26},{10... | collective-permute-start | bytes 1253384 | tf_op jit(solution)/shard_map/ppermute | solution.py:333
  24.6 4.7 %collective-permute-done.1.refs_3_.refs_4_.refs_5_.refs_2_ = bf16[264,768]{1,0:T(8,128)(2,1)S(1)} collective-permute-done((bf16[264,768]{1,0:T(8,128)(2,1)S(1)}, bf16[264,768]{1,0:T(8,128)(2,1)S(1)}, u32[]{:S(2)}, u32[]{:S(2)}) %collective-permute-start.1) | collective-permute-done | bytes 405536 | tf_op jit(solution)/shard_map/ppermute | solution.py:336
  29.3 0.0 collective-permute-done.2.refs_0_
  29.3 1.7 %collective-permute-done.3.refs_4_.refs_6_.refs_8_ = bf16[264,768]{1,0:T(8,128)(2,1)S(1)} collective-permute-done((bf16[264,768]{1,0:T(8,128)(2,1)S(1)}, bf16[264,768]{1,0:T(8,128)(2,1)S(1)}, u32[]{:S(2)}, u32[]{:S(2)}) %collective-permute-start.3) | collective-permute-done | bytes 405536 | tf_op jit(solution)/shard_map/ppermute | solution.py:336
  31.0 0.6 collective-permute-done.refs_0_
  31.6 0.0 collective-permute-start.6
  31.6 1.0 %collective-permute-start.7 = (bf16[264,768]{1,0:T(8,128)(2,1)S(1)}, bf16[264,768]{1,0:T(8,128)(2,1)S(1)}, u32[]{:S(2)}, u32[]{:S(2)}) collective-permute-start(bf16[264,768]{1,0:T(8,128)(2,1)S(1)} %pack.5.refs_2_.refs_0_.refs_3_), channel_id=1, source_target_pairs={{0,2},{1,3},{2,0},{3,1},{4,6},{5,7},{6,4},{7,5},{8,10},{9,11},{10,... | collective-permute-start | bytes 1216520 | tf_op jit(solution)/shard_map/ppermute | solution.py:336
  32.6 0.5 collective-permute-start.8
  33.2 0.6 collective-permute-start.4
  33.7 1.4 %products.4 = (f32[256,128]{1,0:T(8,128)S(1)}, f32[256,128]{1,0:T(8,128)S(1)}, f32[256,128]{1,0:T(8,128)S(1)}, f32[256,128]{1,0:T(8,128)S(1)}, f32[256,128]{1,0:T(8,128)S(1)}, /*index=5*/f32[256,128]{1,0:T(8,128)S(1)}) custom-call(bf16[264,768]{1,0:T(8,128)(2,1)S(1)} %collective-permute-done.2.refs_0_, bf16[264,768]{1,0:T(8,128)(2,1)S(1)} %select.4.refs_1_.refs_2_, ...), custom_call_target="tpu_custom_call" | custom-call | flops 1207959552 | tf_op jit(solution)/shard_map/products/pallas_call | solution.py:399
  35.2 4.2 %collective-permute-done.5.refs_0_ = bf16[272,768]{1,0:T(8,128)(2,1)S(1)} collective-permute-done((bf16[272,768]{1,0:T(8,128)(2,1)S(1)}, bf16[272,768]{1,0:T(8,128)(2,1)S(1)}, u32[]{:S(2)}, u32[]{:S(2)}) %collective-permute-start.5) | collective-permute-done | bytes 417824 | tf_op jit(solution)/shard_map/ppermute | solution.py:333
  39.4 0.0 collective-permute-done.6.refs_8_.refs_11_.refs_7_
  39.4 4.1 %collective-permute-done.7.refs_5_.refs_3_.refs_6_ = bf16[264,768]{1,0:T(8,128)(2,1)S(1)} collective-permute-done((bf16[264,768]{1,0:T(8,128)(2,1)S(1)}, bf16[264,768]{1,0:T(8,128)(2,1)S(1)}, u32[]{:S(2)}, u32[]{:S(2)}) %collective-permute-start.7) | collective-permute-done | bytes 405536 | tf_op jit(solution)/shard_map/ppermute | solution.py:336
  43.5 0.7 collective-permute-done.8.refs_7_.refs_9_
  44.2 1.1 %collective-permute-start.9 = (bf16[264,768]{1,0:T(8,128)(2,1)S(1)}, bf16[264,768]{1,0:T(8,128)(2,1)S(1)}, u32[]{:S(2)}, u32[]{:S(2)}) collective-permute-start(bf16[264,768]{1,0:T(8,128)(2,1)S(1)} %pack.6.refs_3_.refs_1_.refs_4_), channel_id=1, source_target_pairs={{0,2},{1,3},{2,0},{3,1},{4,6},{5,7},{6,4},{7,5},{8,10},{9,11},{10,... | collective-permute-start | bytes 1216520 | tf_op jit(solution)/shard_map/ppermute | solution.py:336
  45.3 0.5 collective-permute-start.10
  45.9 2.7 %products.5 = (f32[256,128]{1,0:T(8,128)S(1)}, f32[256,128]{1,0:T(8,128)S(1)}, f32[256,128]{1,0:T(8,128)S(1)}, f32[256,128]{1,0:T(8,128)S(1)}, f32[256,128]{1,0:...) custom-call(bf16[264,768]{1,0:T(8,128)(2,1)S(1)} %collective-permute-done.2.refs_0_, ...), custom_call_target="tpu_custom_call" | custom-call | flops 2315255808 | tf_op jit(solution)/shard_map/products/pallas_call | solution.py:399
  48.6 8.7 %collective-permute-done.4.refs_0_ = bf16[272,768]{1,0:T(8,128)(2,1)S(1)} collective-permute-done((bf16[272,768]{1,0:T(8,128)(2,1)S(1)}, bf16[272,768]{1,0:T(8,128)(2,1)S(1)}, u32[]{:S(2)}, u32[]{:S(2)}) %collective-permute-start.4) | collective-permute-done | bytes 417824 | tf_op jit(solution)/shard_map/ppermute | solution.py:333
  57.3 0.0 collective-permute-done.9.refs_4_.refs_7_
  57.3 0.0 collective-permute-done.10.refs_10_.refs_8_
  57.3 0.1 pack.8
  57.5 0.1 collective-permute-start.11
  57.6 0.6 collective-permute-start.12
  58.2 0.3 collective-permute-start.13
  58.5 2.9 %products.6 = (f32[256,128]{1,0:T(8,128)S(1)}, f32[256,128]{1,0:T(8,128)S(1)}, f32[256,128]{1,0:T(8,128)S(1)}, f32[256,128]{1,0:T(8,128)S(1)}, f32[256,128]{1,0:...) custom-call(bf16[264,768]{1,0:T(8,128)(2,1)S(1)} %collective-permute, ...), custom_call_target="tpu_custom_call" | custom-call | flops 2516582400 | tf_op jit(solution)/shard_map/products/pallas_call | solution.py:399
  61.4 0.1 collective-permute-done.11.refs_0_
  61.5 0.1 pack.9
  61.7 4.1 %products.7 = (f32[1,256]{1,0:T(1,128)S(1)}, f32[1,256]{1,0:T(1,128)S(1)}, f32[1,256]{1,0:T(1,128)S(1)}, f32[1,256]{1,0:T(1,128)S(1)}, f32[1,256]{1,0:T(1,128)S(...) custom-call(bf16[264,768]{1,0:T(8,128)(2,1)S(1)} %get-tuple-element.158.refs_0_, ...), custom_call_target="tpu_custom_call" | custom-call | flops 3523215360 | tf_op jit(solution)/shard_map/products/pallas_call | solution.py:399
  65.8 3.6 %collective-permute-done.12.refs_5_ = bf16[264,768]{1,0:T(8,128)(2,1)S(1)} collective-permute-done((bf16[264,768]{1,0:T(8,128)(2,1)S(1)}, bf16[264,768]{1,0:T(8,128)(2,1)S(1)}, u32[]{:S(2)}, u32[]{:S(2)}) %collective-permute-start.12) | collective-permute-done | bytes 405536 | tf_op jit(solution)/shard_map/ppermute | solution.py:336
  69.4 0.3 collective-permute-done.13.refs_6_
  69.6 0.0 copy-start
  69.6 1.6 %final.1 = f32[8,1,640]{2,1,0:T(1,128)S(1)} custom-call(bf16[264,768]{1,0:T(8,128)(2,1)S(1)} %get-tuple-element.158.refs_0_, bf16[264,768]{1,0:T(8,128)(2,1)S(1)} %pack.7.refs_2_.refs_4_.refs_5_.refs_1_, bf16[264,768]{1,0:T(8,128)(2,1)S(1)} %collective-permute-done.1.refs_3_.refs_4_.refs_5_.refs_2_, ...), custom_call_target="tpu_custom_call" | custom-call | flops 1107296256 | tf_op jit(solution)/shard_map/final/pallas_call | solution.py:498
  71.2 7.3 %all_to_all.10.back_ref = f32[8,1,640]{2,1,0:T(1,128)S(1)} all-to-all(f32[8,1,640]{2,1,0:T(1,128)S(1)} %final.1), channel_id=1, replica_groups=mesh['gx'=4,'gy'=8] {'gy'}, dimensions={0} | all-to-all | bytes 40960 | tf_op jit(solution)/shard_map/all_to_all | solution.py:508
  78.6 0.0 copy-done
  78.6 0.9 %finish.1 = f32[1,1024]{1,0:T(1,128)} custom-call(s32[2,1024]{1,0:T(2,128)S(1)} %copy-done, f32[8,1,640]{2,1,0:T(1,128)S(1)} %all_to_all.10.back_ref), custom_call_target="tpu_custom_call" | custom-call | tf_op jit(solution)/shard_map/finish/pallas_call | solution.py:509
  (4 shorter events, 0.1 us)
Async XLA Ops:
  0.0 11.0 %copy-start.1 = (bf16[1024,768]{1,0:T(8,128)(2,1)S(1)}, bf16[1024,768]{1,0:T(8,128)(2,1)}, u32[]{:S(2)}) copy-start(bf16[1024,768]{1,0:T(8,128)(2,1)} %param.3) | copy-start | bytes 4718596
  1.9 14.5 %all-to-all-start = ((s32[32,1,32]{2,1,0:T(1,128)}), s32[32,1,32]{2,1,0:T(1,128)S(1)}, u32[]{:S(2)}, u32[]{:S(2)}) async-start(s32[32,1,32]{2,1,0:T(1,128)} %get-tuple-element.92), calls=%async_computation | async-start | bytes 32768 | tf_op jit(solution)/shard_map/all_to_all | solution.py:307
  17.2 14.4 %collective-permute-start = (bf16[272,768]{1,0:T(8,128)(2,1)S(1)}, bf16[272,768]{1,0:T(8,128)(2,1)S(1)}, u32[]{:S(2)}, u32[]{:S(2)}) collective-permute-start(bf16[272,768]{1,0:T(8,128)(2,1)S(1)} %select.3), channel_id=1, source_target_pairs={{0,8},{8,16},{16,24},{24,0},{1,9},{9,17},{17,25},{25,1},{2,10},{10... | collective-permute-start | bytes 1253384 | tf_op jit(solution)/shard_map/ppermute | solution.py:333
  18.6 10.7 %collective-permute-start.1 = (bf16[264,768]{1,0:T(8,128)(2,1)S(1)}, bf16[264,768]{1,0:T(8,128)(2,1)S(1)}, u32[]{:S(2)}, u32[]{:S(2)}) collective-permute-start(bf16[264,768]{1,0:T(8,128)(2,1)S(1)} %select.4.refs_1_.refs_2_), channel_id=1, source_target_pairs={{0,2},{1,3},{2,0},{3,1},{4,6},{5,7},{6,4},{7,5},{8,10},{9,11},{10,... | collective-permute-start | bytes 1216520 | tf_op jit(solution)/shard_map/ppermute | solution.py:336
  19.2 10.1 %collective-permute-start.2 = (bf16[264,768]{1,0:T(8,128)(2,1)S(1)}, bf16[264,768]{1,0:T(8,128)(2,1)S(1)}, u32[]{:S(2)}, u32[]{:S(2)}) collective-permute-start(bf16[264,768]{1,0:T(8,128)(2,1)S(1)} %select.4.refs_1_.refs_2_), channel_id=1, source_target_pairs={{0,1},{1,0},{2,3},{3,2},{4,5},{5,4},{6,7},{7,6},{8,9},{9,8},{10,11... | collective-permute-start | bytes 1216520 | tf_op jit(solution)/shard_map/ppermute | solution.py:336
  19.2 11.8 %collective-permute-start.3 = (bf16[264,768]{1,0:T(8,128)(2,1)S(1)}, bf16[264,768]{1,0:T(8,128)(2,1)S(1)}, u32[]{:S(2)}, u32[]{:S(2)}) collective-permute-start(bf16[264,768]{1,0:T(8,128)(2,1)S(1)} %select.4.refs_1_.refs_2_), channel_id=1, source_target_pairs={{0,4},{1,5},{2,6},{3,7},{4,0},{5,1},{6,2},{7,3},{8,12},{9,13},{10,... | collective-permute-start | bytes 1216520 | tf_op jit(solution)/shard_map/ppermute | solution.py:336
  21.3 18.1 %collective-permute-start.5 = (bf16[272,768]{1,0:T(8,128)(2,1)S(1)}, bf16[272,768]{1,0:T(8,128)(2,1)S(1)}, u32[]{:S(2)}, u32[]{:S(2)}) collective-permute-start(bf16[272,768]{1,0:T(8,128)(2,1)S(1)} %get-tuple-element.101), channel_id=1, source_target_pairs={{0,24},{8,0},{16,8},{24,16},{1,25},{9,1},{17,9},{25,17},{2,26},{10... | collective-permute-start | bytes 1253384 | tf_op jit(solution)/shard_map/ppermute | solution.py:333
  31.6 7.8 %collective-permute-start.6 = (bf16[264,768]{1,0:T(8,128)(2,1)S(1)}, bf16[264,768]{1,0:T(8,128)(2,1)S(1)}, u32[]{:S(2)}, u32[]{:S(2)}) collective-permute-start(bf16[264,768]{1,0:T(8,128)(2,1)S(1)} %collective-permute-done.1.refs_3_.refs_4_.refs_5_.refs_2_), channel_id=1, source_target_pairs={{0,1},{1,0},{2,3},{3,2},{4,5},{5,4},{6,7},{7,6},{8,9},{9,8},{10,11... | collective-permute-start | bytes 1216520 | tf_op jit(solution)/shard_map/ppermute | solution.py:336
  31.6 11.9 %collective-permute-start.7 = (bf16[264,768]{1,0:T(8,128)(2,1)S(1)}, bf16[264,768]{1,0:T(8,128)(2,1)S(1)}, u32[]{:S(2)}, u32[]{:S(2)}) collective-permute-start(bf16[264,768]{1,0:T(8,128)(2,1)S(1)} %pack.5.refs_2_.refs_0_.refs_3_), channel_id=1, source_target_pairs={{0,2},{1,3},{2,0},{3,1},{4,6},{5,7},{6,4},{7,5},{8,10},{9,11},{10,... | collective-permute-start | bytes 1216520 | tf_op jit(solution)/shard_map/ppermute | solution.py:336
  32.6 11.5 %collective-permute-start.8 = (bf16[264,768]{1,0:T(8,128)(2,1)S(1)}, bf16[264,768]{1,0:T(8,128)(2,1)S(1)}, u32[]{:S(2)}, u32[]{:S(2)}) collective-permute-start(bf16[264,768]{1,0:T(8,128)(2,1)S(1)} %pack.5.refs_2_.refs_0_.refs_3_), channel_id=1, source_target_pairs={{0,4},{1,5},{2,6},{3,7},{4,0},{5,1},{6,2},{7,3},{8,12},{9,13},{10,... | collective-permute-start | bytes 1216520 | tf_op jit(solution)/shard_map/ppermute | solution.py:336
  33.2 24.1 %collective-permute-start.4 = (bf16[272,768]{1,0:T(8,128)(2,1)S(1)}, bf16[272,768]{1,0:T(8,128)(2,1)S(1)}, u32[]{:S(2)}, u32[]{:S(2)}) collective-permute-start(bf16[272,768]{1,0:T(8,128)(2,1)S(1)} %get-tuple-element.100), channel_id=1, source_target_pairs={{0,16},{8,24},{16,0},{24,8},{1,17},{9,25},{17,1},{25,9},{2,18},{10... | collective-permute-start | bytes 1253384 | tf_op jit(solution)/shard_map/ppermute | solution.py:333
  44.2 13.1 %collective-permute-start.9 = (bf16[264,768]{1,0:T(8,128)(2,1)S(1)}, bf16[264,768]{1,0:T(8,128)(2,1)S(1)}, u32[]{:S(2)}, u32[]{:S(2)}) collective-permute-start(bf16[264,768]{1,0:T(8,128)(2,1)S(1)} %pack.6.refs_3_.refs_1_.refs_4_), channel_id=1, source_target_pairs={{0,2},{1,3},{2,0},{3,1},{4,6},{5,7},{6,4},{7,5},{8,10},{9,11},{10,... | collective-permute-start | bytes 1216520 | tf_op jit(solution)/shard_map/ppermute | solution.py:336
  45.3 12.0 %collective-permute-start.10 = (bf16[264,768]{1,0:T(8,128)(2,1)S(1)}, bf16[264,768]{1,0:T(8,128)(2,1)S(1)}, u32[]{:S(2)}, u32[]{:S(2)}) collective-permute-start(bf16[264,768]{1,0:T(8,128)(2,1)S(1)} %pack.6.refs_3_.refs_1_.refs_4_), channel_id=1, source_target_pairs={{0,4},{1,5},{2,6},{3,7},{4,0},{5,1},{6,2},{7,3},{8,12},{9,13},{10,... | collective-permute-start | bytes 1216520 | tf_op jit(solution)/shard_map/ppermute | solution.py:336
  57.5 4.1 %collective-permute-start.11 = (bf16[1288,768]{1,0:T(8,128)(2,1)S(1)}, bf16[1288,768]{1,0:T(8,128)(2,1)S(1)}, u32[]{:S(2)}, u32[]{:S(2)}) collective-permute-start(bf16[1288,768]{1,0:T(8,128)(2,1)S(1)} %pack.8), channel_id=1, source_target_pairs={{0,1},{1,0},{2,3},{3,2},{4,5},{5,4},{6,7},{7,6},{8,9},{9,8},{10,11... | collective-permute-start | bytes 5935112 | tf_op jit(solution)/shard_map/ppermute | solution.py:336
  57.6 11.8 %collective-permute-start.12 = (bf16[264,768]{1,0:T(8,128)(2,1)S(1)}, bf16[264,768]{1,0:T(8,128)(2,1)S(1)}, u32[]{:S(2)}, u32[]{:S(2)}) collective-permute-start(bf16[264,768]{1,0:T(8,128)(2,1)S(1)} %pack.7.refs_2_.refs_4_.refs_5_.refs_1_), channel_id=1, source_target_pairs={{0,2},{1,3},{2,0},{3,1},{4,6},{5,7},{6,4},{7,5},{8,10},{9,11},{10,... | collective-permute-start | bytes 1216520 | tf_op jit(solution)/shard_map/ppermute | solution.py:336
  58.2 11.4 %collective-permute-start.13 = (bf16[264,768]{1,0:T(8,128)(2,1)S(1)}, bf16[264,768]{1,0:T(8,128)(2,1)S(1)}, u32[]{:S(2)}, u32[]{:S(2)}) collective-permute-start(bf16[264,768]{1,0:T(8,128)(2,1)S(1)} %pack.7.refs_2_.refs_4_.refs_5_.refs_1_), channel_id=1, source_target_pairs={{0,5},{1,4},{2,7},{3,6},{4,0},{5,1},{6,2},{7,3},{8,13},{9,12},{10,... | collective-permute-start | bytes 1216520 | tf_op jit(solution)/shard_map/ppermute | solution.py:460
  69.6 8.9 %copy-start = (s32[2,1024]{1,0:T(2,128)S(1)}, s32[2,1024]{1,0:T(2,128)}, u32[]{:S(2)}) copy-start(s32[2,1024]{1,0:T(2,128)} %get-tuple-element.91.home_ref) | copy-start | bytes 24580

commit v7 on v6

--- a/solution.py
+++ b/solution.py
@@ -69,9 +69,10 @@
     before = one_hot(iota((128, 128), 0) < iota((128, 128), 1))
     count = jnp.zeros((owners, 1), F32)
     ranks = []
-    for b in range(rows // 128):
-        part = hot[:, b * 128:(b + 1) * 128]
-        rank = dot_nn(part, before) + count
+    parts = [hot[:, b * 128:(b + 1) * 128] for b in range(rows // 128)]
+    inner = dot_nn(jnp.concatenate(parts, axis=0), before)
+    for b, part in enumerate(parts):
+        rank = inner[b * owners:(b + 1) * owners, :] + count
         part32 = part.astype(F32)
         ranks.append(jnp.sum(part32 * rank, axis=0, keepdims=True))
         count = count + jnp.sum(part32, axis=1, keepdims=True)
@@ -81,11 +82,10 @@
     high = lax.shift_right_logical(row, 8).astype(F32)
     zero = jnp.zeros((owners, rows), F32)
 
-    def pick(value):
-        return dot_nt(jnp.where(mask, value, zero).astype(BF16), place)
-
-    asked = pick(low) + 256.0 * pick(high) + float(rows) * pick(cluster.astype(F32))
-    asked = asked.astype(I32)
+    values = [jnp.where(mask, v, zero).astype(BF16) for v in (low, high, cluster.astype(F32))]
+    picked = dot_nt(jnp.concatenate(values, axis=0), place)
+    low, high, held = (picked[i * owners:(i + 1) * owners, :] for i in range(3))
+    asked = (low + 256.0 * high + float(rows) * held).astype(I32)
     for o in range(owners):
         asked_ref[o] = asked[o:o + 1, :]
     plane = lax.shift_right_logical(owner, log2(n_gy))
@@ -116,7 +116,7 @@
         ref[0:chunk, :] = dot_nn(hot, unit_ref[...]).astype(BF16)
         width = unit_ref.shape[1]
         line = jnp.concatenate([flat, jnp.zeros((1, width - chunk), F32)], axis=1)
-        ref[chunk:chunk + SPARE, :] = jnp.where(iota((SPARE, width), 0) == 0, line, 0.0).astype(BF16)
+        ref[chunk:chunk + 1, :] = line.astype(BF16)
 
 
 def column(line):
@@ -132,7 +132,7 @@
 
 
 def more(chunks):
-    return -(-chunks // SPARE) * SPARE
+    return chunks
 
 
 def cluster_line(ref, size, chunk):
@@ -269,7 +269,8 @@
     mid = rest.astype(BF16)
     low = (rest - mid.astype(F32)).astype(BF16)
     here = one_hot(iota((128, rows), 0) == home_ref[1:2, :])
-    value = (dot_nn(high, here) + dot_nn(mid, here)) + dot_nn(low, here)
+    value = dot_nn(jnp.concatenate([high.astype(F32), mid.astype(F32), low.astype(F32)], axis=0).astype(BF16), here)
+    value = (value[0:n_gy] + value[n_gy:2 * n_gy]) + value[2 * n_gy:3 * n_gy]
     own = iota((n_gy, rows), 0) == home_ref[0:1, :]
     out_ref[...] = jnp.sum(jnp.where(own, value, 0.0), axis=0, keepdims=True)
 
@@ -319,7 +320,7 @@
     for steps in [stages[1][:1], stages[0], stages[1][1:] + stages[2]]:
         out = pl.pallas_call(
             functools.partial(select_kernel, dims, steps),
-            out_shape=[shape((chunk + (2 if k else 1) * SPARE, width), BF16) for k in steps],
+            out_shape=[shape((chunk + (SPARE if k else 1), width), BF16) for k in steps],
             in_specs=[in_vmem, in_vmem],
             out_specs=[in_vmem] * len(steps),
             cost_estimate=cost(2 * len(steps) * chunk * rows * width, rows * width),

time: 79.6 us -> 78.5 us (0.986)
  waiting for transfers between devices: 33.7 us -> 32.7 us
    ppermute x3, waiting for transfers between devices: 13.5 us -> 11.9 us  [across(): lax.ppermute(array, 'gx', [(i, (i + step) % n_gx) for i in range(n_gx)])]
where the time goes in v7:
time: 78.5 us; the launch traced here: 78.3 us
  waiting for transfers between devices  32.7 us (42%)
  Pallas kernels  18.7 us (24%)
  starting transfers between devices  17.2 us (22%)
  blocking collectives  7.33 us (9%)
  other arithmetic  2.11 us (3%)
    ppermute x10, waiting for transfers between devices, swap(): return lax.ppermute(array, 'gy', [(i, i ^ mask) for i in range(n_gy)])  15.5 us
    ppermute x3, waiting for transfers between devices, across(): lax.ppermute(array, 'gx', [(i, (i + step) % n_gx) for i in range(n_gx)])  11.9 us
    pallas_call x4, Pallas kernels, products(): pl.pallas_call(functools.partial(product_kernel, pairs, size, chunk, star...  11.1 us
    all_to_all x1, blocking collectives, per_device(): back = lax.all_to_all(send, 'gy', split_axis=0, concat_axis=0, tiled=True)  7.33 us
    all_to_all x1, starting transfers between devices, per_device(): lax.all_to_all(asked, ('gx', 'gy'), split_axis=0, concat_axis=0, tiled=True)  7.3 us
    ppermute x10, starting transfers between devices, swap(): return lax.ppermute(array, 'gy', [(i, i ^ mask) for i in range(n_gy)])  5.15 us
    all_to_all x1, waiting for transfers between devices, per_device(): lax.all_to_all(asked, ('gx', 'gy'), split_axis=0, concat_axis=0, tiled=True)  5 us
    ppermute x3, starting transfers between devices, across(): lax.ppermute(array, 'gx', [(i, (i + step) % n_gx) for i in range(n_gx)])  4.47 us
  transfers between devices with their start and end apart: 15, of which 11 were waited for; matrix products, arithmetic and copies ran while one was open for 3% of the time, Pallas kernels for 17%

profile of v7, /device:TPU:0, one launch (start us, length us, event | category | flops | bytes accessed | tf_op | source)
XLA Modules:
  0.0 78.3 jit_solution(1295052717794638698)
XLA Ops:
  0.0 0.0 copy-start.1
  0.0 1.8 %request.1 = (s32[32,1,32]{2,1,0:T(1,128)}, s32[2,1024]{1,0:T(2,128)}) custom-call(s32[1,25]{1,0:T(1,128)} %sizes_hbm.1, s32[1,1024]{1,0:T(1,128)} %bitcast.2), custom_call_target="tpu_custom_call" | custom-call | tf_op jit(solution)/shard_map/request/pallas_call | solution.py:295
  1.8 7.3 %all-to-all-start = ((s32[32,1,32]{2,1,0:T(1,128)}), s32[32,1,32]{2,1,0:T(1,128)S(1)}, u32[]{:S(2)}, u32[]{:S(2)}) async-start(s32[32,1,32]{2,1,0:T(1,128)} %get-tuple-element.92), calls=%async_computation | async-start | bytes 32768 | tf_op jit(solution)/shard_map/all_to_all | solution.py:308
  9.1 1.8 %fusion = f32[1024]{0:T(1024)S(1)} fusion(bf16[1024,768]{1,0:T(8,128)(2,1)} %param.3), kind=kLoop, calls=%fused_computation.2 | loop fusion | flops 2358272 | bytes 1576960 | tf_op jit(solution)/shard_map/reduce_sum | solution.py:311
  10.9 0.0 copy-done.1
  10.9 0.3 fusion.1.unit_ref
  11.3 5.0 %all-to-all-done.asked_ref = s32[32,1,32]{2,1,0:T(1,128)S(1)} async-done(((s32[32,1,32]{2,1,0:T(1,128)}), s32[32,1,32]{2,1,0:T(1,128)S(1)}, u32[]{:S(2)}, u32[]{:S(2)}) %all-to-all-start) | async-done | bytes 4128 | tf_op jit(solution)/shard_map/all_to_all | solution.py:308
  16.3 0.8 %select.3 = bf16[264,768]{1,0:T(8,128)(2,1)S(1)} custom-call(s32[32,1,32]{2,1,0:T(1,128)S(1)} %all-to-all-done.asked_ref, bf16[1024,768]{1,0:T(8,128)(2,1)S(1)} %fusion.1.unit_ref), custom_call_target="tpu_custom_call" | custom-call | flops 402653184 | bytes 786432 | tf_op jit(solution)/shard_map/select/pallas_call | solution.py:321
  17.1 0.6 collective-permute-start
  17.8 0.8 %select.4.refs_1_.refs_2_ = bf16[257,768]{1,0:T(8,128)(2,1)S(1)} custom-call(s32[32,1,32]{2,1,0:T(1,128)S(1)} %all-to-all-done.asked_ref, bf16[1024,768]{1,0:T(8,128)(2,1)S(1)} %fusion.1.unit_ref), custom_call_target="tpu_custom_call" | custom-call | flops 402653184 | bytes 786432 | tf_op jit(solution)/shard_map/select/pallas_call | solution.py:321
  18.6 0.6 collective-permute-start.1
  19.2 0.0 collective-permute-start.2
  19.2 0.6 collective-permute-start.3
  19.8 1.4 %select.5 = (bf16[264,768]{1,0:T(8,128)(2,1)S(1)}, bf16[264,768]{1,0:T(8,128)(2,1)S(1)}) custom-call(s32[32,1,32]{2,1,0:T(1,128)S(1)} %all-to-all-done.asked_ref, bf16[1024,768]{1,0:T(8,128)(2,1)S(1)} %fusion.1.unit_ref), custom_call_target="tpu_custom_call" | custom-call | flops 805306368 | bytes 786432 | tf_op jit(solution)/shard_map/select/pallas_call | solution.py:321
  21.2 3.3 %collective-permute-start.5 = (bf16[264,768]{1,0:T(8,128)(2,1)S(1)}, bf16[264,768]{1,0:T(8,128)(2,1)S(1)}, u32[]{:S(2)}, u32[]{:S(2)}) collective-permute-start(bf16[264,768]{1,0:T(8,128)(2,1)S(1)} %get-tuple-element.101), channel_id=1, source_target_pairs={{0,24},{8,0},{16,8},{24,16},{1,25},{9,1},{17,9},{25,17},{2,26},{10... | collective-permute-start | bytes 1216520 | tf_op jit(solution)/shard_map/ppermute | solution.py:334
  24.5 4.7 %collective-permute-done.1.refs_3_.refs_4_.refs_5_.refs_2_ = bf16[257,768]{1,0:T(8,128)(2,1)S(1)} collective-permute-done((bf16[257,768]{1,0:T(8,128)(2,1)S(1)}, bf16[257,768]{1,0:T(8,128)(2,1)S(1)}, u32[]{:S(2)}, u32[]{:S(2)}) %collective-permute-start.1) | collective-permute-done | bytes 394784 | tf_op jit(solution)/shard_map/ppermute | solution.py:337
  29.3 0.0 collective-permute-done.2.refs_0_
  29.3 1.7 %collective-permute-done.3.refs_4_.refs_6_.refs_8_ = bf16[257,768]{1,0:T(8,128)(2,1)S(1)} collective-permute-done((bf16[257,768]{1,0:T(8,128)(2,1)S(1)}, bf16[257,768]{1,0:T(8,128)(2,1)S(1)}, u32[]{:S(2)}, u32[]{:S(2)}) %collective-permute-start.3) | collective-permute-done | bytes 394784 | tf_op jit(solution)/shard_map/ppermute | solution.py:337
  31.0 0.3 collective-permute-done.refs_0_
  31.3 0.0 collective-permute-start.6
  31.3 1.3 %collective-permute-start.7 = (bf16[257,768]{1,0:T(8,128)(2,1)S(1)}, bf16[257,768]{1,0:T(8,128)(2,1)S(1)}, u32[]{:S(2)}, u32[]{:S(2)}) collective-permute-start(bf16[257,768]{1,0:T(8,128)(2,1)S(1)} %pack.5.refs_2_.refs_0_.refs_3_), channel_id=1, source_target_pairs={{0,2},{1,3},{2,0},{3,1},{4,6},{5,7},{6,4},{7,5},{8,10},{9,11},{10,... | collective-permute-start | bytes 1184264 | tf_op jit(solution)/shard_map/ppermute | solution.py:337
  32.6 0.5 collective-permute-start.8
  33.1 0.6 collective-permute-start.4
  33.7 1.4 %products.4 = (f32[256,128]{1,0:T(8,128)S(1)}, f32[256,128]{1,0:T(8,128)S(1)}, f32[256,128]{1,0:T(8,128)S(1)}, f32[256,128]{1,0:T(8,128)S(1)}, f32[256,128]{1,0:T(8,128)S(1)}, /*index=5*/f32[256,128]{1,0:T(8,128)S(1)}) custom-call(bf16[257,768]{1,0:T(8,128)(2,1)S(1)} %collective-permute-done.2.refs_0_, bf16[257,768]{1,0:T(8,128)(2,1)S(1)} %select.4.refs_1_.refs_2_, ...), custom_call_target="tpu_custom_call" | custom-call | flops 1207959552 | tf_op jit(solution)/shard_map/products/pallas_call | solution.py:400
  35.1 3.7 %collective-permute-done.5.refs_0_ = bf16[264,768]{1,0:T(8,128)(2,1)S(1)} collective-permute-done((bf16[264,768]{1,0:T(8,128)(2,1)S(1)}, bf16[264,768]{1,0:T(8,128)(2,1)S(1)}, u32[]{:S(2)}, u32[]{:S(2)}) %collective-permute-start.5) | collective-permute-done | bytes 405536 | tf_op jit(solution)/shard_map/ppermute | solution.py:334
  38.8 0.0 collective-permute-done.6.refs_8_.refs_11_.refs_7_
  38.8 4.4 %collective-permute-done.7.refs_5_.refs_3_.refs_6_ = bf16[257,768]{1,0:T(8,128)(2,1)S(1)} collective-permute-done((bf16[257,768]{1,0:T(8,128)(2,1)S(1)}, bf16[257,768]{1,0:T(8,128)(2,1)S(1)}, u32[]{:S(2)}, u32[]{:S(2)}) %collective-permute-start.7) | collective-permute-done | bytes 394784 | tf_op jit(solution)/shard_map/ppermute | solution.py:337
  43.2 0.9 %collective-permute-done.8.refs_7_.refs_9_ = bf16[257,768]{1,0:T(8,128)(2,1)S(1)} collective-permute-done((bf16[257,768]{1,0:T(8,128)(2,1)S(1)}, bf16[257,768]{1,0:T(8,128)(2,1)S(1)}, u32[]{:S(2)}, u32[]{:S(2)}) %collective-permute-start.8) | collective-permute-done | bytes 394784 | tf_op jit(solution)/shard_map/ppermute | solution.py:337
  44.1 0.9 %collective-permute-start.9 = (bf16[257,768]{1,0:T(8,128)(2,1)S(1)}, bf16[257,768]{1,0:T(8,128)(2,1)S(1)}, u32[]{:S(2)}, u32[]{:S(2)}) collective-permute-start(bf16[257,768]{1,0:T(8,128)(2,1)S(1)} %pack.6.refs_3_.refs_1_.refs_4_), channel_id=1, source_target_pairs={{0,2},{1,3},{2,0},{3,1},{4,6},{5,7},{6,4},{7,5},{8,10},{9,11},{10,... | collective-permute-start | bytes 1184264 | tf_op jit(solution)/shard_map/ppermute | solution.py:337
  45.0 0.5 collective-permute-start.10
  45.6 2.7 %products.5 = (f32[256,128]{1,0:T(8,128)S(1)}, f32[256,128]{1,0:T(8,128)S(1)}, f32[256,128]{1,0:T(8,128)S(1)}, f32[256,128]{1,0:T(8,128)S(1)}, f32[256,128]{1,0:...) custom-call(bf16[257,768]{1,0:T(8,128)(2,1)S(1)} %collective-permute-done.2.refs_0_, ...), custom_call_target="tpu_custom_call" | custom-call | flops 2315255808 | tf_op jit(solution)/shard_map/products/pallas_call | solution.py:400
  48.3 7.9 %collective-permute-done.4.refs_0_ = bf16[264,768]{1,0:T(8,128)(2,1)S(1)} collective-permute-done((bf16[264,768]{1,0:T(8,128)(2,1)S(1)}, bf16[264,768]{1,0:T(8,128)(2,1)S(1)}, u32[]{:S(2)}, u32[]{:S(2)}) %collective-permute-start.4) | collective-permute-done | bytes 405536 | tf_op jit(solution)/shard_map/ppermute | solution.py:334
  56.2 0.0 collective-permute-done.9.refs_4_.refs_7_
  56.2 0.0 collective-permute-done.10.refs_10_.refs_8_
  56.2 0.1 pack.8
  56.4 0.1 collective-permute-start.11
  56.5 0.6 collective-permute-start.12
  57.1 0.3 collective-permute-start.13
  57.4 2.9 %products.6 = (f32[256,128]{1,0:T(8,128)S(1)}, f32[256,128]{1,0:T(8,128)S(1)}, f32[256,128]{1,0:T(8,128)S(1)}, f32[256,128]{1,0:T(8,128)S(1)}, f32[256,128]{1,0:...) custom-call(bf16[257,768]{1,0:T(8,128)(2,1)S(1)} %collective-permute, ...), custom_call_target="tpu_custom_call" | custom-call | flops 2516582400 | tf_op jit(solution)/shard_map/products/pallas_call | solution.py:400
  60.3 0.1 collective-permute-done.11.refs_0_
  60.5 0.1 pack.9
  60.6 4.0 %products.7 = (f32[1,256]{1,0:T(1,128)S(1)}, f32[1,256]{1,0:T(1,128)S(1)}, f32[1,256]{1,0:T(1,128)S(1)}, f32[1,256]{1,0:T(1,128)S(1)}, f32[1,256]{1,0:T(1,128)S(...) custom-call(bf16[257,768]{1,0:T(8,128)(2,1)S(1)} %get-tuple-element.158.refs_0_, ...), custom_call_target="tpu_custom_call" | custom-call | flops 3523215360 | tf_op jit(solution)/shard_map/products/pallas_call | solution.py:400
  64.6 3.7 %collective-permute-done.12.refs_5_ = bf16[257,768]{1,0:T(8,128)(2,1)S(1)} collective-permute-done((bf16[257,768]{1,0:T(8,128)(2,1)S(1)}, bf16[257,768]{1,0:T(8,128)(2,1)S(1)}, u32[]{:S(2)}, u32[]{:S(2)}) %collective-permute-start.12) | collective-permute-done | bytes 394784 | tf_op jit(solution)/shard_map/ppermute | solution.py:337
  68.3 0.3 collective-permute-done.13.refs_6_
  68.5 0.0 copy-start
  68.5 1.6 %final.1 = f32[8,1,640]{2,1,0:T(1,128)S(1)} custom-call(bf16[257,768]{1,0:T(8,128)(2,1)S(1)} %get-tuple-element.158.refs_0_, bf16[257,768]{1,0:T(8,128)(2,1)S(1)} %pack.7.refs_2_.refs_4_.refs_5_.refs_1_, bf16[257,768]{1,0:T(8,128)(2,1)S(1)} %collective-permute-done.1.refs_3_.refs_4_.refs_5_.refs_2_, ...), custom_call_target="tpu_custom_call" | custom-call | flops 1107296256 | tf_op jit(solution)/shard_map/final/pallas_call | solution.py:499
  70.2 7.3 %all_to_all.10.back_ref = f32[8,1,640]{2,1,0:T(1,128)S(1)} all-to-all(f32[8,1,640]{2,1,0:T(1,128)S(1)} %final.1), channel_id=1, replica_groups=mesh['gx'=4,'gy'=8] {'gy'}, dimensions={0} | all-to-all | bytes 40960 | tf_op jit(solution)/shard_map/all_to_all | solution.py:509
  77.5 0.0 copy-done
  77.5 0.8 %finish.1 = f32[1,1024]{1,0:T(1,128)} custom-call(s32[2,1024]{1,0:T(2,128)S(1)} %copy-done, f32[8,1,640]{2,1,0:T(1,128)S(1)} %all_to_all.10.back_ref), custom_call_target="tpu_custom_call" | custom-call | tf_op jit(solution)/shard_map/finish/pallas_call | solution.py:510
  (4 shorter events, 0.1 us)
Async XLA Ops:
  0.0 10.9 %copy-start.1 = (bf16[1024,768]{1,0:T(8,128)(2,1)S(1)}, bf16[1024,768]{1,0:T(8,128)(2,1)}, u32[]{:S(2)}) copy-start(bf16[1024,768]{1,0:T(8,128)(2,1)} %param.3) | copy-start | bytes 4718596
  1.8 14.5 %all-to-all-start = ((s32[32,1,32]{2,1,0:T(1,128)}), s32[32,1,32]{2,1,0:T(1,128)S(1)}, u32[]{:S(2)}, u32[]{:S(2)}) async-start(s32[32,1,32]{2,1,0:T(1,128)} %get-tuple-element.92), calls=%async_computation | async-start | bytes 32768 | tf_op jit(solution)/shard_map/all_to_all | solution.py:308
  17.1 14.2 %collective-permute-start = (bf16[264,768]{1,0:T(8,128)(2,1)S(1)}, bf16[264,768]{1,0:T(8,128)(2,1)S(1)}, u32[]{:S(2)}, u32[]{:S(2)}) collective-permute-start(bf16[264,768]{1,0:T(8,128)(2,1)S(1)} %select.3), channel_id=1, source_target_pairs={{0,8},{8,16},{16,24},{24,0},{1,9},{9,17},{17,25},{25,1},{2,10},{10... | collective-permute-start | bytes 1216520 | tf_op jit(solution)/shard_map/ppermute | solution.py:334
  18.6 10.7 %collective-permute-start.1 = (bf16[257,768]{1,0:T(8,128)(2,1)S(1)}, bf16[257,768]{1,0:T(8,128)(2,1)S(1)}, u32[]{:S(2)}, u32[]{:S(2)}) collective-permute-start(bf16[257,768]{1,0:T(8,128)(2,1)S(1)} %select.4.refs_1_.refs_2_), channel_id=1, source_target_pairs={{0,2},{1,3},{2,0},{3,1},{4,6},{5,7},{6,4},{7,5},{8,10},{9,11},{10,... | collective-permute-start | bytes 1184264 | tf_op jit(solution)/shard_map/ppermute | solution.py:337
  19.2 10.1 %collective-permute-start.2 = (bf16[257,768]{1,0:T(8,128)(2,1)S(1)}, bf16[257,768]{1,0:T(8,128)(2,1)S(1)}, u32[]{:S(2)}, u32[]{:S(2)}) collective-permute-start(bf16[257,768]{1,0:T(8,128)(2,1)S(1)} %select.4.refs_1_.refs_2_), channel_id=1, source_target_pairs={{0,1},{1,0},{2,3},{3,2},{4,5},{5,4},{6,7},{7,6},{8,9},{9,8},{10,11... | collective-permute-start | bytes 1184264 | tf_op jit(solution)/shard_map/ppermute | solution.py:337
  19.2 11.8 %collective-permute-start.3 = (bf16[257,768]{1,0:T(8,128)(2,1)S(1)}, bf16[257,768]{1,0:T(8,128)(2,1)S(1)}, u32[]{:S(2)}, u32[]{:S(2)}) collective-permute-start(bf16[257,768]{1,0:T(8,128)(2,1)S(1)} %select.4.refs_1_.refs_2_), channel_id=1, source_target_pairs={{0,4},{1,5},{2,6},{3,7},{4,0},{5,1},{6,2},{7,3},{8,12},{9,13},{10,... | collective-permute-start | bytes 1184264 | tf_op jit(solution)/shard_map/ppermute | solution.py:337
  21.2 17.6 %collective-permute-start.5 = (bf16[264,768]{1,0:T(8,128)(2,1)S(1)}, bf16[264,768]{1,0:T(8,128)(2,1)S(1)}, u32[]{:S(2)}, u32[]{:S(2)}) collective-permute-start(bf16[264,768]{1,0:T(8,128)(2,1)S(1)} %get-tuple-element.101), channel_id=1, source_target_pairs={{0,24},{8,0},{16,8},{24,16},{1,25},{9,1},{17,9},{25,17},{2,26},{10... | collective-permute-start | bytes 1216520 | tf_op jit(solution)/shard_map/ppermute | solution.py:334
  31.3 7.5 %collective-permute-start.6 = (bf16[257,768]{1,0:T(8,128)(2,1)S(1)}, bf16[257,768]{1,0:T(8,128)(2,1)S(1)}, u32[]{:S(2)}, u32[]{:S(2)}) collective-permute-start(bf16[257,768]{1,0:T(8,128)(2,1)S(1)} %collective-permute-done.1.refs_3_.refs_4_.refs_5_.refs_2_), channel_id=1, source_target_pairs={{0,1},{1,0},{2,3},{3,2},{4,5},{5,4},{6,7},{7,6},{8,9},{9,8},{10,11... | collective-permute-start | bytes 1184264 | tf_op jit(solution)/shard_map/ppermute | solution.py:337
  31.3 11.9 %collective-permute-start.7 = (bf16[257,768]{1,0:T(8,128)(2,1)S(1)}, bf16[257,768]{1,0:T(8,128)(2,1)S(1)}, u32[]{:S(2)}, u32[]{:S(2)}) collective-permute-start(bf16[257,768]{1,0:T(8,128)(2,1)S(1)} %pack.5.refs_2_.refs_0_.refs_3_), channel_id=1, source_target_pairs={{0,2},{1,3},{2,0},{3,1},{4,6},{5,7},{6,4},{7,5},{8,10},{9,11},{10,... | collective-permute-start | bytes 1184264 | tf_op jit(solution)/shard_map/ppermute | solution.py:337
  32.6 11.5 %collective-permute-start.8 = (bf16[257,768]{1,0:T(8,128)(2,1)S(1)}, bf16[257,768]{1,0:T(8,128)(2,1)S(1)}, u32[]{:S(2)}, u32[]{:S(2)}) collective-permute-start(bf16[257,768]{1,0:T(8,128)(2,1)S(1)} %pack.5.refs_2_.refs_0_.refs_3_), channel_id=1, source_target_pairs={{0,4},{1,5},{2,6},{3,7},{4,0},{5,1},{6,2},{7,3},{8,12},{9,13},{10,... | collective-permute-start | bytes 1184264 | tf_op jit(solution)/shard_map/ppermute | solution.py:337
  33.1 23.1 %collective-permute-start.4 = (bf16[264,768]{1,0:T(8,128)(2,1)S(1)}, bf16[264,768]{1,0:T(8,128)(2,1)S(1)}, u32[]{:S(2)}, u32[]{:S(2)}) collective-permute-start(bf16[264,768]{1,0:T(8,128)(2,1)S(1)} %get-tuple-element.100), channel_id=1, source_target_pairs={{0,16},{8,24},{16,0},{24,8},{1,17},{9,25},{17,1},{25,9},{2,18},{10... | collective-permute-start | bytes 1216520 | tf_op jit(solution)/shard_map/ppermute | solution.py:334
  44.1 12.1 %collective-permute-start.9 = (bf16[257,768]{1,0:T(8,128)(2,1)S(1)}, bf16[257,768]{1,0:T(8,128)(2,1)S(1)}, u32[]{:S(2)}, u32[]{:S(2)}) collective-permute-start(bf16[257,768]{1,0:T(8,128)(2,1)S(1)} %pack.6.refs_3_.refs_1_.refs_4_), channel_id=1, source_target_pairs={{0,2},{1,3},{2,0},{3,1},{4,6},{5,7},{6,4},{7,5},{8,10},{9,11},{10,... | collective-permute-start | bytes 1184264 | tf_op jit(solution)/shard_map/ppermute | solution.py:337
  45.0 11.2 %collective-permute-start.10 = (bf16[257,768]{1,0:T(8,128)(2,1)S(1)}, bf16[257,768]{1,0:T(8,128)(2,1)S(1)}, u32[]{:S(2)}, u32[]{:S(2)}) collective-permute-start(bf16[257,768]{1,0:T(8,128)(2,1)S(1)} %pack.6.refs_3_.refs_1_.refs_4_), channel_id=1, source_target_pairs={{0,4},{1,5},{2,6},{3,7},{4,0},{5,1},{6,2},{7,3},{8,12},{9,13},{10,... | collective-permute-start | bytes 1184264 | tf_op jit(solution)/shard_map/ppermute | solution.py:337
  56.4 4.1 %collective-permute-start.11 = (bf16[1285,768]{1,0:T(8,128)(2,1)S(1)}, bf16[1285,768]{1,0:T(8,128)(2,1)S(1)}, u32[]{:S(2)}, u32[]{:S(2)}) collective-permute-start(bf16[1285,768]{1,0:T(8,128)(2,1)S(1)} %pack.8), channel_id=1, source_target_pairs={{0,1},{1,0},{2,3},{3,2},{4,5},{5,4},{6,7},{7,6},{8,9},{9,8},{10,11... | collective-permute-start | bytes 5921288 | tf_op jit(solution)/shard_map/ppermute | solution.py:337
  56.5 11.8 %collective-permute-start.12 = (bf16[257,768]{1,0:T(8,128)(2,1)S(1)}, bf16[257,768]{1,0:T(8,128)(2,1)S(1)}, u32[]{:S(2)}, u32[]{:S(2)}) collective-permute-start(bf16[257,768]{1,0:T(8,128)(2,1)S(1)} %pack.7.refs_2_.refs_4_.refs_5_.refs_1_), channel_id=1, source_target_pairs={{0,2},{1,3},{2,0},{3,1},{4,6},{5,7},{6,4},{7,5},{8,10},{9,11},{10,... | collective-permute-start | bytes 1184264 | tf_op jit(solution)/shard_map/ppermute | solution.py:337
  57.1 11.4 %collective-permute-start.13 = (bf16[257,768]{1,0:T(8,128)(2,1)S(1)}, bf16[257,768]{1,0:T(8,128)(2,1)S(1)}, u32[]{:S(2)}, u32[]{:S(2)}) collective-permute-start(bf16[257,768]{1,0:T(8,128)(2,1)S(1)} %pack.7.refs_2_.refs_4_.refs_5_.refs_1_), channel_id=1, source_target_pairs={{0,5},{1,4},{2,7},{3,6},{4,0},{5,1},{6,2},{7,3},{8,13},{9,12},{10,... | collective-permute-start | bytes 1184264 | tf_op jit(solution)/shard_map/ppermute | solution.py:461
  68.5 9.0 %copy-start = (s32[2,1024]{1,0:T(2,128)S(1)}, s32[2,1024]{1,0:T(2,128)}, u32[]{:S(2)}) copy-start(s32[2,1024]{1,0:T(2,128)} %get-tuple-element.91.home_ref) | copy-start | bytes 24580

commit v8 on v0

v8 whole, which is shorter than its diff:
```python
import functools

import jax
import jax.numpy as jnp
from jax import lax
from jax.experimental import pallas as pl
from jax.experimental.pallas import tpu as pltpu
from jax.sharding import PartitionSpec as P

F32 = jnp.float32
BF16 = jnp.bfloat16
I32 = jnp.int32
SPARE = 8
KEYS = 4
VMEM = 24 * 1024 * 1024
LAST = 4
WEIGHT = 20.0


def iota(shape, dim):
    return lax.broadcasted_iota(I32, shape, dim)


def dot_nt(a, b):
    return lax.dot_general(a, b, (((1,), (1,)), ((), ())), preferred_element_type=F32)


def dot_nn(a, b):
    return lax.dot_general(a, b, (((1,), (0,)), ((), ())), preferred_element_type=F32)


def one_hot(mask):
    return jnp.where(mask, 1.0, 0.0).astype(BF16)


def log2(value):
    assert value & (value - 1) == 0
    return value.bit_length() - 1


def params(limit=VMEM):
    return pltpu.CompilerParams(vmem_limit_bytes=limit)


def cost(flops, size):
    return pl.CostEstimate(flops=flops, bytes_accessed=size, transcendentals=0)


def request_kernel(dims, sizes_hbm, members_hbm, asked_ref, home_ref, sizes_ref, members_ref, sems):
    n_gx, n_gy, rows, quota = dims
    copies = [
        pltpu.make_async_copy(members_hbm, members_ref, sems.at[0]),
        pltpu.make_async_copy(sizes_hbm, sizes_ref, sems.at[1]),
    ]
    for copy in copies:
        copy.start()
    for copy in copies:
        copy.wait()
    owners = n_gx * n_gy
    member = members_ref[...]
    owner = lax.shift_right_logical(member, log2(rows))
    row = member & (rows - 1)
    slot = lax.axis_index("gy") * rows + iota((1, rows), 1)
    cluster = jnp.zeros((1, rows), I32)
    end = jnp.int32(0)
    for c in range(sizes_ref.shape[1]):
        end = end + sizes_ref[0, c]
        cluster = cluster + (slot >= end).astype(I32)
    mask = iota((owners, rows), 0) == owner
    hot = one_hot(mask)
    before = one_hot(iota((128, 128), 0) < iota((128, 128), 1))
    count = jnp.zeros((owners, 1), F32)
    ranks = []
    parts = [hot[:, b * 128:(b + 1) * 128] for b in range(rows // 128)]
    inner = dot_nn(jnp.concatenate(parts, axis=0), before)
    for b, part in enumerate(parts):
        rank = inner[b * owners:(b + 1) * owners, :] + count
        part32 = part.astype(F32)
        ranks.append(jnp.sum(part32 * rank, axis=0, keepdims=True))
        count = count + jnp.sum(part32, axis=1, keepdims=True)
    rank = jnp.concatenate(ranks, axis=1).astype(I32)
    place = one_hot(iota((quota, rows), 0) == rank)
    low = (row & 255).astype(F32)
    high = lax.shift_right_logical(row, 8).astype(F32)
    zero = jnp.zeros((owners, rows), F32)

    values = [jnp.where(mask, v, zero).astype(BF16) for v in (low, high, cluster.astype(F32))]
    picked = dot_nt(jnp.concatenate(values, axis=0), place)
    low, high, held = (picked[i * owners:(i + 1) * owners, :] for i in range(3))
    asked = (low + 256.0 * high + float(rows) * held).astype(I32)
    for o in range(owners):
        asked_ref[o] = asked[o:o + 1, :]
    plane = lax.shift_right_logical(owner, log2(n_gy))
    step = (lax.axis_index("gx") - plane) & (n_gx - 1)
    home_ref[0:1, :] = owner & (n_gy - 1)
    home_ref[1:2, :] = step * quota + rank


def select_kernel(dims, parts, asked_ref, unit_ref, *out_refs):
    n_gx, n_gy, rows, quota = dims
    chunk = n_gy * quota
    pick = one_hot((iota((chunk, quota), 0) & (quota - 1)) == iota((chunk, quota), 1))
    block = lax.shift_right_logical(iota((chunk, n_gy), 0), log2(quota))
    own_col = block == iota((chunk, n_gy), 1)
    block_row = lax.shift_right_logical(iota((n_gy, chunk), 1), log2(quota))
    own_row = block_row == iota((n_gy, chunk), 0)
    refs = list(out_refs)
    width = unit_ref.shape[1]
    for step in sorted({k for k, _, _ in parts}):
        plane = (lax.axis_index("gx") + step) & (n_gx - 1)
        wanted = jnp.concatenate([asked_ref[plane * n_gy + d] for d in range(n_gy)], axis=0)
        row = wanted & (rows - 1)
        cluster = lax.shift_right_logical(wanted, log2(rows)).astype(F32).astype(BF16)
        low = (row & 255).astype(F32).astype(BF16)
        high = lax.shift_right_logical(row, 8).astype(F32).astype(BF16)
        index = dot_nt(pick, low) + 256.0 * dot_nt(pick, high)
        index = jnp.sum(jnp.where(own_col, index, 0.0), axis=1, keepdims=True).astype(I32)
        flat = jnp.sum(jnp.where(own_row, dot_nt(cluster, pick), 0.0), axis=0, keepdims=True)
        hot = one_hot(iota((chunk, rows), 1) == index)
        found = dot_nn(hot, unit_ref[...]).astype(BF16)
        for ref, (k, first, count) in zip(out_refs, parts):
            if k == step:
                ref[0:count, :] = found[first:first + count, :]
                line = [flat[:, first:first + count], jnp.zeros((1, width - count), F32)]
                ref[count:count + 1, :] = jnp.concatenate(line, axis=1).astype(BF16)


def column(line):
    parts = []
    for b in range(line.shape[1] // 128):
        wide = jnp.broadcast_to(line[:, b * 128:(b + 1) * 128], (128, 128))
        parts.append(wide.T)
    return jnp.concatenate(parts, axis=0)


def wide(col, lanes):
    return jnp.concatenate([col] * (lanes // 128), axis=1)


def length(parts):
    return sum(count for _, _, count in parts)


def cluster_line(ref, parts):
    size = length(parts)
    block = ref[size:size + len(parts), :].astype(F32)
    return jnp.concatenate([block[r:r + 1, 0:part[2]] for r, part in enumerate(parts)], axis=1)


def pack_kernel(groups, *refs):
    refs = list(refs)
    outs = refs[sum(len(g) for g in groups):]
    for group, out_ref in zip(groups, outs):
        at = 0
        total = sum(length(parts) for parts in group)
        width = out_ref.shape[1]
        lines = []
        for parts in group:
            ref, size = refs.pop(0), length(parts)
            out_ref[at:at + size, :] = ref[0:size, :]
            lines.append(ref[size:size + len(parts), :].astype(F32))
            at += size
        count = sum(len(parts) for parts in group)
        out_ref[total:total + count, :] = jnp.concatenate(lines, axis=0).astype(BF16)


def split_kernel(pieces, ref, *outs):
    total = sum(length(parts) for parts in pieces)
    at = 0
    row = total
    for parts, out_ref in zip(pieces, outs):
        size = length(parts)
        out_ref[0:size, :] = ref[at:at + size, :]
        out_ref[size:size + len(parts), :] = ref[row:row + len(parts), :]
        at += size
        row += len(parts)


def needed(one, two):
    (a, s), (b, t) = sorted([(n[0], int(n[-1])) for n in (one, two)], key=lambda n: "TNXY".index(n[0]))
    if a + b in ("TN", "TX"):
        return s >= t
    if a + b == "NX":
        return s == t or s < t < LAST or s == LAST
    if a + b == "TY":
        return s == LAST or t < LAST
    if a + b == "NY":
        return s == LAST and t < LAST
    return a + b in ("TT", "XY")


def cross(stack, held, inner, parts, refs, stack_ref, col_ref, best_ref):
    at = {}
    size = 0
    for n in stack:
        at[n] = size
        stack_ref[size:size + length(parts[n]), :] = refs[n][0:length(parts[n]), :]
        size += length(parts[n])
    col_ref[...] = column(jnp.concatenate([cluster_line(refs[n], parts[n]) for n in stack], axis=1))
    best_ref[...] = jnp.full((size, 128), -1.0, F32)
    lines = {}
    for k in held + (stack if inner else []):
        near = [n for n in stack if needed(n, k)]
        low = min(at[n] for n in near)
        high = max(at[n] + length(parts[n]) for n in near)
        n_k = length(parts[k])
        sims = dot_nt(stack_ref[low:high, :], refs[k][0:n_k, :])
        keep = wide(col_ref[low:high, :], n_k) == cluster_line(refs[k], parts[k])
        if k in stack:
            keep = keep & (iota((high - low, n_k), 0) + (low - at[k]) != iota((high - low, n_k), 1))
        sims = jnp.where(keep, sims, -1.0)
        best = best_ref[low:high, :]
        for v in range(n_k // 128):
            best = jnp.maximum(best, sims[:, v * 128:(v + 1) * 128])
        best_ref[low:high, :] = best
        if k not in stack:
            lines[k] = jnp.max(sims, axis=0, keepdims=True)
    for n in stack:
        lines[n] = lined(best_ref[at[n]:at[n] + length(parts[n]), :])
    return lines


def product_kernel(stack, held, inner, parts, *refs):
    names = stack + held
    refs = list(refs)
    rows = {n: refs.pop(0) for n in names}
    outs = {n: refs.pop(0) for n in names}
    for n, line in cross(stack, held, inner, parts, rows, *refs).items():
        outs[n][...] = line


def lined(best):
    rows = best.shape[0]
    parts = [jnp.max(best[b * 128:(b + 1) * 128, :].T, axis=0, keepdims=True) for b in range(rows // 128)]
    return jnp.concatenate(parts, axis=1)


def final_kernel(dims, kinds, stack, held, parts, known, *refs):
    n_gx, n_gy, rows, quota = dims
    chunk = n_gy * quota
    refs = list(refs)
    row_refs = {n: refs.pop(0) for n in stack + held}
    lines = {}
    for n in known:
        line = refs.pop(0)[...]
        lines[n] = jnp.maximum(lines[n], line) if n in lines else line
    send_ref = refs.pop(0)
    for n, line in cross(stack, held, True, parts, row_refs, *refs).items():
        lines[n] = jnp.maximum(lines[n], line) if n in lines else line
    whole = {}
    for n in sorted(lines):
        at = 0
        for k, first, count in parts[n]:
            whole.setdefault((n[:-1], k), {})[first] = lines[n][:, at:at + count]
            at += count
    blocks = [jnp.full((n_gy, 128), -1.0, F32)] * len(kinds)
    own = lax.shift_right_logical(iota((n_gy, chunk), 1), log2(quota)) == iota((n_gy, chunk), 0)
    lane = lax.shift_right_logical(iota((n_gy, 128), 1), log2(quota))
    for (kind, k), found in sorted(whole.items()):
        line = jnp.concatenate([found[first] for first in sorted(found)], axis=1)
        held_here = jnp.where(own, line, 0.0)
        fold = held_here[:, 0:128]
        for v in range(1, chunk // 128):
            fold = fold + held_here[:, v * 128:(v + 1) * 128]
        shift = 64
        while shift >= quota:
            fold = fold + pltpu.roll(fold, shift, 1)
            shift //= 2
        at = kinds.index(kind)
        blocks[at] = jnp.where(lane == k, fold, blocks[at])
    everything = jnp.concatenate(blocks, axis=1)
    for d in range(n_gy):
        send_ref[d] = everything[d:d + 1, :]


def far_place(q, m):
    row = q // KEYS
    return q ^ (KEYS * m) ^ (1 if row < row ^ m else 0)


def finish_kernel(dims, home_ref, back_ref, out_ref):
    n_gx, n_gy, rows, quota = dims
    n_query = n_gy // KEYS

    def taken(place, block):
        return jnp.concatenate([back_ref[place(q)][:, block * 128:(block + 1) * 128] for q in range(n_gy)], axis=0)

    found = taken(lambda q: q, 0)
    for m in range(1, n_query):
        found = jnp.maximum(found, taken(lambda q, m=m: far_place(q, m), m))
    for t in (1, 2):
        found = jnp.maximum(found, taken(lambda q, t=t: q ^ t, n_query - 1 + t))
    high = found.astype(BF16)
    rest = found - high.astype(F32)
    mid = rest.astype(BF16)
    low = (rest - mid.astype(F32)).astype(BF16)
    here = one_hot(iota((128, rows), 0) == home_ref[1:2, :])
    value = dot_nn(jnp.concatenate([high.astype(F32), mid.astype(F32), low.astype(F32)], axis=0).astype(BF16), here)
    value = (value[0:n_gy] + value[n_gy:2 * n_gy]) + value[2 * n_gy:3 * n_gy]
    own = iota((n_gy, rows), 0) == home_ref[0:1, :]
    out_ref[...] = jnp.sum(jnp.where(own, value, 0.0), axis=0, keepdims=True)


def shape(dims, dtype):
    return jax.ShapeDtypeStruct(dims, dtype)


def per_device(embeddings, members, sizes):
    rows = members.shape[0]
    width = embeddings.shape[1]
    n_gx = lax.axis_size("gx")
    n_gy = lax.axis_size("gy")
    owners = n_gx * n_gy
    quota = rows // owners
    chunk = n_gy * quota
    n_query = n_gy // KEYS
    dims = (n_gx, n_gy, rows, quota)
    in_vmem = pl.BlockSpec(memory_space=pltpu.VMEM)

    in_hbm = pl.BlockSpec(memory_space=pltpu.HBM)
    asked, home = pl.pallas_call(
        functools.partial(request_kernel, dims),
        out_shape=(shape((owners, 1, quota), I32), shape((2, rows), I32)),
        in_specs=[in_hbm, in_hbm],
        out_specs=(in_vmem, in_vmem),
        scratch_shapes=[
            pltpu.SMEM(sizes.shape, I32),
            pltpu.VMEM((1, rows), I32),
            pltpu.SemaphoreType.DMA((2,)),
        ],
        compiler_params=params(56 * 1024 * 1024),
        name="request",
    )(sizes, members.reshape(1, rows))
    asked = lax.all_to_all(asked, ("gx", "gy"), split_axis=0, concat_axis=0, tiled=True)

    values = embeddings.astype(F32)
    squared = jnp.sum(values * values, axis=1, keepdims=True)
    unit = (values * lax.rsqrt(squared + 1e-06)).astype(BF16)

    full = [(k, 0, chunk) for k in range(n_gx)]
    if n_gx == 4:
        rest = [[(2, 0, chunk // 2)], [(2, chunk // 2, chunk // 2)]]
    else:
        rest = [full[2:-3], full[-3:-1]]
    stages = [[full[0]], [full[1]], [full[-1]]] + rest
    far = ["Y%d" % m for m in range(1, n_query)]
    parts = {kind + str(s): stage for s, stage in enumerate(stages) for kind in ["T", "N", "X"] + far}
    piece = {}
    lines = []

    def meet(*arrays):
        return lax.optimization_barrier(arrays)

    found = {}
    for wanted in [stages[1], stages[0], stages[2] + stages[3] + stages[4]]:
        out = pl.pallas_call(
            functools.partial(select_kernel, dims, wanted),
            out_shape=[shape((count + (SPARE if k else 1), width), BF16) for k, _, count in wanted],
            in_specs=[in_vmem, in_vmem],
            out_specs=[in_vmem] * len(wanted),
            cost_estimate=cost(2 * len(wanted) * chunk * rows * width, rows * width),
            compiler_params=params(),
            name="select",
        )(asked, unit)
        unit, *out = meet(unit, *out)
        found.update(zip(wanted, out))

    def across(part):
        step = part[0]
        return lax.ppermute(found[part], "gx", [(i, (i + step) % n_gx) for i in range(n_gx)])

    def swap(array, mask):
        return lax.ppermute(array, "gy", [(i, i ^ mask) for i in range(n_gy)])

    def pack(arrays, groups):
        out_parts = sum(groups, [])
        return pl.pallas_call(
            functools.partial(pack_kernel, [groups]),
            out_shape=shape((length(out_parts) + len(out_parts), width), BF16),
            in_specs=[in_vmem] * len(arrays),
            out_specs=in_vmem,
            cost_estimate=cost(0, 4 * length(out_parts) * width),
            compiler_params=params(),
            name="pack",
        )(*arrays)

    def land(s, arrays):
        name = "T" + str(s)
        piece[name] = pack(arrays, [[part] for part in stages[s]])
        return name

    def near(s):
        own = piece["T" + str(s)]
        piece["X" + str(s)] = swap(own, 2)
        for m, kind in enumerate(far):
            piece[kind + str(s)] = lax.ppermute(own, "gy", [(q, far_place(q, m + 1)) for q in range(n_gy)])

    def join(names, arrays):
        out = list(meet(*[piece[n] for n in names], *arrays, *[line for _, line in lines]))
        for n in names:
            piece[n] = out.pop(0)
        arrays = [out.pop(0) for _ in arrays]
        lines[:] = [(n, out.pop(0)) for n, _ in lines]
        return arrays

    def scratch(stack):
        rows_in = sum(length(parts[n]) for n in stack)
        return [pltpu.VMEM((rows_in, width), BF16), pltpu.VMEM((rows_in, 128), F32), pltpu.VMEM((rows_in, 128), F32)]

    def products(stack, held, inner=True, weight=0.0):
        names = stack + held
        flops = 2 * width * sum(length(parts[n]) for n in stack) * sum(length(parts[n]) for n in names)
        out = pl.pallas_call(
            functools.partial(product_kernel, stack, held, inner, parts),
            out_shape=[shape((1, length(parts[n])), F32) for n in names],
            in_specs=[in_vmem] * len(names),
            out_specs=[in_vmem] * len(names),
            scratch_shapes=scratch(stack),
            cost_estimate=cost(int(weight * flops), 0),
            compiler_params=params(),
            name="products",
        )(*[piece[n] for n in names])
        lines.extend(zip(names, out))

    def kinds(letters, *numbers):
        out = []
        for n in numbers:
            for letter in letters:
                out += [kind + str(n) for kind in (far if letter == "Y" else [letter])]
        return out

    z1 = [across(part) for part in stages[1]]
    z2 = [across(part) for part in stages[2]]
    piece["T0"] = found[full[0]]
    near(0)
    piece["N0"] = swap(piece["T0"], 1)
    late = stages[3] + stages[4]
    *z1, = join(kinds("TNXY", 0), z1 + [found[part] for part in late])
    for part, array in zip(late, z1[1:]):
        found[part] = array
    z3 = [across(part) for part in stages[3]]
    z4 = [across(part) for part in stages[4]]
    land(1, z1[:1])
    near(1)
    piece["N1"] = swap(piece["T1"], 1)
    products(kinds("NY", 0) + ["T0", "T1", "X0"], [])
    z2 = join(kinds("TNXY", 1), z2)
    land(2, z2)
    near(2)
    products(kinds("NY", 1) + ["T2", "X1"], kinds("TNXY", 0) + ["T1"])
    z3 = join([], z3)
    land(3, z3)
    near(3)
    products(["T3"], kinds("TNXY", 0, 1) + ["T2"])
    products(kinds("YX", 2), kinds("TNXY", 0, 1) + ["T2", "T3"])
    z4 = join(["T2", "T3"], z4)
    land(4, z4)
    near(4)
    group = ["T2", "T3", "T4"]
    both = swap(pack([piece[n] for n in group], [parts[n] for n in group]), 1)
    cores = ["N2", "N3", "N4"]
    out = pl.pallas_call(
        functools.partial(split_kernel, [parts[n] for n in cores]),
        out_shape=[shape((length(parts[n]) + len(parts[n]), width), BF16) for n in cores],
        in_specs=[in_vmem],
        out_specs=[in_vmem] * len(cores),
        cost_estimate=cost(0, 0),
        compiler_params=params(),
        name="split",
    )(both)
    piece.update(zip(cores, out))
    products(kinds("Y", 3) + ["T4", "X3"], kinds("TNXY", 0, 1) + kinds("TXY", 2) + ["T3"], weight=WEIGHT)
    products(cores, kinds("XY", 0, 1, 2, 3) + ["T2", "T3", "T4"], inner=False)
    join(kinds("TNXY", 4), [])
    stack = kinds("YX", 4)
    held = kinds("XY", 0, 1, 2, 3) + ["T4", "N4"]
    shown = ["T"] + far + ["N", "X"]
    names = stack + held
    send = pl.pallas_call(
        functools.partial(final_kernel, dims, shown, stack, held, parts, [n for n, _ in lines]),
        out_shape=shape((n_gy, 1, len(shown) * 128), F32),
        in_specs=[in_vmem] * (len(names) + len(lines)),
        out_specs=in_vmem,
        scratch_shapes=scratch(stack),
        cost_estimate=cost(2 * width * chunk * 8 * chunk, 0),
        compiler_params=params(),
        name="final",
    )(*[piece[n] for n in names], *[line for _, line in lines])

    back = lax.all_to_all(send, "gy", split_axis=0, concat_axis=0, tiled=True)
    out = pl.pallas_call(
        functools.partial(finish_kernel, dims),
        out_shape=shape((1, rows), F32),
        in_specs=[in_vmem, in_vmem],
        out_specs=in_vmem,
        compiler_params=params(),
        name="finish",
    )(home, back)
    return out.reshape(rows)


def solution(mesh):
    return jax.shard_map(
        per_device,
        mesh=mesh,
        in_specs=(P(("gx", "gy"), None), P(("gx", "gy")), P("gx", None)),
        out_specs=P(("gx", "gy")),
        check_vma=False,
    )
```

time: 182 us -> 75.4 us (0.41)
  waiting for transfers between devices: 107 us -> 28.6 us
  Pallas kernels: 0 us -> 19.6 us
  local copies, waits for them, and re-layouts: 18.2 us -> 0.01 us
  matrix products: 18 us -> 0 us
  between operations: 16 us -> 0.19 us
  other arithmetic: 12.1 us -> 2.11 us
  blocking collectives: 0 us -> 7.74 us
  starting transfers between devices: 10 us -> 16.9 us
    all_gather x1 -> x0, waiting for transfers between devices: 67.5 us -> none  [per_device(): piece = lax.all_gather(tile, 'gy', axis=0, tiled=True)]
    all_to_all x2 -> x1, waiting for transfers between devices: 39.8 us -> 5.01 us  [per_device(): lax.all_to_all(asked, ('gx', 'gy'), split_axis=0, concat_axis=0, tiled=True)]
    ppermute x0 -> x17, waiting for transfers between devices: none -> 23.6 us  [the longest x8 9.28 us: swap(): return lax.ppermute(array, 'gy', [(i, i ^ mask) for i in range(n_gy)])]
    pallas_call x0 -> x18, Pallas kernels: none -> 19.6 us  [the longest x6 12.2 us: products(): pl.pallas_call(functools.partial(product_kernel, stack, held, inner, part...]
    dot_general x1 -> x0, matrix products: 18 us -> none  [similar(): lax.dot_general(left, right, (((1,), (1,)), ((), ())), preferred_element_...]
    gather x4 -> x0, local copies, waits for them, and re-layouts: 16.2 us -> none  [the longest x2 5.8 us: per_device(): wanted = members[order] % rows_dev]
    ppermute x0 -> x17, starting transfers between devices: none -> 9.63 us  [the longest x8 4.81 us: swap(): return lax.ppermute(array, 'gy', [(i, i ^ mask) for i in range(n_gy)])]
    sort x2 -> x0, other arithmetic: 9.54 us -> none  [the longest x1 5.17 us: per_device(): order = jnp.argsort(members)]
  transfers between devices with their start and end apart: 3 -> 18, of which waited for: 3 -> 12; matrix products, arithmetic and copies ran while one was open for 3% -> 3% of each run, Pallas kernels for 0% -> 20%
where the time goes in v8:
time: 75.4 us; the launch traced here: 75.2 us
  waiting for transfers between devices  28.6 us (38%)
  Pallas kernels  19.6 us (26%)
  starting transfers between devices  16.9 us (22%)
  blocking collectives  7.74 us (10%)
  other arithmetic  2.11 us (3%)
    pallas_call x6, Pallas kernels, products(): pl.pallas_call(functools.partial(product_kernel, stack, held, inner, part...  12.2 us
    ppermute x8, waiting for transfers between devices, swap(): return lax.ppermute(array, 'gy', [(i, i ^ mask) for i in range(n_gy)])  9.28 us
    ppermute x5, waiting for transfers between devices, near(): lax.ppermute(own, 'gy', [(q, far_place(q, m + 1)) for q in range(n_gy)])  8.65 us
    all_to_all x1, blocking collectives, per_device(): back = lax.all_to_all(send, 'gy', split_axis=0, concat_axis=0, tiled=True)  7.74 us
    all_to_all x1, starting transfers between devices, per_device(): lax.all_to_all(asked, ('gx', 'gy'), split_axis=0, concat_axis=0, tiled=True)  7.3 us
    ppermute x4, waiting for transfers between devices, across(): lax.ppermute(found[part], 'gx', [(i, (i + step) % n_gx) for i in range(n_...  5.65 us
    all_to_all x1, waiting for transfers between devices, per_device(): lax.all_to_all(asked, ('gx', 'gy'), split_axis=0, concat_axis=0, tiled=True)  5.01 us
    ppermute x8, starting transfers between devices, swap(): return lax.ppermute(array, 'gy', [(i, i ^ mask) for i in range(n_gy)])  4.81 us
  transfers between devices with their start and end apart: 18, of which 12 were waited for; matrix products, arithmetic and copies ran while one was open for 3% of the time, Pallas kernels for 20%

profile of v8, /device:TPU:0, one launch (start us, length us, event | category | flops | bytes accessed | tf_op | source)
XLA Modules:
  0.0 75.2 jit_solution(17274187978391236776)
XLA Ops:
  0.0 0.0 copy-start.1
  0.0 1.8 %request.1 = (s32[32,1,32]{2,1,0:T(1,128)}, s32[2,1024]{1,0:T(2,128)}) custom-call(s32[1,25]{1,0:T(1,128)} %sizes_hbm.1, s32[1,1024]{1,0:T(1,128)} %bitcast.2), custom_call_target="tpu_custom_call" | custom-call | tf_op jit(solution)/shard_map/request/pallas_call | solution.py:321
  1.8 7.3 %all-to-all-start = ((s32[32,1,32]{2,1,0:T(1,128)}), s32[32,1,32]{2,1,0:T(1,128)S(1)}, u32[]{:S(2)}, u32[]{:S(2)}) async-start(s32[32,1,32]{2,1,0:T(1,128)} %get-tuple-element.226), calls=%async_computation | async-start | bytes 32768 | tf_op jit(solution)/shard_map/all_to_all | solution.py:334
  9.1 1.8 %fusion = f32[1024]{0:T(1024)S(1)} fusion(bf16[1024,768]{1,0:T(8,128)(2,1)} %param.3), kind=kLoop, calls=%fused_computation.2 | loop fusion | flops 2358272 | bytes 1576960 | tf_op jit(solution)/shard_map/reduce_sum | solution.py:337
  10.9 0.0 copy-done.1
  11.0 0.3 fusion.1.unit_ref
  11.3 5.0 %all-to-all-done.asked_ref = s32[32,1,32]{2,1,0:T(1,128)S(1)} async-done(((s32[32,1,32]{2,1,0:T(1,128)}), s32[32,1,32]{2,1,0:T(1,128)S(1)}, u32[]{:S(2)}, u32[]{:S(2)}) %all-to-all-start) | async-done | bytes 4128 | tf_op jit(solution)/shard_map/all_to_all | solution.py:334
  16.3 0.8 %select.3 = bf16[264,768]{1,0:T(8,128)(2,1)S(1)} custom-call(s32[32,1,32]{2,1,0:T(1,128)S(1)} %all-to-all-done.asked_ref, bf16[1024,768]{1,0:T(8,128)(2,1)S(1)} %fusion.1.unit_ref), custom_call_target="tpu_custom_call" | custom-call | flops 402653184 | bytes 786432 | tf_op jit(solution)/shard_map/select/pallas_call | solution.py:356
  17.1 0.6 collective-permute-start.3
  17.8 0.8 %select.4.refs_2_.refs_4_.refs_1_.refs_3_ = bf16[257,768]{1,0:T(8,128)(2,1)S(1)} custom-call(s32[32,1,32]{2,1,0:T(1,128)S(1)} %all-to-all-done.asked_ref, bf16[1024,768]{1,0:T(8,128)(2,1)S(1)} %fusion.1.unit_ref), custom_call_target="tpu_custom_call" | custom-call | flops 402653184 | bytes 786432 | tf_op jit(solution)/shard_map/select/pallas_call | solution.py:356
  18.6 0.1 collective-permute-start.2
  18.7 0.6 collective-permute-start.1
  19.3 0.4 collective-permute-start
  19.7 1.4 %select.5 = (bf16[264,768]{1,0:T(8,128)(2,1)S(1)}, bf16[136,768]{1,0:T(8,128)(2,1)S(1)}, bf16[136,768]{1,0:T(8,128)(2,1)S(1)}) custom-call(s32[32,1,32]{2,1,0:T(1,128)S(1)} %all-to-all-done.asked_ref, bf16[1024,768]{1,0:T(8,128)(2,1)S(1)} %fusion.1.unit_ref), custom_call_target="tpu_custom_call" | custom-call | flops 1207959552 | bytes 786432 | tf_op jit(solution)/shard_map/select/pallas_call | solution.py:356
  21.1 3.3 %collective-permute-start.7 = (bf16[264,768]{1,0:T(8,128)(2,1)S(1)}, bf16[264,768]{1,0:T(8,128)(2,1)S(1)}, u32[]{:S(2)}, u32[]{:S(2)}) collective-permute-start(bf16[264,768]{1,0:T(8,128)(2,1)S(1)} %get-tuple-element.237), channel_id=1, source_target_pairs={{0,24},{8,0},{16,8},{24,16},{1,25},{9,1},{17,9},{25,17},{2,26},{10... | collective-permute-start | bytes 1216520 | tf_op jit(solution)/shard_map/ppermute | solution.py:370
  24.4 5.0 %collective-permute-done.2.refs_1_.refs_7_.refs_4_.refs_5_.refs_6_.refs_3_ = bf16[257,768]{1,0:T(8,128)(2,1)S(1)} collective-permute-done((bf16[257,768]{1,0:T(8,128)(2,1)S(1)}, bf16[257,768]{1,0:T(8,128)(2,1)S(1)}, u32[]{:S(2)}, u32[]{:S(2)}) %collective-permute-start.2) | collective-permute-done | bytes 394784 | tf_op jit(solution)/shard_map/ppermute | solution.py:396
  29.4 1.2 %collective-permute-done.1.refs_4_.refs_6_.refs_3_.refs_5_.refs_2_ = bf16[257,768]{1,0:T(8,128)(2,1)S(1)} collective-permute-done((bf16[257,768]{1,0:T(8,128)(2,1)S(1)}, bf16[257,768]{1,0:T(8,128)(2,1)S(1)}, u32[]{:S(2)}, u32[]{:S(2)}) %collective-permute-start.1) | collective-permute-done | bytes 394784 | tf_op jit(solution)/shard_map/ppermute | solution.py:373
  30.6 0.0 collective-permute-done.refs_0_.refs_5_.refs_2_.refs_3_.refs_4_
  30.6 0.7 collective-permute-done.3.refs_0_
  31.3 0.1 collective-permute-start.6
  31.4 0.6 collective-permute-start.5
  32.0 0.4 collective-permute-start.4
  32.4 0.0 collective-permute-start.8
  32.4 2.4 %products.6 = (f32[1,256]{1,0:T(1,128)S(1)}, f32[1,256]{1,0:T(1,128)S(1)}, f32[1,256]{1,0:T(1,128)S(1)}, f32[1,256]{1,0:T(1,128)S(1)}, f32[1,256]{1,0:T(1,128)S(1)}) custom-call(bf16[257,768]{1,0:T(8,128)(2,1)S(1)} %collective-permute-done.refs_0_.refs_5_.refs_2_.refs_3_.refs_4_, ...), custom_call_target="tpu_custom_call" | custom-call | tf_op jit(solution)/shard_map/products/pallas_call | solution.py:413
  34.8 4.0 %collective-permute-done.7.refs_0_ = bf16[264,768]{1,0:T(8,128)(2,1)S(1)} collective-permute-done((bf16[264,768]{1,0:T(8,128)(2,1)S(1)}, bf16[264,768]{1,0:T(8,128)(2,1)S(1)}, u32[]{:S(2)}, u32[]{:S(2)}) %collective-permute-start.7) | collective-permute-done | bytes 405536 | tf_op jit(solution)/shard_map/ppermute | solution.py:370
  38.8 3.0 %collective-permute-done.6.refs_1_.refs_8_.refs_9_.refs_10_.refs_6_.refs_5_ = bf16[257,768]{1,0:T(8,128)(2,1)S(1)} collective-permute-done((bf16[257,768]{1,0:T(8,128)(2,1)S(1)}, bf16[257,768]{1,0:T(8,128)(2,1)S(1)}, u32[]{:S(2)}, u32[]{:S(2)}) %collective-permute-start.6) | collective-permute-done | bytes 394784 | tf_op jit(solution)/shard_map/ppermute | solution.py:396
  41.8 1.5 %collective-permute-done.5.refs_3_.refs_7_.refs_8_.refs_9_.refs_5_.refs_4_ = bf16[257,768]{1,0:T(8,128)(2,1)S(1)} collective-permute-done((bf16[257,768]{1,0:T(8,128)(2,1)S(1)}, bf16[257,768]{1,0:T(8,128)(2,1)S(1)}, u32[]{:S(2)}, u32[]{:S(2)}) %collective-permute-start.5) | collective-permute-done | bytes 394784 | tf_op jit(solution)/shard_map/ppermute | solution.py:373
  43.3 0.0 collective-permute-done.4.refs_0_.refs_6_.refs_7_.refs_8_
  43.4 0.7 collective-permute-start.11
  44.0 0.0 collective-permute-start.10
  44.1 0.0 collective-permute-start.9
  44.1 2.8 %products.7 = (f32[1,256]{1,0:T(1,128)S(1)}, f32[1,256]{1,0:T(1,128)S(1)}, f32[1,256]{1,0:T(1,128)S(1)}, f32[1,256]{1,0:T(1,128)S(1)}, f32[1,256]{1,0:T(1,128)S(...) custom-call(bf16[257,768]{1,0:T(8,128)(2,1)S(1)} %collective-permute-done.4.refs_, ...), custom_call_target="tpu_custom_call" | custom-call | tf_op jit(solution)/shard_map/products/pallas_call | solution.py:413
  46.8 1.0 %collective-permute-done.8.refs_0_ = bf16[136,768]{1,0:T(8,128)(2,1)S(1)} collective-permute-done((bf16[136,768]{1,0:T(8,128)(2,1)S(1)}, bf16[136,768]{1,0:T(8,128)(2,1)S(1)}, u32[]{:S(2)}, u32[]{:S(2)}) %collective-permute-start.8) | collective-permute-done | bytes 208928 | tf_op jit(solution)/shard_map/ppermute | solution.py:370
  47.8 0.6 collective-permute-start.16
  48.4 0.5 collective-permute-start.15
  48.9 1.4 %products.8 = (f32[1,128]{1,0:T(1,128)S(1)}, f32[1,256]{1,0:T(1,128)S(1)}, f32[1,256]{1,0:T(1,128)S(1)}, f32[1,256]{1,0:T(1,128)S(1)}, f32[1,256]{1,0:T(1,128)S(...) custom-call(bf16[129,768]{1,0:T(8,128)(2,1)S(1)} %pack.7.refs_0_.ref, ...), custom_call_target="tpu_custom_call" | custom-call | tf_op jit(solution)/shard_map/products/pallas_call | solution.py:413
  50.4 5.3 %collective-permute-done.11.refs_1_.refs_12_.refs_7_.refs_6_ = bf16[257,768]{1,0:T(8,128)(2,1)S(1)} collective-permute-done((bf16[257,768]{1,0:T(8,128)(2,1)S(1)}, bf16[257,768]{1,0:T(8,128)(2,1)S(1)}, u32[]{:S(2)}, u32[]{:S(2)}) %collective-permute-start.11) | collective-permute-done | bytes 394784 | tf_op jit(solution)/shard_map/ppermute | solution.py:373
  55.7 0.7 collective-permute-done.10.refs_0_.refs_13_.refs_8_.refs_7_
  56.4 1.8 %products.9 = (f32[1,256]{1,0:T(1,128)S(1)}, f32[1,256]{1,0:T(1,128)S(1)}, f32[1,256]{1,0:T(1,128)S(1)}, f32[1,256]{1,0:T(1,128)S(1)}, f32[1,256]{1,0:T(1,128)S(...) custom-call(bf16[257,768]{1,0:T(8,128)(2,1)S(1)} %collective-permute, ...), custom_call_target="tpu_custom_call" | custom-call | tf_op jit(solution)/shard_map/products/pallas_call | solution.py:413
  58.1 0.0 collective-permute-done.9.refs_0_
  58.2 0.2 collective-permute-start.14
  58.4 1.5 %collective-permute-start.13 = (bf16[129,768]{1,0:T(8,128)(2,1)S(1)}, bf16[129,768]{1,0:T(8,128)(2,1)S(1)}, u32[]{:S(2)}, u32[]{:S(2)}) collective-permute-start(bf16[129,768]{1,0:T(8,128)(2,1)S(1)} %pack.8.refs_2_.refs_1_.refs_13_.refs_10_), channel_id=1, source_target_pairs={{0,2},{1,3},{2,0},{3,1},{4,6},{5,7},{6,4},{7,5},{8,10},{9,11},{10,... | collective-permute-start | bytes 594440 | tf_op jit(solution)/shard_map/ppermute | solution.py:373
  59.9 0.1 pack.9
  60.0 0.1 collective-permute-start.12
  60.0 0.0 collective-permute-done.16.refs_2_.refs_9_.refs_8_
  60.0 0.0 collective-permute-done.15.refs_0_.refs_10_.refs_9_
  60.1 2.0 %products.10 = (f32[1,128]{1,0:T(1,128)S(1)}, f32[1,128]{1,0:T(1,128)S(1)}, f32[1,128]{1,0:T(1,128)S(1)}, f32[1,256]{1,0:T(1,128)S(1)}, f32[1,256]{1,0:T(1,128)S...) custom-call(bf16[129,768]{1,0:T(8,128)(2,1)S(1)} %collective-permute, ...), custom_call_target="tpu_custom_call" | custom-call | flops 39258685440 | tf_op jit(solution)/shard_map/products/pallas_call | solution.py:413
  62.0 0.3 collective-permute-done.12.ref
  62.3 0.1 split.1
  62.4 1.9 %products.11 = (f32[1,256]{1,0:T(1,128)S(1)}, f32[1,128]{1,0:T(1,128)S(1)}, f32[1,128]{1,0:T(1,128)S(1)}, f32[1,256]{1,0:T(1,128)S(1)}, f32[1,256]{1,0:T(1,128)S...) custom-call(bf16[257,768]{1,0:T(8,128)(2,1)S(1)} %get-tuple-element., ...), custom_call_target="tpu_custom_call" | custom-call | tf_op jit(solution)/shard_map/products/pallas_call | solution.py:413
  64.2 0.0 collective-permute-done.14.refs_0_
  64.3 0.9 %collective-permute-done.13.refs_1_ = bf16[129,768]{1,0:T(8,128)(2,1)S(1)} collective-permute-done((bf16[129,768]{1,0:T(8,128)(2,1)S(1)}, bf16[129,768]{1,0:T(8,128)(2,1)S(1)}, u32[]{:S(2)}, u32[]{:S(2)}) %collective-permute-start.13) | collective-permute-done | bytes 198176 | tf_op jit(solution)/shard_map/ppermute | solution.py:373
  65.2 0.0 copy-start
  65.2 1.5 %final.1 = f32[8,1,512]{2,1,0:T(1,128)S(1)} custom-call(bf16[129,768]{1,0:T(8,128)(2,1)S(1)} %collective-permute-done.14.refs_0_, bf16[129,768]{1,0:T(8,128)(2,1)S(1)} %collective-permute-done.13.refs_1_, bf16[257,768]{1,0:T(8,128)(2,1)S(1)} %collective-permute-done.1.refs_4_.refs_6_.refs_3_.refs_5_.refs_2_, ...), custom_call_target="tpu_custom_call" | custom-call | flops 805306368 | tf_op jit(solution)/shard_map/final/pallas_call | solution.py:479
  66.7 7.7 %all_to_all.10.back_ref = f32[8,1,512]{2,1,0:T(1,128)S(1)} all-to-all(f32[8,1,512]{2,1,0:T(1,128)S(1)} %final.1), channel_id=1, replica_groups=mesh['gx'=4,'gy'=8] {'gy'}, dimensions={0} | all-to-all | bytes 32768 | tf_op jit(solution)/shard_map/all_to_all | solution.py:490
  74.4 0.0 copy-done
  74.4 0.8 %finish.1 = f32[1,1024]{1,0:T(1,128)} custom-call(s32[2,1024]{1,0:T(2,128)S(1)} %copy-done, f32[8,1,512]{2,1,0:T(1,128)S(1)} %all_to_all.10.back_ref), custom_call_target="tpu_custom_call" | custom-call | tf_op jit(solution)/shard_map/finish/pallas_call | solution.py:491
  (5 shorter events, 0.1 us)
Async XLA Ops:
  0.0 10.9 %copy-start.1 = (bf16[1024,768]{1,0:T(8,128)(2,1)S(1)}, bf16[1024,768]{1,0:T(8,128)(2,1)}, u32[]{:S(2)}) copy-start(bf16[1024,768]{1,0:T(8,128)(2,1)} %param.3) | copy-start | bytes 4718596
  1.8 14.5 %all-to-all-start = ((s32[32,1,32]{2,1,0:T(1,128)}), s32[32,1,32]{2,1,0:T(1,128)S(1)}, u32[]{:S(2)}, u32[]{:S(2)}) async-start(s32[32,1,32]{2,1,0:T(1,128)} %get-tuple-element.226), calls=%async_computation | async-start | bytes 32768 | tf_op jit(solution)/shard_map/all_to_all | solution.py:334
  17.1 14.2 %collective-permute-start.3 = (bf16[264,768]{1,0:T(8,128)(2,1)S(1)}, bf16[264,768]{1,0:T(8,128)(2,1)S(1)}, u32[]{:S(2)}, u32[]{:S(2)}) collective-permute-start(bf16[264,768]{1,0:T(8,128)(2,1)S(1)} %select.3), channel_id=1, source_target_pairs={{0,8},{8,16},{16,24},{24,0},{1,9},{9,17},{17,25},{25,1},{2,10},{10... | collective-permute-start | bytes 1216520 | tf_op jit(solution)/shard_map/ppermute | solution.py:370
  18.6 10.8 %collective-permute-start.2 = (bf16[257,768]{1,0:T(8,128)(2,1)S(1)}, bf16[257,768]{1,0:T(8,128)(2,1)S(1)}, u32[]{:S(2)}, u32[]{:S(2)}) collective-permute-start(bf16[257,768]{1,0:T(8,128)(2,1)S(1)} %select.4.refs_2_.refs_4_.refs_1_.refs_3_), channel_id=1, source_target_pairs={{0,5},{1,4},{2,7},{3,6},{4,0},{5,1},{6,2},{7,3},{8,13},{9,12},{10,... | collective-permute-start | bytes 1184264 | tf_op jit(solution)/shard_map/ppermute | solution.py:396
  18.7 11.9 %collective-permute-start.1 = (bf16[257,768]{1,0:T(8,128)(2,1)S(1)}, bf16[257,768]{1,0:T(8,128)(2,1)S(1)}, u32[]{:S(2)}, u32[]{:S(2)}) collective-permute-start(bf16[257,768]{1,0:T(8,128)(2,1)S(1)} %select.4.refs_2_.refs_4_.refs_1_.refs_3_), channel_id=1, source_target_pairs={{0,2},{1,3},{2,0},{3,1},{4,6},{5,7},{6,4},{7,5},{8,10},{9,11},{10,... | collective-permute-start | bytes 1184264 | tf_op jit(solution)/shard_map/ppermute | solution.py:373
  19.3 11.3 %collective-permute-start = (bf16[257,768]{1,0:T(8,128)(2,1)S(1)}, bf16[257,768]{1,0:T(8,128)(2,1)S(1)}, u32[]{:S(2)}, u32[]{:S(2)}) collective-permute-start(bf16[257,768]{1,0:T(8,128)(2,1)S(1)} %select.4.refs_2_.refs_4_.refs_1_.refs_3_), channel_id=1, source_target_pairs={{0,1},{1,0},{2,3},{3,2},{4,5},{5,4},{6,7},{7,6},{8,9},{9,8},{10,11... | collective-permute-start | bytes 1184264 | tf_op jit(solution)/shard_map/ppermute | solution.py:373
  21.1 17.8 %collective-permute-start.7 = (bf16[264,768]{1,0:T(8,128)(2,1)S(1)}, bf16[264,768]{1,0:T(8,128)(2,1)S(1)}, u32[]{:S(2)}, u32[]{:S(2)}) collective-permute-start(bf16[264,768]{1,0:T(8,128)(2,1)S(1)} %get-tuple-element.237), channel_id=1, source_target_pairs={{0,24},{8,0},{16,8},{24,16},{1,25},{9,1},{17,9},{25,17},{2,26},{10... | collective-permute-start | bytes 1216520 | tf_op jit(solution)/shard_map/ppermute | solution.py:370
  31.3 10.5 %collective-permute-start.6 = (bf16[257,768]{1,0:T(8,128)(2,1)S(1)}, bf16[257,768]{1,0:T(8,128)(2,1)S(1)}, u32[]{:S(2)}, u32[]{:S(2)}) collective-permute-start(bf16[257,768]{1,0:T(8,128)(2,1)S(1)} %pack.5.refs_3_.refs_8_.refs_5_.refs_6_.refs_7_), channel_id=1, source_target_pairs={{0,5},{1,4},{2,7},{3,6},{4,0},{5,1},{6,2},{7,3},{8,13},{9,12},{10,... | collective-permute-start | bytes 1184264 | tf_op jit(solution)/shard_map/ppermute | solution.py:396
  31.4 11.9 %collective-permute-start.5 = (bf16[257,768]{1,0:T(8,128)(2,1)S(1)}, bf16[257,768]{1,0:T(8,128)(2,1)S(1)}, u32[]{:S(2)}, u32[]{:S(2)}) collective-permute-start(bf16[257,768]{1,0:T(8,128)(2,1)S(1)} %pack.5.refs_3_.refs_8_.refs_5_.refs_6_.refs_7_), channel_id=1, source_target_pairs={{0,2},{1,3},{2,0},{3,1},{4,6},{5,7},{6,4},{7,5},{8,10},{9,11},{10,... | collective-permute-start | bytes 1184264 | tf_op jit(solution)/shard_map/ppermute | solution.py:373
  32.0 11.4 %collective-permute-start.4 = (bf16[257,768]{1,0:T(8,128)(2,1)S(1)}, bf16[257,768]{1,0:T(8,128)(2,1)S(1)}, u32[]{:S(2)}, u32[]{:S(2)}) collective-permute-start(bf16[257,768]{1,0:T(8,128)(2,1)S(1)} %pack.5.refs_3_.refs_8_.refs_5_.refs_6_.refs_7_), channel_id=1, source_target_pairs={{0,1},{1,0},{2,3},{3,2},{4,5},{5,4},{6,7},{7,6},{8,9},{9,8},{10,11... | collective-permute-start | bytes 1184264 | tf_op jit(solution)/shard_map/ppermute | solution.py:373
  32.4 15.4 %collective-permute-start.8 = (bf16[136,768]{1,0:T(8,128)(2,1)S(1)}, bf16[136,768]{1,0:T(8,128)(2,1)S(1)}, u32[]{:S(2)}, u32[]{:S(2)}) collective-permute-start(bf16[136,768]{1,0:T(8,128)(2,1)S(1)} %get-tuple-element.248), channel_id=1, source_target_pairs={{0,16},{8,24},{16,0},{24,8},{1,17},{9,25},{17,1},{25,9},{2,18},{10... | collective-permute-start | bytes 626696 | tf_op jit(solution)/shard_map/ppermute | solution.py:370
  43.4 12.3 %collective-permute-start.11 = (bf16[257,768]{1,0:T(8,128)(2,1)S(1)}, bf16[257,768]{1,0:T(8,128)(2,1)S(1)}, u32[]{:S(2)}, u32[]{:S(2)}) collective-permute-start(bf16[257,768]{1,0:T(8,128)(2,1)S(1)} %pack.6.refs_2_.refs_9_.refs_10_.refs_0_.refs_11_), channel_id=1, source_target_pairs={{0,2},{1,3},{2,0},{3,1},{4,6},{5,7},{6,4},{7,5},{8,10},{9,11},{10,... | collective-permute-start | bytes 1184264 | tf_op jit(solution)/shard_map/ppermute | solution.py:373
  44.0 12.3 %collective-permute-start.10 = (bf16[257,768]{1,0:T(8,128)(2,1)S(1)}, bf16[257,768]{1,0:T(8,128)(2,1)S(1)}, u32[]{:S(2)}, u32[]{:S(2)}) collective-permute-start(bf16[257,768]{1,0:T(8,128)(2,1)S(1)} %pack.6.refs_2_.refs_9_.refs_10_.refs_0_.refs_11_), channel_id=1, source_target_pairs={{0,5},{1,4},{2,7},{3,6},{4,0},{5,1},{6,2},{7,3},{8,13},{9,12},{10,... | collective-permute-start | bytes 1184264 | tf_op jit(solution)/shard_map/ppermute | solution.py:396
  44.1 14.1 %collective-permute-start.9 = (bf16[136,768]{1,0:T(8,128)(2,1)S(1)}, bf16[136,768]{1,0:T(8,128)(2,1)S(1)}, u32[]{:S(2)}, u32[]{:S(2)}) collective-permute-start(bf16[136,768]{1,0:T(8,128)(2,1)S(1)} %get-tuple-element.268), channel_id=1, source_target_pairs={{0,16},{8,24},{16,0},{24,8},{1,17},{9,25},{17,1},{25,9},{2,18},{10... | collective-permute-start | bytes 626696 | tf_op jit(solution)/shard_map/ppermute | solution.py:370
  47.8 12.2 %collective-permute-start.16 = (bf16[129,768]{1,0:T(8,128)(2,1)S(1)}, bf16[129,768]{1,0:T(8,128)(2,1)S(1)}, u32[]{:S(2)}, u32[]{:S(2)}) collective-permute-start(bf16[129,768]{1,0:T(8,128)(2,1)S(1)} %pack.7.refs_0_.refs_11_.refs_1_.refs_14_.refs_12_), channel_id=1, source_target_pairs={{0,2},{1,3},{2,0},{3,1},{4,6},{5,7},{6,4},{7,5},{8,10},{9,11},{10,... | collective-permute-start | bytes 594440 | tf_op jit(solution)/shard_map/ppermute | solution.py:373
  48.4 11.6 %collective-permute-start.15 = (bf16[129,768]{1,0:T(8,128)(2,1)S(1)}, bf16[129,768]{1,0:T(8,128)(2,1)S(1)}, u32[]{:S(2)}, u32[]{:S(2)}) collective-permute-start(bf16[129,768]{1,0:T(8,128)(2,1)S(1)} %pack.7.refs_0_.refs_11_.refs_1_.refs_14_.refs_12_), channel_id=1, source_target_pairs={{0,5},{1,4},{2,7},{3,6},{4,0},{5,1},{6,2},{7,3},{8,13},{9,12},{10,... | collective-permute-start | bytes 594440 | tf_op jit(solution)/shard_map/ppermute | solution.py:396
  58.2 6.1 %collective-permute-start.14 = (bf16[129,768]{1,0:T(8,128)(2,1)S(1)}, bf16[129,768]{1,0:T(8,128)(2,1)S(1)}, u32[]{:S(2)}, u32[]{:S(2)}) collective-permute-start(bf16[129,768]{1,0:T(8,128)(2,1)S(1)} %pack.8.refs_2_.refs_1_.refs_13_.refs_10_), channel_id=1, source_target_pairs={{0,5},{1,4},{2,7},{3,6},{4,0},{5,1},{6,2},{7,3},{8,13},{9,12},{10,... | collective-permute-start | bytes 594440 | tf_op jit(solution)/shard_map/ppermute | solution.py:396
  58.4 6.7 %collective-permute-start.13 = (bf16[129,768]{1,0:T(8,128)(2,1)S(1)}, bf16[129,768]{1,0:T(8,128)(2,1)S(1)}, u32[]{:S(2)}, u32[]{:S(2)}) collective-permute-start(bf16[129,768]{1,0:T(8,128)(2,1)S(1)} %pack.8.refs_2_.refs_1_.refs_13_.refs_10_), channel_id=1, source_target_pairs={{0,2},{1,3},{2,0},{3,1},{4,6},{5,7},{6,4},{7,5},{8,10},{9,11},{10,... | collective-permute-start | bytes 594440 | tf_op jit(solution)/shard_map/ppermute | solution.py:373
  60.0 2.4 %collective-permute-start.12 = (bf16[515,768]{1,0:T(8,128)(2,1)S(1)}, bf16[515,768]{1,0:T(8,128)(2,1)S(1)}, u32[]{:S(2)}, u32[]{:S(2)}) collective-permute-start(bf16[515,768]{1,0:T(8,128)(2,1)S(1)} %pack.9), channel_id=1, source_target_pairs={{0,1},{1,0},{2,3},{3,2},{4,5},{5,4},{6,7},{7,6},{8,9},{9,8},{10,11... | collective-permute-start | bytes 2373128 | tf_op jit(solution)/shard_map/ppermute | solution.py:373
  65.2 9.3 %copy-start = (s32[2,1024]{1,0:T(2,128)S(1)}, s32[2,1024]{1,0:T(2,128)}, u32[]{:S(2)}) copy-start(s32[2,1024]{1,0:T(2,128)} %get-tuple-element.225.home_ref) | copy-start | bytes 24580

commit v9 on v8

--- a/solution.py
+++ b/solution.py
@@ -444,7 +444,7 @@
     near(1)
     piece["N1"] = swap(piece["T1"], 1)
     products(kinds("NY", 0) + ["T0", "T1", "X0"], [])
-    z2 = join(kinds("TNXY", 1), z2)
+    z2 = join(kinds("TN", 1), z2)
     land(2, z2)
     near(2)
     products(kinds("NY", 1) + ["T2", "X1"], kinds("TNXY", 0) + ["T1"])

time: 75.4 us -> 75.2 us (level)
  starting transfers between devices: 16.9 us -> 17.7 us
    ppermute x4, waiting for transfers between devices: 5.65 us -> 10.5 us  [across(): lax.ppermute(found[part], 'gx', [(i, (i + step) % n_gx) for i in range(n_...]
    ppermute x5, waiting for transfers between devices: 8.65 us -> 5.95 us  [near(): lax.ppermute(own, 'gy', [(q, far_place(q, m + 1)) for q in range(n_gy)])]
    ppermute x8, waiting for transfers between devices: 9.28 us -> 6.62 us  [swap(): return lax.ppermute(array, 'gy', [(i, i ^ mask) for i in range(n_gy)])]
  transfers between devices with their start and end apart: 18 -> 18, of which waited for: 12 -> 11; matrix products, arithmetic and copies ran while one was open for 3% -> 3% of each run, Pallas kernels for 20% -> 20%
where the time goes in v9:
time: 75.2 us; the launch traced here: 75 us
  waiting for transfers between devices  28.1 us (37%)
  Pallas kernels  19.6 us (26%)
  starting transfers between devices  17.7 us (24%)
  blocking collectives  7.29 us (10%)
  other arithmetic  2.11 us (3%)
    pallas_call x6, Pallas kernels, products(): pl.pallas_call(functools.partial(product_kernel, stack, held, inner, part...  12.2 us
    ppermute x4, waiting for transfers between devices, across(): lax.ppermute(found[part], 'gx', [(i, (i + step) % n_gx) for i in range(n_...  10.5 us
    all_to_all x1, starting transfers between devices, per_device(): lax.all_to_all(asked, ('gx', 'gy'), split_axis=0, concat_axis=0, tiled=True)  7.3 us
    all_to_all x1, blocking collectives, per_device(): back = lax.all_to_all(send, 'gy', split_axis=0, concat_axis=0, tiled=True)  7.29 us
    ppermute x8, waiting for transfers between devices, swap(): return lax.ppermute(array, 'gy', [(i, i ^ mask) for i in range(n_gy)])  6.62 us
    ppermute x5, waiting for transfers between devices, near(): lax.ppermute(own, 'gy', [(q, far_place(q, m + 1)) for q in range(n_gy)])  5.95 us
    ppermute x8, starting transfers between devices, swap(): return lax.ppermute(array, 'gy', [(i, i ^ mask) for i in range(n_gy)])  5.22 us
    all_to_all x1, waiting for transfers between devices, per_device(): lax.all_to_all(asked, ('gx', 'gy'), split_axis=0, concat_axis=0, tiled=True)  5.01 us
  transfers between devices with their start and end apart: 18, of which 11 were waited for; matrix products, arithmetic and copies ran while one was open for 3% of the time, Pallas kernels for 20%

profile of v9, /device:TPU:0, one launch (start us, length us, event | category | flops | bytes accessed | tf_op | source)
XLA Modules:
  0.0 75.0 jit_solution(11220104563903127438)
XLA Ops:
  0.0 0.0 copy-start.1
  0.0 1.8 %request.1 = (s32[32,1,32]{2,1,0:T(1,128)}, s32[2,1024]{1,0:T(2,128)}) custom-call(s32[1,25]{1,0:T(1,128)} %sizes_hbm.1, s32[1,1024]{1,0:T(1,128)} %bitcast.2), custom_call_target="tpu_custom_call" | custom-call | tf_op jit(solution)/shard_map/request/pallas_call | solution.py:321
  1.8 7.3 %all-to-all-start = ((s32[32,1,32]{2,1,0:T(1,128)}), s32[32,1,32]{2,1,0:T(1,128)S(1)}, u32[]{:S(2)}, u32[]{:S(2)}) async-start(s32[32,1,32]{2,1,0:T(1,128)} %get-tuple-element.224), calls=%async_computation | async-start | bytes 32768 | tf_op jit(solution)/shard_map/all_to_all | solution.py:334
  9.1 1.8 %fusion = f32[1024]{0:T(1024)S(1)} fusion(bf16[1024,768]{1,0:T(8,128)(2,1)} %param.3), kind=kLoop, calls=%fused_computation.2 | loop fusion | flops 2358272 | bytes 1576960 | tf_op jit(solution)/shard_map/reduce_sum | solution.py:337
  10.9 0.0 copy-done.1
  11.0 0.3 fusion.1.unit_ref
  11.3 5.0 %all-to-all-done.asked_ref = s32[32,1,32]{2,1,0:T(1,128)S(1)} async-done(((s32[32,1,32]{2,1,0:T(1,128)}), s32[32,1,32]{2,1,0:T(1,128)S(1)}, u32[]{:S(2)}, u32[]{:S(2)}) %all-to-all-start) | async-done | bytes 4128 | tf_op jit(solution)/shard_map/all_to_all | solution.py:334
  16.3 0.8 %select.3 = bf16[264,768]{1,0:T(8,128)(2,1)S(1)} custom-call(s32[32,1,32]{2,1,0:T(1,128)S(1)} %all-to-all-done.asked_ref, bf16[1024,768]{1,0:T(8,128)(2,1)S(1)} %fusion.1.unit_ref), custom_call_target="tpu_custom_call" | custom-call | flops 402653184 | bytes 786432 | tf_op jit(solution)/shard_map/select/pallas_call | solution.py:356
  17.1 0.6 collective-permute-start.3
  17.8 0.8 %select.4.refs_2_.refs_4_.refs_1_.refs_3_ = bf16[257,768]{1,0:T(8,128)(2,1)S(1)} custom-call(s32[32,1,32]{2,1,0:T(1,128)S(1)} %all-to-all-done.asked_ref, bf16[1024,768]{1,0:T(8,128)(2,1)S(1)} %fusion.1.unit_ref), custom_call_target="tpu_custom_call" | custom-call | flops 402653184 | bytes 786432 | tf_op jit(solution)/shard_map/select/pallas_call | solution.py:356
  18.6 0.1 collective-permute-start.2
  18.7 0.6 collective-permute-start.1
  19.3 0.4 collective-permute-start
  19.7 1.4 %select.5 = (bf16[264,768]{1,0:T(8,128)(2,1)S(1)}, bf16[136,768]{1,0:T(8,128)(2,1)S(1)}, bf16[136,768]{1,0:T(8,128)(2,1)S(1)}) custom-call(s32[32,1,32]{2,1,0:T(1,128)S(1)} %all-to-all-done.asked_ref, bf16[1024,768]{1,0:T(8,128)(2,1)S(1)} %fusion.1.unit_ref), custom_call_target="tpu_custom_call" | custom-call | flops 1207959552 | bytes 786432 | tf_op jit(solution)/shard_map/select/pallas_call | solution.py:356
  21.1 3.3 %collective-permute-start.5 = (bf16[264,768]{1,0:T(8,128)(2,1)S(1)}, bf16[264,768]{1,0:T(8,128)(2,1)S(1)}, u32[]{:S(2)}, u32[]{:S(2)}) collective-permute-start(bf16[264,768]{1,0:T(8,128)(2,1)S(1)} %get-tuple-element.235), channel_id=1, source_target_pairs={{0,24},{8,0},{16,8},{24,16},{1,25},{9,1},{17,9},{25,17},{2,26},{10... | collective-permute-start | bytes 1216520 | tf_op jit(solution)/shard_map/ppermute | solution.py:370
  24.4 5.0 %collective-permute-done.2.refs_1_.refs_7_.refs_4_.refs_5_.refs_6_.refs_3_ = bf16[257,768]{1,0:T(8,128)(2,1)S(1)} collective-permute-done((bf16[257,768]{1,0:T(8,128)(2,1)S(1)}, bf16[257,768]{1,0:T(8,128)(2,1)S(1)}, u32[]{:S(2)}, u32[]{:S(2)}) %collective-permute-start.2) | collective-permute-done | bytes 394784 | tf_op jit(solution)/shard_map/ppermute | solution.py:396
  29.4 1.2 %collective-permute-done.1.refs_4_.refs_6_.refs_3_.refs_5_.refs_2_ = bf16[257,768]{1,0:T(8,128)(2,1)S(1)} collective-permute-done((bf16[257,768]{1,0:T(8,128)(2,1)S(1)}, bf16[257,768]{1,0:T(8,128)(2,1)S(1)}, u32[]{:S(2)}, u32[]{:S(2)}) %collective-permute-start.1) | collective-permute-done | bytes 394784 | tf_op jit(solution)/shard_map/ppermute | solution.py:373
  30.6 0.0 collective-permute-done.refs_0_.refs_5_.refs_2_.refs_3_.refs_4_
  30.6 0.7 collective-permute-done.3.refs_0_
  31.3 0.1 collective-permute-start.4
  31.4 0.6 collective-permute-start.8
  32.0 0.4 collective-permute-start.7
  32.4 0.0 collective-permute-start.6
  32.4 2.4 %products.6 = (f32[1,256]{1,0:T(1,128)S(1)}, f32[1,256]{1,0:T(1,128)S(1)}, f32[1,256]{1,0:T(1,128)S(1)}, f32[1,256]{1,0:T(1,128)S(1)}, f32[1,256]{1,0:T(1,128)S(1)}) custom-call(bf16[257,768]{1,0:T(8,128)(2,1)S(1)} %collective-permute-done.refs_0_.refs_5_.refs_2_.refs_3_.refs_4_, ...), custom_call_target="tpu_custom_call" | custom-call | tf_op jit(solution)/shard_map/products/pallas_call | solution.py:413
  34.9 4.0 %collective-permute-done.5.refs_0_ = bf16[264,768]{1,0:T(8,128)(2,1)S(1)} collective-permute-done((bf16[264,768]{1,0:T(8,128)(2,1)S(1)}, bf16[264,768]{1,0:T(8,128)(2,1)S(1)}, u32[]{:S(2)}, u32[]{:S(2)}) %collective-permute-start.5) | collective-permute-done | bytes 405536 | tf_op jit(solution)/shard_map/ppermute | solution.py:370
  38.8 0.0 collective-permute-done.4.refs_0_.refs_6_.refs_7_.refs_8_
  38.9 0.6 collective-permute-start.11
  39.5 0.0 collective-permute-start.10
  39.5 4.2 %collective-permute-done.8.refs_3_.refs_7_.refs_8_.refs_9_.refs_5_.refs_4_ = bf16[257,768]{1,0:T(8,128)(2,1)S(1)} collective-permute-done((bf16[257,768]{1,0:T(8,128)(2,1)S(1)}, bf16[257,768]{1,0:T(8,128)(2,1)S(1)}, u32[]{:S(2)}, u32[]{:S(2)}) %collective-permute-start.8) | collective-permute-done | bytes 394784 | tf_op jit(solution)/shard_map/ppermute | solution.py:373
  43.6 0.0 collective-permute-start.9
  43.6 0.6 collective-permute-done.7.refs_1_.refs_8_.refs_9_.refs_10_.refs_6_.refs_5_
  44.2 2.8 %products.7 = (f32[1,256]{1,0:T(1,128)S(1)}, f32[1,256]{1,0:T(1,128)S(1)}, f32[1,256]{1,0:T(1,128)S(1)}, f32[1,256]{1,0:T(1,128)S(1)}, f32[1,256]{1,0:T(1,128)S(...) custom-call(bf16[257,768]{1,0:T(8,128)(2,1)S(1)} %collective-permute-done.4.refs_, ...), custom_call_target="tpu_custom_call" | custom-call | tf_op jit(solution)/shard_map/products/pallas_call | solution.py:413
  47.0 5.4 %collective-permute-done.6.refs_0_ = bf16[136,768]{1,0:T(8,128)(2,1)S(1)} collective-permute-done((bf16[136,768]{1,0:T(8,128)(2,1)S(1)}, bf16[136,768]{1,0:T(8,128)(2,1)S(1)}, u32[]{:S(2)}, u32[]{:S(2)}) %collective-permute-start.6) | collective-permute-done | bytes 208928 | tf_op jit(solution)/shard_map/ppermute | solution.py:370
  52.3 0.6 collective-permute-start.16
  52.9 0.0 collective-permute-start.15
  53.0 1.4 %products.8 = (f32[1,128]{1,0:T(1,128)S(1)}, f32[1,256]{1,0:T(1,128)S(1)}, f32[1,256]{1,0:T(1,128)S(1)}, f32[1,256]{1,0:T(1,128)S(1)}, f32[1,256]{1,0:T(1,128)S(...) custom-call(bf16[129,768]{1,0:T(8,128)(2,1)S(1)} %pack.7.refs_0_.ref, ...), custom_call_target="tpu_custom_call" | custom-call | tf_op jit(solution)/shard_map/products/pallas_call | solution.py:413
  54.4 0.0 collective-permute-done.11.refs_1_.refs_12_.refs_7_.refs_6_
  54.4 0.0 collective-permute-done.10.refs_0_.refs_13_.refs_8_.refs_7_
  54.4 1.8 %products.9 = (f32[1,256]{1,0:T(1,128)S(1)}, f32[1,256]{1,0:T(1,128)S(1)}, f32[1,256]{1,0:T(1,128)S(1)}, f32[1,256]{1,0:T(1,128)S(1)}, f32[1,256]{1,0:T(1,128)S(...) custom-call(bf16[257,768]{1,0:T(8,128)(2,1)S(1)} %collective-permute, ...), custom_call_target="tpu_custom_call" | custom-call | tf_op jit(solution)/shard_map/products/pallas_call | solution.py:413
  56.2 0.5 collective-permute-done.9.refs_0_
  56.8 0.8 %collective-permute-start.14 = (bf16[129,768]{1,0:T(8,128)(2,1)S(1)}, bf16[129,768]{1,0:T(8,128)(2,1)S(1)}, u32[]{:S(2)}, u32[]{:S(2)}) collective-permute-start(bf16[129,768]{1,0:T(8,128)(2,1)S(1)} %pack.8.refs_2_.refs_1_.refs_13_.refs_10_), channel_id=1, source_target_pairs={{0,5},{1,4},{2,7},{3,6},{4,0},{5,1},{6,2},{7,3},{8,13},{9,12},{10,... | collective-permute-start | bytes 594440 | tf_op jit(solution)/shard_map/ppermute | solution.py:396
  57.5 1.5 %collective-permute-start.13 = (bf16[129,768]{1,0:T(8,128)(2,1)S(1)}, bf16[129,768]{1,0:T(8,128)(2,1)S(1)}, u32[]{:S(2)}, u32[]{:S(2)}) collective-permute-start(bf16[129,768]{1,0:T(8,128)(2,1)S(1)} %pack.8.refs_2_.refs_1_.refs_13_.refs_10_), channel_id=1, source_target_pairs={{0,2},{1,3},{2,0},{3,1},{4,6},{5,7},{6,4},{7,5},{8,10},{9,11},{10,... | collective-permute-start | bytes 594440 | tf_op jit(solution)/shard_map/ppermute | solution.py:373
  59.0 0.1 pack.9
  59.0 0.9 %collective-permute-start.12 = (bf16[515,768]{1,0:T(8,128)(2,1)S(1)}, bf16[515,768]{1,0:T(8,128)(2,1)S(1)}, u32[]{:S(2)}, u32[]{:S(2)}) collective-permute-start(bf16[515,768]{1,0:T(8,128)(2,1)S(1)} %pack.9), channel_id=1, source_target_pairs={{0,1},{1,0},{2,3},{3,2},{4,5},{5,4},{6,7},{7,6},{8,9},{9,8},{10,11... | collective-permute-start | bytes 2373128 | tf_op jit(solution)/shard_map/ppermute | solution.py:373
  59.9 0.0 collective-permute-done.16.refs_2_.refs_9_.refs_8_
  59.9 0.0 collective-permute-done.15.refs_0_.refs_10_.refs_9_
  59.9 2.0 %products.10 = (f32[1,128]{1,0:T(1,128)S(1)}, f32[1,128]{1,0:T(1,128)S(1)}, f32[1,128]{1,0:T(1,128)S(1)}, f32[1,256]{1,0:T(1,128)S(1)}, f32[1,256]{1,0:T(1,128)S...) custom-call(bf16[129,768]{1,0:T(8,128)(2,1)S(1)} %collective-permute, ...), custom_call_target="tpu_custom_call" | custom-call | flops 39258685440 | tf_op jit(solution)/shard_map/products/pallas_call | solution.py:413
  61.9 0.0 collective-permute-done.12.ref
  61.9 0.1 split.1
  62.0 1.9 %products.11 = (f32[1,256]{1,0:T(1,128)S(1)}, f32[1,128]{1,0:T(1,128)S(1)}, f32[1,128]{1,0:T(1,128)S(1)}, f32[1,256]{1,0:T(1,128)S(1)}, f32[1,256]{1,0:T(1,128)S...) custom-call(bf16[257,768]{1,0:T(8,128)(2,1)S(1)} %get-tuple-element., ...), custom_call_target="tpu_custom_call" | custom-call | tf_op jit(solution)/shard_map/products/pallas_call | solution.py:413
  63.9 0.3 collective-permute-done.14.refs_0_
  64.2 1.2 %collective-permute-done.13.refs_1_ = bf16[129,768]{1,0:T(8,128)(2,1)S(1)} collective-permute-done((bf16[129,768]{1,0:T(8,128)(2,1)S(1)}, bf16[129,768]{1,0:T(8,128)(2,1)S(1)}, u32[]{:S(2)}, u32[]{:S(2)}) %collective-permute-start.13) | collective-permute-done | bytes 198176 | tf_op jit(solution)/shard_map/ppermute | solution.py:373
  65.4 0.0 copy-start
  65.4 1.5 %final.1 = f32[8,1,512]{2,1,0:T(1,128)S(1)} custom-call(bf16[129,768]{1,0:T(8,128)(2,1)S(1)} %collective-permute-done.14.refs_0_, bf16[129,768]{1,0:T(8,128)(2,1)S(1)} %collective-permute-done.13.refs_1_, bf16[257,768]{1,0:T(8,128)(2,1)S(1)} %collective-permute-done.1.refs_4_.refs_6_.refs_3_.refs_5_.refs_2_, ...), custom_call_target="tpu_custom_call" | custom-call | flops 805306368 | tf_op jit(solution)/shard_map/final/pallas_call | solution.py:479
  66.9 7.3 %all_to_all.10.back_ref = f32[8,1,512]{2,1,0:T(1,128)S(1)} all-to-all(f32[8,1,512]{2,1,0:T(1,128)S(1)} %final.1), channel_id=1, replica_groups=mesh['gx'=4,'gy'=8] {'gy'}, dimensions={0} | all-to-all | bytes 32768 | tf_op jit(solution)/shard_map/all_to_all | solution.py:490
  74.2 0.0 copy-done
  74.2 0.8 %finish.1 = f32[1,1024]{1,0:T(1,128)} custom-call(s32[2,1024]{1,0:T(2,128)S(1)} %copy-done, f32[8,1,512]{2,1,0:T(1,128)S(1)} %all_to_all.10.back_ref), custom_call_target="tpu_custom_call" | custom-call | tf_op jit(solution)/shard_map/finish/pallas_call | solution.py:491
  (5 shorter events, 0.1 us)
Async XLA Ops:
  0.0 10.9 %copy-start.1 = (bf16[1024,768]{1,0:T(8,128)(2,1)S(1)}, bf16[1024,768]{1,0:T(8,128)(2,1)}, u32[]{:S(2)}) copy-start(bf16[1024,768]{1,0:T(8,128)(2,1)} %param.3) | copy-start | bytes 4718596
  1.8 14.5 %all-to-all-start = ((s32[32,1,32]{2,1,0:T(1,128)}), s32[32,1,32]{2,1,0:T(1,128)S(1)}, u32[]{:S(2)}, u32[]{:S(2)}) async-start(s32[32,1,32]{2,1,0:T(1,128)} %get-tuple-element.224), calls=%async_computation | async-start | bytes 32768 | tf_op jit(solution)/shard_map/all_to_all | solution.py:334
  17.1 14.2 %collective-permute-start.3 = (bf16[264,768]{1,0:T(8,128)(2,1)S(1)}, bf16[264,768]{1,0:T(8,128)(2,1)S(1)}, u32[]{:S(2)}, u32[]{:S(2)}) collective-permute-start(bf16[264,768]{1,0:T(8,128)(2,1)S(1)} %select.3), channel_id=1, source_target_pairs={{0,8},{8,16},{16,24},{24,0},{1,9},{9,17},{17,25},{25,1},{2,10},{10... | collective-permute-start | bytes 1216520 | tf_op jit(solution)/shard_map/ppermute | solution.py:370
  18.6 10.8 %collective-permute-start.2 = (bf16[257,768]{1,0:T(8,128)(2,1)S(1)}, bf16[257,768]{1,0:T(8,128)(2,1)S(1)}, u32[]{:S(2)}, u32[]{:S(2)}) collective-permute-start(bf16[257,768]{1,0:T(8,128)(2,1)S(1)} %select.4.refs_2_.refs_4_.refs_1_.refs_3_), channel_id=1, source_target_pairs={{0,5},{1,4},{2,7},{3,6},{4,0},{5,1},{6,2},{7,3},{8,13},{9,12},{10,... | collective-permute-start | bytes 1184264 | tf_op jit(solution)/shard_map/ppermute | solution.py:396
  18.7 11.9 %collective-permute-start.1 = (bf16[257,768]{1,0:T(8,128)(2,1)S(1)}, bf16[257,768]{1,0:T(8,128)(2,1)S(1)}, u32[]{:S(2)}, u32[]{:S(2)}) collective-permute-start(bf16[257,768]{1,0:T(8,128)(2,1)S(1)} %select.4.refs_2_.refs_4_.refs_1_.refs_3_), channel_id=1, source_target_pairs={{0,2},{1,3},{2,0},{3,1},{4,6},{5,7},{6,4},{7,5},{8,10},{9,11},{10,... | collective-permute-start | bytes 1184264 | tf_op jit(solution)/shard_map/ppermute | solution.py:373
  19.3 11.3 %collective-permute-start = (bf16[257,768]{1,0:T(8,128)(2,1)S(1)}, bf16[257,768]{1,0:T(8,128)(2,1)S(1)}, u32[]{:S(2)}, u32[]{:S(2)}) collective-permute-start(bf16[257,768]{1,0:T(8,128)(2,1)S(1)} %select.4.refs_2_.refs_4_.refs_1_.refs_3_), channel_id=1, source_target_pairs={{0,1},{1,0},{2,3},{3,2},{4,5},{5,4},{6,7},{7,6},{8,9},{9,8},{10,11... | collective-permute-start | bytes 1184264 | tf_op jit(solution)/shard_map/ppermute | solution.py:373
  21.1 17.8 %collective-permute-start.5 = (bf16[264,768]{1,0:T(8,128)(2,1)S(1)}, bf16[264,768]{1,0:T(8,128)(2,1)S(1)}, u32[]{:S(2)}, u32[]{:S(2)}) collective-permute-start(bf16[264,768]{1,0:T(8,128)(2,1)S(1)} %get-tuple-element.235), channel_id=1, source_target_pairs={{0,24},{8,0},{16,8},{24,16},{1,25},{9,1},{17,9},{25,17},{2,26},{10... | collective-permute-start | bytes 1216520 | tf_op jit(solution)/shard_map/ppermute | solution.py:370
  31.3 7.5 %collective-permute-start.4 = (bf16[257,768]{1,0:T(8,128)(2,1)S(1)}, bf16[257,768]{1,0:T(8,128)(2,1)S(1)}, u32[]{:S(2)}, u32[]{:S(2)}) collective-permute-start(bf16[257,768]{1,0:T(8,128)(2,1)S(1)} %pack.5.refs_3_.refs_8_.refs_5_.refs_6_.refs_7_), channel_id=1, source_target_pairs={{0,1},{1,0},{2,3},{3,2},{4,5},{5,4},{6,7},{7,6},{8,9},{9,8},{10,11... | collective-permute-start | bytes 1184264 | tf_op jit(solution)/shard_map/ppermute | solution.py:373
  31.4 12.2 %collective-permute-start.8 = (bf16[257,768]{1,0:T(8,128)(2,1)S(1)}, bf16[257,768]{1,0:T(8,128)(2,1)S(1)}, u32[]{:S(2)}, u32[]{:S(2)}) collective-permute-start(bf16[257,768]{1,0:T(8,128)(2,1)S(1)} %pack.5.refs_3_.refs_8_.refs_5_.refs_6_.refs_7_), channel_id=1, source_target_pairs={{0,2},{1,3},{2,0},{3,1},{4,6},{5,7},{6,4},{7,5},{8,10},{9,11},{10,... | collective-permute-start | bytes 1184264 | tf_op jit(solution)/shard_map/ppermute | solution.py:373
  32.0 12.2 %collective-permute-start.7 = (bf16[257,768]{1,0:T(8,128)(2,1)S(1)}, bf16[257,768]{1,0:T(8,128)(2,1)S(1)}, u32[]{:S(2)}, u32[]{:S(2)}) collective-permute-start(bf16[257,768]{1,0:T(8,128)(2,1)S(1)} %pack.5.refs_3_.refs_8_.refs_5_.refs_6_.refs_7_), channel_id=1, source_target_pairs={{0,5},{1,4},{2,7},{3,6},{4,0},{5,1},{6,2},{7,3},{8,13},{9,12},{10,... | collective-permute-start | bytes 1184264 | tf_op jit(solution)/shard_map/ppermute | solution.py:396
  32.4 19.9 %collective-permute-start.6 = (bf16[136,768]{1,0:T(8,128)(2,1)S(1)}, bf16[136,768]{1,0:T(8,128)(2,1)S(1)}, u32[]{:S(2)}, u32[]{:S(2)}) collective-permute-start(bf16[136,768]{1,0:T(8,128)(2,1)S(1)} %get-tuple-element.246), channel_id=1, source_target_pairs={{0,16},{8,24},{16,0},{24,8},{1,17},{9,25},{17,1},{25,9},{2,18},{10... | collective-permute-start | bytes 626696 | tf_op jit(solution)/shard_map/ppermute | solution.py:370
  38.9 15.5 %collective-permute-start.11 = (bf16[257,768]{1,0:T(8,128)(2,1)S(1)}, bf16[257,768]{1,0:T(8,128)(2,1)S(1)}, u32[]{:S(2)}, u32[]{:S(2)}) collective-permute-start(bf16[257,768]{1,0:T(8,128)(2,1)S(1)} %pack.6.refs_2_.refs_9_.refs_10_.refs_0_.refs_11_), channel_id=1, source_target_pairs={{0,2},{1,3},{2,0},{3,1},{4,6},{5,7},{6,4},{7,5},{8,10},{9,11},{10,... | collective-permute-start | bytes 1184264 | tf_op jit(solution)/shard_map/ppermute | solution.py:373
  39.5 14.9 %collective-permute-start.10 = (bf16[257,768]{1,0:T(8,128)(2,1)S(1)}, bf16[257,768]{1,0:T(8,128)(2,1)S(1)}, u32[]{:S(2)}, u32[]{:S(2)}) collective-permute-start(bf16[257,768]{1,0:T(8,128)(2,1)S(1)} %pack.6.refs_2_.refs_9_.refs_10_.refs_0_.refs_11_), channel_id=1, source_target_pairs={{0,5},{1,4},{2,7},{3,6},{4,0},{5,1},{6,2},{7,3},{8,13},{9,12},{10,... | collective-permute-start | bytes 1184264 | tf_op jit(solution)/shard_map/ppermute | solution.py:396
  43.6 13.1 %collective-permute-start.9 = (bf16[136,768]{1,0:T(8,128)(2,1)S(1)}, bf16[136,768]{1,0:T(8,128)(2,1)S(1)}, u32[]{:S(2)}, u32[]{:S(2)}) collective-permute-start(bf16[136,768]{1,0:T(8,128)(2,1)S(1)} %get-tuple-element.264), channel_id=1, source_target_pairs={{0,16},{8,24},{16,0},{24,8},{1,17},{9,25},{17,1},{25,9},{2,18},{10... | collective-permute-start | bytes 626696 | tf_op jit(solution)/shard_map/ppermute | solution.py:370
  52.3 7.6 %collective-permute-start.16 = (bf16[129,768]{1,0:T(8,128)(2,1)S(1)}, bf16[129,768]{1,0:T(8,128)(2,1)S(1)}, u32[]{:S(2)}, u32[]{:S(2)}) collective-permute-start(bf16[129,768]{1,0:T(8,128)(2,1)S(1)} %pack.7.refs_0_.refs_11_.refs_1_.refs_14_.refs_12_), channel_id=1, source_target_pairs={{0,2},{1,3},{2,0},{3,1},{4,6},{5,7},{6,4},{7,5},{8,10},{9,11},{10,... | collective-permute-start | bytes 594440 | tf_op jit(solution)/shard_map/ppermute | solution.py:373
  52.9 7.0 %collective-permute-start.15 = (bf16[129,768]{1,0:T(8,128)(2,1)S(1)}, bf16[129,768]{1,0:T(8,128)(2,1)S(1)}, u32[]{:S(2)}, u32[]{:S(2)}) collective-permute-start(bf16[129,768]{1,0:T(8,128)(2,1)S(1)} %pack.7.refs_0_.refs_11_.refs_1_.refs_14_.refs_12_), channel_id=1, source_target_pairs={{0,5},{1,4},{2,7},{3,6},{4,0},{5,1},{6,2},{7,3},{8,13},{9,12},{10,... | collective-permute-start | bytes 594440 | tf_op jit(solution)/shard_map/ppermute | solution.py:396
  56.8 7.4 %collective-permute-start.14 = (bf16[129,768]{1,0:T(8,128)(2,1)S(1)}, bf16[129,768]{1,0:T(8,128)(2,1)S(1)}, u32[]{:S(2)}, u32[]{:S(2)}) collective-permute-start(bf16[129,768]{1,0:T(8,128)(2,1)S(1)} %pack.8.refs_2_.refs_1_.refs_13_.refs_10_), channel_id=1, source_target_pairs={{0,5},{1,4},{2,7},{3,6},{4,0},{5,1},{6,2},{7,3},{8,13},{9,12},{10,... | collective-permute-start | bytes 594440 | tf_op jit(solution)/shard_map/ppermute | solution.py:396
  57.5 7.9 %collective-permute-start.13 = (bf16[129,768]{1,0:T(8,128)(2,1)S(1)}, bf16[129,768]{1,0:T(8,128)(2,1)S(1)}, u32[]{:S(2)}, u32[]{:S(2)}) collective-permute-start(bf16[129,768]{1,0:T(8,128)(2,1)S(1)} %pack.8.refs_2_.refs_1_.refs_13_.refs_10_), channel_id=1, source_target_pairs={{0,2},{1,3},{2,0},{3,1},{4,6},{5,7},{6,4},{7,5},{8,10},{9,11},{10,... | collective-permute-start | bytes 594440 | tf_op jit(solution)/shard_map/ppermute | solution.py:373
  59.0 2.9 %collective-permute-start.12 = (bf16[515,768]{1,0:T(8,128)(2,1)S(1)}, bf16[515,768]{1,0:T(8,128)(2,1)S(1)}, u32[]{:S(2)}, u32[]{:S(2)}) collective-permute-start(bf16[515,768]{1,0:T(8,128)(2,1)S(1)} %pack.9), channel_id=1, source_target_pairs={{0,1},{1,0},{2,3},{3,2},{4,5},{5,4},{6,7},{7,6},{8,9},{9,8},{10,11... | collective-permute-start | bytes 2373128 | tf_op jit(solution)/shard_map/ppermute | solution.py:373
  65.4 8.8 %copy-start = (s32[2,1024]{1,0:T(2,128)S(1)}, s32[2,1024]{1,0:T(2,128)}, u32[]{:S(2)}) copy-start(s32[2,1024]{1,0:T(2,128)} %get-tuple-element.223.home_ref) | copy-start | bytes 24580

commit v10 on v9

--- a/solution.py
+++ b/solution.py
@@ -471,9 +471,10 @@
     piece.update(zip(cores, out))
     products(kinds("Y", 3) + ["T4", "X3"], kinds("TNXY", 0, 1) + kinds("TXY", 2) + ["T3"], weight=WEIGHT)
     products(cores, kinds("XY", 0, 1, 2, 3) + ["T2", "T3", "T4"], inner=False)
-    join(kinds("TNXY", 4), [])
+    join(kinds("Y", 4), [])
+    products(kinds("Y", 4), kinds("X", 0, 1, 2, 3) + ["T4"], inner=False)
     stack = kinds("YX", 4)
-    held = kinds("XY", 0, 1, 2, 3) + ["T4", "N4"]
+    held = kinds("Y", 0, 1, 2, 3) + ["T4", "N4"]
     shown = ["T"] + far + ["N", "X"]
     names = stack + held
     send = pl.pallas_call(

time: 75.2 us -> 75.1 us (level)
  waiting for transfers between devices: 28.1 us -> 26.2 us
  starting transfers between devices: 17.7 us -> 18.9 us
    ppermute x5, waiting for transfers between devices: 5.95 us -> 4.4 us  [near(): lax.ppermute(own, 'gy', [(q, far_place(q, m + 1)) for q in range(n_gy)])]
    ppermute x4, waiting for transfers between devices: 10.5 us -> 9.26 us  [across(): lax.ppermute(found[part], 'gx', [(i, (i + step) % n_gx) for i in range(n_...]
    ppermute x8, waiting for transfers between devices: 6.62 us -> 7.56 us  [swap(): return lax.ppermute(array, 'gy', [(i, i ^ mask) for i in range(n_gy)])]
    ppermute x5, starting transfers between devices: 1.24 us -> 2.1 us  [near(): lax.ppermute(own, 'gy', [(q, far_place(q, m + 1)) for q in range(n_gy)])]
    pallas_call x6 -> x7, Pallas kernels: 12.2 us -> 12.9 us  [products(): pl.pallas_call(functools.partial(product_kernel, stack, held, inner, part...]
  transfers between devices with their start and end apart: 18 -> 18, of which waited for: 11 -> 12; matrix products, arithmetic and copies ran while one was open for 3% -> 3% of each run, Pallas kernels for 20% -> 21%
where the time goes in v10:
time: 75.1 us; the launch traced here: 74.9 us
  waiting for transfers between devices  26.2 us (35%)
  Pallas kernels  19.9 us (26%)
  starting transfers between devices  18.9 us (25%)
  blocking collectives  7.61 us (10%)
  other arithmetic  2.11 us (3%)
    pallas_call x7, Pallas kernels, products(): pl.pallas_call(functools.partial(product_kernel, stack, held, inner, part...  12.9 us
    ppermute x4, waiting for transfers between devices, across(): lax.ppermute(found[part], 'gx', [(i, (i + step) % n_gx) for i in range(n_...  9.26 us
    all_to_all x1, blocking collectives, per_device(): back = lax.all_to_all(send, 'gy', split_axis=0, concat_axis=0, tiled=True)  7.61 us
    ppermute x8, waiting for transfers between devices, swap(): return lax.ppermute(array, 'gy', [(i, i ^ mask) for i in range(n_gy)])  7.56 us
    all_to_all x1, starting transfers between devices, per_device(): lax.all_to_all(asked, ('gx', 'gy'), split_axis=0, concat_axis=0, tiled=True)  7.3 us
    ppermute x8, starting transfers between devices, swap(): return lax.ppermute(array, 'gy', [(i, i ^ mask) for i in range(n_gy)])  5.02 us
    all_to_all x1, waiting for transfers between devices, per_device(): lax.all_to_all(asked, ('gx', 'gy'), split_axis=0, concat_axis=0, tiled=True)  5 us
    ppermute x4, starting transfers between devices, across(): lax.ppermute(found[part], 'gx', [(i, (i + step) % n_gx) for i in range(n_...  4.48 us
  transfers between devices with their start and end apart: 18, of which 12 were waited for; matrix products, arithmetic and copies ran while one was open for 3% of the time, Pallas kernels for 21%

profile of v10, /device:TPU:0, one launch (start us, length us, event | category | flops | bytes accessed | tf_op | source)
XLA Modules:
  0.0 74.9 jit_solution(11945210490106803768)
XLA Ops:
  0.0 0.0 copy-start.1
  0.0 1.8 %request.1 = (s32[32,1,32]{2,1,0:T(1,128)}, s32[2,1024]{1,0:T(2,128)}) custom-call(s32[1,25]{1,0:T(1,128)} %sizes_hbm.1, s32[1,1024]{1,0:T(1,128)} %bitcast.2), custom_call_target="tpu_custom_call" | custom-call | tf_op jit(solution)/shard_map/request/pallas_call | solution.py:321
  1.8 7.3 %all-to-all-start = ((s32[32,1,32]{2,1,0:T(1,128)}), s32[32,1,32]{2,1,0:T(1,128)S(1)}, u32[]{:S(2)}, u32[]{:S(2)}) async-start(s32[32,1,32]{2,1,0:T(1,128)} %get-tuple-element.227), calls=%async_computation | async-start | bytes 32768 | tf_op jit(solution)/shard_map/all_to_all | solution.py:334
  9.1 1.8 %fusion = f32[1024]{0:T(1024)S(1)} fusion(bf16[1024,768]{1,0:T(8,128)(2,1)} %param.3), kind=kLoop, calls=%fused_computation.2 | loop fusion | flops 2358272 | bytes 1576960 | tf_op jit(solution)/shard_map/reduce_sum | solution.py:337
  10.9 0.0 copy-done.1
  10.9 0.3 fusion.1.unit_ref
  11.3 5.0 %all-to-all-done.asked_ref = s32[32,1,32]{2,1,0:T(1,128)S(1)} async-done(((s32[32,1,32]{2,1,0:T(1,128)}), s32[32,1,32]{2,1,0:T(1,128)S(1)}, u32[]{:S(2)}, u32[]{:S(2)}) %all-to-all-start) | async-done | bytes 4128 | tf_op jit(solution)/shard_map/all_to_all | solution.py:334
  16.3 0.8 %select.3 = bf16[264,768]{1,0:T(8,128)(2,1)S(1)} custom-call(s32[32,1,32]{2,1,0:T(1,128)S(1)} %all-to-all-done.asked_ref, bf16[1024,768]{1,0:T(8,128)(2,1)S(1)} %fusion.1.unit_ref), custom_call_target="tpu_custom_call" | custom-call | flops 402653184 | bytes 786432 | tf_op jit(solution)/shard_map/select/pallas_call | solution.py:356
  17.1 0.6 collective-permute-start.3
  17.8 0.8 %select.4.refs_2_.refs_4_.refs_1_.refs_3_ = bf16[257,768]{1,0:T(8,128)(2,1)S(1)} custom-call(s32[32,1,32]{2,1,0:T(1,128)S(1)} %all-to-all-done.asked_ref, bf16[1024,768]{1,0:T(8,128)(2,1)S(1)} %fusion.1.unit_ref), custom_call_target="tpu_custom_call" | custom-call | flops 402653184 | bytes 786432 | tf_op jit(solution)/shard_map/select/pallas_call | solution.py:356
  18.6 0.1 collective-permute-start
  18.7 0.6 collective-permute-start.1
  19.3 0.4 collective-permute-start.2
  19.7 1.4 %select.5 = (bf16[264,768]{1,0:T(8,128)(2,1)S(1)}, bf16[136,768]{1,0:T(8,128)(2,1)S(1)}, bf16[136,768]{1,0:T(8,128)(2,1)S(1)}) custom-call(s32[32,1,32]{2,1,0:T(1,128)S(1)} %all-to-all-done.asked_ref, bf16[1024,768]{1,0:T(8,128)(2,1)S(1)} %fusion.1.unit_ref), custom_call_target="tpu_custom_call" | custom-call | flops 1207959552 | bytes 786432 | tf_op jit(solution)/shard_map/select/pallas_call | solution.py:356
  21.1 3.3 %collective-permute-start.5 = (bf16[264,768]{1,0:T(8,128)(2,1)S(1)}, bf16[264,768]{1,0:T(8,128)(2,1)S(1)}, u32[]{:S(2)}, u32[]{:S(2)}) collective-permute-start(bf16[264,768]{1,0:T(8,128)(2,1)S(1)} %get-tuple-element.238), channel_id=1, source_target_pairs={{0,24},{8,0},{16,8},{24,16},{1,25},{9,1},{17,9},{25,17},{2,26},{10... | collective-permute-start | bytes 1216520 | tf_op jit(solution)/shard_map/ppermute | solution.py:370
  24.4 0.0 collective-permute-done.refs_0_.refs_5_.refs_2_.refs_3_.refs_4_
  24.4 6.1 %collective-permute-done.1.refs_4_.refs_6_.refs_3_.refs_5_.refs_1_ = bf16[257,768]{1,0:T(8,128)(2,1)S(1)} collective-permute-done((bf16[257,768]{1,0:T(8,128)(2,1)S(1)}, bf16[257,768]{1,0:T(8,128)(2,1)S(1)}, u32[]{:S(2)}, u32[]{:S(2)}) %collective-permute-start.1) | collective-permute-done | bytes 394784 | tf_op jit(solution)/shard_map/ppermute | solution.py:373
  30.5 0.2 collective-permute-done.2.refs_1_.refs_7_.refs_4_.refs_5_.refs_6_.refs_2_
  30.7 0.6 collective-permute-done.3.refs_0_
  31.3 0.1 collective-permute-start.4
  31.4 0.6 collective-permute-start.7
  32.0 0.8 %collective-permute-start.8 = (bf16[257,768]{1,0:T(8,128)(2,1)S(1)}, bf16[257,768]{1,0:T(8,128)(2,1)S(1)}, u32[]{:S(2)}, u32[]{:S(2)}) collective-permute-start(bf16[257,768]{1,0:T(8,128)(2,1)S(1)} %pack.5.refs_3_.refs_8_.refs_5_.refs_6_.refs_7_), channel_id=1, source_target_pairs={{0,2},{1,3},{2,0},{3,1},{4,6},{5,7},{6,4},{7,5},{8,10},{9,11},{10,... | collective-permute-start | bytes 1184264 | tf_op jit(solution)/shard_map/ppermute | solution.py:373
  32.9 0.6 collective-permute-start.6
  33.4 2.5 %products.7 = (f32[1,256]{1,0:T(1,128)S(1)}, f32[1,256]{1,0:T(1,128)S(1)}, f32[1,256]{1,0:T(1,128)S(1)}, f32[1,256]{1,0:T(1,128)S(1)}, f32[1,256]{1,0:T(1,128)S(1)}) custom-call(bf16[257,768]{1,0:T(8,128)(2,1)S(1)} %collective-permute-done.refs_0_.refs_5_.refs_2_.refs_3_.refs_4_, ...), custom_call_target="tpu_custom_call" | custom-call | tf_op jit(solution)/shard_map/products/pallas_call | solution.py:413
  35.9 2.9 %collective-permute-done.5.refs_0_ = bf16[264,768]{1,0:T(8,128)(2,1)S(1)} collective-permute-done((bf16[264,768]{1,0:T(8,128)(2,1)S(1)}, bf16[264,768]{1,0:T(8,128)(2,1)S(1)}, u32[]{:S(2)}, u32[]{:S(2)}) %collective-permute-start.5) | collective-permute-done | bytes 405536 | tf_op jit(solution)/shard_map/ppermute | solution.py:370
  38.8 0.0 collective-permute-done.4.refs_0_.refs_6_.refs_7_.refs_8_
  38.9 0.2 collective-permute-start.10
  39.0 0.6 collective-permute-start.11
  39.6 4.0 %collective-permute-done.7.refs_1_.refs_8_.refs_9_.refs_10_.refs_6_.refs_3_ = bf16[257,768]{1,0:T(8,128)(2,1)S(1)} collective-permute-done((bf16[257,768]{1,0:T(8,128)(2,1)S(1)}, bf16[257,768]{1,0:T(8,128)(2,1)S(1)}, u32[]{:S(2)}, u32[]{:S(2)}) %collective-permute-start.7) | collective-permute-done | bytes 394784 | tf_op jit(solution)/shard_map/ppermute | solution.py:396
  43.6 0.0 collective-permute-start.9
  43.6 0.6 collective-permute-done.8.refs_3_.refs_7_.refs_8_.refs_9_.refs_5_.refs_2_
  44.3 2.8 %products.8 = (f32[1,256]{1,0:T(1,128)S(1)}, f32[1,256]{1,0:T(1,128)S(1)}, f32[1,256]{1,0:T(1,128)S(1)}, f32[1,256]{1,0:T(1,128)S(1)}, f32[1,256]{1,0:T(1,128)S(...) custom-call(bf16[257,768]{1,0:T(8,128)(2,1)S(1)} %collective-permute-done.4.refs_, ...), custom_call_target="tpu_custom_call" | custom-call | tf_op jit(solution)/shard_map/products/pallas_call | solution.py:413
  47.0 5.3 %collective-permute-done.6.refs_0_ = bf16[136,768]{1,0:T(8,128)(2,1)S(1)} collective-permute-done((bf16[136,768]{1,0:T(8,128)(2,1)S(1)}, bf16[136,768]{1,0:T(8,128)(2,1)S(1)}, u32[]{:S(2)}, u32[]{:S(2)}) %collective-permute-start.6) | collective-permute-done | bytes 208928 | tf_op jit(solution)/shard_map/ppermute | solution.py:370
  52.3 0.1 collective-permute-start.13
  52.4 0.6 collective-permute-start.14
  53.0 1.4 %products.9 = (f32[1,128]{1,0:T(1,128)S(1)}, f32[1,256]{1,0:T(1,128)S(1)}, f32[1,256]{1,0:T(1,128)S(1)}, f32[1,256]{1,0:T(1,128)S(1)}, f32[1,256]{1,0:T(1,128)S(...) custom-call(bf16[129,768]{1,0:T(8,128)(2,1)S(1)} %pack.7.refs_0_.ref, ...), custom_call_target="tpu_custom_call" | custom-call | tf_op jit(solution)/shard_map/products/pallas_call | solution.py:413
  54.4 0.0 collective-permute-done.10.refs_0_.refs_13_.refs_8_.refs_4_
  54.4 0.0 collective-permute-done.11.refs_1_.refs_12_.refs_7_.refs_3_
  54.4 1.8 %products.10 = (f32[1,256]{1,0:T(1,128)S(1)}, f32[1,256]{1,0:T(1,128)S(1)}, f32[1,256]{1,0:T(1,128)S(1)}, f32[1,256]{1,0:T(1,128)S(1)}, f32[1,256]{1,0:T(1,128)S...) custom-call(bf16[257,768]{1,0:T(8,128)(2,1)S(1)} %collective-permute, ...), custom_call_target="tpu_custom_call" | custom-call | tf_op jit(solution)/shard_map/products/pallas_call | solution.py:413
  56.3 0.5 collective-permute-done.9.refs_0_
  56.7 0.8 %collective-permute-start.12 = (bf16[129,768]{1,0:T(8,128)(2,1)S(1)}, bf16[129,768]{1,0:T(8,128)(2,1)S(1)}, u32[]{:S(2)}, u32[]{:S(2)}) collective-permute-start(bf16[129,768]{1,0:T(8,128)(2,1)S(1)} %pack.8.refs_1_.refs_2_.refs_13_.refs_5_.refs_6_), channel_id=1, source_target_pairs={{0,5},{1,4},{2,7},{3,6},{4,0},{5,1},{6,2},{7,3},{8,13},{9,12},{10,... | collective-permute-start | bytes 594440 | tf_op jit(solution)/shard_map/ppermute | solution.py:396
  57.5 1.5 %collective-permute-start.16 = (bf16[129,768]{1,0:T(8,128)(2,1)S(1)}, bf16[129,768]{1,0:T(8,128)(2,1)S(1)}, u32[]{:S(2)}, u32[]{:S(2)}) collective-permute-start(bf16[129,768]{1,0:T(8,128)(2,1)S(1)} %pack.8.refs_1_.refs_2_.refs_13_.refs_5_.refs_6_), channel_id=1, source_target_pairs={{0,2},{1,3},{2,0},{3,1},{4,6},{5,7},{6,4},{7,5},{8,10},{9,11},{10,... | collective-permute-start | bytes 594440 | tf_op jit(solution)/shard_map/ppermute | solution.py:373
  59.0 0.1 pack.9
  59.1 0.9 %collective-permute-start.15 = (bf16[515,768]{1,0:T(8,128)(2,1)S(1)}, bf16[515,768]{1,0:T(8,128)(2,1)S(1)}, u32[]{:S(2)}, u32[]{:S(2)}) collective-permute-start(bf16[515,768]{1,0:T(8,128)(2,1)S(1)} %pack.9), channel_id=1, source_target_pairs={{0,1},{1,0},{2,3},{3,2},{4,5},{5,4},{6,7},{7,6},{8,9},{9,8},{10,11... | collective-permute-start | bytes 2373128 | tf_op jit(solution)/shard_map/ppermute | solution.py:373
  59.9 0.0 collective-permute-done.13.refs_0_.refs_10_.refs_5_
  59.9 0.2 collective-permute-done.14.refs_2_.refs_9_.refs_4_
  60.1 2.0 %products.11 = (f32[1,128]{1,0:T(1,128)S(1)}, f32[1,128]{1,0:T(1,128)S(1)}, f32[1,128]{1,0:T(1,128)S(1)}, f32[1,256]{1,0:T(1,128)S(1)}, f32[1,256]{1,0:T(1,128)S...) custom-call(bf16[129,768]{1,0:T(8,128)(2,1)S(1)} %collective-permute, ...), custom_call_target="tpu_custom_call" | custom-call | flops 39258685440 | tf_op jit(solution)/shard_map/products/pallas_call | solution.py:413
  62.1 0.0 collective-permute-done.15.ref
  62.1 0.1 split.1
  62.1 1.8 %products.12 = (f32[1,256]{1,0:T(1,128)S(1)}, f32[1,128]{1,0:T(1,128)S(1)}, f32[1,128]{1,0:T(1,128)S(1)}, f32[1,256]{1,0:T(1,128)S(1)}, f32[1,256]{1,0:T(1,128)S...) custom-call(bf16[257,768]{1,0:T(8,128)(2,1)S(1)} %get-tuple-element., ...), custom_call_target="tpu_custom_call" | custom-call | tf_op jit(solution)/shard_map/products/pallas_call | solution.py:413
  64.0 0.1 collective-permute-done.12.refs_0_
  64.1 0.7 products.13
  64.8 0.0 copy-start
  64.8 0.6 collective-permute-done.16.refs_1_
  65.5 1.1 %final.1 = f32[8,1,512]{2,1,0:T(1,128)S(1)} custom-call(bf16[129,768]{1,0:T(8,128)(2,1)S(1)} %collective-permute-done.12.refs_0_, bf16[129,768]{1,0:T(8,128)(2,1)S(1)} %collective-permute-done.16.refs_1_, bf16[257,768]{1,0:T(8,128)(2,1)S(1)} %collective-permute-done.2.refs_1_.refs_7_.refs_4_.refs_5_.refs_6_.refs_2_, ...), custom_call_target="tpu_custom_call" | custom-call | flops 805306368 | tf_op jit(solution)/shard_map/final/pallas_call | solution.py:480
  66.5 7.6 %all_to_all.10.back_ref = f32[8,1,512]{2,1,0:T(1,128)S(1)} all-to-all(f32[8,1,512]{2,1,0:T(1,128)S(1)} %final.1), channel_id=1, replica_groups=mesh['gx'=4,'gy'=8] {'gy'}, dimensions={0} | all-to-all | bytes 32768 | tf_op jit(solution)/shard_map/all_to_all | solution.py:491
  74.1 0.0 copy-done
  74.1 0.8 %finish.1 = f32[1,1024]{1,0:T(1,128)} custom-call(s32[2,1024]{1,0:T(2,128)S(1)} %copy-done, f32[8,1,512]{2,1,0:T(1,128)S(1)} %all_to_all.10.back_ref), custom_call_target="tpu_custom_call" | custom-call | tf_op jit(solution)/shard_map/finish/pallas_call | solution.py:492
  (5 shorter events, 0.1 us)
Async XLA Ops:
  0.0 10.9 %copy-start.1 = (bf16[1024,768]{1,0:T(8,128)(2,1)S(1)}, bf16[1024,768]{1,0:T(8,128)(2,1)}, u32[]{:S(2)}) copy-start(bf16[1024,768]{1,0:T(8,128)(2,1)} %param.3) | copy-start | bytes 4718596
  1.8 14.5 %all-to-all-start = ((s32[32,1,32]{2,1,0:T(1,128)}), s32[32,1,32]{2,1,0:T(1,128)S(1)}, u32[]{:S(2)}, u32[]{:S(2)}) async-start(s32[32,1,32]{2,1,0:T(1,128)} %get-tuple-element.227), calls=%async_computation | async-start | bytes 32768 | tf_op jit(solution)/shard_map/all_to_all | solution.py:334
  17.1 14.2 %collective-permute-start.3 = (bf16[264,768]{1,0:T(8,128)(2,1)S(1)}, bf16[264,768]{1,0:T(8,128)(2,1)S(1)}, u32[]{:S(2)}, u32[]{:S(2)}) collective-permute-start(bf16[264,768]{1,0:T(8,128)(2,1)S(1)} %select.3), channel_id=1, source_target_pairs={{0,8},{8,16},{16,24},{24,0},{1,9},{9,17},{17,25},{25,1},{2,10},{10... | collective-permute-start | bytes 1216520 | tf_op jit(solution)/shard_map/ppermute | solution.py:370
  18.6 5.8 %collective-permute-start = (bf16[257,768]{1,0:T(8,128)(2,1)S(1)}, bf16[257,768]{1,0:T(8,128)(2,1)S(1)}, u32[]{:S(2)}, u32[]{:S(2)}) collective-permute-start(bf16[257,768]{1,0:T(8,128)(2,1)S(1)} %select.4.refs_2_.refs_4_.refs_1_.refs_3_), channel_id=1, source_target_pairs={{0,1},{1,0},{2,3},{3,2},{4,5},{5,4},{6,7},{7,6},{8,9},{9,8},{10,11... | collective-permute-start | bytes 1184264 | tf_op jit(solution)/shard_map/ppermute | solution.py:373
  18.7 11.8 %collective-permute-start.1 = (bf16[257,768]{1,0:T(8,128)(2,1)S(1)}, bf16[257,768]{1,0:T(8,128)(2,1)S(1)}, u32[]{:S(2)}, u32[]{:S(2)}) collective-permute-start(bf16[257,768]{1,0:T(8,128)(2,1)S(1)} %select.4.refs_2_.refs_4_.refs_1_.refs_3_), channel_id=1, source_target_pairs={{0,2},{1,3},{2,0},{3,1},{4,6},{5,7},{6,4},{7,5},{8,10},{9,11},{10,... | collective-permute-start | bytes 1184264 | tf_op jit(solution)/shard_map/ppermute | solution.py:373
  19.3 11.4 %collective-permute-start.2 = (bf16[257,768]{1,0:T(8,128)(2,1)S(1)}, bf16[257,768]{1,0:T(8,128)(2,1)S(1)}, u32[]{:S(2)}, u32[]{:S(2)}) collective-permute-start(bf16[257,768]{1,0:T(8,128)(2,1)S(1)} %select.4.refs_2_.refs_4_.refs_1_.refs_3_), channel_id=1, source_target_pairs={{0,5},{1,4},{2,7},{3,6},{4,0},{5,1},{6,2},{7,3},{8,13},{9,12},{10,... | collective-permute-start | bytes 1184264 | tf_op jit(solution)/shard_map/ppermute | solution.py:396
  21.1 17.7 %collective-permute-start.5 = (bf16[264,768]{1,0:T(8,128)(2,1)S(1)}, bf16[264,768]{1,0:T(8,128)(2,1)S(1)}, u32[]{:S(2)}, u32[]{:S(2)}) collective-permute-start(bf16[264,768]{1,0:T(8,128)(2,1)S(1)} %get-tuple-element.238), channel_id=1, source_target_pairs={{0,24},{8,0},{16,8},{24,16},{1,25},{9,1},{17,9},{25,17},{2,26},{10... | collective-permute-start | bytes 1216520 | tf_op jit(solution)/shard_map/ppermute | solution.py:370
  31.3 7.5 %collective-permute-start.4 = (bf16[257,768]{1,0:T(8,128)(2,1)S(1)}, bf16[257,768]{1,0:T(8,128)(2,1)S(1)}, u32[]{:S(2)}, u32[]{:S(2)}) collective-permute-start(bf16[257,768]{1,0:T(8,128)(2,1)S(1)} %pack.5.refs_3_.refs_8_.refs_5_.refs_6_.refs_7_), channel_id=1, source_target_pairs={{0,1},{1,0},{2,3},{3,2},{4,5},{5,4},{6,7},{7,6},{8,9},{9,8},{10,11... | collective-permute-start | bytes 1184264 | tf_op jit(solution)/shard_map/ppermute | solution.py:373
  31.4 12.2 %collective-permute-start.7 = (bf16[257,768]{1,0:T(8,128)(2,1)S(1)}, bf16[257,768]{1,0:T(8,128)(2,1)S(1)}, u32[]{:S(2)}, u32[]{:S(2)}) collective-permute-start(bf16[257,768]{1,0:T(8,128)(2,1)S(1)} %pack.5.refs_3_.refs_8_.refs_5_.refs_6_.refs_7_), channel_id=1, source_target_pairs={{0,5},{1,4},{2,7},{3,6},{4,0},{5,1},{6,2},{7,3},{8,13},{9,12},{10,... | collective-permute-start | bytes 1184264 | tf_op jit(solution)/shard_map/ppermute | solution.py:396
  32.0 12.2 %collective-permute-start.8 = (bf16[257,768]{1,0:T(8,128)(2,1)S(1)}, bf16[257,768]{1,0:T(8,128)(2,1)S(1)}, u32[]{:S(2)}, u32[]{:S(2)}) collective-permute-start(bf16[257,768]{1,0:T(8,128)(2,1)S(1)} %pack.5.refs_3_.refs_8_.refs_5_.refs_6_.refs_7_), channel_id=1, source_target_pairs={{0,2},{1,3},{2,0},{3,1},{4,6},{5,7},{6,4},{7,5},{8,10},{9,11},{10,... | collective-permute-start | bytes 1184264 | tf_op jit(solution)/shard_map/ppermute | solution.py:373
  32.9 19.4 %collective-permute-start.6 = (bf16[136,768]{1,0:T(8,128)(2,1)S(1)}, bf16[136,768]{1,0:T(8,128)(2,1)S(1)}, u32[]{:S(2)}, u32[]{:S(2)}) collective-permute-start(bf16[136,768]{1,0:T(8,128)(2,1)S(1)} %get-tuple-element.249), channel_id=1, source_target_pairs={{0,16},{8,24},{16,0},{24,8},{1,17},{9,25},{17,1},{25,9},{2,18},{10... | collective-permute-start | bytes 626696 | tf_op jit(solution)/shard_map/ppermute | solution.py:370
  38.9 15.6 %collective-permute-start.10 = (bf16[257,768]{1,0:T(8,128)(2,1)S(1)}, bf16[257,768]{1,0:T(8,128)(2,1)S(1)}, u32[]{:S(2)}, u32[]{:S(2)}) collective-permute-start(bf16[257,768]{1,0:T(8,128)(2,1)S(1)} %pack.6.refs_2_.refs_9_.refs_10_.refs_11_.refs_0_), channel_id=1, source_target_pairs={{0,5},{1,4},{2,7},{3,6},{4,0},{5,1},{6,2},{7,3},{8,13},{9,12},{10,... | collective-permute-start | bytes 1184264 | tf_op jit(solution)/shard_map/ppermute | solution.py:396
  39.0 15.4 %collective-permute-start.11 = (bf16[257,768]{1,0:T(8,128)(2,1)S(1)}, bf16[257,768]{1,0:T(8,128)(2,1)S(1)}, u32[]{:S(2)}, u32[]{:S(2)}) collective-permute-start(bf16[257,768]{1,0:T(8,128)(2,1)S(1)} %pack.6.refs_2_.refs_9_.refs_10_.refs_11_.refs_0_), channel_id=1, source_target_pairs={{0,2},{1,3},{2,0},{3,1},{4,6},{5,7},{6,4},{7,5},{8,10},{9,11},{10,... | collective-permute-start | bytes 1184264 | tf_op jit(solution)/shard_map/ppermute | solution.py:373
  43.6 13.1 %collective-permute-start.9 = (bf16[136,768]{1,0:T(8,128)(2,1)S(1)}, bf16[136,768]{1,0:T(8,128)(2,1)S(1)}, u32[]{:S(2)}, u32[]{:S(2)}) collective-permute-start(bf16[136,768]{1,0:T(8,128)(2,1)S(1)} %get-tuple-element.267), channel_id=1, source_target_pairs={{0,16},{8,24},{16,0},{24,8},{1,17},{9,25},{17,1},{25,9},{2,18},{10... | collective-permute-start | bytes 626696 | tf_op jit(solution)/shard_map/ppermute | solution.py:370
  52.3 7.6 %collective-permute-start.13 = (bf16[129,768]{1,0:T(8,128)(2,1)S(1)}, bf16[129,768]{1,0:T(8,128)(2,1)S(1)}, u32[]{:S(2)}, u32[]{:S(2)}) collective-permute-start(bf16[129,768]{1,0:T(8,128)(2,1)S(1)} %pack.7.refs_0_.refs_11_.refs_14_.refs_1_.refs_12_), channel_id=1, source_target_pairs={{0,5},{1,4},{2,7},{3,6},{4,0},{5,1},{6,2},{7,3},{8,13},{9,12},{10,... | collective-permute-start | bytes 594440 | tf_op jit(solution)/shard_map/ppermute | solution.py:396
  52.4 7.7 %collective-permute-start.14 = (bf16[129,768]{1,0:T(8,128)(2,1)S(1)}, bf16[129,768]{1,0:T(8,128)(2,1)S(1)}, u32[]{:S(2)}, u32[]{:S(2)}) collective-permute-start(bf16[129,768]{1,0:T(8,128)(2,1)S(1)} %pack.7.refs_0_.refs_11_.refs_14_.refs_1_.refs_12_), channel_id=1, source_target_pairs={{0,2},{1,3},{2,0},{3,1},{4,6},{5,7},{6,4},{7,5},{8,10},{9,11},{10,... | collective-permute-start | bytes 594440 | tf_op jit(solution)/shard_map/ppermute | solution.py:373
  56.7 7.4 %collective-permute-start.12 = (bf16[129,768]{1,0:T(8,128)(2,1)S(1)}, bf16[129,768]{1,0:T(8,128)(2,1)S(1)}, u32[]{:S(2)}, u32[]{:S(2)}) collective-permute-start(bf16[129,768]{1,0:T(8,128)(2,1)S(1)} %pack.8.refs_1_.refs_2_.refs_13_.refs_5_.refs_6_), channel_id=1, source_target_pairs={{0,5},{1,4},{2,7},{3,6},{4,0},{5,1},{6,2},{7,3},{8,13},{9,12},{10,... | collective-permute-start | bytes 594440 | tf_op jit(solution)/shard_map/ppermute | solution.py:396
  57.5 7.9 %collective-permute-start.16 = (bf16[129,768]{1,0:T(8,128)(2,1)S(1)}, bf16[129,768]{1,0:T(8,128)(2,1)S(1)}, u32[]{:S(2)}, u32[]{:S(2)}) collective-permute-start(bf16[129,768]{1,0:T(8,128)(2,1)S(1)} %pack.8.refs_1_.refs_2_.refs_13_.refs_5_.refs_6_), channel_id=1, source_target_pairs={{0,2},{1,3},{2,0},{3,1},{4,6},{5,7},{6,4},{7,5},{8,10},{9,11},{10,... | collective-permute-start | bytes 594440 | tf_op jit(solution)/shard_map/ppermute | solution.py:373
  59.1 3.0 %collective-permute-start.15 = (bf16[515,768]{1,0:T(8,128)(2,1)S(1)}, bf16[515,768]{1,0:T(8,128)(2,1)S(1)}, u32[]{:S(2)}, u32[]{:S(2)}) collective-permute-start(bf16[515,768]{1,0:T(8,128)(2,1)S(1)} %pack.9), channel_id=1, source_target_pairs={{0,1},{1,0},{2,3},{3,2},{4,5},{5,4},{6,7},{7,6},{8,9},{9,8},{10,11... | collective-permute-start | bytes 2373128 | tf_op jit(solution)/shard_map/ppermute | solution.py:373
  64.8 9.3 %copy-start = (s32[2,1024]{1,0:T(2,128)S(1)}, s32[2,1024]{1,0:T(2,128)}, u32[]{:S(2)}) copy-start(s32[2,1024]{1,0:T(2,128)} %get-tuple-element.226.home_ref) | copy-start | bytes 24580

commit v11 on v10

--- a/solution.py
+++ b/solution.py
@@ -87,9 +87,10 @@
     values = [jnp.where(mask, v, zero).astype(BF16) for v in (low, high, cluster.astype(F32))]
     picked = dot_nt(jnp.concatenate(values, axis=0), place)
     low, high, held = (picked[i * owners:(i + 1) * owners, :] for i in range(3))
-    asked = (low + 256.0 * high + float(rows) * held).astype(I32)
+    asked = (low + 256.0 * high).astype(I32)
+    held = held.astype(I32)
     for o in range(owners):
-        asked_ref[o] = asked[o:o + 1, :]
+        asked_ref[o] = jnp.concatenate([asked[o:o + 1, :], held[o:o + 1, :]], axis=0)
     plane = lax.shift_right_logical(owner, log2(n_gy))
     step = (lax.axis_index("gx") - plane) & (n_gx - 1)
     home_ref[0:1, :] = owner & (n_gy - 1)
@@ -108,9 +109,8 @@
     width = unit_ref.shape[1]
     for step in sorted({k for k, _, _ in parts}):
         plane = (lax.axis_index("gx") + step) & (n_gx - 1)
-        wanted = jnp.concatenate([asked_ref[plane * n_gy + d] for d in range(n_gy)], axis=0)
-        row = wanted & (rows - 1)
-        cluster = lax.shift_right_logical(wanted, log2(rows)).astype(F32).astype(BF16)
+        row = jnp.concatenate([asked_ref[plane * n_gy + d, 0:1, :] for d in range(n_gy)], axis=0)
+        cluster = jnp.concatenate([asked_ref[plane * n_gy + d, 1:2, :] for d in range(n_gy)], axis=0).astype(F32).astype(BF16)
         low = (row & 255).astype(F32).astype(BF16)
         high = lax.shift_right_logical(row, 8).astype(F32).astype(BF16)
         index = dot_nt(pick, low) + 256.0 * dot_nt(pick, high)
@@ -320,7 +320,7 @@
     in_hbm = pl.BlockSpec(memory_space=pltpu.HBM)
     asked, home = pl.pallas_call(
         functools.partial(request_kernel, dims),
-        out_shape=(shape((owners, 1, quota), I32), shape((2, rows), I32)),
+        out_shape=(shape((owners, 2, quota), I32), shape((2, rows), I32)),
         in_specs=[in_hbm, in_hbm],
         out_specs=(in_vmem, in_vmem),
         scratch_shapes=[

time: 75.1 us -> 75.5 us (level)
  transfers between devices with their start and end apart: 18 -> 18, of which waited for: 12 -> 12; matrix products, arithmetic and copies ran while one was open for 3% -> 3% of each run, Pallas kernels for 21% -> 20%
where the time goes in v11:
time: 75.5 us; the launch traced here: 75.3 us
  waiting for transfers between devices  26.3 us (35%)
  Pallas kernels  19.9 us (26%)
  starting transfers between devices  19.1 us (25%)
  blocking collectives  7.65 us (10%)
  other arithmetic  2.11 us (3%)
    pallas_call x7, Pallas kernels, products(): pl.pallas_call(functools.partial(product_kernel, stack, held, inner, part...  12.9 us
    ppermute x4, waiting for transfers between devices, across(): lax.ppermute(found[part], 'gx', [(i, (i + step) % n_gx) for i in range(n_...  9.71 us
    all_to_all x1, blocking collectives, per_device(): back = lax.all_to_all(send, 'gy', split_axis=0, concat_axis=0, tiled=True)  7.65 us
    ppermute x8, waiting for transfers between devices, swap(): return lax.ppermute(array, 'gy', [(i, i ^ mask) for i in range(n_gy)])  7.55 us
    all_to_all x1, starting transfers between devices, per_device(): lax.all_to_all(asked, ('gx', 'gy'), split_axis=0, concat_axis=0, tiled=True)  7.3 us
    all_to_all x1, waiting for transfers between devices, per_device(): lax.all_to_all(asked, ('gx', 'gy'), split_axis=0, concat_axis=0, tiled=True)  5.11 us
    ppermute x8, starting transfers between devices, swap(): return lax.ppermute(array, 'gy', [(i, i ^ mask) for i in range(n_gy)])  5 us
    ppermute x4, starting transfers between devices, across(): lax.ppermute(found[part], 'gx', [(i, (i + step) % n_gx) for i in range(n_...  4.53 us
  transfers between devices with their start and end apart: 18, of which 12 were waited for; matrix products, arithmetic and copies ran while one was open for 3% of the time, Pallas kernels for 20%

profile of v11, /device:TPU:0, one launch (start us, length us, event | category | flops | bytes accessed | tf_op | source)
XLA Modules:
  0.0 75.3 jit_solution(10739783201219550113)
XLA Ops:
  0.0 0.0 copy-start.1
  0.0 1.8 %request.1 = (s32[32,2,32]{2,1,0:T(2,128)}, s32[2,1024]{1,0:T(2,128)}) custom-call(s32[1,25]{1,0:T(1,128)} %sizes_hbm.1, s32[1,1024]{1,0:T(1,128)} %bitcast.2), custom_call_target="tpu_custom_call" | custom-call | tf_op jit(solution)/shard_map/request/pallas_call | solution.py:321
  1.8 7.3 %all-to-all-start = ((s32[32,2,32]{2,1,0:T(2,128)}), s32[32,2,32]{2,1,0:T(2,128)S(1)}, u32[]{:S(2)}, u32[]{:S(2)}) async-start(s32[32,2,32]{2,1,0:T(2,128)} %get-tuple-element.227), calls=%async_computation | async-start | bytes 65536 | tf_op jit(solution)/shard_map/all_to_all | solution.py:334
  9.1 1.8 %fusion = f32[1024]{0:T(1024)S(1)} fusion(bf16[1024,768]{1,0:T(8,128)(2,1)} %param.3), kind=kLoop, calls=%fused_computation.2 | loop fusion | flops 2358272 | bytes 1576960 | tf_op jit(solution)/shard_map/reduce_sum | solution.py:337
  10.9 0.0 copy-done.1
  11.0 0.3 fusion.1.unit_ref
  11.3 5.1 %all-to-all-done.asked_ref = s32[32,2,32]{2,1,0:T(2,128)S(1)} async-done(((s32[32,2,32]{2,1,0:T(2,128)}), s32[32,2,32]{2,1,0:T(2,128)S(1)}, u32[]{:S(2)}, u32[]{:S(2)}) %all-to-all-start) | async-done | bytes 8224 | tf_op jit(solution)/shard_map/all_to_all | solution.py:334
  16.4 0.8 %select.3 = bf16[264,768]{1,0:T(8,128)(2,1)S(1)} custom-call(s32[32,2,32]{2,1,0:T(2,128)S(1)} %all-to-all-done.asked_ref, bf16[1024,768]{1,0:T(8,128)(2,1)S(1)} %fusion.1.unit_ref), custom_call_target="tpu_custom_call" | custom-call | flops 402653184 | bytes 786432 | tf_op jit(solution)/shard_map/select/pallas_call | solution.py:356
  17.2 0.6 collective-permute-start.3
  17.9 0.8 %select.4.refs_2_.refs_4_.refs_1_.refs_3_ = bf16[257,768]{1,0:T(8,128)(2,1)S(1)} custom-call(s32[32,2,32]{2,1,0:T(2,128)S(1)} %all-to-all-done.asked_ref, bf16[1024,768]{1,0:T(8,128)(2,1)S(1)} %fusion.1.unit_ref), custom_call_target="tpu_custom_call" | custom-call | flops 402653184 | bytes 786432 | tf_op jit(solution)/shard_map/select/pallas_call | solution.py:356
  18.7 0.1 collective-permute-start
  18.8 0.6 collective-permute-start.1
  19.3 0.5 collective-permute-start.2
  19.8 1.4 %select.5 = (bf16[264,768]{1,0:T(8,128)(2,1)S(1)}, bf16[136,768]{1,0:T(8,128)(2,1)S(1)}, bf16[136,768]{1,0:T(8,128)(2,1)S(1)}) custom-call(s32[32,2,32]{2,1,0:T(2,128)S(1)} %all-to-all-done.asked_ref, bf16[1024,768]{1,0:T(8,128)(2,1)S(1)} %fusion.1.unit_ref), custom_call_target="tpu_custom_call" | custom-call | flops 1207959552 | bytes 786432 | tf_op jit(solution)/shard_map/select/pallas_call | solution.py:356
  21.2 3.3 %collective-permute-start.5 = (bf16[264,768]{1,0:T(8,128)(2,1)S(1)}, bf16[264,768]{1,0:T(8,128)(2,1)S(1)}, u32[]{:S(2)}, u32[]{:S(2)}) collective-permute-start(bf16[264,768]{1,0:T(8,128)(2,1)S(1)} %get-tuple-element.238), channel_id=1, source_target_pairs={{0,24},{8,0},{16,8},{24,16},{1,25},{9,1},{17,9},{25,17},{2,26},{10... | collective-permute-start | bytes 1216520 | tf_op jit(solution)/shard_map/ppermute | solution.py:370
  24.5 0.0 collective-permute-done.refs_0_.refs_5_.refs_2_.refs_3_.refs_4_
  24.5 6.1 %collective-permute-done.1.refs_4_.refs_6_.refs_3_.refs_5_.refs_1_ = bf16[257,768]{1,0:T(8,128)(2,1)S(1)} collective-permute-done((bf16[257,768]{1,0:T(8,128)(2,1)S(1)}, bf16[257,768]{1,0:T(8,128)(2,1)S(1)}, u32[]{:S(2)}, u32[]{:S(2)}) %collective-permute-start.1) | collective-permute-done | bytes 394784 | tf_op jit(solution)/shard_map/ppermute | solution.py:373
  30.6 0.2 collective-permute-done.2.refs_1_.refs_7_.refs_4_.refs_5_.refs_6_.refs_2_
  30.8 0.6 collective-permute-done.3.refs_0_
  31.4 0.1 collective-permute-start.4
  31.5 0.7 collective-permute-start.7
  32.1 0.9 %collective-permute-start.8 = (bf16[257,768]{1,0:T(8,128)(2,1)S(1)}, bf16[257,768]{1,0:T(8,128)(2,1)S(1)}, u32[]{:S(2)}, u32[]{:S(2)}) collective-permute-start(bf16[257,768]{1,0:T(8,128)(2,1)S(1)} %pack.5.refs_3_.refs_8_.refs_5_.refs_6_.refs_7_), channel_id=1, source_target_pairs={{0,2},{1,3},{2,0},{3,1},{4,6},{5,7},{6,4},{7,5},{8,10},{9,11},{10,... | collective-permute-start | bytes 1184264 | tf_op jit(solution)/shard_map/ppermute | solution.py:373
  33.0 0.6 collective-permute-start.6
  33.6 2.5 %products.7 = (f32[1,256]{1,0:T(1,128)S(1)}, f32[1,256]{1,0:T(1,128)S(1)}, f32[1,256]{1,0:T(1,128)S(1)}, f32[1,256]{1,0:T(1,128)S(1)}, f32[1,256]{1,0:T(1,128)S(1)}) custom-call(bf16[257,768]{1,0:T(8,128)(2,1)S(1)} %collective-permute-done.refs_0_.refs_5_.refs_2_.refs_3_.refs_4_, ...), custom_call_target="tpu_custom_call" | custom-call | tf_op jit(solution)/shard_map/products/pallas_call | solution.py:413
  36.0 3.1 %collective-permute-done.5.refs_0_ = bf16[264,768]{1,0:T(8,128)(2,1)S(1)} collective-permute-done((bf16[264,768]{1,0:T(8,128)(2,1)S(1)}, bf16[264,768]{1,0:T(8,128)(2,1)S(1)}, u32[]{:S(2)}, u32[]{:S(2)}) %collective-permute-start.5) | collective-permute-done | bytes 405536 | tf_op jit(solution)/shard_map/ppermute | solution.py:370
  39.2 0.0 collective-permute-done.4.refs_0_.refs_6_.refs_7_.refs_8_
  39.2 0.2 collective-permute-start.10
  39.4 0.6 collective-permute-start.11
  40.0 3.7 %collective-permute-done.7.refs_1_.refs_8_.refs_9_.refs_10_.refs_6_.refs_3_ = bf16[257,768]{1,0:T(8,128)(2,1)S(1)} collective-permute-done((bf16[257,768]{1,0:T(8,128)(2,1)S(1)}, bf16[257,768]{1,0:T(8,128)(2,1)S(1)}, u32[]{:S(2)}, u32[]{:S(2)}) %collective-permute-start.7) | collective-permute-done | bytes 394784 | tf_op jit(solution)/shard_map/ppermute | solution.py:396
  43.7 0.0 collective-permute-start.9
  43.7 0.6 collective-permute-done.8.refs_3_.refs_7_.refs_8_.refs_9_.refs_5_.refs_2_
  44.4 2.8 %products.8 = (f32[1,256]{1,0:T(1,128)S(1)}, f32[1,256]{1,0:T(1,128)S(1)}, f32[1,256]{1,0:T(1,128)S(1)}, f32[1,256]{1,0:T(1,128)S(1)}, f32[1,256]{1,0:T(1,128)S(...) custom-call(bf16[257,768]{1,0:T(8,128)(2,1)S(1)} %collective-permute-done.4.refs_, ...), custom_call_target="tpu_custom_call" | custom-call | tf_op jit(solution)/shard_map/products/pallas_call | solution.py:413
  47.1 5.5 %collective-permute-done.6.refs_0_ = bf16[136,768]{1,0:T(8,128)(2,1)S(1)} collective-permute-done((bf16[136,768]{1,0:T(8,128)(2,1)S(1)}, bf16[136,768]{1,0:T(8,128)(2,1)S(1)}, u32[]{:S(2)}, u32[]{:S(2)}) %collective-permute-start.6) | collective-permute-done | bytes 208928 | tf_op jit(solution)/shard_map/ppermute | solution.py:370
  52.7 0.2 collective-permute-start.13
  52.8 0.5 collective-permute-start.14
  53.3 1.4 %products.9 = (f32[1,128]{1,0:T(1,128)S(1)}, f32[1,256]{1,0:T(1,128)S(1)}, f32[1,256]{1,0:T(1,128)S(1)}, f32[1,256]{1,0:T(1,128)S(1)}, f32[1,256]{1,0:T(1,128)S(...) custom-call(bf16[129,768]{1,0:T(8,128)(2,1)S(1)} %pack.7.refs_0_.ref, ...), custom_call_target="tpu_custom_call" | custom-call | tf_op jit(solution)/shard_map/products/pallas_call | solution.py:413
  54.7 0.0 collective-permute-done.10.refs_0_.refs_13_.refs_8_.refs_4_
  54.7 0.0 collective-permute-done.11.refs_1_.refs_12_.refs_7_.refs_3_
  54.8 1.8 %products.10 = (f32[1,256]{1,0:T(1,128)S(1)}, f32[1,256]{1,0:T(1,128)S(1)}, f32[1,256]{1,0:T(1,128)S(1)}, f32[1,256]{1,0:T(1,128)S(1)}, f32[1,256]{1,0:T(1,128)S...) custom-call(bf16[257,768]{1,0:T(8,128)(2,1)S(1)} %collective-permute, ...), custom_call_target="tpu_custom_call" | custom-call | tf_op jit(solution)/shard_map/products/pallas_call | solution.py:413
  56.6 0.5 collective-permute-done.9.refs_0_
  57.1 0.7 collective-permute-start.12
  57.8 1.5 %collective-permute-start.16 = (bf16[129,768]{1,0:T(8,128)(2,1)S(1)}, bf16[129,768]{1,0:T(8,128)(2,1)S(1)}, u32[]{:S(2)}, u32[]{:S(2)}) collective-permute-start(bf16[129,768]{1,0:T(8,128)(2,1)S(1)} %pack.8.refs_1_.refs_2_.refs_13_.refs_5_.refs_6_), channel_id=1, source_target_pairs={{0,2},{1,3},{2,0},{3,1},{4,6},{5,7},{6,4},{7,5},{8,10},{9,11},{10,... | collective-permute-start | bytes 594440 | tf_op jit(solution)/shard_map/ppermute | solution.py:373
  59.4 0.1 pack.9
  59.4 0.9 %collective-permute-start.15 = (bf16[515,768]{1,0:T(8,128)(2,1)S(1)}, bf16[515,768]{1,0:T(8,128)(2,1)S(1)}, u32[]{:S(2)}, u32[]{:S(2)}) collective-permute-start(bf16[515,768]{1,0:T(8,128)(2,1)S(1)} %pack.9), channel_id=1, source_target_pairs={{0,1},{1,0},{2,3},{3,2},{4,5},{5,4},{6,7},{7,6},{8,9},{9,8},{10,11... | collective-permute-start | bytes 2373128 | tf_op jit(solution)/shard_map/ppermute | solution.py:373
  60.3 0.0 collective-permute-done.13.refs_0_.refs_10_.refs_5_
  60.3 0.2 collective-permute-done.14.refs_2_.refs_9_.refs_4_
  60.5 2.0 %products.11 = (f32[1,128]{1,0:T(1,128)S(1)}, f32[1,128]{1,0:T(1,128)S(1)}, f32[1,128]{1,0:T(1,128)S(1)}, f32[1,256]{1,0:T(1,128)S(1)}, f32[1,256]{1,0:T(1,128)S...) custom-call(bf16[129,768]{1,0:T(8,128)(2,1)S(1)} %collective-permute, ...), custom_call_target="tpu_custom_call" | custom-call | flops 39258685440 | tf_op jit(solution)/shard_map/products/pallas_call | solution.py:413
  62.5 0.0 collective-permute-done.15.ref
  62.5 0.1 split.1
  62.5 1.8 %products.12 = (f32[1,256]{1,0:T(1,128)S(1)}, f32[1,128]{1,0:T(1,128)S(1)}, f32[1,128]{1,0:T(1,128)S(1)}, f32[1,256]{1,0:T(1,128)S(1)}, f32[1,256]{1,0:T(1,128)S...) custom-call(bf16[257,768]{1,0:T(8,128)(2,1)S(1)} %get-tuple-element., ...), custom_call_target="tpu_custom_call" | custom-call | tf_op jit(solution)/shard_map/products/pallas_call | solution.py:413
  64.4 0.1 collective-permute-done.12.refs_0_
  64.5 0.7 products.13
  65.1 0.0 copy-start
  65.2 0.6 collective-permute-done.16.refs_1_
  65.8 1.1 %final.1 = f32[8,1,512]{2,1,0:T(1,128)S(1)} custom-call(bf16[129,768]{1,0:T(8,128)(2,1)S(1)} %collective-permute-done.12.refs_0_, bf16[129,768]{1,0:T(8,128)(2,1)S(1)} %collective-permute-done.16.refs_1_, bf16[257,768]{1,0:T(8,128)(2,1)S(1)} %collective-permute-done.2.refs_1_.refs_7_.refs_4_.refs_5_.refs_6_.refs_2_, ...), custom_call_target="tpu_custom_call" | custom-call | flops 805306368 | tf_op jit(solution)/shard_map/final/pallas_call | solution.py:480
  66.8 7.6 %all_to_all.10.back_ref = f32[8,1,512]{2,1,0:T(1,128)S(1)} all-to-all(f32[8,1,512]{2,1,0:T(1,128)S(1)} %final.1), channel_id=1, replica_groups=mesh['gx'=4,'gy'=8] {'gy'}, dimensions={0} | all-to-all | bytes 32768 | tf_op jit(solution)/shard_map/all_to_all | solution.py:491
  74.5 0.0 copy-done
  74.5 0.8 %finish.1 = f32[1,1024]{1,0:T(1,128)} custom-call(s32[2,1024]{1,0:T(2,128)S(1)} %copy-done, f32[8,1,512]{2,1,0:T(1,128)S(1)} %all_to_all.10.back_ref), custom_call_target="tpu_custom_call" | custom-call | tf_op jit(solution)/shard_map/finish/pallas_call | solution.py:492
  (5 shorter events, 0.1 us)
Async XLA Ops:
  0.0 10.9 %copy-start.1 = (bf16[1024,768]{1,0:T(8,128)(2,1)S(1)}, bf16[1024,768]{1,0:T(8,128)(2,1)}, u32[]{:S(2)}) copy-start(bf16[1024,768]{1,0:T(8,128)(2,1)} %param.3) | copy-start | bytes 4718596
  1.8 14.6 %all-to-all-start = ((s32[32,2,32]{2,1,0:T(2,128)}), s32[32,2,32]{2,1,0:T(2,128)S(1)}, u32[]{:S(2)}, u32[]{:S(2)}) async-start(s32[32,2,32]{2,1,0:T(2,128)} %get-tuple-element.227), calls=%async_computation | async-start | bytes 65536 | tf_op jit(solution)/shard_map/all_to_all | solution.py:334
  17.2 14.1 %collective-permute-start.3 = (bf16[264,768]{1,0:T(8,128)(2,1)S(1)}, bf16[264,768]{1,0:T(8,128)(2,1)S(1)}, u32[]{:S(2)}, u32[]{:S(2)}) collective-permute-start(bf16[264,768]{1,0:T(8,128)(2,1)S(1)} %select.3), channel_id=1, source_target_pairs={{0,8},{8,16},{16,24},{24,0},{1,9},{9,17},{17,25},{25,1},{2,10},{10... | collective-permute-start | bytes 1216520 | tf_op jit(solution)/shard_map/ppermute | solution.py:370
  18.7 5.8 %collective-permute-start = (bf16[257,768]{1,0:T(8,128)(2,1)S(1)}, bf16[257,768]{1,0:T(8,128)(2,1)S(1)}, u32[]{:S(2)}, u32[]{:S(2)}) collective-permute-start(bf16[257,768]{1,0:T(8,128)(2,1)S(1)} %select.4.refs_2_.refs_4_.refs_1_.refs_3_), channel_id=1, source_target_pairs={{0,1},{1,0},{2,3},{3,2},{4,5},{5,4},{6,7},{7,6},{8,9},{9,8},{10,11... | collective-permute-start | bytes 1184264 | tf_op jit(solution)/shard_map/ppermute | solution.py:373
  18.8 11.8 %collective-permute-start.1 = (bf16[257,768]{1,0:T(8,128)(2,1)S(1)}, bf16[257,768]{1,0:T(8,128)(2,1)S(1)}, u32[]{:S(2)}, u32[]{:S(2)}) collective-permute-start(bf16[257,768]{1,0:T(8,128)(2,1)S(1)} %select.4.refs_2_.refs_4_.refs_1_.refs_3_), channel_id=1, source_target_pairs={{0,2},{1,3},{2,0},{3,1},{4,6},{5,7},{6,4},{7,5},{8,10},{9,11},{10,... | collective-permute-start | bytes 1184264 | tf_op jit(solution)/shard_map/ppermute | solution.py:373
  19.3 11.4 %collective-permute-start.2 = (bf16[257,768]{1,0:T(8,128)(2,1)S(1)}, bf16[257,768]{1,0:T(8,128)(2,1)S(1)}, u32[]{:S(2)}, u32[]{:S(2)}) collective-permute-start(bf16[257,768]{1,0:T(8,128)(2,1)S(1)} %select.4.refs_2_.refs_4_.refs_1_.refs_3_), channel_id=1, source_target_pairs={{0,5},{1,4},{2,7},{3,6},{4,0},{5,1},{6,2},{7,3},{8,13},{9,12},{10,... | collective-permute-start | bytes 1184264 | tf_op jit(solution)/shard_map/ppermute | solution.py:396
  21.2 17.9 %collective-permute-start.5 = (bf16[264,768]{1,0:T(8,128)(2,1)S(1)}, bf16[264,768]{1,0:T(8,128)(2,1)S(1)}, u32[]{:S(2)}, u32[]{:S(2)}) collective-permute-start(bf16[264,768]{1,0:T(8,128)(2,1)S(1)} %get-tuple-element.238), channel_id=1, source_target_pairs={{0,24},{8,0},{16,8},{24,16},{1,25},{9,1},{17,9},{25,17},{2,26},{10... | collective-permute-start | bytes 1216520 | tf_op jit(solution)/shard_map/ppermute | solution.py:370
  31.4 7.8 %collective-permute-start.4 = (bf16[257,768]{1,0:T(8,128)(2,1)S(1)}, bf16[257,768]{1,0:T(8,128)(2,1)S(1)}, u32[]{:S(2)}, u32[]{:S(2)}) collective-permute-start(bf16[257,768]{1,0:T(8,128)(2,1)S(1)} %pack.5.refs_3_.refs_8_.refs_5_.refs_6_.refs_7_), channel_id=1, source_target_pairs={{0,1},{1,0},{2,3},{3,2},{4,5},{5,4},{6,7},{7,6},{8,9},{9,8},{10,11... | collective-permute-start | bytes 1184264 | tf_op jit(solution)/shard_map/ppermute | solution.py:373
  31.5 12.2 %collective-permute-start.7 = (bf16[257,768]{1,0:T(8,128)(2,1)S(1)}, bf16[257,768]{1,0:T(8,128)(2,1)S(1)}, u32[]{:S(2)}, u32[]{:S(2)}) collective-permute-start(bf16[257,768]{1,0:T(8,128)(2,1)S(1)} %pack.5.refs_3_.refs_8_.refs_5_.refs_6_.refs_7_), channel_id=1, source_target_pairs={{0,5},{1,4},{2,7},{3,6},{4,0},{5,1},{6,2},{7,3},{8,13},{9,12},{10,... | collective-permute-start | bytes 1184264 | tf_op jit(solution)/shard_map/ppermute | solution.py:396
  32.1 12.2 %collective-permute-start.8 = (bf16[257,768]{1,0:T(8,128)(2,1)S(1)}, bf16[257,768]{1,0:T(8,128)(2,1)S(1)}, u32[]{:S(2)}, u32[]{:S(2)}) collective-permute-start(bf16[257,768]{1,0:T(8,128)(2,1)S(1)} %pack.5.refs_3_.refs_8_.refs_5_.refs_6_.refs_7_), channel_id=1, source_target_pairs={{0,2},{1,3},{2,0},{3,1},{4,6},{5,7},{6,4},{7,5},{8,10},{9,11},{10,... | collective-permute-start | bytes 1184264 | tf_op jit(solution)/shard_map/ppermute | solution.py:373
  33.0 19.7 %collective-permute-start.6 = (bf16[136,768]{1,0:T(8,128)(2,1)S(1)}, bf16[136,768]{1,0:T(8,128)(2,1)S(1)}, u32[]{:S(2)}, u32[]{:S(2)}) collective-permute-start(bf16[136,768]{1,0:T(8,128)(2,1)S(1)} %get-tuple-element.249), channel_id=1, source_target_pairs={{0,16},{8,24},{16,0},{24,8},{1,17},{9,25},{17,1},{25,9},{2,18},{10... | collective-permute-start | bytes 626696 | tf_op jit(solution)/shard_map/ppermute | solution.py:370
  39.2 15.5 %collective-permute-start.10 = (bf16[257,768]{1,0:T(8,128)(2,1)S(1)}, bf16[257,768]{1,0:T(8,128)(2,1)S(1)}, u32[]{:S(2)}, u32[]{:S(2)}) collective-permute-start(bf16[257,768]{1,0:T(8,128)(2,1)S(1)} %pack.6.refs_2_.refs_9_.refs_10_.refs_11_.refs_0_), channel_id=1, source_target_pairs={{0,5},{1,4},{2,7},{3,6},{4,0},{5,1},{6,2},{7,3},{8,13},{9,12},{10,... | collective-permute-start | bytes 1184264 | tf_op jit(solution)/shard_map/ppermute | solution.py:396
  39.4 15.3 %collective-permute-start.11 = (bf16[257,768]{1,0:T(8,128)(2,1)S(1)}, bf16[257,768]{1,0:T(8,128)(2,1)S(1)}, u32[]{:S(2)}, u32[]{:S(2)}) collective-permute-start(bf16[257,768]{1,0:T(8,128)(2,1)S(1)} %pack.6.refs_2_.refs_9_.refs_10_.refs_11_.refs_0_), channel_id=1, source_target_pairs={{0,2},{1,3},{2,0},{3,1},{4,6},{5,7},{6,4},{7,5},{8,10},{9,11},{10,... | collective-permute-start | bytes 1184264 | tf_op jit(solution)/shard_map/ppermute | solution.py:373
  43.7 13.4 %collective-permute-start.9 = (bf16[136,768]{1,0:T(8,128)(2,1)S(1)}, bf16[136,768]{1,0:T(8,128)(2,1)S(1)}, u32[]{:S(2)}, u32[]{:S(2)}) collective-permute-start(bf16[136,768]{1,0:T(8,128)(2,1)S(1)} %get-tuple-element.267), channel_id=1, source_target_pairs={{0,16},{8,24},{16,0},{24,8},{1,17},{9,25},{17,1},{25,9},{2,18},{10... | collective-permute-start | bytes 626696 | tf_op jit(solution)/shard_map/ppermute | solution.py:370
  52.7 7.6 %collective-permute-start.13 = (bf16[129,768]{1,0:T(8,128)(2,1)S(1)}, bf16[129,768]{1,0:T(8,128)(2,1)S(1)}, u32[]{:S(2)}, u32[]{:S(2)}) collective-permute-start(bf16[129,768]{1,0:T(8,128)(2,1)S(1)} %pack.7.refs_0_.refs_11_.refs_14_.refs_1_.refs_12_), channel_id=1, source_target_pairs={{0,5},{1,4},{2,7},{3,6},{4,0},{5,1},{6,2},{7,3},{8,13},{9,12},{10,... | collective-permute-start | bytes 594440 | tf_op jit(solution)/shard_map/ppermute | solution.py:396
  52.8 7.7 %collective-permute-start.14 = (bf16[129,768]{1,0:T(8,128)(2,1)S(1)}, bf16[129,768]{1,0:T(8,128)(2,1)S(1)}, u32[]{:S(2)}, u32[]{:S(2)}) collective-permute-start(bf16[129,768]{1,0:T(8,128)(2,1)S(1)} %pack.7.refs_0_.refs_11_.refs_14_.refs_1_.refs_12_), channel_id=1, source_target_pairs={{0,2},{1,3},{2,0},{3,1},{4,6},{5,7},{6,4},{7,5},{8,10},{9,11},{10,... | collective-permute-start | bytes 594440 | tf_op jit(solution)/shard_map/ppermute | solution.py:373
  57.1 7.4 %collective-permute-start.12 = (bf16[129,768]{1,0:T(8,128)(2,1)S(1)}, bf16[129,768]{1,0:T(8,128)(2,1)S(1)}, u32[]{:S(2)}, u32[]{:S(2)}) collective-permute-start(bf16[129,768]{1,0:T(8,128)(2,1)S(1)} %pack.8.refs_1_.refs_2_.refs_13_.refs_5_.refs_6_), channel_id=1, source_target_pairs={{0,5},{1,4},{2,7},{3,6},{4,0},{5,1},{6,2},{7,3},{8,13},{9,12},{10,... | collective-permute-start | bytes 594440 | tf_op jit(solution)/shard_map/ppermute | solution.py:396
  57.8 7.9 %collective-permute-start.16 = (bf16[129,768]{1,0:T(8,128)(2,1)S(1)}, bf16[129,768]{1,0:T(8,128)(2,1)S(1)}, u32[]{:S(2)}, u32[]{:S(2)}) collective-permute-start(bf16[129,768]{1,0:T(8,128)(2,1)S(1)} %pack.8.refs_1_.refs_2_.refs_13_.refs_5_.refs_6_), channel_id=1, source_target_pairs={{0,2},{1,3},{2,0},{3,1},{4,6},{5,7},{6,4},{7,5},{8,10},{9,11},{10,... | collective-permute-start | bytes 594440 | tf_op jit(solution)/shard_map/ppermute | solution.py:373
  59.4 3.0 %collective-permute-start.15 = (bf16[515,768]{1,0:T(8,128)(2,1)S(1)}, bf16[515,768]{1,0:T(8,128)(2,1)S(1)}, u32[]{:S(2)}, u32[]{:S(2)}) collective-permute-start(bf16[515,768]{1,0:T(8,128)(2,1)S(1)} %pack.9), channel_id=1, source_target_pairs={{0,1},{1,0},{2,3},{3,2},{4,5},{5,4},{6,7},{7,6},{8,9},{9,8},{10,11... | collective-permute-start | bytes 2373128 | tf_op jit(solution)/shard_map/ppermute | solution.py:373
  65.1 9.3 %copy-start = (s32[2,1024]{1,0:T(2,128)S(1)}, s32[2,1024]{1,0:T(2,128)}, u32[]{:S(2)}) copy-start(s32[2,1024]{1,0:T(2,128)} %get-tuple-element.226.home_ref) | copy-start | bytes 24580
